TPU v7x, 128 devices: a whole 4x4x4 slice. The times are simulated.
128 devices in a mesh: frame: 16 (over z_lo, x, core), head: 8 (over z_hi, y).
Axes of the slice: x: 4, y: 4, z: 4 (z_hi: 2, z_lo: 2; z = z_hi * 2 + z_lo), core: 2. Of those that a mesh axis runs over, the one named last changes fastest.
Arguments:
- query_in: bfloat16 [16384, 5120], P(('frame', 'head')), may hold values from -9 to 9
- key_in: bfloat16 [16384, 5120], P(('frame', 'head')), may hold values from -5 to 5
- value_in: bfloat16 [16384, 5120], P(('frame', 'head')), may hold values from -6 to 6
- out_grad: bfloat16 [16384, 5120], P(('frame', 'head')), may hold values from -6 to 6
- key_blocks: int32 [40, 128, 12], P('head', 'frame'), may hold values from 0 to 127, as said below
- block_count: int32 [40, 128], P('head', 'frame'), may hold values from 1 to 12
Outputs:
- query_grad: bfloat16 [16384, 5120], P(('frame', 'head'))
- key_grad: bfloat16 [16384, 5120], P(('frame', 'head'))
- value_grad: bfloat16 [16384, 5120], P(('frame', 'head'))
Inputs may be any that keep to these rules, and one draw needn't show every extreme that they name: `key_blocks`: for each head and query block b, the first block_count entries are distinct, include b itself, and name blocks whose run b // 8 differs from that of b by at most 2; later entries equal b.
All inputs are finite; a program needn't handle non-finite values.
Results may differ from a plain program's by a relative error of at most 0.017.
Values may be sent and summed in bfloat16 or wider, within the bound.
No kernel may reach another device: no remote copies, remote signals or barrier semaphores. Data moves between devices by JAX's collectives and lax.ppermute only.
A program may use at most 192 MiB of HBM per device.

v0:
```python
import jax
import jax.numpy as jnp
from jax import lax
from jax.sharding import PartitionSpec as P

HD = 128
BLK = 128
BAND = 2
BPD = 8
MAXK = 12


NEG_FILL = -1e30


def shifted(value, axis, steps):
    count = lax.axis_size(axis)
    leading, last = (max(0, -steps), min(count, count - steps))
    return lax.ppermute(value, axis, [(source, source + steps) for source in range(leading, last)])


def head_grads(query_blk, key_sel, value_sel, grad_blk, visible):
    scaling = query_blk.shape[-1] ** (-0.5)
    f32 = jnp.float32
    scores = jnp.einsum("qid,qmjd->qimj", query_blk, key_sel, preferred_element_type=f32) * scaling
    usable = visible[:, None, :, None]
    scores = jnp.where(usable, scores, NEG_FILL)
    row_max = jnp.max(scores, axis=(2, 3), keepdims=True)
    weights = jnp.where(usable, jnp.exp(scores - row_max), 0.0)
    row_sum = jnp.sum(weights, axis=(2, 3), keepdims=True)
    prob_full = weights / row_sum
    prob_half = prob_full.astype(jnp.bfloat16)
    attended = jnp.einsum("qimj,qmjd->qid", prob_half, value_sel, preferred_element_type=f32)
    row_dot = jnp.sum(grad_blk.astype(f32) * attended, axis=-1)[:, :, None, None]
    prob_grad = jnp.einsum("qid,qmjd->qimj", grad_blk, value_sel, preferred_element_type=f32)
    score_grad = (prob_full * (prob_grad - row_dot)).astype(jnp.bfloat16)
    grad_query = (
        jnp.einsum("qimj,qmjd->qid", score_grad, key_sel, preferred_element_type=f32) * scaling
    )
    grad_key = (
        jnp.einsum("qimj,qid->qmjd", score_grad, query_blk, preferred_element_type=f32) * scaling
    )
    grad_value = jnp.einsum("qimj,qid->qmjd", prob_half, grad_blk, preferred_element_type=f32)
    return (grad_query, grad_key, grad_value)


def band_fetch(stacked, offset):
    return shifted(stacked, "frame", -offset)


def shards(query_in, key_in, value_in, out_grad, key_blocks, block_count):
    queries, key_run, value_run, grad_run = (
        lax.all_to_all(query_in, "head", split_axis=1, concat_axis=0, tiled=True),
        lax.all_to_all(key_in, "head", split_axis=1, concat_axis=0, tiled=True),
        lax.all_to_all(value_in, "head", split_axis=1, concat_axis=0, tiled=True),
        lax.all_to_all(out_grad, "head", split_axis=1, concat_axis=0, tiled=True),
    )
    run_tokens = queries.shape[0]
    local_feat = queries.shape[1]
    local_heads = local_feat // HD
    nblocks = (2 * BAND + 1) * BPD
    stacked = jnp.stack([key_run, value_run])
    pieces = []
    for offset in range(-BAND, BAND + 1):
        if offset == 0:
            pieces.append(stacked)
        else:
            pieces.append(band_fetch(stacked, offset))
    banded = jnp.concatenate(pieces, axis=1)
    banded = jnp.transpose(banded.reshape(2, nblocks, BLK, local_heads, HD), (3, 0, 1, 2, 4))
    first_block = (lax.axis_index("frame") - BAND) * BPD
    block_ids = key_blocks - first_block

    def to_heads(array):
        return jnp.transpose(array.reshape(run_tokens, local_heads, HD), (1, 0, 2)).reshape(
            local_heads, BPD, BLK, HD
        )

    def per_head(members):
        query_h, grad_h, band_h, ids_h, counts_h = members
        visible = jnp.arange(MAXK, dtype=jnp.int32)[None, :] < counts_h[:, None]
        grad_query, grad_key, grad_value = head_grads(
            query_h, band_h[0][ids_h], band_h[1][ids_h], grad_h, visible
        )
        onehot = (
            ids_h.reshape(-1)[:, None] == jnp.arange(nblocks, dtype=jnp.int32)[None, :]
        ).astype(jnp.float32)
        summed_in = jnp.stack([grad_key, grad_value]).reshape(2, BPD * MAXK, BLK, HD)
        summed = jnp.einsum("sn,asjd->anjd", onehot, summed_in, precision=lax.Precision.HIGHEST)
        return (grad_query, summed)

    grad_query, partials = lax.map(
        per_head, (to_heads(queries), to_heads(grad_run), banded, block_ids, block_count)
    )
    partials = partials.reshape(local_heads, 2, 2 * BAND + 1, BPD, BLK, HD)

    def segment(distance):
        return partials[:, :, distance + BAND]

    collected = segment(0)
    for distance in range(-BAND, BAND + 1):
        if distance != 0:
            collected = collected + shifted(
                segment(distance).astype(jnp.bfloat16), "frame", distance
            ).astype(jnp.float32)

    def to_tokens(array):
        return (
            jnp.transpose(array.reshape(local_heads, run_tokens, HD), (1, 0, 2))
            .reshape(run_tokens, local_feat)
            .astype(jnp.bfloat16)
        )

    returned = (
        lax.all_to_all(to_tokens(grad_query), "head", split_axis=0, concat_axis=1, tiled=True),
        lax.all_to_all(to_tokens(collected[:, 0]), "head", split_axis=0, concat_axis=1, tiled=True),
        lax.all_to_all(to_tokens(collected[:, 1]), "head", split_axis=0, concat_axis=1, tiled=True),
    )
    return (returned[0], returned[1], returned[2])


def solution(mesh):
    return jax.shard_map(
        shards,
        mesh=mesh,
        in_specs=(
            P(("frame", "head"), None),
            P(("frame", "head"), None),
            P(("frame", "head"), None),
            P(("frame", "head"), None),
            P("head", "frame", None),
            P("head", "frame"),
        ),
        out_specs=(
            P(("frame", "head"), None),
            P(("frame", "head"), None),
            P(("frame", "head"), None),
        ),
        check_vma=False,
    )
```

profile of v0, /device:TPU:2, one launch (start us, length us, event | category | flops | bytes accessed | tf_op | source)
XLA Modules:
  0.0 643.0 jit_solution(3567615836064792214)
XLA Ops:
  0.6 2.5 copy.76
  3.2 7.8 %all-to-all-start.1 = ((bf16[128,8,640]{0,2,1:T(8,128)(2,1)}), bf16[128,8,640]{0,2,1:T(8,128)(2,1)S(1)}, u32[]{:S(2)}, u32[]{:S(2)}) async-start(bf16[128,8,640]{0,2,1:T(8,128)(2,1)} %bitcast.28), calls=%async_computation.1 | async-start | bytes 2621440 | tf_op jit(solution)/shard_map/all_to_all | solution.py:54
  12.4 18.6 %all-to-all-done.1 = bf16[128,8,640]{0,2,1:T(8,128)(2,1)S(1)} async-done(((bf16[128,8,640]{0,2,1:T(8,128)(2,1)}), bf16[128,8,640]{0,2,1:T(8,128)(2,1)S(1)}, u32[]{:S(2)}, u32[]{:S(2)}) %all-to-all-start.1) | async-done | bytes 1310752 | tf_op jit(solution)/shard_map/all_to_all | solution.py:54
  31.0 4.3 all-to-all-start.2
  36.0 19.4 %all-to-all-done.2 = bf16[128,8,640]{0,2,1:T(8,128)(2,1)} async-done(((bf16[128,8,640]{0,2,1:T(8,128)(2,1)}), bf16[128,8,640]{0,2,1:T(8,128)(2,1)}, u32[]{:S(2)}, u32[]{:S(2)}) %all-to-all-start.2) | async-done | bytes 1310752 | tf_op jit(solution)/shard_map/all_to_all | solution.py:55
  58.9 3.4 collective-permute-start
  66.6 4.3 all-to-all-start
  70.9 3.6 collective-permute-start.2
  77.0 2.5 copy.81
  79.4 12.6 %all-to-all-done = bf16[128,8,640]{0,2,1:T(8,128)(2,1)} async-done(((bf16[128,8,640]{0,2,1:T(8,128)(2,1)}), bf16[128,8,640]{0,2,1:T(8,128)(2,1)}, u32[]{:S(2)}, u32[]{:S(2)}) %all-to-all-start) | async-done | bytes 1310752 | tf_op jit(solution)/shard_map/all_to_all | solution.py:53
  92.0 4.3 all-to-all-start.3
  96.4 3.2 copy.75
  99.6 3.2 reshape.133
  105.2 11.7 %all-to-all-done.3 = bf16[128,8,640]{0,2,1:T(8,128)(2,1)} async-done(((bf16[128,8,640]{0,2,1:T(8,128)(2,1)}), bf16[128,8,640]{0,2,1:T(8,128)(2,1)}, u32[]{:S(2)}, u32[]{:S(2)}) %all-to-all-start.3) | async-done | bytes 1310752 | tf_op jit(solution)/shard_map/all_to_all | solution.py:56
  116.9 3.2 copy.82
  120.1 3.2 reshape.136
  125.8 3.5 constant_dynamic-update-slice_fusion.4
  129.3 18.4 %collective-permute-done.1 = bf16[2,1024,640]{2,1,0:T(8,128)(2,1)} collective-permute-done((bf16[2,1024,640]{2,1,0:T(8,128)(2,1)}, bf16[2,1024,640]{2,1,0:T(8,128)(2,1)}, u32[]{:S(2)}, u32[]{:S(2)}) %collective-permute-start.1) | collective-permute-done | bytes 2621472 | tf_op jit(solution)/shard_map/ppermute | solution.py:19
  147.6 3.5 constant_dynamic-update-slice_fusion.3
  152.8 3.5 constant_dynamic-update-slice_fusion.1
  156.3 5.6 collective-permute-done.3
  161.9 3.4 constant_dynamic-update-slice_fusion
  165.3 17.6 %copy.80 = bf16[2,5120,640]{1,2,0:T(8,128)(2,1)} copy(bf16[2,5120,640]{2,1,0:T(8,128)(2,1)} %constant_dynamic-update-slice_fusion) | data formatting | bytes 26214400 | tf_op jit(solution)/shard_map/concatenate | solution.py:69
  182.9 11.8 %copy.120 = bf16[160,8,40,128]{3,2,1,0:T(8,128)(2,1)} copy(bf16[160,8,40,128]{3,1,2,0:T(8,128)(2,1)} %bitcast.207) | data formatting | bytes 26214400
  194.7 230.8 %while.12 = (s32[]{:T(128)}, bf16[5,8,128,128]{3,2,1,0:T(8,128)(2,1)}, f32[5,2,40,128,128]{4,2,3,1,0:T(8,128)}, s32[5,8]{1,0:T(8,128)}, bf16[5,8,128,128]{3,2,1,...) while((s32[]{:T(128)}, ...), condition=%wide.region_4.5_spmd, body=%wide.region_0.4_spmd.sunk | while | flops 3975153920 | bytes 151837488 | solution.py:92
  215.6 2.5 gather_fusion.1
  218.1 4.1 gather_fusion
  235.0 3.6 copy.141
  240.6 3.6 copy.142
  244.2 7.9 %bitcast_dynamic-update-slice_fusion.2 = f32[5,2,40,128,128]{4,2,3,1,0:T(8,128)} fusion(f32[5,2,40,128,128]{4,2,3,1,0:T(8,128)} %get-tuple-element.180, s32[]{:T(128)S(6)} %copy.152, f32[1,96,128,128]{3,1,2,0:T(8,128)S(1)} %copy.141, f32[1,96,128,128]{3,1,2,0:T(8,128)S(1)} %copy.142, s32[96]{0:T(128)S(1)} %eq.34), kind=kOutput, calls=%fused_computation.10.clone.1 | convolution fusion | flops 1513099008 | bytes 17826180 | tf_op jit(solution)/shard_map/while/body/eval_jaxpr/sn,asjd->anjd/dot_general | solution.py:89
  259.0 2.5 gather_fusion.1
  261.5 4.1 gather_fusion
  278.4 3.6 copy.141
  284.0 3.6 copy.142
  287.6 7.9 %bitcast_dynamic-update-slice_fusion.2 = f32[5,2,40,128,128]{4,2,3,1,0:T(8,128)} fusion(f32[5,2,40,128,128]{4,2,3,1,0:T(8,128)} %get-tuple-element.180, s32[]{:T(128)S(6)} %copy.152, f32[1,96,128,128]{3,1,2,0:T(8,128)S(1)} %copy.141, f32[1,96,128,128]{3,1,2,0:T(8,128)S(1)} %copy.142, s32[96]{0:T(128)S(1)} %eq.34), kind=kOutput, calls=%fused_computation.10.clone.1 | convolution fusion | flops 1513099008 | bytes 17826180 | tf_op jit(solution)/shard_map/while/body/eval_jaxpr/sn,asjd->anjd/dot_general | solution.py:89
  302.4 2.5 gather_fusion.1
  304.9 4.1 gather_fusion
  321.8 3.6 copy.141
  327.4 3.6 copy.142
  331.0 7.8 %bitcast_dynamic-update-slice_fusion.2 = f32[5,2,40,128,128]{4,2,3,1,0:T(8,128)} fusion(f32[5,2,40,128,128]{4,2,3,1,0:T(8,128)} %get-tuple-element.180, s32[]{:T(128)S(6)} %copy.152, f32[1,96,128,128]{3,1,2,0:T(8,128)S(1)} %copy.141, f32[1,96,128,128]{3,1,2,0:T(8,128)S(1)} %copy.142, s32[96]{0:T(128)S(1)} %eq.34), kind=kOutput, calls=%fused_computation.10.clone.1 | convolution fusion | flops 1513099008 | bytes 17826180 | tf_op jit(solution)/shard_map/while/body/eval_jaxpr/sn,asjd->anjd/dot_general | solution.py:89
  345.7 2.5 gather_fusion.1
  348.2 4.1 gather_fusion
  365.1 3.6 copy.141
  370.7 3.6 copy.142
  374.3 7.8 %bitcast_dynamic-update-slice_fusion.2 = f32[5,2,40,128,128]{4,2,3,1,0:T(8,128)} fusion(f32[5,2,40,128,128]{4,2,3,1,0:T(8,128)} %get-tuple-element.180, s32[]{:T(128)S(6)} %copy.152, f32[1,96,128,128]{3,1,2,0:T(8,128)S(1)} %copy.141, f32[1,96,128,128]{3,1,2,0:T(8,128)S(1)} %copy.142, s32[96]{0:T(128)S(1)} %eq.34), kind=kOutput, calls=%fused_computation.10.clone.1 | convolution fusion | flops 1513099008 | bytes 17826180 | tf_op jit(solution)/shard_map/while/body/eval_jaxpr/sn,asjd->anjd/dot_general | solution.py:89
  389.0 2.5 gather_fusion.1
  391.5 4.1 gather_fusion
  408.4 3.6 copy.141
  414.0 3.6 copy.142
  417.6 7.9 %bitcast_dynamic-update-slice_fusion.2 = f32[5,2,40,128,128]{4,2,3,1,0:T(8,128)} fusion(f32[5,2,40,128,128]{4,2,3,1,0:T(8,128)} %get-tuple-element.180, s32[]{:T(128)S(6)} %copy.152, f32[1,96,128,128]{3,1,2,0:T(8,128)S(1)} %copy.141, f32[1,96,128,128]{3,1,2,0:T(8,128)S(1)} %copy.142, s32[96]{0:T(128)S(1)} %eq.34), kind=kOutput, calls=%fused_computation.10.clone.1 | convolution fusion | flops 1513099008 | bytes 17826180 | tf_op jit(solution)/shard_map/while/body/eval_jaxpr/sn,asjd->anjd/dot_general | solution.py:89
  425.5 14.5 %copy.88 = bf16[5,2,40,128,128]{4,3,2,1,0:T(8,128)(2,1)S(1)} copy(f32[5,2,40,128,128]{4,2,3,1,0:T(8,128)} %get-tuple-element.47) | data formatting | bytes 39321600 | tf_op jit(solution)/shard_map/while | solution.py:92
  440.0 5.1 slice_bitcast_fusion.3
  445.1 50.3 %collective-permute-start.4 = (bf16[5,2,8,128,128]{4,3,2,1,0:T(8,128)(2,1)}, bf16[5,2,8,128,128]{4,3,2,1,0:T(8,128)(2,1)}, u32[]{:S(2)}, u32[]{:S(2)}) collective-permute-start(bf16[5,2,8,128,128]{4,3,2,1,0:T(8,128)(2,1)} %get-tuple-element.100), channel_id=1, source_target_pairs={{16,0},{24,8},{32,16},{40,24},{48,32},{56,40},{64,48},{72,56},{80,... | collective-permute-start | bytes 7864328 | tf_op jit(solution)/shard_map/ppermute | solution.py:19
  499.2 4.2 collective-permute-start.5
  505.7 4.3 all-to-all-start.4
  510.0 2.9 slice.46
  512.8 38.9 %collective-permute-done.4 = bf16[5,2,8,128,128]{4,3,2,1,0:T(8,128)(2,1)} collective-permute-done((bf16[5,2,8,128,128]{4,3,2,1,0:T(8,128)(2,1)}, bf16[5,2,8,128,128]{4,3,2,1,0:T(8,128)(2,1)}, u32[]{:S(2)}, u32[]{:S(2)}) %collective-permute-start.4) | collective-permute-done | bytes 2621472 | tf_op jit(solution)/shard_map/ppermute | solution.py:19
  551.7 5.7 collective-permute-done.7
  557.4 26.5 %collective-permute-done.6 = bf16[5,2,8,128,128]{4,3,2,1,0:T(8,128)(2,1)} collective-permute-done((bf16[5,2,8,128,128]{4,3,2,1,0:T(8,128)(2,1)}, bf16[5,2,8,128,128]{4,3,2,1,0:T(8,128)(2,1)}, u32[]{:S(2)}, u32[]{:S(2)}) %collective-permute-start.6) | collective-permute-done | bytes 2621472 | tf_op jit(solution)/shard_map/ppermute | solution.py:19
  583.9 7.0 %fusion.49 = bf16[5,2,8,128,128]{4,3,2,1,0:T(8,128)(2,1)S(1)} fusion(f32[5,2,1,8,128,128]{5,3,2,4,1,0:T(8,128)S(1)} %slice.46, bf16[5,2,8,128,128]{4,3,2,1,0:T(8,128)(2,1)} %collective-permute-done.7, bf16[5,2,8,128,128]{4,3,2,1,0:T(8,128)(2,1)} %collective-permute-done.6, bf16[5,2,8,128,128]{4,3,2,1,0:T(8,128)(2,1)} %collective-permute-done.5, ...), kind=kLoop, calls=%fused_computation.55 | loop fusion | flops 11796480 | bytes 18350080 | tf_op jit(solution)/shard_map/convert.1
  595.6 3.6 all-to-all-start.5
  603.6 13.9 %all-to-all-done.5 = bf16[8,128,640]{1,2,0:T(8,128)(2,1)S(1)} async-done(((bf16[8,128,640]{1,2,0:T(8,128)(2,1)}), bf16[8,128,640]{1,2,0:T(8,128)(2,1)S(1)}, u32[]{:S(2)}, u32[]{:S(2)}) %all-to-all-start.5) | async-done | bytes 1310752 | tf_op jit(solution)/shard_map/all_to_all | solution.py:116
  617.5 3.6 all-to-all-start.6
  625.0 16.2 %all-to-all-done.6 = bf16[8,128,640]{1,2,0:T(8,128)(2,1)S(1)} async-done(((bf16[8,128,640]{1,2,0:T(8,128)(2,1)}), bf16[8,128,640]{1,2,0:T(8,128)(2,1)S(1)}, u32[]{:S(2)}, u32[]{:S(2)}) %all-to-all-start.6) | async-done | bytes 1310752 | tf_op jit(solution)/shard_map/all_to_all | solution.py:117
  (138 shorter events, 147.6 us)
Async XLA Ops:
  0.6 10.3 %copy-start.1 = (bf16[128,5120]{1,0:T(8,128)(2,1)S(1)}, bf16[128,5120]{1,0:T(8,128)(2,1)}, u32[]{:S(2)}) copy-start(bf16[128,5120]{1,0:T(8,128)(2,1)} %param.10) | copy-start | bytes 3932164
  3.2 27.8 %all-to-all-start.1 = ((bf16[128,8,640]{0,2,1:T(8,128)(2,1)}), bf16[128,8,640]{0,2,1:T(8,128)(2,1)S(1)}, u32[]{:S(2)}, u32[]{:S(2)}) async-start(bf16[128,8,640]{0,2,1:T(8,128)(2,1)} %bitcast.28), calls=%async_computation.1 | async-start | bytes 2621440 | tf_op jit(solution)/shard_map/all_to_all | solution.py:54
  31.0 24.4 %all-to-all-start.2 = ((bf16[128,8,640]{0,2,1:T(8,128)(2,1)}), bf16[128,8,640]{0,2,1:T(8,128)(2,1)}, u32[]{:S(2)}, u32[]{:S(2)}) async-start(bf16[128,8,640]{0,2,1:T(8,128)(2,1)} %bitcast.31), calls=%async_computation.2 | async-start | bytes 2621440 | tf_op jit(solution)/shard_map/all_to_all | solution.py:55
  58.9 66.9 %collective-permute-start = (bf16[2,1024,640]{2,1,0:T(8,128)(2,1)}, bf16[2,1024,640]{2,1,0:T(8,128)(2,1)}, u32[]{:S(2)}, u32[]{:S(2)}) collective-permute-start(bf16[2,1024,640]{2,1,0:T(8,128)(2,1)} %pad_maximum_fusion), channel_id=1, source_target_pairs={{0,16},{8,24},{16,32},{24,40},{32,48},{40,56},{48,64},{56,72},{64,... | collective-permute-start | bytes 7864328 | tf_op jit(solution)/shard_map/ppermute | solution.py:19
  62.3 85.3 %collective-permute-start.1 = (bf16[2,1024,640]{2,1,0:T(8,128)(2,1)}, bf16[2,1024,640]{2,1,0:T(8,128)(2,1)}, u32[]{:S(2)}, u32[]{:S(2)}) collective-permute-start(bf16[2,1024,640]{2,1,0:T(8,128)(2,1)} %pad_maximum_fusion), channel_id=1, source_target_pairs={{0,8},{8,16},{16,24},{24,32},{32,40},{40,48},{48,56},{56,64},{64,7... | collective-permute-start | bytes 7864328 | tf_op jit(solution)/shard_map/ppermute | solution.py:19
  66.6 25.4 %all-to-all-start = ((bf16[128,8,640]{0,2,1:T(8,128)(2,1)}), bf16[128,8,640]{0,2,1:T(8,128)(2,1)}, u32[]{:S(2)}, u32[]{:S(2)}) async-start(bf16[128,8,640]{0,2,1:T(8,128)(2,1)} %bitcast.221), calls=%async_computation | async-start | bytes 2621440 | tf_op jit(solution)/shard_map/all_to_all | solution.py:53
  70.9 25.4 %copy-start.4 = (s32[5,8,12]{2,1,0:T(8,128)S(1)}, s32[5,8,12]{2,1,0:T(8,128)}, u32[]{:S(2)}) copy-start(s32[5,8,12]{2,1,0:T(8,128)} %param.12) | copy-start | bytes 5764
  70.9 81.9 %collective-permute-start.2 = (bf16[2,1024,640]{2,1,0:T(8,128)(2,1)}, bf16[2,1024,640]{2,1,0:T(8,128)(2,1)}, u32[]{:S(2)}, u32[]{:S(2)}) collective-permute-start(bf16[2,1024,640]{2,1,0:T(8,128)(2,1)} %pad_maximum_fusion), channel_id=1, source_target_pairs={{8,0},{16,8},{24,16},{32,24},{40,32},{48,40},{56,48},{64,56},{72,6... | collective-permute-start | bytes 7864328 | tf_op jit(solution)/shard_map/ppermute | solution.py:19
  74.6 87.3 %collective-permute-start.3 = (bf16[2,1024,640]{2,1,0:T(8,128)(2,1)}, bf16[2,1024,640]{2,1,0:T(8,128)(2,1)}, u32[]{:S(2)}, u32[]{:S(2)}) collective-permute-start(bf16[2,1024,640]{2,1,0:T(8,128)(2,1)} %pad_maximum_fusion), channel_id=1, source_target_pairs={{16,0},{24,8},{32,16},{40,24},{48,32},{56,40},{64,48},{72,56},{80,... | collective-permute-start | bytes 7864328 | tf_op jit(solution)/shard_map/ppermute | solution.py:19
  92.0 24.9 %all-to-all-start.3 = ((bf16[128,8,640]{0,2,1:T(8,128)(2,1)}), bf16[128,8,640]{0,2,1:T(8,128)(2,1)}, u32[]{:S(2)}, u32[]{:S(2)}) async-start(bf16[128,8,640]{0,2,1:T(8,128)(2,1)} %bitcast.218), calls=%async_computation.3 | async-start | bytes 2621440 | tf_op jit(solution)/shard_map/all_to_all | solution.py:56
  224.1 1.9 copy-start
  224.1 2.3 copy-start.2
  267.5 1.9 copy-start
  267.5 2.3 copy-start.2
  310.9 1.9 copy-start
  310.9 2.3 copy-start.2
  354.2 1.9 copy-start
  354.2 2.3 copy-start.2
  397.5 1.9 copy-start
  397.5 2.3 copy-start.2
  440.0 63.4 %copy-start.3 = (bf16[5,8,128,128]{3,2,1,0:T(8,128)(2,1)S(1)}, bf16[5,8,128,128]{3,2,1,0:T(8,128)(2,1)}, u32[]{:S(2)}) copy-start(bf16[5,8,128,128]{3,2,1,0:T(8,128)(2,1)} %get-tuple-element.46) | copy-start | bytes 3932164
  445.1 106.6 %collective-permute-start.4 = (bf16[5,2,8,128,128]{4,3,2,1,0:T(8,128)(2,1)}, bf16[5,2,8,128,128]{4,3,2,1,0:T(8,128)(2,1)}, u32[]{:S(2)}, u32[]{:S(2)}) collective-permute-start(bf16[5,2,8,128,128]{4,3,2,1,0:T(8,128)(2,1)} %get-tuple-element.100), channel_id=1, source_target_pairs={{16,0},{24,8},{32,16},{40,24},{48,32},{56,40},{64,48},{72,56},{80,... | collective-permute-start | bytes 7864328 | tf_op jit(solution)/shard_map/ppermute | solution.py:19
  495.4 62.0 %collective-permute-start.7 = (bf16[5,2,8,128,128]{4,3,2,1,0:T(8,128)(2,1)}, bf16[5,2,8,128,128]{4,3,2,1,0:T(8,128)(2,1)}, u32[]{:S(2)}, u32[]{:S(2)}) collective-permute-start(bf16[5,2,8,128,128]{4,3,2,1,0:T(8,128)(2,1)} %get-tuple-element.101), channel_id=1, source_target_pairs={{0,16},{8,24},{16,32},{24,40},{32,48},{40,56},{48,64},{56,72},{64,... | collective-permute-start | bytes 7864328 | tf_op jit(solution)/shard_map/ppermute | solution.py:19
  497.3 86.6 %collective-permute-start.6 = (bf16[5,2,8,128,128]{4,3,2,1,0:T(8,128)(2,1)}, bf16[5,2,8,128,128]{4,3,2,1,0:T(8,128)(2,1)}, u32[]{:S(2)}, u32[]{:S(2)}) collective-permute-start(bf16[5,2,8,128,128]{4,3,2,1,0:T(8,128)(2,1)} %get-tuple-element.102), channel_id=1, source_target_pairs={{0,8},{8,16},{16,24},{24,32},{32,40},{40,48},{48,56},{56,64},{64,7... | collective-permute-start | bytes 7864328 | tf_op jit(solution)/shard_map/ppermute | solution.py:19
  499.2 84.7 %collective-permute-start.5 = (bf16[5,2,8,128,128]{4,3,2,1,0:T(8,128)(2,1)}, bf16[5,2,8,128,128]{4,3,2,1,0:T(8,128)(2,1)}, u32[]{:S(2)}, u32[]{:S(2)}) collective-permute-start(bf16[5,2,8,128,128]{4,3,2,1,0:T(8,128)(2,1)} %get-tuple-element.103), channel_id=1, source_target_pairs={{8,0},{16,8},{24,16},{32,24},{40,32},{48,40},{56,48},{64,56},{72,6... | collective-permute-start | bytes 7864328 | tf_op jit(solution)/shard_map/ppermute | solution.py:19
  505.7 90.0 %all-to-all-start.4 = ((bf16[8,128,640]{1,2,0:T(8,128)(2,1)}), bf16[8,128,640]{1,2,0:T(8,128)(2,1)}, u32[]{:S(2)}, u32[]{:S(2)}) async-start(bf16[8,128,640]{1,2,0:T(8,128)(2,1)} %copy.87), calls=%async_computation.4 | async-start | bytes 2621440 | tf_op jit(solution)/shard_map/all_to_all | solution.py:115
  595.6 21.9 %all-to-all-start.5 = ((bf16[8,128,640]{1,2,0:T(8,128)(2,1)}), bf16[8,128,640]{1,2,0:T(8,128)(2,1)S(1)}, u32[]{:S(2)}, u32[]{:S(2)}) async-start(bf16[8,128,640]{1,2,0:T(8,128)(2,1)} %copy.94), calls=%async_computation.5 | async-start | bytes 2621440 | tf_op jit(solution)/shard_map/all_to_all | solution.py:116
  617.5 23.6 %all-to-all-start.6 = ((bf16[8,128,640]{1,2,0:T(8,128)(2,1)}), bf16[8,128,640]{1,2,0:T(8,128)(2,1)S(1)}, u32[]{:S(2)}, u32[]{:S(2)}) async-start(bf16[8,128,640]{1,2,0:T(8,128)(2,1)} %copy.96), calls=%async_computation.6 | async-start | bytes 2621440 | tf_op jit(solution)/shard_map/all_to_all | solution.py:117
where the time goes:
time: 652 us; the launch traced here: 643 us
  local copies, waits for them, and re-layouts  216 us (33%)
  waiting for transfers between devices  187 us (29%)
  starting transfers between devices  102 us (16%)
  matrix products  102 us (16%)
  other arithmetic  20.4 us (3%)
  loops' own time  14.4 us (2%)
    ppermute x8, waiting for transfers between devices, shifted(): lax.ppermute(value, axis, [(source, source + steps) for source in range(l...  95 us
    ppermute x8, starting transfers between devices, shifted(): lax.ppermute(value, axis, [(source, source + steps) for source in range(l...  69.6 us
    unnamed x20, local copies, waits for them, and re-layouts  40.1 us
    dot_general x5, matrix products, per_head(): jnp.einsum('sn,asjd->anjd', onehot, summed_in, precision=lax.Precision.HI...  39.2 us
    another operation x10, local copies, waits for them, and re-layouts, per_head(): jnp.stack([grad_key, grad_value]).reshape(2, BPD * MAXK, BLK, HD)  36.4 us
    concatenate x2, local copies, waits for them, and re-layouts, shards(): banded = jnp.concatenate(pieces, axis=1)  21.1 us
    while x30, local copies, waits for them, and re-layouts  20.6 us
    gather x5, local copies, waits for them, and re-layouts, per_head(): band_h[1][ids_h]  20.3 us
  transfers between devices with their start and end apart: 15, of which 11 were waited for; matrix products, arithmetic and copies ran while one was open for 10% of the time, Pallas kernels for 0%

commit v1 on v0

v1 whole, which is shorter than its diff:
```python
import jax
import jax.numpy as jnp
from jax import lax
from jax.experimental import pallas as pl
from jax.experimental.pallas import tpu as pltpu
from jax.sharding import PartitionSpec as P

HD = 128
BLK = 128
BAND = 2
BPD = 8
MAXK = 12
HPD = 5
CHUNKS = ((0, 5),)
GROUP = 4
NEG = -1e30
LOG2E = 1.4426950408889634
SCALE = HD**-0.5
F32 = jnp.float32
BF16 = jnp.bfloat16
NT = (((1,), (1,)), ((), ()))
NN = (((1,), (0,)), ((), ()))
TN = (((0,), (0,)), ((), ()))

M2, SIB, OWN, OUTER, P2 = range(5)
WINDOW = 5 * BPD


def dot(a, b, dims):
    return lax.dot_general(a, b, dims, preferred_element_type=F32)


def fold(x):
    return x.reshape(-1, 8, HD)


def query_block(n_keys, h, b, ids_ref, count, qd, kv, acc, dq, kcat, s_scr, dp_scr, ds_scr):
    q = qd[h, b, 0]
    do = qd[h, b, 1]
    base = (h * BPD + b) * MAXK
    m8 = jnp.full((8, HD), NEG, F32)
    index = [ids_ref[base + s] for s in range(n_keys)]
    for s in range(n_keys):
        k = kv[h, index[s], 0]
        kcat[pl.ds(s * BLK, BLK), :] = k
        st = dot(k, q, NT)
        if s > n_keys - GROUP:
            st = jnp.where(s < count, st, NEG)
        s_scr[s] = st
        m8 = jnp.maximum(m8, jnp.max(fold(st), axis=0))
        dp_scr[s] = dot(kv[h, index[s], 1], do, NT)
    m = jnp.max(m8, axis=0, keepdims=True) * (SCALE * LOG2E)
    l8 = jnp.zeros((8, HD), F32)
    r8 = jnp.zeros((8, HD), F32)
    for s in range(n_keys):
        p = jnp.exp2(s_scr[s] * (SCALE * LOG2E) - m)
        s_scr[s] = p
        l8 += jnp.sum(fold(p), axis=0)
        r8 += jnp.sum(fold(p * dp_scr[s]), axis=0)
    inv = 1.0 / jnp.sum(l8, axis=0, keepdims=True)
    rd = jnp.sum(r8, axis=0, keepdims=True) * inv
    for s in range(n_keys):
        p = s_scr[s] * inv
        ds = (p * (dp_scr[s] - rd)).astype(BF16)
        ds_scr[pl.ds(s * BLK, BLK), :] = ds
        acc[index[s], 0] += dot(ds, q, NN)
        acc[index[s], 1] += dot(p.astype(BF16), do, NN)
    rows = pl.ds(0, n_keys * BLK)
    dq[h, b] = (dot(ds_scr[rows, :], kcat[rows, :], TN) * SCALE).astype(BF16)


def attention_kernel(
    n, ids_ref, cnt_ref, m2_in, sib_in, own_in, outer_in, p2_in, qd_in,
    dq_out, m2_out, sx_out, own_out, p2_out,
    kv, qd, acc, stage, dq, kcat, s_scr, dp_scr, ds_scr, in_sem, out_sem, dq_sem,
):
    sources = (m2_in, sib_in, own_in, outer_in, p2_in)

    def fetch(h, i):
        if i == 5:
            return pltpu.make_async_copy(qd_in.at[:, h], qd.at[h], in_sem.at[h, 5])
        return pltpu.make_async_copy(
            sources[i].at[:, h], kv.at[h, pl.ds(i * BPD, BPD)], in_sem.at[h, i]
        )

    def put(h, i):
        slot = h % 2
        target = (m2_out, sx_out.at[0], own_out, sx_out.at[1], p2_out)[i]
        return pltpu.make_async_copy(
            stage.at[slot, pl.ds(i * BPD, BPD)], target.at[:, h], out_sem.at[slot, i]
        )

    for h in range(n):
        for i in range(6):
            fetch(h, i).start()
    for h in range(n):
        acc[...] = jnp.zeros_like(acc)
        for i in range(6):
            fetch(h, i).wait()

        def one(b, carry):
            count = cnt_ref[h * BPD + b]
            for upto in range(GROUP, MAXK + 1, GROUP):

                @pl.when((count > upto - GROUP) & (count <= upto))
                def _():
                    query_block(
                        upto, h, b, ids_ref, count, qd, kv, acc, dq, kcat, s_scr, dp_scr, ds_scr
                    )

            return carry

        lax.fori_loop(0, BPD, one, 0)
        if h >= 2:
            for i in range(5):
                put(h - 2, i).wait()

        def convert(i, carry):
            stage[h % 2, i, 0] = (acc[i, 0] * SCALE).astype(BF16)
            stage[h % 2, i, 1] = acc[i, 1].astype(BF16)
            return carry

        lax.fori_loop(0, WINDOW, convert, 0)
        for i in range(5):
            put(h, i).start()
        pltpu.make_async_copy(dq.at[h], dq_out.at[:, h], dq_sem.at[h]).start()
    for h in range(max(0, n - 2), n):
        for i in range(5):
            put(h, i).wait()
    for h in range(n):
        pltpu.make_async_copy(dq.at[h], dq_out.at[:, h], dq_sem.at[h]).wait()


def attention(ids, counts, m2, sib, own, outer, p2, qd):
    n = own.shape[1]
    block = jax.ShapeDtypeStruct((BPD, n, 2, BLK, HD), BF16)
    smem = pl.BlockSpec(memory_space=pltpu.SMEM)
    hbm = pl.BlockSpec(memory_space=pl.ANY)
    pairs = n * BPD * 8
    return pl.pallas_call(
        lambda *refs: attention_kernel(n, *refs),
        out_shape=(
            jax.ShapeDtypeStruct((BPD, n, BLK, HD), BF16),
            block,
            jax.ShapeDtypeStruct((2, BPD, n, 2, BLK, HD), BF16),
            block,
            block,
        ),
        in_specs=[smem, smem] + [hbm] * 6,
        out_specs=[hbm] * 5,
        scratch_shapes=[
            pltpu.VMEM((n, WINDOW, 2, BLK, HD), BF16),
            pltpu.VMEM((n, BPD, 2, BLK, HD), BF16),
            pltpu.VMEM((WINDOW, 2, BLK, HD), F32),
            pltpu.VMEM((2, WINDOW, 2, BLK, HD), BF16),
            pltpu.VMEM((n, BPD, BLK, HD), BF16),
            pltpu.VMEM((MAXK * BLK, HD), BF16),
            pltpu.VMEM((MAXK, BLK, HD), F32),
            pltpu.VMEM((MAXK, BLK, HD), F32),
            pltpu.VMEM((MAXK * BLK, HD), BF16),
            pltpu.SemaphoreType.DMA((n, 6)),
            pltpu.SemaphoreType.DMA((2, 5)),
            pltpu.SemaphoreType.DMA((n,)),
        ],
        compiler_params=pltpu.CompilerParams(vmem_limit_bytes=48 * 2**20),
        cost_estimate=pl.CostEstimate(
            flops=pairs * 10 * BLK * BLK * HD,
            bytes_accessed=n * 12 * BPD * 2 * BLK * HD * 2,
            transcendentals=pairs * BLK * BLK,
        ),
    )(ids, counts, m2, sib, own, outer, p2, qd)


def shift(value, axis, steps):
    count = lax.axis_size(axis)
    pairs = [(s, s + steps) for s in range(max(0, -steps), min(count, count - steps))]
    return lax.ppermute(value, axis, pairs)


def swap(value, senders=(0, 1)):
    count = lax.axis_size("frame")
    return lax.ppermute(value, "frame", [(s, s ^ 1) for s in range(count) if s % 2 in senders])


def exchange_in(first, second, lo, hi):
    def split(x):
        x = x.reshape(BLK, -1, HPD, HD)[:, :, lo:hi]
        return jnp.transpose(x, (1, 2, 0, 3))

    return lax.all_to_all(jnp.stack([split(first), split(second)], axis=2), "head", 0, 0)


def shards(query_in, key_in, value_in, out_grad, key_blocks, block_count):
    frame = lax.axis_index("frame")
    core = frame % 2
    rel = key_blocks - (frame - BAND) * BPD
    run = rel // BPD
    side = jnp.where(run == 1 + 2 * (1 - core), SIB, OUTER)
    role = jnp.where(run % 2 == 1, side, run)
    ids = role * BPD + rel % BPD

    results = []
    for lo, hi in CHUNKS:
        own = exchange_in(key_in, value_in, lo, hi)
        below = shift(own, "frame", 2)
        above = shift(own, "frame", -2)
        sib = swap(own)
        qd = exchange_in(query_in, out_grad, lo, hi)
        outer = jnp.where(core == 0, swap(below, (1,)), swap(above, (0,)))
        dq, m2, sx, mine, p2 = attention(
            ids[lo:hi].reshape(-1), block_count[lo:hi].reshape(-1), below, sib, own, outer, above, qd
        )
        sx = swap(sx)
        m2 = m2 + jnp.where(core == 1, sx[1], 0)
        p2 = p2 + jnp.where(core == 0, sx[1], 0)
        from_above = shift(m2, "frame", -2)
        from_below = shift(p2, "frame", 2)
        total = sum(x.astype(F32) for x in (mine, sx[0], from_above, from_below)).astype(BF16)
        dq = lax.all_to_all(dq, "head", 0, 0)
        total = lax.all_to_all(total, "head", 0, 0)
        results.append((dq, total[:, :, 0], total[:, :, 1]))

    def to_tokens(parts):
        whole = jnp.concatenate(parts, axis=1)
        return jnp.transpose(whole, (2, 0, 1, 3)).reshape(BLK, -1)

    return tuple(to_tokens([part[i] for part in results]) for i in range(3))


def solution(mesh):
    tokens = P(("frame", "head"), None)
    return jax.shard_map(
        shards,
        mesh=mesh,
        in_specs=(tokens, tokens, tokens, tokens, P("head", "frame", None), P("head", "frame")),
        out_specs=(tokens, tokens, tokens),
        check_vma=False,
    )
```

time: 652 us -> 380 us (0.58)
  the two profiles are of different devices: /device:TPU:2 before, /device:TPU:8 now
where the time goes in v1:
time: 380 us; the launch traced here: 377 us
  waiting for transfers between devices  184 us (48%)
  Pallas kernels  54.8 us (14%)
  starting transfers between devices  48.1 us (13%)
  blocking collectives  41.5 us (11%)
  local copies, waits for them, and re-layouts  28.4 us (7%)
  other arithmetic  19.3 us (5%)
    ppermute x4, waiting for transfers between devices, shift(): return lax.ppermute(value, axis, pairs)  96.7 us
    pallas_call x1, Pallas kernels, attention(): pl.pallas_call(lambda *refs: attention_kernel(n, *refs), out_shape=(jax.S...  54.8 us
    all_to_all x1, blocking collectives, exchange_in(): lax.all_to_all(jnp.stack([split(first), split(second)], axis=2), 'head',...  41.5 us
    all_to_all x1, waiting for transfers between devices, exchange_in(): lax.all_to_all(jnp.stack([split(first), split(second)], axis=2), 'head',...  32.9 us
    all_to_all x1, waiting for transfers between devices, shards(): total = lax.all_to_all(total, 'head', 0, 0)  30.4 us
    unnamed x21, local copies, waits for them, and re-layouts  16.4 us
    ppermute x4, starting transfers between devices, shift(): return lax.ppermute(value, axis, pairs)  15.8 us
    all_to_all x1, waiting for transfers between devices, shards(): dq = lax.all_to_all(dq, 'head', 0, 0)  15.2 us
  transfers between devices with their start and end apart: 11, of which 7 were waited for; matrix products, arithmetic and copies ran while one was open for 7% of the time, Pallas kernels for 0%

profile of v1, /device:TPU:8, one launch (start us, length us, event | category | flops | bytes accessed | tf_op | source)
XLA Modules:
  0.0 376.5 jit_solution(10863335488339445123)
XLA Ops:
  0.6 1.8 copy.9
  2.4 0.8 copy.10
  3.2 2.4 copy.11
  5.6 1.8 copy.12
  7.4 0.3 pad_maximum_fusion
  7.7 0.0 copy-start.4
  7.7 41.5 %all_to_all.20.refs_4_ = bf16[8,5,2,128,128]{4,3,2,1,0:T(8,128)(2,1)} all-to-all(bf16[8,5,2,128,128]{4,3,2,1,0:T(8,128)(2,1)S(1)} %pad_maximum_fusion), channel_id=1, replica_groups=mesh['frame'=16,'head'=8] {'head'}, dimensions={0} | all-to-all | bytes 5242880 | tf_op jit(solution)/shard_map/all_to_all | solution.py:190
  49.2 1.3 collective-permute-start.3
  50.5 6.1 %collective-permute-start = (bf16[8,5,2,128,128]{4,3,2,1,0:T(8,128)(2,1)}, bf16[8,5,2,128,128]{4,3,2,1,0:T(8,128)(2,1)}, u32[]{:S(2)}, u32[]{:S(2)}) collective-permute-start(bf16[8,5,2,128,128]{4,3,2,1,0:T(8,128)(2,1)} %all_to_all.20.refs_4_), channel_id=1, source_target_pairs={{0,16},{8,24},{16,32},{24,40},{32,48},{40,56},{48,64},{56,72},{64,... | collective-permute-start | bytes 7864328 | tf_op jit(solution)/shard_map/ppermute | solution.py:177
  56.6 52.2 %collective-permute-done.3.refs_6_ = bf16[8,5,2,128,128]{4,3,2,1,0:T(8,128)(2,1)} collective-permute-done((bf16[8,5,2,128,128]{4,3,2,1,0:T(8,128)(2,1)}, bf16[8,5,2,128,128]{4,3,2,1,0:T(8,128)(2,1)}, u32[]{:S(2)}, u32[]{:S(2)}) %collective-permute-start.3) | collective-permute-done | bytes 2621472 | tf_op jit(solution)/shard_map/ppermute | solution.py:177
  108.8 2.9 collective-permute-start.4
  111.7 0.0 collective-permute-done.refs_2_
  111.7 1.3 collective-permute-start.2
  113.0 2.6 collective-permute-start.1
  115.6 0.0 copy-done.4
  115.6 0.8 copy.13
  116.4 0.8 copy.14
  117.1 2.4 copy.15
  119.6 1.8 copy.16
  121.3 1.8 pad_maximum_fusion.1
  123.2 0.0 copy-start.6
  123.2 0.0 copy-start.5
  123.2 4.5 %all-to-all-start.1 = ((bf16[8,5,2,128,128]{4,3,2,1,0:T(8,128)(2,1)}), bf16[8,5,2,128,128]{4,3,2,1,0:T(8,128)(2,1)S(1)}, u32[]{:S(2)}, u32[]{:S(2)}) async-start(bf16[8,5,2,128,128]{4,3,2,1,0:T(8,128)(2,1)} %pad_maximum_fusion.1), calls=%async_computation.1 | async-start | bytes 5242880 | tf_op jit(solution)/shard_map/all_to_all | solution.py:190
  127.7 0.0 copy-done.6
  127.7 0.1 reshape.42.refs_1_
  127.8 0.0 copy-done.5
  127.8 0.1 reshape.41.refs_0_
  127.9 0.0 collective-permute-done.4
  127.9 0.0 collective-permute-done.2
  128.0 3.5 broadcast_select_fusion.refs_5_
  131.4 32.9 %all-to-all-done.1.refs_7_ = bf16[8,5,2,128,128]{4,3,2,1,0:T(8,128)(2,1)S(1)} async-done(((bf16[8,5,2,128,128]{4,3,2,1,0:T(8,128)(2,1)}), bf16[8,5,2,128,128]{4,3,2,1,0:T(8,128)(2,1)S(1)}, u32[]{:S(2)}, u32[]{:S(2)}) %all-to-all-start.1) | async-done | bytes 2621472 | tf_op jit(solution)/shard_map/all_to_all | solution.py:190
  164.3 0.0 copy-start.3
  164.3 1.6 copy-done.3
  165.8 0.0 collective-permute-done.1.refs_3_
  165.8 54.8 %shard_map.85 = (bf16[8,5,128,128]{3,2,1,0:T(8,128)(2,1)S(1)}, bf16[8,5,2,128,128]{4,3,2,1,0:T(8,128)(2,1)S(1)}, bf16[2,8,5,2,128,128]{5,4,3,2,1,0:T(8,128)(2,1)...) custom-call(s32[480]{0:T(512)S(1)} %reshape.41.refs_0_, s32[40]{0:T(128)S(1)} %reshape.42.refs_1_, ...), custom_call_target="tpu_custom_call" | custom-call | flops 6710886400 | bytes 31457280 | tf_op jit(solution)/shard_map/pallas_call | solution.py:140
  220.7 0.0 copy-start
  220.7 1.0 copy-done
  221.7 1.5 collective-permute-start.5
  223.2 8.6 %collective-permute-done.5 = bf16[2,8,5,2,128,128]{5,4,3,2,1,0:T(8,128)(2,1)} collective-permute-done((bf16[2,8,5,2,128,128]{5,4,3,2,1,0:T(8,128)(2,1)}, bf16[2,8,5,2,128,128]{5,4,3,2,1,0:T(8,128)(2,1)}, u32[]{:S(2)}, u32[]{:S(2)}) %collective-permute-start.5) | collective-permute-done | bytes 5242912 | tf_op jit(solution)/shard_map/ppermute | solution.py:182
  231.9 5.3 %bitcast_add_fusion.1 = (bf16[8,5,2,128,128]{4,3,2,1,0:T(8,128)(2,1)}, bf16[8,5,2,128,128]{4,3,2,1,0:T(8,128)(2,1)}) fusion(bf16[8,5,2,128,128]{4,3,2,1,0:T(8,128)(2,1)S(1)} %get-tuple-element.11, pred[]{:T(512)S(6)} %eq.26, bf16[2,8,5,2,128,128]{5,4,3,2,1,0:T(8,128)(2,1)} %collective-permute-done.5, bf16[8,5,2,128,128]{4,3,2,1,0:T(8,128)(2,1)} %get-tuple-element.12, ...), kind=kLoop, calls=%fused_computation.8 | loop fusion | flops 5242880 | bytes 13107202 | tf_op jit(solution)/shard_map/add | solution.py:214
  237.2 1.3 collective-permute-start.6
  238.5 7.1 %collective-permute-start.7 = (bf16[8,5,2,128,128]{4,3,2,1,0:T(8,128)(2,1)}, bf16[8,5,2,128,128]{4,3,2,1,0:T(8,128)(2,1)}, u32[]{:S(2)}, u32[]{:S(2)}) collective-permute-start(bf16[8,5,2,128,128]{4,3,2,1,0:T(8,128)(2,1)} %get-tuple-element.17), channel_id=1, source_target_pairs={{0,16},{8,24},{16,32},{24,40},{32,48},{40,56},{48,64},{56,72},{64,... | collective-permute-start | bytes 7864328 | tf_op jit(solution)/shard_map/ppermute | solution.py:177
  245.6 11.0 %all-to-all-start.2 = ((bf16[8,5,128,128]{3,2,1,0:T(8,128)(2,1)}), bf16[8,5,128,128]{3,2,1,0:T(8,128)(2,1)S(1)}, u32[]{:S(2)}, u32[]{:S(2)}) async-start(bf16[8,5,128,128]{3,2,1,0:T(8,128)(2,1)} %copy-done), calls=%async_computation.2 | async-start | bytes 2621440 | tf_op jit(solution)/shard_map/all_to_all | solution.py:219
  256.6 43.2 %collective-permute-done.6 = bf16[8,5,2,128,128]{4,3,2,1,0:T(8,128)(2,1)} collective-permute-done((bf16[8,5,2,128,128]{4,3,2,1,0:T(8,128)(2,1)}, bf16[8,5,2,128,128]{4,3,2,1,0:T(8,128)(2,1)}, u32[]{:S(2)}, u32[]{:S(2)}) %collective-permute-start.6) | collective-permute-done | bytes 2621472 | tf_op jit(solution)/shard_map/ppermute | solution.py:177
  299.9 1.2 collective-permute-done.7
  301.0 8.4 %fusion.2 = bf16[8,5,2,128,128]{4,3,2,1,0:T(8,128)(2,1)} fusion(bf16[8,5,2,128,128]{4,3,2,1,0:T(8,128)(2,1)} %collective-permute-done.7, bf16[8,5,2,128,128]{4,3,2,1,0:T(8,128)(2,1)} %collective-permute-done.6, bf16[8,5,2,128,128]{4,3,2,1,0:T(8,128)(2,1)} %get-tuple-element.9, bf16[2,8,5,2,128,128]{5,4,3,2,1,0:T(8,128)(2,1)} %collective-permute-done.5), kind=kLoop, calls=%fused_computation.3 | loop fusion | flops 10485760 | bytes 13107200 | tf_op jit(solution)/shard_map/convert_element_type | solution.py:218
  309.4 15.2 %all-to-all-done.2 = bf16[8,5,128,128]{3,2,1,0:T(8,128)(2,1)S(1)} async-done(((bf16[8,5,128,128]{3,2,1,0:T(8,128)(2,1)}), bf16[8,5,128,128]{3,2,1,0:T(8,128)(2,1)S(1)}, u32[]{:S(2)}, u32[]{:S(2)}) %all-to-all-start.2) | async-done | bytes 1310752 | tf_op jit(solution)/shard_map/all_to_all | solution.py:219
  324.6 0.0 copy-start.2
  324.6 1.1 copy-done.2
  325.7 8.5 %all-to-all-start.3 = ((bf16[8,5,2,128,128]{4,3,2,1,0:T(8,128)(2,1)}), bf16[8,5,2,128,128]{4,3,2,1,0:T(8,128)(2,1)S(1)}, u32[]{:S(2)}, u32[]{:S(2)}) async-start(bf16[8,5,2,128,128]{4,3,2,1,0:T(8,128)(2,1)} %fusion.2), calls=%async_computation.3 | async-start | bytes 5242880 | tf_op jit(solution)/shard_map/all_to_all | solution.py:220
  334.1 2.4 copy.17
  336.5 2.4 copy.20
  339.0 30.4 %all-to-all-done.3 = bf16[8,5,2,128,128]{4,3,2,1,0:T(8,128)(2,1)S(1)} async-done(((bf16[8,5,2,128,128]{4,3,2,1,0:T(8,128)(2,1)}), bf16[8,5,2,128,128]{4,3,2,1,0:T(8,128)(2,1)S(1)}, u32[]{:S(2)}, u32[]{:S(2)}) %all-to-all-start.3) | async-done | bytes 2621472 | tf_op jit(solution)/shard_map/all_to_all | solution.py:220
  369.3 1.7 slice_bitcast_fusion.1
  371.0 0.0 copy-start.1
  371.0 1.9 copy.19
  372.9 1.4 copy.22
  374.3 0.0 copy-done.1
  374.3 0.8 copy.18
  375.1 1.4 copy.21
  (1 shorter events, 0.0 us)
Async XLA Ops:
  7.7 107.9 %copy-start.4 = (bf16[128,5120]{1,0:T(8,128)(2,1)S(1)}, bf16[128,5120]{1,0:T(8,128)(2,1)}, u32[]{:S(2)}) copy-start(bf16[128,5120]{1,0:T(8,128)(2,1)} %param.6) | copy-start | bytes 3932164
  49.2 59.6 %collective-permute-start.3 = (bf16[8,5,2,128,128]{4,3,2,1,0:T(8,128)(2,1)}, bf16[8,5,2,128,128]{4,3,2,1,0:T(8,128)(2,1)}, u32[]{:S(2)}, u32[]{:S(2)}) collective-permute-start(bf16[8,5,2,128,128]{4,3,2,1,0:T(8,128)(2,1)} %all_to_all.20.refs_4_), channel_id=1, source_target_pairs={{16,0},{24,8},{32,16},{40,24},{48,32},{56,40},{64,48},{72,56},{80,... | collective-permute-start | bytes 7864328 | tf_op jit(solution)/shard_map/ppermute | solution.py:177
  50.5 61.2 %collective-permute-start = (bf16[8,5,2,128,128]{4,3,2,1,0:T(8,128)(2,1)}, bf16[8,5,2,128,128]{4,3,2,1,0:T(8,128)(2,1)}, u32[]{:S(2)}, u32[]{:S(2)}) collective-permute-start(bf16[8,5,2,128,128]{4,3,2,1,0:T(8,128)(2,1)} %all_to_all.20.refs_4_), channel_id=1, source_target_pairs={{0,16},{8,24},{16,32},{24,40},{32,48},{40,56},{48,64},{56,72},{64,... | collective-permute-start | bytes 7864328 | tf_op jit(solution)/shard_map/ppermute | solution.py:177
  108.8 19.1 %collective-permute-start.4 = (bf16[8,5,2,128,128]{4,3,2,1,0:T(8,128)(2,1)}, bf16[8,5,2,128,128]{4,3,2,1,0:T(8,128)(2,1)}, u32[]{:S(2)}, u32[]{:S(2)}) collective-permute-start(bf16[8,5,2,128,128]{4,3,2,1,0:T(8,128)(2,1)} %collective-permute-done.3.refs_6_), channel_id=1, source_target_pairs={{0,8},{16,24},{32,40},{48,56},{64,72},{80,88},{96,104},{112,120},{... | collective-permute-start | bytes 7864328 | tf_op jit(solution)/shard_map/ppermute | solution.py:182
  111.7 16.3 %collective-permute-start.2 = (bf16[8,5,2,128,128]{4,3,2,1,0:T(8,128)(2,1)}, bf16[8,5,2,128,128]{4,3,2,1,0:T(8,128)(2,1)}, u32[]{:S(2)}, u32[]{:S(2)}) collective-permute-start(bf16[8,5,2,128,128]{4,3,2,1,0:T(8,128)(2,1)} %collective-permute-done.refs_2_), channel_id=1, source_target_pairs={{8,0},{24,16},{40,32},{56,48},{72,64},{88,80},{104,96},{120,112},{... | collective-permute-start | bytes 7864328 | tf_op jit(solution)/shard_map/ppermute | solution.py:182
  113.0 52.9 %collective-permute-start.1 = (bf16[8,5,2,128,128]{4,3,2,1,0:T(8,128)(2,1)}, bf16[8,5,2,128,128]{4,3,2,1,0:T(8,128)(2,1)}, u32[]{:S(2)}, u32[]{:S(2)}) collective-permute-start(bf16[8,5,2,128,128]{4,3,2,1,0:T(8,128)(2,1)} %all_to_all.20.refs_4_), channel_id=1, source_target_pairs={{0,8},{8,0},{16,24},{24,16},{32,40},{40,32},{48,56},{56,48},{64,72... | collective-permute-start | bytes 7864328 | tf_op jit(solution)/shard_map/ppermute | solution.py:182
  123.2 4.5 %copy-start.6 = (s32[5,8]{1,0:T(8,128)S(1)}, s32[5,8]{1,0:T(8,128)}, u32[]{:S(2)}) copy-start(s32[5,8]{1,0:T(8,128)} %param.11) | copy-start | bytes 484
  123.2 4.6 %copy-start.5 = (s32[5,8,12]{2,1,0:T(8,128)S(1)}, s32[5,8,12]{2,1,0:T(8,128)}, u32[]{:S(2)}) copy-start(s32[5,8,12]{2,1,0:T(8,128)} %param.10) | copy-start | bytes 5764
  123.2 41.1 %all-to-all-start.1 = ((bf16[8,5,2,128,128]{4,3,2,1,0:T(8,128)(2,1)}), bf16[8,5,2,128,128]{4,3,2,1,0:T(8,128)(2,1)S(1)}, u32[]{:S(2)}, u32[]{:S(2)}) async-start(bf16[8,5,2,128,128]{4,3,2,1,0:T(8,128)(2,1)} %pad_maximum_fusion.1), calls=%async_computation.1 | async-start | bytes 5242880 | tf_op jit(solution)/shard_map/all_to_all | solution.py:190
  164.3 1.6 copy-start.3
  220.7 1.1 copy-start
  221.7 10.1 %collective-permute-start.5 = (bf16[2,8,5,2,128,128]{5,4,3,2,1,0:T(8,128)(2,1)}, bf16[2,8,5,2,128,128]{5,4,3,2,1,0:T(8,128)(2,1)}, u32[]{:S(2)}, u32[]{:S(2)}) collective-permute-start(bf16[2,8,5,2,128,128]{5,4,3,2,1,0:T(8,128)(2,1)} %get-tuple-element.10), channel_id=1, source_target_pairs={{0,8},{8,0},{16,24},{24,16},{32,40},{40,32},{48,56},{56,48},{64,72... | collective-permute-start | bytes 15728648 | tf_op jit(solution)/shard_map/ppermute | solution.py:182
  237.2 62.7 %collective-permute-start.6 = (bf16[8,5,2,128,128]{4,3,2,1,0:T(8,128)(2,1)}, bf16[8,5,2,128,128]{4,3,2,1,0:T(8,128)(2,1)}, u32[]{:S(2)}, u32[]{:S(2)}) collective-permute-start(bf16[8,5,2,128,128]{4,3,2,1,0:T(8,128)(2,1)} %get-tuple-element.16), channel_id=1, source_target_pairs={{16,0},{24,8},{32,16},{40,24},{48,32},{56,40},{64,48},{72,56},{80,... | collective-permute-start | bytes 7864328 | tf_op jit(solution)/shard_map/ppermute | solution.py:177
  238.5 62.6 %collective-permute-start.7 = (bf16[8,5,2,128,128]{4,3,2,1,0:T(8,128)(2,1)}, bf16[8,5,2,128,128]{4,3,2,1,0:T(8,128)(2,1)}, u32[]{:S(2)}, u32[]{:S(2)}) collective-permute-start(bf16[8,5,2,128,128]{4,3,2,1,0:T(8,128)(2,1)} %get-tuple-element.17), channel_id=1, source_target_pairs={{0,16},{8,24},{16,32},{24,40},{32,48},{40,56},{48,64},{56,72},{64,... | collective-permute-start | bytes 7864328 | tf_op jit(solution)/shard_map/ppermute | solution.py:177
  245.6 79.0 %all-to-all-start.2 = ((bf16[8,5,128,128]{3,2,1,0:T(8,128)(2,1)}), bf16[8,5,128,128]{3,2,1,0:T(8,128)(2,1)S(1)}, u32[]{:S(2)}, u32[]{:S(2)}) async-start(bf16[8,5,128,128]{3,2,1,0:T(8,128)(2,1)} %copy-done), calls=%async_computation.2 | async-start | bytes 2621440 | tf_op jit(solution)/shard_map/all_to_all | solution.py:219
  324.6 1.1 copy-start.2
  325.7 43.7 %all-to-all-start.3 = ((bf16[8,5,2,128,128]{4,3,2,1,0:T(8,128)(2,1)}), bf16[8,5,2,128,128]{4,3,2,1,0:T(8,128)(2,1)S(1)}, u32[]{:S(2)}, u32[]{:S(2)}) async-start(bf16[8,5,2,128,128]{4,3,2,1,0:T(8,128)(2,1)} %fusion.2), calls=%async_computation.3 | async-start | bytes 5242880 | tf_op jit(solution)/shard_map/all_to_all | solution.py:220
  371.0 3.3 copy-start.1

commit v2 on v1

v2 whole, which is shorter than its diff:
```python
import functools

import jax
import jax.numpy as jnp
from jax import lax
from jax.experimental import pallas as pl
from jax.experimental.pallas import tpu as pltpu
from jax.sharding import Mesh
from jax.sharding import PartitionSpec as P

HD = 128
BLK = 128
BAND = 2
BPD = 8
MAXK = 12
HPG = 5
GROUP = 4
ATTENTION_COST = 10
VMEM_LIMIT = 56 * 2**20
NEG = -1e30
LOG2E = 1.4426950408889634
SCALE = HD**-0.5
ORDER = (
    (0, True, None),
    (1, True, None),
    (0, False, None),
    (2, True, 0),
    (1, False, 1),
    (2, False, None),
)
F32 = jnp.float32
BF16 = jnp.bfloat16
NT = (((1,), (1,)), ((), ()))
NN = (((1,), (0,)), ((), ()))
TN = (((0,), (0,)), ((), ()))


def dot(a, b, dims):
    return lax.dot_general(a, b, dims, preferred_element_type=F32)


def fold(x):
    return x.reshape(-1, 8, HD)


def query_block(n_keys, b, ids_ref, count, qd, kv, acc, dq, kcat, s_scr, dp_scr, ds_scr):
    q = qd[b, 0]
    do = qd[b, 1]
    base = b * MAXK
    m8 = jnp.full((8, HD), NEG, F32)
    index = [ids_ref[base + s] for s in range(n_keys)]
    for s in range(n_keys):
        k = kv[index[s], 0]
        kcat[pl.ds(s * BLK, BLK), :] = k
        st = dot(k, q, NT)
        if s > n_keys - GROUP:
            st = jnp.where(s < count, st, NEG)
        s_scr[s] = st
        m8 = jnp.maximum(m8, jnp.max(fold(st), axis=0))
        dp_scr[s] = dot(kv[index[s], 1], do, NT)
    m = jnp.max(m8, axis=0, keepdims=True) * (SCALE * LOG2E)
    l8 = jnp.zeros((8, HD), F32)
    r8 = jnp.zeros((8, HD), F32)
    for s in range(n_keys):
        p = jnp.exp2(s_scr[s] * (SCALE * LOG2E) - m)
        s_scr[s] = p
        l8 += jnp.sum(fold(p), axis=0)
        r8 += jnp.sum(fold(p * dp_scr[s]), axis=0)
    inv = 1.0 / jnp.sum(l8, axis=0, keepdims=True)
    rd = jnp.sum(r8, axis=0, keepdims=True) * inv
    for s in range(n_keys):
        p = s_scr[s] * inv
        ds = (p * (dp_scr[s] - rd)).astype(BF16)
        ds_scr[pl.ds(s * BLK, BLK), :] = ds
        acc[index[s], 0] += dot(ds, q, NN)
        acc[index[s], 1] += dot(p.astype(BF16), do, NN)
    rows = pl.ds(0, n_keys * BLK)
    dq[...] = (dot(ds_scr[rows, :], kcat[rows, :], TN) * SCALE).astype(BF16)


def attention_kernel(parts, size, n_query, ids_ref, cnt_ref, *refs):
    sources, refs = refs[:parts], refs[parts:]
    qd_in, dq_out, refs = refs[0], refs[1], refs[2:]
    targets, refs = refs[:parts], refs[parts:]
    kv, qd, acc, stage, dq, kcat, s_scr, dp_scr, ds_scr, in_sem, out_sem = refs
    fetches = [
        pltpu.make_async_copy(sources[i], kv.at[pl.ds(i * size, size)], in_sem.at[i])
        for i in range(parts)
    ] + [pltpu.make_async_copy(qd_in, qd, in_sem.at[parts])]
    for copy in fetches:
        copy.start()
    acc[...] = jnp.zeros_like(acc)
    for copy in fetches:
        copy.wait()

    first = cnt_ref[n_query]
    if n_query < dq.shape[0]:
        dq[...] = jnp.zeros_like(dq)

    def one(b, carry):
        count = cnt_ref[b]
        for upto in range(GROUP, MAXK + 1, GROUP):

            @pl.when((count > upto - GROUP) & (count <= upto))
            def _():
                query_block(upto, b, ids_ref, count, qd, kv, acc, dq.at[first + b], kcat, s_scr, dp_scr, ds_scr)

        return carry

    lax.fori_loop(0, n_query, one, 0)
    puts = [pltpu.make_async_copy(dq, dq_out, out_sem.at[parts])]
    puts[0].start()
    for i in range(parts):

        def convert(j, carry):
            stage[j, 0] = (acc[j, 0] * SCALE).astype(BF16)
            stage[j, 1] = acc[j, 1].astype(BF16)
            return carry

        lax.fori_loop(i * size, (i + 1) * size, convert, 0)
        puts.append(
            pltpu.make_async_copy(stage.at[pl.ds(i * size, size)], targets[i], out_sem.at[i])
        )
        puts[-1].start()
    for copy in puts:
        copy.wait()


def attention(ids, counts, sources, qd):
    parts, size, n_query = len(sources), sources[0].shape[0], qd.shape[0]
    window = parts * size
    smem = pl.BlockSpec(memory_space=pltpu.SMEM)
    hbm = pl.BlockSpec(memory_space=pl.ANY)
    pairs = n_query * 8
    out = pl.pallas_call(
        functools.partial(attention_kernel, parts, size, n_query),
        out_shape=[jax.ShapeDtypeStruct((size, BLK, HD), BF16)]
        + [jax.ShapeDtypeStruct((size, 2, BLK, HD), BF16)] * parts,
        in_specs=[smem, smem] + [hbm] * (parts + 1),
        out_specs=[hbm] * (parts + 1),
        scratch_shapes=[
            pltpu.VMEM((window, 2, BLK, HD), BF16),
            pltpu.VMEM((n_query, 2, BLK, HD), BF16),
            pltpu.VMEM((window, 2, BLK, HD), F32),
            pltpu.VMEM((window, 2, BLK, HD), BF16),
            pltpu.VMEM((size, BLK, HD), BF16),
            pltpu.VMEM((MAXK * BLK, HD), BF16),
            pltpu.VMEM((MAXK, BLK, HD), F32),
            pltpu.VMEM((MAXK, BLK, HD), F32),
            pltpu.VMEM((MAXK * BLK, HD), BF16),
            pltpu.SemaphoreType.DMA((parts + 1,)),
            pltpu.SemaphoreType.DMA((parts + 1,)),
        ],
        compiler_params=pltpu.CompilerParams(vmem_limit_bytes=VMEM_LIMIT),
        cost_estimate=pl.CostEstimate(
            flops=pairs * ATTENTION_COST * BLK * BLK * HD,
            bytes_accessed=(2 * window + n_query) * 2 * BLK * HD * 2,
            transcendentals=pairs * BLK * BLK,
        ),
        name="attention",
    )(ids, counts, *sources, qd)
    return out[0], out[1:]


def split_kernel(k_ref, v_ref, q_ref, g_ref, kv0_ref, kv1_ref, kv2_ref, qd0_ref, qd1_ref, qd2_ref):
    sides = ((k_ref, v_ref, kv0_ref, kv1_ref, kv2_ref), (q_ref, g_ref, qd0_ref, qd1_ref, qd2_ref))
    for first, second, a0_ref, a1_ref, a2_ref in sides:
        for t, ref in enumerate((first, second)):
            for j in range(a0_ref.shape[1]):

                def head(m):
                    return ref[:, (j * HPG + m) * HD : (j * HPG + m + 1) * HD]

                for core in range(2):
                    a0_ref[core, j, t] = head(2 * core)
                    a1_ref[core, j, t] = head(2 * core + 1)
                for core in range(a2_ref.shape[0]):
                    a2_ref[core, j, t] = head(4)


def split_heads(key_in, value_in, query_in, out_grad):
    groups, step = key_in.shape[1] // (HPG * HD), 2
    a = jax.ShapeDtypeStruct((2, groups, 2, BLK, HD), BF16)
    b = jax.ShapeDtypeStruct((1, groups, 2, BLK, HD), BF16)
    a_spec = pl.BlockSpec((2, step, 2, BLK, HD), lambda j: (0, j, 0, 0, 0))
    b_spec = pl.BlockSpec((1, step, 2, BLK, HD), lambda j: (0, j, 0, 0, 0))
    x_spec = pl.BlockSpec((BLK, step * HPG * HD), lambda j: (0, j))
    out = pl.pallas_call(
        split_kernel,
        grid=(groups // step,),
        out_shape=(a, a, a, a, a, b),
        in_specs=[x_spec] * 4,
        out_specs=(a_spec,) * 5 + (b_spec,),
        compiler_params=pltpu.CompilerParams(vmem_limit_bytes=VMEM_LIMIT),
        cost_estimate=pl.CostEstimate(flops=0, bytes_accessed=16 * key_in.size, transcendentals=0),
        name="split_heads",
    )(key_in, value_in, query_in, out_grad)
    flat = [x.reshape(-1, 2, BLK, HD) for x in out]
    return flat[:3], flat[3:]


def join_kernel(a0_ref, a1_ref, a2_ref, *outs):
    for t, ref in enumerate(outs):
        for j in range(a0_ref.shape[1]):

            def put(m, value):
                ref[:, (j * HPG + m) * HD : (j * HPG + m + 1) * HD] = value

            for core in range(2):
                put(2 * core, a0_ref[core, j, t])
                put(2 * core + 1, a1_ref[core, j, t])
            put(4, (a2_ref[0, j, t].astype(F32) + a2_ref[1, j, t].astype(F32)).astype(BF16))


def join_heads(*parts):
    groups, step = parts[0].shape[0] // 2, 2
    out = jax.ShapeDtypeStruct((BLK, groups * HPG * HD), BF16)
    return pl.pallas_call(
        join_kernel,
        grid=(groups // step,),
        out_shape=(out,) * 3,
        in_specs=[pl.BlockSpec((2, step, 3, BLK, HD), lambda j: (0, j, 0, 0, 0))] * 3,
        out_specs=(pl.BlockSpec((BLK, step * HPG * HD), lambda j: (0, j)),) * 3,
        compiler_params=pltpu.CompilerParams(vmem_limit_bytes=VMEM_LIMIT),
        cost_estimate=pl.CostEstimate(
            flops=0, bytes_accessed=groups * HPG * 3 * BLK * HD * 4, transcendentals=0
        ),
        name="join_heads",
    )(*[x.reshape(2, groups, 3, BLK, HD) for x in parts])


def total_kernel(dq_ref, own_ref, *refs):
    terms, out_ref = refs[:-1], refs[-1]
    out_ref[:, 0] = dq_ref[...]
    total = own_ref[...].astype(F32)
    for term in terms:
        total += term[...].astype(F32)
    out_ref[:, 1:] = total.astype(BF16)


def total_grads(dq, own, terms):
    blocks, step = dq.shape[0], 4
    kv_spec = pl.BlockSpec((step, 2, BLK, HD), lambda i: (i, 0, 0, 0))
    return pl.pallas_call(
        total_kernel,
        grid=(blocks // step,),
        out_shape=jax.ShapeDtypeStruct((blocks, 3, BLK, HD), BF16),
        in_specs=[pl.BlockSpec((step, BLK, HD), lambda i: (i, 0, 0))] + [kv_spec] * (1 + len(terms)),
        out_specs=pl.BlockSpec((step, 3, BLK, HD), lambda i: (i, 0, 0, 0)),
        cost_estimate=pl.CostEstimate(
            flops=0, bytes_accessed=(6 + 2 * len(terms)) * dq.size * 2, transcendentals=0
        ),
        name="total_grads",
    )(dq, own, *terms)


def shift(value, axes, steps):
    count = lax.axis_size(axes)
    pairs = [(s, s + steps) for s in range(max(0, -steps), min(count, count - steps))]
    return lax.ppermute(value, axes, pairs)


PAIR = ("core", "group")
RUNS = ("chip", "core")


def exchange(x, axes):
    return lax.all_to_all(x, axes, 0, 0)


def masks(key_blocks, block_count):
    chip, core = lax.axis_index("chip"), lax.axis_index("core")
    packed = jnp.concatenate([key_blocks, block_count[:, :, None]], axis=2)
    mine = lax.dynamic_slice_in_dim(packed, 2 * core, 2, 0)
    theirs = lax.dynamic_slice_in_dim(packed, 2 - 2 * core, 2, 0)
    theirs = lax.ppermute(theirs, "core", [(0, 1), (1, 0)])
    first, second = jnp.where(core == 0, mine, theirs), jnp.where(core == 0, theirs, mine)
    both = jnp.concatenate([first, second], axis=1)
    first_block = (2 * chip - BAND) * BPD
    result = []
    for part, row in ((both[0], 0), (both[1], 0), (packed[4], core * BPD)):
        counts = jnp.append(part[:, MAXK], jnp.int32(row))
        result.append(((part[:, :MAXK] - first_block).reshape(-1), counts))
    return result


def after(x, *done):
    return lax.optimization_barrier((x, *done))[0]


def shards(query_in, key_in, value_in, out_grad, key_blocks, block_count):
    lists = masks(key_blocks, block_count)
    kv, qd = split_heads(key_in, value_in, query_in, out_grad)
    own, queries, near, last = [None] * 3, [None] * 3, [None] * 3, ()
    for part, is_kv, wait_for in ORDER:
        ready = last if wait_for is None else (*last, *near[wait_for])
        source = after(kv[part] if is_kv else qd[part], *ready)
        got = exchange(source, PAIR if is_kv or part < 2 else "group")
        last = (got,)
        if is_kv:
            own[part] = got
            near[part] = (shift(got, "chip", 1), shift(got, "chip", -1))
        else:
            queries[part] = got
    done = []
    for part, (ids, counts) in enumerate(lists):
        sources = (near[part][0], own[part], near[part][1])
        dq, grads = attention(ids, after(counts, *[x[0] for x in done[-1:]]), sources, queries[part])
        done.append((dq, grads[1], [shift(grads[0], "chip", -1), shift(grads[2], "chip", 1)]))
    back = []
    for part, (dq, mine, terms) in enumerate(done):
        later = [x[0] for x in done[part + 1 : part + 2]] + list(near[2])
        total = total_grads(after(dq, *later, *back[-1:]), mine, terms)
        back.append(exchange(total, PAIR))
    return tuple(join_heads(*back))


def solution(mesh):
    chips = mesh.shape["frame"] // 2
    mesh = Mesh(mesh.devices.reshape(chips, 2, -1), ("chip", "core", "group"))
    tokens = P(("chip", "core", "group"), None)
    return jax.shard_map(
        shards,
        mesh=mesh,
        in_specs=(tokens,) * 4 + (P("group", RUNS, None), P("group", RUNS)),
        out_specs=(tokens,) * 3,
        check_vma=False,
    )
```

time: 380 us -> 386 us (1.016)
  starting transfers between devices: 48.1 us -> 97.3 us
  waiting for transfers between devices: 184 us -> 140 us
  Pallas kernels: 54.8 us -> 84.2 us
  local copies, waits for them, and re-layouts: 28.4 us -> 6.83 us
  other arithmetic: 19.3 us -> 1.45 us
  blocking collectives: 41.5 us -> 51.9 us
    ppermute x8 -> x13, waiting for transfers between devices: 105 us -> 1.05 us  [the longest x1 1.02 us: masks(): theirs = lax.ppermute(theirs, 'core', [(0, 1), (1, 0)])]
    all_to_all x3 -> x7, waiting for transfers between devices: 78.4 us -> 139 us  [exchange(): return lax.all_to_all(x, axes, 0, 0)]
    all_to_all x3 -> x7, starting transfers between devices: 24 us -> 63.5 us  [exchange(): return lax.all_to_all(x, axes, 0, 0)]
    pallas_call x1 -> x8, Pallas kernels: 54.8 us -> 84.2 us  [the longest x3 61.4 us: attention(): pl.pallas_call(functools.partial(attention_kernel, parts, size, n_query),...]
    unnamed x21 -> x24, local copies, waits for them, and re-layouts: 16.4 us -> 4.27 us
    all_to_all x1 -> x2, blocking collectives: 41.5 us -> 51.9 us  [exchange(): return lax.all_to_all(x, axes, 0, 0)]
    ppermute x8 -> x13, starting transfers between devices: 24 us -> 33.8 us  [the longest x12 33.6 us: shift(): return lax.ppermute(value, axes, pairs)]
    convert_element_type x1 -> x0, other arithmetic: 8.39 us -> none  [shards(): sum((x.astype(F32) for x in (mine, sx[0], from_above, from_below)))]
  transfers between devices with their start and end apart: 11 -> 20, of which waited for: 7 -> 6; matrix products, arithmetic and copies ran while one was open for 7% -> 1% of each run, Pallas kernels for 0% -> 17%
where the time goes in v2:
time: 386 us; the launch traced here: 382 us
  waiting for transfers between devices  140 us (36%)
  starting transfers between devices  97.3 us (25%)
  Pallas kernels  84.2 us (22%)
  blocking collectives  51.9 us (13%)
  local copies, waits for them, and re-layouts  6.83 us (2%)
    all_to_all x7, waiting for transfers between devices, exchange(): return lax.all_to_all(x, axes, 0, 0)  139 us
    all_to_all x7, starting transfers between devices, exchange(): return lax.all_to_all(x, axes, 0, 0)  63.5 us
    pallas_call x3, Pallas kernels, attention(): pl.pallas_call(functools.partial(attention_kernel, parts, size, n_query),...  61.4 us
    all_to_all x2, blocking collectives, exchange(): return lax.all_to_all(x, axes, 0, 0)  51.9 us
    ppermute x12, starting transfers between devices, shift(): return lax.ppermute(value, axes, pairs)  33.6 us
    pallas_call x3, Pallas kernels, total_grads(): pl.pallas_call(total_kernel, grid=(blocks // step,), out_shape=jax.ShapeD...  12.3 us
  transfers between devices with their start and end apart: 20, of which 6 were waited for; matrix products, arithmetic and copies ran while one was open for 1% of the time, Pallas kernels for 17%

profile of v2, /device:TPU:8, one launch (start us, length us, event | category | flops | bytes accessed | tf_op | source)
XLA Modules:
  0.0 382.2 jit_solution(5922615663394752265)
XLA Ops:
  0.6 5.7 %split_heads.1 = (bf16[2,8,2,128,128]{4,3,2,1,0:T(8,128)(2,1)}, bf16[2,8,2,128,128]{4,3,2,1,0:T(8,128)(2,1)}, bf16[2,8,2,128,128]{4,3,2,1,0:T(8,128)(2,1)}, bf16...) custom-call(bf16[128,5120]{1,0:T(8,128)(2,1)} %k_ref.1, ...), custom_call_target="tpu_custom_call" | custom-call | bytes 10485760 | tf_op jit(solution)/shard_map/split_heads/pallas_call | solution.py:188
  6.3 24.8 %all_to_all.45.refs_1_ = bf16[16,2,128,128]{3,2,1,0:T(8,128)(2,1)S(1)} all-to-all(bf16[16,2,128,128]{3,2,1,0:T(8,128)(2,1)} %bitcast.22), channel_id=1, replica_groups=mesh['chip'=8,'core'=2,'group'=8] {'core','group'}, dimensions={0} | all-to-all | bytes 2097152 | tf_op jit(solution)/shard_map/all_to_all | solution.py:268
  31.1 4.9 %all-to-all-start.1 = ((bf16[16,2,128,128]{3,2,1,0:T(8,128)(2,1)}), bf16[16,2,128,128]{3,2,1,0:T(8,128)(2,1)S(1)}, u32[]{:S(2)}, u32[]{:S(2)}) async-start(bf16[16,2,128,128]{3,2,1,0:T(8,128)(2,1)} %bitcast.4), calls=%async_computation.1 | async-start | bytes 2097152 | tf_op jit(solution)/shard_map/all_to_all | solution.py:268
  36.0 4.4 %collective-permute-start.1 = (bf16[16,2,128,128]{3,2,1,0:T(8,128)(2,1)S(1)}, bf16[16,2,128,128]{3,2,1,0:T(8,128)(2,1)}, u32[]{:S(2)}, u32[]{:S(2)}) collective-permute-start(bf16[16,2,128,128]{3,2,1,0:T(8,128)(2,1)S(1)} %all_to_all.45.refs_1_), channel_id=1, source_target_pairs={{0,16},{16,32},{32,48},{48,64},{64,80},{80,96},{96,112},{1,17},{17... | collective-permute-start | bytes 3145736 | tf_op jit(solution)/shard_map/ppermute | solution.py:260
  40.4 1.3 collective-permute-start.2
  41.6 51.4 %all-to-all-done.1.refs_1_ = bf16[16,2,128,128]{3,2,1,0:T(8,128)(2,1)S(1)} async-done(((bf16[16,2,128,128]{3,2,1,0:T(8,128)(2,1)}), bf16[16,2,128,128]{3,2,1,0:T(8,128)(2,1)S(1)}, u32[]{:S(2)}, u32[]{:S(2)}) %all-to-all-start.1) | async-done | bytes 1048608 | tf_op jit(solution)/shard_map/all_to_all | solution.py:268
  93.0 8.1 %all-to-all-start.2 = ((bf16[16,2,128,128]{3,2,1,0:T(8,128)(2,1)}), bf16[16,2,128,128]{3,2,1,0:T(8,128)(2,1)S(1)}, u32[]{:S(2)}, u32[]{:S(2)}) async-start(bf16[16,2,128,128]{3,2,1,0:T(8,128)(2,1)} %bitcast.21), calls=%async_computation.2 | async-start | bytes 2097152 | tf_op jit(solution)/shard_map/all_to_all | solution.py:268
  101.2 0.0 copy-start.10
  101.2 2.4 collective-permute-start.3
  103.6 1.3 collective-permute-start.4
  104.9 0.0 collective-permute-done.1.refs_0_
  104.9 0.0 collective-permute-done.2.refs_2_
  104.9 15.2 %all-to-all-done.2.refs_3_ = bf16[16,2,128,128]{3,2,1,0:T(8,128)(2,1)S(1)} async-done(((bf16[16,2,128,128]{3,2,1,0:T(8,128)(2,1)}), bf16[16,2,128,128]{3,2,1,0:T(8,128)(2,1)S(1)}, u32[]{:S(2)}, u32[]{:S(2)}) %all-to-all-start.2) | async-done | bytes 1048608 | tf_op jit(solution)/shard_map/all_to_all | solution.py:268
  120.0 1.0 copy-done.9
  121.0 23.8 %all-to-all-start.3 = ((bf16[16,2,128,128]{3,2,1,0:T(8,128)(2,1)}), bf16[16,2,128,128]{3,2,1,0:T(8,128)(2,1)S(1)}, u32[]{:S(2)}, u32[]{:S(2)}) async-start(bf16[16,2,128,128]{3,2,1,0:T(8,128)(2,1)} %bitcast.20), calls=%async_computation.3 | async-start | bytes 2097152 | tf_op jit(solution)/shard_map/all_to_all | solution.py:268
  144.8 0.1 copy.10
  144.9 0.1 fusion.2
  145.0 0.2 collective-permute-start
  145.2 1.0 collective-permute-done
  146.2 0.1 broadcast_select_fusion
  146.3 0.2 slice_reduce_fusion.1
  146.5 0.0 collective-permute-done.3.refs_0_
  146.5 14.8 %all-to-all-done.3.refs_1_ = bf16[16,2,128,128]{3,2,1,0:T(8,128)(2,1)S(1)} async-done(((bf16[16,2,128,128]{3,2,1,0:T(8,128)(2,1)}), bf16[16,2,128,128]{3,2,1,0:T(8,128)(2,1)S(1)}, u32[]{:S(2)}, u32[]{:S(2)}) %all-to-all-start.3) | async-done | bytes 1048608 | tf_op jit(solution)/shard_map/all_to_all | solution.py:268
  161.3 5.5 %all-to-all-start.4 = ((bf16[16,2,128,128]{3,2,1,0:T(8,128)(2,1)}), bf16[16,2,128,128]{3,2,1,0:T(8,128)(2,1)}, u32[]{:S(2)}, u32[]{:S(2)}) async-start(bf16[16,2,128,128]{3,2,1,0:T(8,128)(2,1)} %bitcast.6), calls=%async_computation.4 | async-start | bytes 2097152 | tf_op jit(solution)/shard_map/all_to_all | solution.py:268
  166.8 0.2 slice_reduce_fusion
  167.0 0.7 reshape.49.ids_ref
  167.7 0.6 pad_add_fusion.2
  168.3 2.3 collective-permute-start.5
  170.6 1.3 collective-permute-start.6
  171.9 23.2 %attention.3 = (bf16[16,128,128]{2,1,0:T(8,128)(2,1)}, bf16[16,2,128,128]{3,2,1,0:T(8,128)(2,1)}, bf16[16,2,128,128]{3,2,1,0:T(8,128)(2,1)}, bf16[16,2,128,128]{3,2,1,0:T(8,128)(2,1)}) custom-call(s32[192]{0:T(256)} %reshape.49.ids_ref, s32[17]{0:T(128)} %get-tuple-element.64.cnt_ref, bf16[16,2,128,128]{3,2,1,0:T(8,128)(2,1)} %collective-permute-done.1.refs_0_, ...), custom_call_target="tpu_custom_call" | custom-call | flops 2684354560 | bytes 7340032 | tf_op jit(solution)/shard_map/attention/pallas_call | solution.py:135
  195.1 1.3 collective-permute-start.7
  196.4 5.7 %collective-permute-start.8 = (bf16[16,2,128,128]{3,2,1,0:T(8,128)(2,1)}, bf16[16,2,128,128]{3,2,1,0:T(8,128)(2,1)S(1)}, u32[]{:S(2)}, u32[]{:S(2)}) collective-permute-start(bf16[16,2,128,128]{3,2,1,0:T(8,128)(2,1)} %get-tuple-element.46), channel_id=1, source_target_pairs={{0,16},{16,32},{32,48},{48,64},{64,80},{80,96},{96,112},{1,17},{17... | collective-permute-start | bytes 3145736 | tf_op jit(solution)/shard_map/ppermute | solution.py:260
  202.1 0.0 all-to-all-done.4.refs_3_
  202.1 7.8 %all-to-all-start.6 = ((bf16[8,2,128,128]{3,2,1,0:T(8,128)(2,1)}), bf16[8,2,128,128]{3,2,1,0:T(8,128)(2,1)}, u32[]{:S(2)}, u32[]{:S(2)}) async-start(bf16[8,2,128,128]{3,2,1,0:T(8,128)(2,1)} %bitcast.23), calls=%async_computation.6 | async-start | bytes 1048576 | tf_op jit(solution)/shard_map/all_to_all | solution.py:268
  209.9 0.7 reshape.53.ids_ref
  210.6 23.6 %attention.4 = (bf16[16,128,128]{2,1,0:T(8,128)(2,1)}, bf16[16,2,128,128]{3,2,1,0:T(8,128)(2,1)}, bf16[16,2,128,128]{3,2,1,0:T(8,128)(2,1)}, bf16[16,2,128,128]{3,2,1,0:T(8,128)(2,1)}) custom-call(s32[192]{0:T(256)} %reshape.53.ids_ref, s32[17]{0:T(128)} %get-tuple-element.37.cnt_ref, bf16[16,2,128,128]{3,2,1,0:T(8,128)(2,1)} %collective-permute-done.3.refs_0_, ...), custom_call_target="tpu_custom_call" | custom-call | flops 2684354560 | bytes 7340032 | tf_op jit(solution)/shard_map/attention/pallas_call | solution.py:135
  234.2 0.0 collective-permute-done.6.refs_2_
  234.2 0.0 collective-permute-done.7.refs_0_
  234.2 0.0 copy-start.2
  234.2 0.0 collective-permute-done.8.refs_1_
  234.2 0.0 copy-start.3
  234.2 0.9 copy-done.2
  235.2 0.3 copy-done.3
  235.5 4.1 %total_grads.3 = bf16[16,3,128,128]{3,2,1,0:T(8,128)(2,1)} custom-call(bf16[16,128,128]{2,1,0:T(8,128)(2,1)} %get-tuple-element.43.dq_ref, bf16[16,2,128,128]{3,2,1,0:T(8,128)(2,1)} %get-tuple-element.44.own_ref, bf16[16,2,128,128]{3,2,1,0:T(8,128)(2,1)} %copy-done.2, bf16[16,2,128,128]{3,2,1,0:T(8,128)(2,1)} %copy-done.3), custom_call_target="tpu_custom_call" | custom-call | bytes 5242880 | tf_op jit(solution)/shard_map/total_grads/pallas_call | solution.py:244
  239.6 8.5 %all-to-all-start.5 = ((bf16[16,3,128,128]{3,2,1,0:T(8,128)(2,1)}), bf16[16,3,128,128]{3,2,1,0:T(8,128)(2,1)S(1)}, u32[]{:S(2)}, u32[]{:S(2)}) async-start(bf16[16,3,128,128]{3,2,1,0:T(8,128)(2,1)} %total_grads.3), calls=%async_computation.5 | async-start | bytes 3145728 | tf_op jit(solution)/shard_map/all_to_all | solution.py:268
  248.1 1.3 collective-permute-start.9
  249.4 5.7 %collective-permute-start.10 = (bf16[16,2,128,128]{3,2,1,0:T(8,128)(2,1)}, bf16[16,2,128,128]{3,2,1,0:T(8,128)(2,1)}, u32[]{:S(2)}, u32[]{:S(2)}) collective-permute-start(bf16[16,2,128,128]{3,2,1,0:T(8,128)(2,1)} %get-tuple-element.54), channel_id=1, source_target_pairs={{0,16},{16,32},{32,48},{48,64},{64,80},{80,96},{96,112},{1,17},{17... | collective-permute-start | bytes 3145736 | tf_op jit(solution)/shard_map/ppermute | solution.py:260
  255.1 0.1 fusion.5
  255.2 0.6 reshape.57.ids_ref
  255.8 0.2 slice_reduce_fusion.2
  255.9 0.6 pad_add_fusion.4.cnt_ref
  256.5 14.6 %attention.5 = (bf16[16,128,128]{2,1,0:T(8,128)(2,1)}, bf16[16,2,128,128]{3,2,1,0:T(8,128)(2,1)}, bf16[16,2,128,128]{3,2,1,0:T(8,128)(2,1)}, bf16[16,2,128,128]{3,2,1,0:T(8,128)(2,1)}) custom-call(s32[96]{0:T(128)} %reshape.57.ids_ref, s32[9]{0:T(128)} %pad_add_fusion.4.cnt_ref, bf16[16,2,128,128]{3,2,1,0:T(8,128)(2,1)} %collective-permute-done.5.refs_0_, ...), custom_call_target="tpu_custom_call" | custom-call | flops 1342177280 | bytes 6815744 | tf_op jit(solution)/shard_map/attention/pallas_call | solution.py:135
  271.1 20.5 %all-to-all-done.5 = bf16[16,3,128,128]{3,2,1,0:T(8,128)(2,1)S(1)} async-done(((bf16[16,3,128,128]{3,2,1,0:T(8,128)(2,1)}), bf16[16,3,128,128]{3,2,1,0:T(8,128)(2,1)S(1)}, u32[]{:S(2)}, u32[]{:S(2)}) %all-to-all-start.5) | async-done | bytes 1572896 | tf_op jit(solution)/shard_map/all_to_all | solution.py:268
  291.6 0.0 collective-permute-done.9.refs_0_
  291.7 1.0 copy-done.4
  292.6 4.1 %total_grads.4 = bf16[16,3,128,128]{3,2,1,0:T(8,128)(2,1)} custom-call(bf16[16,128,128]{2,1,0:T(8,128)(2,1)} %get-tuple-element.51.dq_ref, bf16[16,2,128,128]{3,2,1,0:T(8,128)(2,1)} %get-tuple-element.52.own_ref, bf16[16,2,128,128]{3,2,1,0:T(8,128)(2,1)} %copy-done.4, bf16[16,2,128,128]{3,2,1,0:T(8,128)(2,1)} %collective-permute-done.10.refs_1_), custom_call_target="tpu_custom_call" | custom-call | bytes 5242880 | tf_op jit(solution)/shard_map/total_grads/pallas_call | solution.py:244
  296.8 4.8 %all-to-all-start.7 = ((bf16[16,3,128,128]{3,2,1,0:T(8,128)(2,1)}), bf16[16,3,128,128]{3,2,1,0:T(8,128)(2,1)S(1)}, u32[]{:S(2)}, u32[]{:S(2)}) async-start(bf16[16,3,128,128]{3,2,1,0:T(8,128)(2,1)} %total_grads.4), calls=%async_computation.7 | async-start | bytes 3145728 | tf_op jit(solution)/shard_map/all_to_all | solution.py:268
  301.6 1.3 collective-permute-start.11
  302.9 5.5 %collective-permute-start.12 = (bf16[16,2,128,128]{3,2,1,0:T(8,128)(2,1)}, bf16[16,2,128,128]{3,2,1,0:T(8,128)(2,1)}, u32[]{:S(2)}, u32[]{:S(2)}) collective-permute-start(bf16[16,2,128,128]{3,2,1,0:T(8,128)(2,1)} %get-tuple-element.58), channel_id=1, source_target_pairs={{0,16},{16,32},{32,48},{48,64},{64,80},{80,96},{96,112},{1,17},{17... | collective-permute-start | bytes 3145736 | tf_op jit(solution)/shard_map/ppermute | solution.py:260
  308.4 36.7 %all-to-all-done.7 = bf16[16,3,128,128]{3,2,1,0:T(8,128)(2,1)S(1)} async-done(((bf16[16,3,128,128]{3,2,1,0:T(8,128)(2,1)}), bf16[16,3,128,128]{3,2,1,0:T(8,128)(2,1)S(1)}, u32[]{:S(2)}, u32[]{:S(2)}) %all-to-all-start.7) | async-done | bytes 1572896 | tf_op jit(solution)/shard_map/all_to_all | solution.py:268
  345.1 1.0 copy-done.5
  346.1 4.1 %total_grads.5 = bf16[16,3,128,128]{3,2,1,0:T(8,128)(2,1)} custom-call(bf16[16,128,128]{2,1,0:T(8,128)(2,1)} %get-tuple-element.55.dq_ref, bf16[16,2,128,128]{3,2,1,0:T(8,128)(2,1)} %get-tuple-element.56.own_ref, bf16[16,2,128,128]{3,2,1,0:T(8,128)(2,1)} %copy-done.5, bf16[16,2,128,128]{3,2,1,0:T(8,128)(2,1)} %collective-permute-done.12.refs_1_), custom_call_target="tpu_custom_call" | custom-call | bytes 5242880 | tf_op jit(solution)/shard_map/total_grads/pallas_call | solution.py:244
  350.2 27.1 %all_to_all.46 = bf16[16,3,128,128]{3,2,1,0:T(8,128)(2,1)} all-to-all(bf16[16,3,128,128]{3,2,1,0:T(8,128)(2,1)} %total_grads.5), channel_id=1, replica_groups=mesh['chip'=8,'core'=2,'group'=8] {'core','group'}, dimensions={0} | all-to-all | bytes 3145728 | tf_op jit(solution)/shard_map/all_to_all | solution.py:268
  377.3 4.9 %join_heads.1 = (bf16[128,5120]{1,0:T(8,128)(2,1)}, bf16[128,5120]{1,0:T(8,128)(2,1)}, bf16[128,5120]{1,0:T(8,128)(2,1)}) custom-call(bf16[2,8,3,128,128]{4,3,2,1,0:T(8,128)(2,1)} %bitcast.17, bf16[2,8,3,128,128]{4,3,2,1,0:T(8,128)(2,1)} %bitcast.18, bf16[2,8,3,128,128]{4,3,2,1,0:T(8,128)(2,1)} %bitcast.19), custom_call_target="tpu_custom_call" | custom-call | bytes 7864320 | tf_op jit(solution)/shard_map/join_heads/pallas_call | solution.py:218
  (26 shorter events, 0.1 us)
Async XLA Ops:
  31.1 62.0 %copy-start.8 = (bf16[16,2,128,128]{3,2,1,0:T(8,128)(2,1)}, bf16[16,2,128,128]{3,2,1,0:T(8,128)(2,1)S(1)}, u32[]{:S(2)}) copy-start(bf16[16,2,128,128]{3,2,1,0:T(8,128)(2,1)S(1)} %all_to_all.45.refs_1_) | copy-start | bytes 3145732
  31.1 62.0 %all-to-all-start.1 = ((bf16[16,2,128,128]{3,2,1,0:T(8,128)(2,1)}), bf16[16,2,128,128]{3,2,1,0:T(8,128)(2,1)S(1)}, u32[]{:S(2)}, u32[]{:S(2)}) async-start(bf16[16,2,128,128]{3,2,1,0:T(8,128)(2,1)} %bitcast.4), calls=%async_computation.1 | async-start | bytes 2097152 | tf_op jit(solution)/shard_map/all_to_all | solution.py:268
  36.0 68.9 %collective-permute-start.1 = (bf16[16,2,128,128]{3,2,1,0:T(8,128)(2,1)S(1)}, bf16[16,2,128,128]{3,2,1,0:T(8,128)(2,1)}, u32[]{:S(2)}, u32[]{:S(2)}) collective-permute-start(bf16[16,2,128,128]{3,2,1,0:T(8,128)(2,1)S(1)} %all_to_all.45.refs_1_), channel_id=1, source_target_pairs={{0,16},{16,32},{32,48},{48,64},{64,80},{80,96},{96,112},{1,17},{17... | collective-permute-start | bytes 3145736 | tf_op jit(solution)/shard_map/ppermute | solution.py:260
  40.4 64.5 %collective-permute-start.2 = (bf16[16,2,128,128]{3,2,1,0:T(8,128)(2,1)S(1)}, bf16[16,2,128,128]{3,2,1,0:T(8,128)(2,1)}, u32[]{:S(2)}, u32[]{:S(2)}) collective-permute-start(bf16[16,2,128,128]{3,2,1,0:T(8,128)(2,1)S(1)} %all_to_all.45.refs_1_), channel_id=1, source_target_pairs={{16,0},{32,16},{48,32},{64,48},{80,64},{96,80},{112,96},{17,1},{33... | collective-permute-start | bytes 3145736 | tf_op jit(solution)/shard_map/ppermute | solution.py:260
  93.0 28.0 %copy-start.7 = (bf16[16,2,128,128]{3,2,1,0:T(8,128)(2,1)}, bf16[16,2,128,128]{3,2,1,0:T(8,128)(2,1)S(1)}, u32[]{:S(2)}) copy-start(bf16[16,2,128,128]{3,2,1,0:T(8,128)(2,1)S(1)} %all-to-all-done.1.refs_1_) | copy-start | bytes 3145732
  93.0 27.0 %all-to-all-start.2 = ((bf16[16,2,128,128]{3,2,1,0:T(8,128)(2,1)}), bf16[16,2,128,128]{3,2,1,0:T(8,128)(2,1)S(1)}, u32[]{:S(2)}, u32[]{:S(2)}) async-start(bf16[16,2,128,128]{3,2,1,0:T(8,128)(2,1)} %bitcast.21), calls=%async_computation.2 | async-start | bytes 2097152 | tf_op jit(solution)/shard_map/all_to_all | solution.py:268
  101.2 43.7 %copy-start.11 = (s32[5,8]{1,0:T(8,128)S(1)}, s32[5,8]{1,0:T(8,128)}, u32[]{:S(2)}) copy-start(s32[5,8]{1,0:T(8,128)} %param.11) | copy-start | bytes 484
  101.2 43.8 %copy-start.10 = (s32[5,8,12]{2,1,0:T(8,128)S(1)}, s32[5,8,12]{2,1,0:T(8,128)}, u32[]{:S(2)}) copy-start(s32[5,8,12]{2,1,0:T(8,128)} %param.10) | copy-start | bytes 5764
  101.2 45.3 %collective-permute-start.3 = (bf16[16,2,128,128]{3,2,1,0:T(8,128)(2,1)S(1)}, bf16[16,2,128,128]{3,2,1,0:T(8,128)(2,1)}, u32[]{:S(2)}, u32[]{:S(2)}) collective-permute-start(bf16[16,2,128,128]{3,2,1,0:T(8,128)(2,1)S(1)} %all-to-all-done.1.refs_1_), channel_id=1, source_target_pairs={{0,16},{16,32},{32,48},{48,64},{64,80},{80,96},{96,112},{1,17},{17... | collective-permute-start | bytes 3145736 | tf_op jit(solution)/shard_map/ppermute | solution.py:260
  103.6 42.9 %collective-permute-start.4 = (bf16[16,2,128,128]{3,2,1,0:T(8,128)(2,1)S(1)}, bf16[16,2,128,128]{3,2,1,0:T(8,128)(2,1)}, u32[]{:S(2)}, u32[]{:S(2)}) collective-permute-start(bf16[16,2,128,128]{3,2,1,0:T(8,128)(2,1)S(1)} %all-to-all-done.1.refs_1_), channel_id=1, source_target_pairs={{16,0},{32,16},{48,32},{64,48},{80,64},{96,80},{112,96},{17,1},{33... | collective-permute-start | bytes 3145736 | tf_op jit(solution)/shard_map/ppermute | solution.py:260
  120.0 1.0 copy-start.9
  121.0 40.3 %all-to-all-start.3 = ((bf16[16,2,128,128]{3,2,1,0:T(8,128)(2,1)}), bf16[16,2,128,128]{3,2,1,0:T(8,128)(2,1)S(1)}, u32[]{:S(2)}, u32[]{:S(2)}) async-start(bf16[16,2,128,128]{3,2,1,0:T(8,128)(2,1)} %bitcast.20), calls=%async_computation.3 | async-start | bytes 2097152 | tf_op jit(solution)/shard_map/all_to_all | solution.py:268
  145.0 1.2 collective-permute-start
  161.3 33.8 %copy-start.6 = (bf16[16,2,128,128]{3,2,1,0:T(8,128)(2,1)}, bf16[16,2,128,128]{3,2,1,0:T(8,128)(2,1)S(1)}, u32[]{:S(2)}) copy-start(bf16[16,2,128,128]{3,2,1,0:T(8,128)(2,1)S(1)} %all-to-all-done.3.refs_1_) | copy-start | bytes 3145732
  161.3 40.8 %all-to-all-start.4 = ((bf16[16,2,128,128]{3,2,1,0:T(8,128)(2,1)}), bf16[16,2,128,128]{3,2,1,0:T(8,128)(2,1)}, u32[]{:S(2)}, u32[]{:S(2)}) async-start(bf16[16,2,128,128]{3,2,1,0:T(8,128)(2,1)} %bitcast.6), calls=%async_computation.4 | async-start | bytes 2097152 | tf_op jit(solution)/shard_map/all_to_all | solution.py:268
  168.3 65.8 %collective-permute-start.5 = (bf16[16,2,128,128]{3,2,1,0:T(8,128)(2,1)S(1)}, bf16[16,2,128,128]{3,2,1,0:T(8,128)(2,1)}, u32[]{:S(2)}, u32[]{:S(2)}) collective-permute-start(bf16[16,2,128,128]{3,2,1,0:T(8,128)(2,1)S(1)} %all-to-all-done.3.refs_1_), channel_id=1, source_target_pairs={{0,16},{16,32},{32,48},{48,64},{64,80},{80,96},{96,112},{1,17},{17... | collective-permute-start | bytes 3145736 | tf_op jit(solution)/shard_map/ppermute | solution.py:260
  170.6 63.6 %collective-permute-start.6 = (bf16[16,2,128,128]{3,2,1,0:T(8,128)(2,1)S(1)}, bf16[16,2,128,128]{3,2,1,0:T(8,128)(2,1)}, u32[]{:S(2)}, u32[]{:S(2)}) collective-permute-start(bf16[16,2,128,128]{3,2,1,0:T(8,128)(2,1)S(1)} %all-to-all-done.3.refs_1_), channel_id=1, source_target_pairs={{16,0},{32,16},{48,32},{64,48},{80,64},{96,80},{112,96},{17,1},{33... | collective-permute-start | bytes 3145736 | tf_op jit(solution)/shard_map/ppermute | solution.py:260
  195.1 39.1 %collective-permute-start.7 = (bf16[16,2,128,128]{3,2,1,0:T(8,128)(2,1)}, bf16[16,2,128,128]{3,2,1,0:T(8,128)(2,1)S(1)}, u32[]{:S(2)}, u32[]{:S(2)}) collective-permute-start(bf16[16,2,128,128]{3,2,1,0:T(8,128)(2,1)} %get-tuple-element.45), channel_id=1, source_target_pairs={{16,0},{32,16},{48,32},{64,48},{80,64},{96,80},{112,96},{17,1},{33... | collective-permute-start | bytes 3145736 | tf_op jit(solution)/shard_map/ppermute | solution.py:260
  196.4 37.8 %collective-permute-start.8 = (bf16[16,2,128,128]{3,2,1,0:T(8,128)(2,1)}, bf16[16,2,128,128]{3,2,1,0:T(8,128)(2,1)S(1)}, u32[]{:S(2)}, u32[]{:S(2)}) collective-permute-start(bf16[16,2,128,128]{3,2,1,0:T(8,128)(2,1)} %get-tuple-element.46), channel_id=1, source_target_pairs={{0,16},{16,32},{32,48},{48,64},{64,80},{80,96},{96,112},{1,17},{17... | collective-permute-start | bytes 3145736 | tf_op jit(solution)/shard_map/ppermute | solution.py:260
  202.1 37.5 %all-to-all-start.6 = ((bf16[8,2,128,128]{3,2,1,0:T(8,128)(2,1)}), bf16[8,2,128,128]{3,2,1,0:T(8,128)(2,1)}, u32[]{:S(2)}, u32[]{:S(2)}) async-start(bf16[8,2,128,128]{3,2,1,0:T(8,128)(2,1)} %bitcast.23), calls=%async_computation.6 | async-start | bytes 1048576 | tf_op jit(solution)/shard_map/all_to_all | solution.py:268
  234.2 1.0 copy-start.2
  234.2 1.3 copy-start.3
  239.6 52.0 %all-to-all-start.5 = ((bf16[16,3,128,128]{3,2,1,0:T(8,128)(2,1)}), bf16[16,3,128,128]{3,2,1,0:T(8,128)(2,1)S(1)}, u32[]{:S(2)}, u32[]{:S(2)}) async-start(bf16[16,3,128,128]{3,2,1,0:T(8,128)(2,1)} %total_grads.3), calls=%async_computation.5 | async-start | bytes 3145728 | tf_op jit(solution)/shard_map/all_to_all | solution.py:268
  248.1 43.5 %collective-permute-start.9 = (bf16[16,2,128,128]{3,2,1,0:T(8,128)(2,1)}, bf16[16,2,128,128]{3,2,1,0:T(8,128)(2,1)S(1)}, u32[]{:S(2)}, u32[]{:S(2)}) collective-permute-start(bf16[16,2,128,128]{3,2,1,0:T(8,128)(2,1)} %get-tuple-element.53), channel_id=1, source_target_pairs={{16,0},{32,16},{48,32},{64,48},{80,64},{96,80},{112,96},{17,1},{33... | collective-permute-start | bytes 3145736 | tf_op jit(solution)/shard_map/ppermute | solution.py:260
  249.4 42.2 %collective-permute-start.10 = (bf16[16,2,128,128]{3,2,1,0:T(8,128)(2,1)}, bf16[16,2,128,128]{3,2,1,0:T(8,128)(2,1)}, u32[]{:S(2)}, u32[]{:S(2)}) collective-permute-start(bf16[16,2,128,128]{3,2,1,0:T(8,128)(2,1)} %get-tuple-element.54), channel_id=1, source_target_pairs={{0,16},{16,32},{32,48},{48,64},{64,80},{80,96},{96,112},{1,17},{17... | collective-permute-start | bytes 3145736 | tf_op jit(solution)/shard_map/ppermute | solution.py:260
  291.6 5.1 %copy-start = (bf16[16,3,128,128]{3,2,1,0:T(8,128)(2,1)}, bf16[16,3,128,128]{3,2,1,0:T(8,128)(2,1)S(1)}, u32[]{:S(2)}) copy-start(bf16[16,3,128,128]{3,2,1,0:T(8,128)(2,1)S(1)} %all-to-all-done.5) | copy-start | bytes 4718596
  291.6 1.0 copy-start.4
  296.8 48.3 %all-to-all-start.7 = ((bf16[16,3,128,128]{3,2,1,0:T(8,128)(2,1)}), bf16[16,3,128,128]{3,2,1,0:T(8,128)(2,1)S(1)}, u32[]{:S(2)}, u32[]{:S(2)}) async-start(bf16[16,3,128,128]{3,2,1,0:T(8,128)(2,1)} %total_grads.4), calls=%async_computation.7 | async-start | bytes 3145728 | tf_op jit(solution)/shard_map/all_to_all | solution.py:268
  301.6 43.5 %collective-permute-start.11 = (bf16[16,2,128,128]{3,2,1,0:T(8,128)(2,1)}, bf16[16,2,128,128]{3,2,1,0:T(8,128)(2,1)S(1)}, u32[]{:S(2)}, u32[]{:S(2)}) collective-permute-start(bf16[16,2,128,128]{3,2,1,0:T(8,128)(2,1)} %get-tuple-element.57), channel_id=1, source_target_pairs={{16,0},{32,16},{48,32},{64,48},{80,64},{96,80},{112,96},{17,1},{33... | collective-permute-start | bytes 3145736 | tf_op jit(solution)/shard_map/ppermute | solution.py:260
  302.9 42.2 %collective-permute-start.12 = (bf16[16,2,128,128]{3,2,1,0:T(8,128)(2,1)}, bf16[16,2,128,128]{3,2,1,0:T(8,128)(2,1)}, u32[]{:S(2)}, u32[]{:S(2)}) collective-permute-start(bf16[16,2,128,128]{3,2,1,0:T(8,128)(2,1)} %get-tuple-element.58), channel_id=1, source_target_pairs={{0,16},{16,32},{32,48},{48,64},{64,80},{80,96},{96,112},{1,17},{17... | collective-permute-start | bytes 3145736 | tf_op jit(solution)/shard_map/ppermute | solution.py:260
  345.1 5.1 %copy-start.1 = (bf16[16,3,128,128]{3,2,1,0:T(8,128)(2,1)}, bf16[16,3,128,128]{3,2,1,0:T(8,128)(2,1)S(1)}, u32[]{:S(2)}) copy-start(bf16[16,3,128,128]{3,2,1,0:T(8,128)(2,1)S(1)} %all-to-all-done.7) | copy-start | bytes 4718596
  345.1 1.0 copy-start.5

commit v3 on v2

--- a/solution.py
+++ b/solution.py
@@ -256,8 +256,7 @@
 
 def shift(value, axes, steps):
     count = lax.axis_size(axes)
-    pairs = [(s, s + steps) for s in range(max(0, -steps), min(count, count - steps))]
-    return lax.ppermute(value, axes, pairs)
+    return lax.ppermute(value, axes, [(s, (s + steps) % count) for s in range(count)])
 
 
 PAIR = ("core", "group")

time: 386 us -> 385 us (level)
  starting transfers between devices: 97.3 us -> 65.9 us
  waiting for transfers between devices: 140 us -> 168 us
    ppermute x12, waiting for transfers between devices: 0.03 us -> 23.7 us  [shift(): lax.ppermute(value, axes, [(s, (s + steps) % count) for s in range(count)])]
    all_to_all x7, starting transfers between devices: 63.5 us -> 43.6 us  [exchange(): return lax.all_to_all(x, axes, 0, 0)]
    ppermute x12, starting transfers between devices: 33.6 us -> 22.2 us  [shift(): lax.ppermute(value, axes, [(s, (s + steps) % count) for s in range(count)])]
    all_to_all x7, waiting for transfers between devices: 139 us -> 143 us  [exchange(): return lax.all_to_all(x, axes, 0, 0)]
  transfers between devices with their start and end apart: 20 -> 20, of which waited for: 6 -> 11; matrix products, arithmetic and copies ran while one was open for 1% -> 1% of each run, Pallas kernels for 17% -> 18%
where the time goes in v3:
time: 385 us; the launch traced here: 381 us
  waiting for transfers between devices  168 us (44%)
  Pallas kernels  85.4 us (22%)
  starting transfers between devices  65.9 us (17%)
  blocking collectives  54.6 us (14%)
  local copies, waits for them, and re-layouts  4.85 us (1%)
    all_to_all x7, waiting for transfers between devices, exchange(): return lax.all_to_all(x, axes, 0, 0)  143 us
    pallas_call x3, Pallas kernels, attention(): pl.pallas_call(functools.partial(attention_kernel, parts, size, n_query),...  62.6 us
    all_to_all x2, blocking collectives, exchange(): return lax.all_to_all(x, axes, 0, 0)  54.6 us
    all_to_all x7, starting transfers between devices, exchange(): return lax.all_to_all(x, axes, 0, 0)  43.6 us
    ppermute x12, waiting for transfers between devices, shift(): lax.ppermute(value, axes, [(s, (s + steps) % count) for s in range(count)])  23.7 us
    ppermute x12, starting transfers between devices, shift(): lax.ppermute(value, axes, [(s, (s + steps) % count) for s in range(count)])  22.2 us
    pallas_call x3, Pallas kernels, total_grads(): pl.pallas_call(total_kernel, grid=(blocks // step,), out_shape=jax.ShapeD...  12.3 us
  transfers between devices with their start and end apart: 20, of which 11 were waited for; matrix products, arithmetic and copies ran while one was open for 1% of the time, Pallas kernels for 18%

profile of v3, /device:TPU:8, one launch (start us, length us, event | category | flops | bytes accessed | tf_op | source)
XLA Modules:
  0.0 380.7 jit_solution(10063353772273073400)
XLA Ops:
  0.6 5.7 %split_heads.1 = (bf16[2,8,2,128,128]{4,3,2,1,0:T(8,128)(2,1)}, bf16[2,8,2,128,128]{4,3,2,1,0:T(8,128)(2,1)}, bf16[2,8,2,128,128]{4,3,2,1,0:T(8,128)(2,1)}, bf16...) custom-call(bf16[128,5120]{1,0:T(8,128)(2,1)} %k_ref.1, ...), custom_call_target="tpu_custom_call" | custom-call | bytes 10485760 | tf_op jit(solution)/shard_map/split_heads/pallas_call | solution.py:188
  6.3 24.8 %all_to_all.45.refs_1_ = bf16[16,2,128,128]{3,2,1,0:T(8,128)(2,1)S(1)} all-to-all(bf16[16,2,128,128]{3,2,1,0:T(8,128)(2,1)} %bitcast.22), channel_id=1, replica_groups=mesh['chip'=8,'core'=2,'group'=8] {'core','group'}, dimensions={0} | all-to-all | bytes 2097152 | tf_op jit(solution)/shard_map/all_to_all | solution.py:267
  31.1 4.9 %all-to-all-start.1 = ((bf16[16,2,128,128]{3,2,1,0:T(8,128)(2,1)}), bf16[16,2,128,128]{3,2,1,0:T(8,128)(2,1)S(1)}, u32[]{:S(2)}, u32[]{:S(2)}) async-start(bf16[16,2,128,128]{3,2,1,0:T(8,128)(2,1)} %bitcast.4), calls=%async_computation.1 | async-start | bytes 2097152 | tf_op jit(solution)/shard_map/all_to_all | solution.py:267
  36.0 1.5 collective-permute-start.1
  37.5 2.6 collective-permute-start.2
  40.1 33.8 %all-to-all-done.1.refs_1_ = bf16[16,2,128,128]{3,2,1,0:T(8,128)(2,1)S(1)} async-done(((bf16[16,2,128,128]{3,2,1,0:T(8,128)(2,1)}), bf16[16,2,128,128]{3,2,1,0:T(8,128)(2,1)S(1)}, u32[]{:S(2)}, u32[]{:S(2)}) %all-to-all-start.1) | async-done | bytes 1048608 | tf_op jit(solution)/shard_map/all_to_all | solution.py:267
  73.9 4.8 %all-to-all-start.2 = ((bf16[16,2,128,128]{3,2,1,0:T(8,128)(2,1)}), bf16[16,2,128,128]{3,2,1,0:T(8,128)(2,1)S(1)}, u32[]{:S(2)}, u32[]{:S(2)}) async-start(bf16[16,2,128,128]{3,2,1,0:T(8,128)(2,1)} %bitcast.21), calls=%async_computation.2 | async-start | bytes 2097152 | tf_op jit(solution)/shard_map/all_to_all | solution.py:267
  78.7 0.0 copy-start.10
  78.7 0.1 collective-permute-start.3
  78.8 4.1 %collective-permute-start.4 = (bf16[16,2,128,128]{3,2,1,0:T(8,128)(2,1)S(1)}, bf16[16,2,128,128]{3,2,1,0:T(8,128)(2,1)}, u32[]{:S(2)}, u32[]{:S(2)}) collective-permute-start(bf16[16,2,128,128]{3,2,1,0:T(8,128)(2,1)S(1)} %all-to-all-done.1.refs_1_), channel_id=1, source_target_pairs={{0,112},{16,0},{32,16},{48,32},{64,48},{80,64},{96,80},{112,96},{1... | collective-permute-start | bytes 3145736 | tf_op jit(solution)/shard_map/ppermute | solution.py:259
  82.9 0.0 collective-permute-done.1.refs_0_
  82.9 0.0 collective-permute-done.2.refs_2_
  82.9 33.6 %all-to-all-done.2.refs_3_ = bf16[16,2,128,128]{3,2,1,0:T(8,128)(2,1)S(1)} async-done(((bf16[16,2,128,128]{3,2,1,0:T(8,128)(2,1)}), bf16[16,2,128,128]{3,2,1,0:T(8,128)(2,1)S(1)}, u32[]{:S(2)}, u32[]{:S(2)}) %all-to-all-start.2) | async-done | bytes 1048608 | tf_op jit(solution)/shard_map/all_to_all | solution.py:267
  116.6 1.0 copy-done.9
  117.5 4.8 %all-to-all-start.3 = ((bf16[16,2,128,128]{3,2,1,0:T(8,128)(2,1)}), bf16[16,2,128,128]{3,2,1,0:T(8,128)(2,1)S(1)}, u32[]{:S(2)}, u32[]{:S(2)}) async-start(bf16[16,2,128,128]{3,2,1,0:T(8,128)(2,1)} %bitcast.20), calls=%async_computation.3 | async-start | bytes 2097152 | tf_op jit(solution)/shard_map/all_to_all | solution.py:267
  122.4 0.1 copy.10
  122.5 0.1 fusion.2
  122.5 0.2 collective-permute-start
  122.7 1.0 collective-permute-done
  123.7 0.1 broadcast_select_fusion
  123.8 0.2 slice_reduce_fusion.1
  124.0 0.0 collective-permute-done.3.refs_0_
  124.0 14.8 %all-to-all-done.3.refs_1_ = bf16[16,2,128,128]{3,2,1,0:T(8,128)(2,1)S(1)} async-done(((bf16[16,2,128,128]{3,2,1,0:T(8,128)(2,1)}), bf16[16,2,128,128]{3,2,1,0:T(8,128)(2,1)S(1)}, u32[]{:S(2)}, u32[]{:S(2)}) %all-to-all-start.3) | async-done | bytes 1048608 | tf_op jit(solution)/shard_map/all_to_all | solution.py:267
  138.8 5.5 %all-to-all-start.4 = ((bf16[16,2,128,128]{3,2,1,0:T(8,128)(2,1)}), bf16[16,2,128,128]{3,2,1,0:T(8,128)(2,1)}, u32[]{:S(2)}, u32[]{:S(2)}) async-start(bf16[16,2,128,128]{3,2,1,0:T(8,128)(2,1)} %bitcast.6), calls=%async_computation.4 | async-start | bytes 2097152 | tf_op jit(solution)/shard_map/all_to_all | solution.py:267
  144.4 0.2 slice_reduce_fusion
  144.6 0.7 reshape.49.ids_ref
  145.2 0.6 pad_add_fusion.2
  145.9 0.0 collective-permute-start.5
  145.9 4.1 %collective-permute-start.6 = (bf16[16,2,128,128]{3,2,1,0:T(8,128)(2,1)S(1)}, bf16[16,2,128,128]{3,2,1,0:T(8,128)(2,1)}, u32[]{:S(2)}, u32[]{:S(2)}) collective-permute-start(bf16[16,2,128,128]{3,2,1,0:T(8,128)(2,1)S(1)} %all-to-all-done.3.refs_1_), channel_id=1, source_target_pairs={{0,112},{16,0},{32,16},{48,32},{64,48},{80,64},{96,80},{112,96},{1... | collective-permute-start | bytes 3145736 | tf_op jit(solution)/shard_map/ppermute | solution.py:259
  150.0 26.0 %attention.3 = (bf16[16,128,128]{2,1,0:T(8,128)(2,1)}, bf16[16,2,128,128]{3,2,1,0:T(8,128)(2,1)}, bf16[16,2,128,128]{3,2,1,0:T(8,128)(2,1)}, bf16[16,2,128,128]{3,2,1,0:T(8,128)(2,1)}) custom-call(s32[192]{0:T(256)} %reshape.49.ids_ref, s32[17]{0:T(128)} %get-tuple-element.64.cnt_ref, bf16[16,2,128,128]{3,2,1,0:T(8,128)(2,1)} %collective-permute-done.1.refs_0_, ...), custom_call_target="tpu_custom_call" | custom-call | flops 2684354560 | bytes 7340032 | tf_op jit(solution)/shard_map/attention/pallas_call | solution.py:135
  176.0 0.1 collective-permute-start.7
  176.1 2.0 collective-permute-start.8
  178.1 23.4 %all-to-all-done.4.refs_3_ = bf16[16,2,128,128]{3,2,1,0:T(8,128)(2,1)} async-done(((bf16[16,2,128,128]{3,2,1,0:T(8,128)(2,1)}), bf16[16,2,128,128]{3,2,1,0:T(8,128)(2,1)}, u32[]{:S(2)}, u32[]{:S(2)}) %all-to-all-start.4) | async-done | bytes 1048608 | tf_op jit(solution)/shard_map/all_to_all | solution.py:267
  201.5 7.9 %all-to-all-start.6 = ((bf16[8,2,128,128]{3,2,1,0:T(8,128)(2,1)}), bf16[8,2,128,128]{3,2,1,0:T(8,128)(2,1)}, u32[]{:S(2)}, u32[]{:S(2)}) async-start(bf16[8,2,128,128]{3,2,1,0:T(8,128)(2,1)} %bitcast.23), calls=%async_computation.6 | async-start | bytes 1048576 | tf_op jit(solution)/shard_map/all_to_all | solution.py:267
  209.4 0.7 reshape.53.ids_ref
  210.1 23.2 %attention.4 = (bf16[16,128,128]{2,1,0:T(8,128)(2,1)}, bf16[16,2,128,128]{3,2,1,0:T(8,128)(2,1)}, bf16[16,2,128,128]{3,2,1,0:T(8,128)(2,1)}, bf16[16,2,128,128]{3,2,1,0:T(8,128)(2,1)}) custom-call(s32[192]{0:T(256)} %reshape.53.ids_ref, s32[17]{0:T(128)} %get-tuple-element.37.cnt_ref, bf16[16,2,128,128]{3,2,1,0:T(8,128)(2,1)} %collective-permute-done.3.refs_0_, ...), custom_call_target="tpu_custom_call" | custom-call | flops 2684354560 | bytes 7340032 | tf_op jit(solution)/shard_map/attention/pallas_call | solution.py:135
  233.3 0.0 collective-permute-done.5.refs_0_
  233.3 0.0 collective-permute-done.6.refs_2_
  233.3 0.0 copy-start.2
  233.3 0.0 collective-permute-done.8.refs_1_
  233.3 0.0 copy-start.3
  233.4 0.9 copy-done.2
  234.3 0.3 copy-done.3
  234.6 4.1 %total_grads.3 = bf16[16,3,128,128]{3,2,1,0:T(8,128)(2,1)} custom-call(bf16[16,128,128]{2,1,0:T(8,128)(2,1)} %get-tuple-element.43.dq_ref, bf16[16,2,128,128]{3,2,1,0:T(8,128)(2,1)} %get-tuple-element.44.own_ref, bf16[16,2,128,128]{3,2,1,0:T(8,128)(2,1)} %copy-done.2, bf16[16,2,128,128]{3,2,1,0:T(8,128)(2,1)} %copy-done.3), custom_call_target="tpu_custom_call" | custom-call | bytes 5242880 | tf_op jit(solution)/shard_map/total_grads/pallas_call | solution.py:244
  238.7 0.0 all-to-all-done.6.refs_3_
  238.7 8.0 %all-to-all-start.5 = ((bf16[16,3,128,128]{3,2,1,0:T(8,128)(2,1)}), bf16[16,3,128,128]{3,2,1,0:T(8,128)(2,1)S(1)}, u32[]{:S(2)}, u32[]{:S(2)}) async-start(bf16[16,3,128,128]{3,2,1,0:T(8,128)(2,1)} %total_grads.3), calls=%async_computation.5 | async-start | bytes 3145728 | tf_op jit(solution)/shard_map/all_to_all | solution.py:267
  246.7 3.8 %collective-permute-start.9 = (bf16[16,2,128,128]{3,2,1,0:T(8,128)(2,1)}, bf16[16,2,128,128]{3,2,1,0:T(8,128)(2,1)S(1)}, u32[]{:S(2)}, u32[]{:S(2)}) collective-permute-start(bf16[16,2,128,128]{3,2,1,0:T(8,128)(2,1)} %get-tuple-element.53), channel_id=1, source_target_pairs={{0,112},{16,0},{32,16},{48,32},{64,48},{80,64},{96,80},{112,96},{1... | collective-permute-start | bytes 3145736 | tf_op jit(solution)/shard_map/ppermute | solution.py:259
  250.5 0.1 fusion.5
  250.6 0.6 reshape.57.ids_ref
  251.2 0.2 slice_reduce_fusion.2
  251.4 0.6 pad_add_fusion.4.cnt_ref
  252.0 13.4 %attention.5 = (bf16[16,128,128]{2,1,0:T(8,128)(2,1)}, bf16[16,2,128,128]{3,2,1,0:T(8,128)(2,1)}, bf16[16,2,128,128]{3,2,1,0:T(8,128)(2,1)}, bf16[16,2,128,128]{3,2,1,0:T(8,128)(2,1)}) custom-call(s32[96]{0:T(128)} %reshape.57.ids_ref, s32[9]{0:T(128)} %pad_add_fusion.4.cnt_ref, bf16[16,2,128,128]{3,2,1,0:T(8,128)(2,1)} %collective-permute-done.5.refs_0_, ...), custom_call_target="tpu_custom_call" | custom-call | flops 1342177280 | bytes 6815744 | tf_op jit(solution)/shard_map/attention/pallas_call | solution.py:135
  265.3 11.3 %all-to-all-done.5 = bf16[16,3,128,128]{3,2,1,0:T(8,128)(2,1)S(1)} async-done(((bf16[16,3,128,128]{3,2,1,0:T(8,128)(2,1)}), bf16[16,3,128,128]{3,2,1,0:T(8,128)(2,1)S(1)}, u32[]{:S(2)}, u32[]{:S(2)}) %all-to-all-start.5) | async-done | bytes 1572896 | tf_op jit(solution)/shard_map/all_to_all | solution.py:267
  276.6 8.9 %collective-permute-done.9.refs_0_ = bf16[16,2,128,128]{3,2,1,0:T(8,128)(2,1)S(1)} collective-permute-done((bf16[16,2,128,128]{3,2,1,0:T(8,128)(2,1)}, bf16[16,2,128,128]{3,2,1,0:T(8,128)(2,1)S(1)}, u32[]{:S(2)}, u32[]{:S(2)}) %collective-permute-start.9) | collective-permute-done | bytes 1048608 | tf_op jit(solution)/shard_map/ppermute | solution.py:259
  285.5 3.0 collective-permute-done.10.refs_1_
  288.4 4.1 %total_grads.4 = bf16[16,3,128,128]{3,2,1,0:T(8,128)(2,1)} custom-call(bf16[16,128,128]{2,1,0:T(8,128)(2,1)} %get-tuple-element.51.dq_ref, bf16[16,2,128,128]{3,2,1,0:T(8,128)(2,1)} %get-tuple-element.52.own_ref, bf16[16,2,128,128]{3,2,1,0:T(8,128)(2,1)} %copy-done.4, bf16[16,2,128,128]{3,2,1,0:T(8,128)(2,1)} %collective-permute-done.10.refs_1_), custom_call_target="tpu_custom_call" | custom-call | bytes 5242880 | tf_op jit(solution)/shard_map/total_grads/pallas_call | solution.py:244
  292.6 7.6 %all-to-all-start.7 = ((bf16[16,3,128,128]{3,2,1,0:T(8,128)(2,1)}), bf16[16,3,128,128]{3,2,1,0:T(8,128)(2,1)S(1)}, u32[]{:S(2)}, u32[]{:S(2)}) async-start(bf16[16,3,128,128]{3,2,1,0:T(8,128)(2,1)} %total_grads.4), calls=%async_computation.7 | async-start | bytes 3145728 | tf_op jit(solution)/shard_map/all_to_all | solution.py:267
  300.1 3.8 %collective-permute-start.11 = (bf16[16,2,128,128]{3,2,1,0:T(8,128)(2,1)}, bf16[16,2,128,128]{3,2,1,0:T(8,128)(2,1)S(1)}, u32[]{:S(2)}, u32[]{:S(2)}) collective-permute-start(bf16[16,2,128,128]{3,2,1,0:T(8,128)(2,1)} %get-tuple-element.57), channel_id=1, source_target_pairs={{0,112},{16,0},{32,16},{48,32},{64,48},{80,64},{96,80},{112,96},{1... | collective-permute-start | bytes 3145736 | tf_op jit(solution)/shard_map/ppermute | solution.py:259
  304.0 26.1 %all-to-all-done.7 = bf16[16,3,128,128]{3,2,1,0:T(8,128)(2,1)S(1)} async-done(((bf16[16,3,128,128]{3,2,1,0:T(8,128)(2,1)}), bf16[16,3,128,128]{3,2,1,0:T(8,128)(2,1)S(1)}, u32[]{:S(2)}, u32[]{:S(2)}) %all-to-all-start.7) | async-done | bytes 1572896 | tf_op jit(solution)/shard_map/all_to_all | solution.py:267
  330.0 8.9 %collective-permute-done.11.refs_0_ = bf16[16,2,128,128]{3,2,1,0:T(8,128)(2,1)S(1)} collective-permute-done((bf16[16,2,128,128]{3,2,1,0:T(8,128)(2,1)}, bf16[16,2,128,128]{3,2,1,0:T(8,128)(2,1)S(1)}, u32[]{:S(2)}, u32[]{:S(2)}) %collective-permute-start.11) | collective-permute-done | bytes 1048608 | tf_op jit(solution)/shard_map/ppermute | solution.py:259
  338.9 3.0 collective-permute-done.12.refs_1_
  341.9 4.1 %total_grads.5 = bf16[16,3,128,128]{3,2,1,0:T(8,128)(2,1)} custom-call(bf16[16,128,128]{2,1,0:T(8,128)(2,1)} %get-tuple-element.55.dq_ref, bf16[16,2,128,128]{3,2,1,0:T(8,128)(2,1)} %get-tuple-element.56.own_ref, bf16[16,2,128,128]{3,2,1,0:T(8,128)(2,1)} %copy-done.5, bf16[16,2,128,128]{3,2,1,0:T(8,128)(2,1)} %collective-permute-done.12.refs_1_), custom_call_target="tpu_custom_call" | custom-call | bytes 5242880 | tf_op jit(solution)/shard_map/total_grads/pallas_call | solution.py:244
  346.0 29.9 %all_to_all.46 = bf16[16,3,128,128]{3,2,1,0:T(8,128)(2,1)} all-to-all(bf16[16,3,128,128]{3,2,1,0:T(8,128)(2,1)} %total_grads.5), channel_id=1, replica_groups=mesh['chip'=8,'core'=2,'group'=8] {'core','group'}, dimensions={0} | all-to-all | bytes 3145728 | tf_op jit(solution)/shard_map/all_to_all | solution.py:267
  375.8 4.9 %join_heads.1 = (bf16[128,5120]{1,0:T(8,128)(2,1)}, bf16[128,5120]{1,0:T(8,128)(2,1)}, bf16[128,5120]{1,0:T(8,128)(2,1)}) custom-call(bf16[2,8,3,128,128]{4,3,2,1,0:T(8,128)(2,1)} %bitcast.17, bf16[2,8,3,128,128]{4,3,2,1,0:T(8,128)(2,1)} %bitcast.18, bf16[2,8,3,128,128]{4,3,2,1,0:T(8,128)(2,1)} %bitcast.19), custom_call_target="tpu_custom_call" | custom-call | bytes 7864320 | tf_op jit(solution)/shard_map/join_heads/pallas_call | solution.py:218
  (26 shorter events, 0.1 us)
Async XLA Ops:
  31.1 42.8 %copy-start.8 = (bf16[16,2,128,128]{3,2,1,0:T(8,128)(2,1)}, bf16[16,2,128,128]{3,2,1,0:T(8,128)(2,1)S(1)}, u32[]{:S(2)}) copy-start(bf16[16,2,128,128]{3,2,1,0:T(8,128)(2,1)S(1)} %all_to_all.45.refs_1_) | copy-start | bytes 3145732
  31.1 42.8 %all-to-all-start.1 = ((bf16[16,2,128,128]{3,2,1,0:T(8,128)(2,1)}), bf16[16,2,128,128]{3,2,1,0:T(8,128)(2,1)S(1)}, u32[]{:S(2)}, u32[]{:S(2)}) async-start(bf16[16,2,128,128]{3,2,1,0:T(8,128)(2,1)} %bitcast.4), calls=%async_computation.1 | async-start | bytes 2097152 | tf_op jit(solution)/shard_map/all_to_all | solution.py:267
  36.0 47.0 %collective-permute-start.1 = (bf16[16,2,128,128]{3,2,1,0:T(8,128)(2,1)S(1)}, bf16[16,2,128,128]{3,2,1,0:T(8,128)(2,1)}, u32[]{:S(2)}, u32[]{:S(2)}) collective-permute-start(bf16[16,2,128,128]{3,2,1,0:T(8,128)(2,1)S(1)} %all_to_all.45.refs_1_), channel_id=1, source_target_pairs={{0,16},{16,32},{32,48},{48,64},{64,80},{80,96},{96,112},{112,0},{1... | collective-permute-start | bytes 3145736 | tf_op jit(solution)/shard_map/ppermute | solution.py:259
  37.5 45.5 %collective-permute-start.2 = (bf16[16,2,128,128]{3,2,1,0:T(8,128)(2,1)S(1)}, bf16[16,2,128,128]{3,2,1,0:T(8,128)(2,1)}, u32[]{:S(2)}, u32[]{:S(2)}) collective-permute-start(bf16[16,2,128,128]{3,2,1,0:T(8,128)(2,1)S(1)} %all_to_all.45.refs_1_), channel_id=1, source_target_pairs={{0,112},{16,0},{32,16},{48,32},{64,48},{80,64},{96,80},{112,96},{1... | collective-permute-start | bytes 3145736 | tf_op jit(solution)/shard_map/ppermute | solution.py:259
  73.9 43.7 %copy-start.7 = (bf16[16,2,128,128]{3,2,1,0:T(8,128)(2,1)}, bf16[16,2,128,128]{3,2,1,0:T(8,128)(2,1)S(1)}, u32[]{:S(2)}) copy-start(bf16[16,2,128,128]{3,2,1,0:T(8,128)(2,1)S(1)} %all-to-all-done.1.refs_1_) | copy-start | bytes 3145732
  73.9 42.7 %all-to-all-start.2 = ((bf16[16,2,128,128]{3,2,1,0:T(8,128)(2,1)}), bf16[16,2,128,128]{3,2,1,0:T(8,128)(2,1)S(1)}, u32[]{:S(2)}, u32[]{:S(2)}) async-start(bf16[16,2,128,128]{3,2,1,0:T(8,128)(2,1)} %bitcast.21), calls=%async_computation.2 | async-start | bytes 2097152 | tf_op jit(solution)/shard_map/all_to_all | solution.py:267
  78.7 43.7 %copy-start.11 = (s32[5,8]{1,0:T(8,128)S(1)}, s32[5,8]{1,0:T(8,128)}, u32[]{:S(2)}) copy-start(s32[5,8]{1,0:T(8,128)} %param.11) | copy-start | bytes 484
  78.7 43.8 %copy-start.10 = (s32[5,8,12]{2,1,0:T(8,128)S(1)}, s32[5,8,12]{2,1,0:T(8,128)}, u32[]{:S(2)}) copy-start(s32[5,8,12]{2,1,0:T(8,128)} %param.10) | copy-start | bytes 5764
  78.7 45.3 %collective-permute-start.3 = (bf16[16,2,128,128]{3,2,1,0:T(8,128)(2,1)S(1)}, bf16[16,2,128,128]{3,2,1,0:T(8,128)(2,1)}, u32[]{:S(2)}, u32[]{:S(2)}) collective-permute-start(bf16[16,2,128,128]{3,2,1,0:T(8,128)(2,1)S(1)} %all-to-all-done.1.refs_1_), channel_id=1, source_target_pairs={{0,16},{16,32},{32,48},{48,64},{64,80},{80,96},{96,112},{112,0},{1... | collective-permute-start | bytes 3145736 | tf_op jit(solution)/shard_map/ppermute | solution.py:259
  78.8 45.2 %collective-permute-start.4 = (bf16[16,2,128,128]{3,2,1,0:T(8,128)(2,1)S(1)}, bf16[16,2,128,128]{3,2,1,0:T(8,128)(2,1)}, u32[]{:S(2)}, u32[]{:S(2)}) collective-permute-start(bf16[16,2,128,128]{3,2,1,0:T(8,128)(2,1)S(1)} %all-to-all-done.1.refs_1_), channel_id=1, source_target_pairs={{0,112},{16,0},{32,16},{48,32},{64,48},{80,64},{96,80},{112,96},{1... | collective-permute-start | bytes 3145736 | tf_op jit(solution)/shard_map/ppermute | solution.py:259
  116.6 1.0 copy-start.9
  117.5 21.3 %all-to-all-start.3 = ((bf16[16,2,128,128]{3,2,1,0:T(8,128)(2,1)}), bf16[16,2,128,128]{3,2,1,0:T(8,128)(2,1)S(1)}, u32[]{:S(2)}, u32[]{:S(2)}) async-start(bf16[16,2,128,128]{3,2,1,0:T(8,128)(2,1)} %bitcast.20), calls=%async_computation.3 | async-start | bytes 2097152 | tf_op jit(solution)/shard_map/all_to_all | solution.py:267
  122.5 1.2 collective-permute-start
  138.8 37.2 %copy-start.6 = (bf16[16,2,128,128]{3,2,1,0:T(8,128)(2,1)}, bf16[16,2,128,128]{3,2,1,0:T(8,128)(2,1)S(1)}, u32[]{:S(2)}) copy-start(bf16[16,2,128,128]{3,2,1,0:T(8,128)(2,1)S(1)} %all-to-all-done.3.refs_1_) | copy-start | bytes 3145732
  138.8 62.6 %all-to-all-start.4 = ((bf16[16,2,128,128]{3,2,1,0:T(8,128)(2,1)}), bf16[16,2,128,128]{3,2,1,0:T(8,128)(2,1)}, u32[]{:S(2)}, u32[]{:S(2)}) async-start(bf16[16,2,128,128]{3,2,1,0:T(8,128)(2,1)} %bitcast.6), calls=%async_computation.4 | async-start | bytes 2097152 | tf_op jit(solution)/shard_map/all_to_all | solution.py:267
  145.9 87.4 %collective-permute-start.5 = (bf16[16,2,128,128]{3,2,1,0:T(8,128)(2,1)S(1)}, bf16[16,2,128,128]{3,2,1,0:T(8,128)(2,1)}, u32[]{:S(2)}, u32[]{:S(2)}) collective-permute-start(bf16[16,2,128,128]{3,2,1,0:T(8,128)(2,1)S(1)} %all-to-all-done.3.refs_1_), channel_id=1, source_target_pairs={{0,16},{16,32},{32,48},{48,64},{64,80},{80,96},{96,112},{112,0},{1... | collective-permute-start | bytes 3145736 | tf_op jit(solution)/shard_map/ppermute | solution.py:259
  145.9 87.4 %collective-permute-start.6 = (bf16[16,2,128,128]{3,2,1,0:T(8,128)(2,1)S(1)}, bf16[16,2,128,128]{3,2,1,0:T(8,128)(2,1)}, u32[]{:S(2)}, u32[]{:S(2)}) collective-permute-start(bf16[16,2,128,128]{3,2,1,0:T(8,128)(2,1)S(1)} %all-to-all-done.3.refs_1_), channel_id=1, source_target_pairs={{0,112},{16,0},{32,16},{48,32},{64,48},{80,64},{96,80},{112,96},{1... | collective-permute-start | bytes 3145736 | tf_op jit(solution)/shard_map/ppermute | solution.py:259
  176.0 57.3 %collective-permute-start.7 = (bf16[16,2,128,128]{3,2,1,0:T(8,128)(2,1)}, bf16[16,2,128,128]{3,2,1,0:T(8,128)(2,1)S(1)}, u32[]{:S(2)}, u32[]{:S(2)}) collective-permute-start(bf16[16,2,128,128]{3,2,1,0:T(8,128)(2,1)} %get-tuple-element.45), channel_id=1, source_target_pairs={{0,112},{16,0},{32,16},{48,32},{64,48},{80,64},{96,80},{112,96},{1... | collective-permute-start | bytes 3145736 | tf_op jit(solution)/shard_map/ppermute | solution.py:259
  176.1 57.3 %collective-permute-start.8 = (bf16[16,2,128,128]{3,2,1,0:T(8,128)(2,1)}, bf16[16,2,128,128]{3,2,1,0:T(8,128)(2,1)S(1)}, u32[]{:S(2)}, u32[]{:S(2)}) collective-permute-start(bf16[16,2,128,128]{3,2,1,0:T(8,128)(2,1)} %get-tuple-element.46), channel_id=1, source_target_pairs={{0,16},{16,32},{32,48},{48,64},{64,80},{80,96},{96,112},{112,0},{1... | collective-permute-start | bytes 3145736 | tf_op jit(solution)/shard_map/ppermute | solution.py:259
  201.5 37.3 %all-to-all-start.6 = ((bf16[8,2,128,128]{3,2,1,0:T(8,128)(2,1)}), bf16[8,2,128,128]{3,2,1,0:T(8,128)(2,1)}, u32[]{:S(2)}, u32[]{:S(2)}) async-start(bf16[8,2,128,128]{3,2,1,0:T(8,128)(2,1)} %bitcast.23), calls=%async_computation.6 | async-start | bytes 1048576 | tf_op jit(solution)/shard_map/all_to_all | solution.py:267
  233.3 1.0 copy-start.2
  233.3 1.3 copy-start.3
  238.7 37.9 %all-to-all-start.5 = ((bf16[16,3,128,128]{3,2,1,0:T(8,128)(2,1)}), bf16[16,3,128,128]{3,2,1,0:T(8,128)(2,1)S(1)}, u32[]{:S(2)}, u32[]{:S(2)}) async-start(bf16[16,3,128,128]{3,2,1,0:T(8,128)(2,1)} %total_grads.3), calls=%async_computation.5 | async-start | bytes 3145728 | tf_op jit(solution)/shard_map/all_to_all | solution.py:267
  246.7 38.7 %collective-permute-start.9 = (bf16[16,2,128,128]{3,2,1,0:T(8,128)(2,1)}, bf16[16,2,128,128]{3,2,1,0:T(8,128)(2,1)S(1)}, u32[]{:S(2)}, u32[]{:S(2)}) collective-permute-start(bf16[16,2,128,128]{3,2,1,0:T(8,128)(2,1)} %get-tuple-element.53), channel_id=1, source_target_pairs={{0,112},{16,0},{32,16},{48,32},{64,48},{80,64},{96,80},{112,96},{1... | collective-permute-start | bytes 3145736 | tf_op jit(solution)/shard_map/ppermute | solution.py:259
  250.5 37.9 %collective-permute-start.10 = (bf16[16,2,128,128]{3,2,1,0:T(8,128)(2,1)}, bf16[16,2,128,128]{3,2,1,0:T(8,128)(2,1)}, u32[]{:S(2)}, u32[]{:S(2)}) collective-permute-start(bf16[16,2,128,128]{3,2,1,0:T(8,128)(2,1)} %get-tuple-element.54), channel_id=1, source_target_pairs={{0,16},{16,32},{32,48},{48,64},{64,80},{80,96},{96,112},{112,0},{1... | collective-permute-start | bytes 3145736 | tf_op jit(solution)/shard_map/ppermute | solution.py:259
  276.6 16.0 %copy-start = (bf16[16,3,128,128]{3,2,1,0:T(8,128)(2,1)}, bf16[16,3,128,128]{3,2,1,0:T(8,128)(2,1)S(1)}, u32[]{:S(2)}) copy-start(bf16[16,3,128,128]{3,2,1,0:T(8,128)(2,1)S(1)} %all-to-all-done.5) | copy-start | bytes 4718596
  285.5 3.0 copy-start.4
  292.6 37.5 %all-to-all-start.7 = ((bf16[16,3,128,128]{3,2,1,0:T(8,128)(2,1)}), bf16[16,3,128,128]{3,2,1,0:T(8,128)(2,1)S(1)}, u32[]{:S(2)}, u32[]{:S(2)}) async-start(bf16[16,3,128,128]{3,2,1,0:T(8,128)(2,1)} %total_grads.4), calls=%async_computation.7 | async-start | bytes 3145728 | tf_op jit(solution)/shard_map/all_to_all | solution.py:267
  300.1 38.7 %collective-permute-start.11 = (bf16[16,2,128,128]{3,2,1,0:T(8,128)(2,1)}, bf16[16,2,128,128]{3,2,1,0:T(8,128)(2,1)S(1)}, u32[]{:S(2)}, u32[]{:S(2)}) collective-permute-start(bf16[16,2,128,128]{3,2,1,0:T(8,128)(2,1)} %get-tuple-element.57), channel_id=1, source_target_pairs={{0,112},{16,0},{32,16},{48,32},{64,48},{80,64},{96,80},{112,96},{1... | collective-permute-start | bytes 3145736 | tf_op jit(solution)/shard_map/ppermute | solution.py:259
  304.0 37.9 %collective-permute-start.12 = (bf16[16,2,128,128]{3,2,1,0:T(8,128)(2,1)}, bf16[16,2,128,128]{3,2,1,0:T(8,128)(2,1)}, u32[]{:S(2)}, u32[]{:S(2)}) collective-permute-start(bf16[16,2,128,128]{3,2,1,0:T(8,128)(2,1)} %get-tuple-element.58), channel_id=1, source_target_pairs={{0,16},{16,32},{32,48},{48,64},{64,80},{80,96},{96,112},{112,0},{1... | collective-permute-start | bytes 3145736 | tf_op jit(solution)/shard_map/ppermute | solution.py:259
  330.0 16.0 %copy-start.1 = (bf16[16,3,128,128]{3,2,1,0:T(8,128)(2,1)}, bf16[16,3,128,128]{3,2,1,0:T(8,128)(2,1)S(1)}, u32[]{:S(2)}) copy-start(bf16[16,3,128,128]{3,2,1,0:T(8,128)(2,1)S(1)} %all-to-all-done.7) | copy-start | bytes 4718596
  338.9 3.0 copy-start.5

commit v4 on v3

v4 whole, which is shorter than its diff:
```python
import functools

import jax
import jax.numpy as jnp
from jax import lax
from jax.experimental import pallas as pl
from jax.experimental.pallas import tpu as pltpu
from jax.sharding import Mesh
from jax.sharding import PartitionSpec as P

HD = 128
BLK = 128
BAND = 2
BPD = 8
MAXK = 12
HPG = 5
GROUP = 4
ATTENTION_COST = 10
VMEM_LIMIT = 56 * 2**20
NEG = -1e30
LOG2E = 1.4426950408889634
SCALE = HD**-0.5
F32 = jnp.float32
BF16 = jnp.bfloat16
NT = (((1,), (1,)), ((), ()))
NN = (((1,), (0,)), ((), ()))
TN = (((0,), (0,)), ((), ()))


def dot(a, b, dims):
    return lax.dot_general(a, b, dims, preferred_element_type=F32)


def fold(x):
    return x.reshape(-1, 8, HD)


def query_block(n_keys, b, ids_ref, count, qd, keys, values, acc, dq, kcat, s_scr, dp_scr, ds_scr):
    q = qd[b, 0]
    do = qd[b, 1]
    base = b * MAXK
    m8 = jnp.full((8, HD), NEG, F32)
    index = [ids_ref[base + s] for s in range(n_keys)]
    for s in range(n_keys):
        k = keys[index[s]]
        kcat[pl.ds(s * BLK, BLK), :] = k
        st = dot(k, q, NT)
        if s > n_keys - GROUP:
            st = jnp.where(s < count, st, NEG)
        s_scr[s] = st
        m8 = jnp.maximum(m8, jnp.max(fold(st), axis=0))
        dp_scr[s] = dot(values[index[s]], do, NT)
    m = jnp.max(m8, axis=0, keepdims=True) * (SCALE * LOG2E)
    l8 = jnp.zeros((8, HD), F32)
    r8 = jnp.zeros((8, HD), F32)
    for s in range(n_keys):
        p = jnp.exp2(s_scr[s] * (SCALE * LOG2E) - m)
        s_scr[s] = p
        l8 += jnp.sum(fold(p), axis=0)
        r8 += jnp.sum(fold(p * dp_scr[s]), axis=0)
    inv = 1.0 / jnp.sum(l8, axis=0, keepdims=True)
    rd = jnp.sum(r8, axis=0, keepdims=True) * inv
    for s in range(n_keys):
        p = s_scr[s] * inv
        ds = (p * (dp_scr[s] - rd)).astype(BF16)
        ds_scr[pl.ds(s * BLK, BLK), :] = ds
        acc[index[s], 0] += dot(ds, q, NN)
        acc[index[s], 1] += dot(p.astype(BF16), do, NN)
    rows = pl.ds(0, n_keys * BLK)
    dq[...] = (dot(ds_scr[rows, :], kcat[rows, :], TN) * SCALE).astype(BF16)


def attention_kernel(size, n_query, fetches, ids_ref, cnt_ref, place_ref, *refs):
    sources, refs = refs[: len(fetches)], refs[len(fetches) :]
    qd_in, dq_out, left_out, own_out, right_out = refs[:5]
    keys, values, qd, acc, stage, dq, kcat, s_scr, dp_scr, ds_scr, in_sem, out_sem = refs[5:]
    copies = []
    for source, fetch in zip(sources, fetches):
        for src, t, i in fetch(source, place_ref):
            dst = (keys, values)[t].at[pl.ds(i * size, size)]
            copies.append(pltpu.make_async_copy(src, dst, in_sem.at[len(copies)]))
    q_rows = qd_in.at[pl.ds(pl.multiple_of(place_ref[0], 8), n_query)]
    copies.append(pltpu.make_async_copy(q_rows, qd, in_sem.at[len(copies)]))
    for copy in copies:
        copy.start()
    acc[...] = jnp.zeros_like(acc)
    first = place_ref[1]
    if n_query < size:
        dq[...] = jnp.zeros_like(dq)
    for copy in copies:
        copy.wait()

    def one(b, carry):
        count = cnt_ref[b]
        for upto in range(GROUP, MAXK + 1, GROUP):

            @pl.when((count > upto - GROUP) & (count <= upto))
            def _():
                query_block(
                    upto, b, ids_ref, count, qd, keys, values, acc, dq.at[first + b], kcat, s_scr, dp_scr, ds_scr
                )

        return carry

    lax.fori_loop(0, n_query, one, 0)
    puts = [pltpu.make_async_copy(dq, dq_out, out_sem.at[3])]
    puts[0].start()
    for i, target in enumerate((left_out, own_out, right_out)):

        def convert(j, carry):
            stage[j, 0] = (acc[j, 0] * SCALE).astype(BF16)
            stage[j, 1] = acc[j, 1].astype(BF16)
            return carry

        lax.fori_loop(i * size, (i + 1) * size, convert, 0)
        puts.append(pltpu.make_async_copy(stage.at[pl.ds(i * size, size)], target, out_sem.at[i]))
        puts[-1].start()
    for copy in puts:
        copy.wait()


def attention(ids, counts, place, sources, fetches, qd, n_query, size):
    window = 3 * size
    smem = pl.BlockSpec(memory_space=pltpu.SMEM)
    hbm = pl.BlockSpec(memory_space=pl.ANY)
    pairs = n_query * 8
    out = pl.pallas_call(
        functools.partial(attention_kernel, size, n_query, fetches),
        out_shape=[jax.ShapeDtypeStruct((size, BLK, HD), BF16)]
        + [jax.ShapeDtypeStruct((size, 2, BLK, HD), BF16)] * 3,
        in_specs=[smem] * 3 + [hbm] * (len(sources) + 1),
        out_specs=[hbm] * 4,
        scratch_shapes=[
            pltpu.VMEM((window, BLK, HD), BF16),
            pltpu.VMEM((window, BLK, HD), BF16),
            pltpu.VMEM((n_query, 2, BLK, HD), BF16),
            pltpu.VMEM((window, 2, BLK, HD), F32),
            pltpu.VMEM((window, 2, BLK, HD), BF16),
            pltpu.VMEM((size, BLK, HD), BF16),
            pltpu.VMEM((MAXK * BLK, HD), BF16),
            pltpu.VMEM((MAXK, BLK, HD), F32),
            pltpu.VMEM((MAXK, BLK, HD), F32),
            pltpu.VMEM((MAXK * BLK, HD), BF16),
            pltpu.SemaphoreType.DMA((7,)),
            pltpu.SemaphoreType.DMA((4,)),
        ],
        compiler_params=pltpu.CompilerParams(vmem_limit_bytes=VMEM_LIMIT),
        cost_estimate=pl.CostEstimate(
            flops=pairs * ATTENTION_COST * BLK * BLK * HD,
            bytes_accessed=(2 * window + n_query) * 2 * BLK * HD * 2,
            transcendentals=pairs * BLK * BLK,
        ),
        name="attention",
    )(ids, counts, place, *sources, qd)
    return out[0], out[1:]


def split_kernel(k_ref, v_ref, q_ref, g_ref, ka_ref, va_ref, qda_ref, kvb_ref, qdb_ref):
    for j in range(ka_ref.shape[1]):

        def head(ref, m):
            return ref[:, (j * HPG + m) * HD : (j * HPG + m + 1) * HD]

        for m in range(4):
            ka_ref[m, j] = head(k_ref, m)
            va_ref[m, j] = head(v_ref, m)
            qda_ref[m, j, 0] = head(q_ref, m)
            qda_ref[m, j, 1] = head(g_ref, m)
        for core in range(2):
            kvb_ref[core, j, 0] = head(k_ref, 4)
            kvb_ref[core, j, 1] = head(v_ref, 4)
        qdb_ref[j, 0] = head(q_ref, 4)
        qdb_ref[j, 1] = head(g_ref, 4)


def split_heads(key_in, value_in, query_in, out_grad):
    groups, step = key_in.shape[1] // (HPG * HD), 2

    one = pl.BlockSpec((4, step, BLK, HD), lambda j: (0, j, 0, 0))
    two = pl.BlockSpec((4, step, 2, BLK, HD), lambda j: (0, j, 0, 0, 0))
    kvb = pl.BlockSpec((2, step, 2, BLK, HD), lambda j: (0, j, 0, 0, 0))
    qdb = pl.BlockSpec((step, 2, BLK, HD), lambda j: (j, 0, 0, 0))
    shapes = ((4, groups), (4, groups), (4, groups, 2), (2, groups, 2), (groups, 2))
    ka, va, qda, kvb_out, qdb_out = pl.pallas_call(
        split_kernel,
        grid=(groups // step,),
        out_shape=tuple(jax.ShapeDtypeStruct((*x, BLK, HD), BF16) for x in shapes),
        in_specs=[pl.BlockSpec((BLK, step * HPG * HD), lambda j: (0, j))] * 4,
        out_specs=(one, one, two, kvb, qdb),
        compiler_params=pltpu.CompilerParams(vmem_limit_bytes=VMEM_LIMIT),
        cost_estimate=pl.CostEstimate(flops=0, bytes_accessed=16 * key_in.size, transcendentals=0),
        name="split_heads",
    )(key_in, value_in, query_in, out_grad)
    flat = 4 * groups
    return (
        ka.reshape(flat, BLK, HD),
        va.reshape(flat, BLK, HD),
        qda.reshape(flat, 2, BLK, HD),
        kvb_out.reshape(2 * groups, 2, BLK, HD),
        qdb_out,
    )


def join_kernel(dqa_ref, dkva_ref, b_ref, *outs):
    for t, ref in enumerate(outs):
        for j in range(dqa_ref.shape[1]):

            def put(m, value):
                ref[:, (j * HPG + m) * HD : (j * HPG + m + 1) * HD] = value

            for m in range(4):
                put(m, dqa_ref[m, j] if t == 0 else dkva_ref[m, j, t - 1])
            put(4, (b_ref[0, j, t].astype(F32) + b_ref[1, j, t].astype(F32)).astype(BF16))


def join_heads(dqa, dkva, back_b):
    groups, step = dqa.shape[0] // 4, 2
    out = jax.ShapeDtypeStruct((BLK, groups * HPG * HD), BF16)
    return pl.pallas_call(
        join_kernel,
        grid=(groups // step,),
        out_shape=(out,) * 3,
        in_specs=[
            pl.BlockSpec((4, step, BLK, HD), lambda j: (0, j, 0, 0)),
            pl.BlockSpec((4, step, 2, BLK, HD), lambda j: (0, j, 0, 0, 0)),
            pl.BlockSpec((2, step, 3, BLK, HD), lambda j: (0, j, 0, 0, 0)),
        ],
        out_specs=(pl.BlockSpec((BLK, step * HPG * HD), lambda j: (0, j)),) * 3,
        compiler_params=pltpu.CompilerParams(vmem_limit_bytes=VMEM_LIMIT),
        cost_estimate=pl.CostEstimate(
            flops=0, bytes_accessed=groups * HPG * 3 * BLK * HD * 4, transcendentals=0
        ),
        name="join_heads",
    )(
        dqa.reshape(4, groups, BLK, HD),
        dkva.reshape(4, groups, 2, BLK, HD),
        back_b.reshape(2, groups, 3, BLK, HD),
    )


def total_kernel(dq_ref, own_ref, *refs):
    terms, out_ref = refs[:-1], refs[-1]
    out_ref[:, 0] = dq_ref[...]
    total = own_ref[...].astype(F32)
    for term in terms:
        total += term[...].astype(F32)
    out_ref[:, 1:] = total.astype(BF16)


def total_grads(dq, own, terms):
    blocks, step = dq.shape[0], 4
    kv_spec = pl.BlockSpec((step, 2, BLK, HD), lambda i: (i, 0, 0, 0))
    return pl.pallas_call(
        total_kernel,
        grid=(blocks // step,),
        out_shape=jax.ShapeDtypeStruct((blocks, 3, BLK, HD), BF16),
        in_specs=[pl.BlockSpec((step, BLK, HD), lambda i: (i, 0, 0))] + [kv_spec] * (1 + len(terms)),
        out_specs=pl.BlockSpec((step, 3, BLK, HD), lambda i: (i, 0, 0, 0)),
        cost_estimate=pl.CostEstimate(
            flops=0, bytes_accessed=(6 + 2 * len(terms)) * dq.size * 2, transcendentals=0
        ),
        name="total_grads",
    )(dq, own, *terms)


def both_halves_kernel(x_ref, own0, own1, right0, right1, left0, left1, out_ref):
    x = x_ref[0]
    for s, own in enumerate((own0, own1)):
        right = jnp.where(x == x_ref[1], (right1, right0)[s][...], (right0, right1)[s][...])
        left = jnp.where(x == 0, (left1, left0)[s][...], (left0, left1)[s][...])
        total = own[...].astype(F32) + right.astype(F32) + left.astype(F32)
        out_ref[s] = total.astype(BF16)


def both_halves(x, last, own, from_right, from_left):
    blocks, step = own[0].shape[0], 4
    spec = pl.BlockSpec((step, 2, BLK, HD), lambda i: (i, 0, 0, 0))
    out = pl.pallas_call(
        both_halves_kernel,
        grid=(blocks // step,),
        out_shape=jax.ShapeDtypeStruct((2, blocks, 2, BLK, HD), BF16),
        in_specs=[pl.BlockSpec(memory_space=pltpu.SMEM)] + [spec] * 6,
        out_specs=pl.BlockSpec((2, step, 2, BLK, HD), lambda i: (0, i, 0, 0, 0)),
        cost_estimate=pl.CostEstimate(flops=0, bytes_accessed=16 * own[0].size, transcendentals=0),
        name="both_halves",
    )(jnp.stack([x, jnp.int32(last)]), *own, *from_right, *from_left)
    return out.reshape(2 * blocks, 2, BLK, HD)


WIDE = ("half", "core", "group")
PAIR = ("core", "group")
CHIPS = ("half", "x")


def shift(value, axes, steps):
    count = lax.axis_size(axes)
    return lax.ppermute(value, axes, [(s, (s + steps) % count) for s in range(count)])


def exchange(x, axes):
    return lax.all_to_all(x, axes, 0, 0, tiled=True)


def after(x, *done):
    return lax.optimization_barrier((x, *done))[0]


def shards(query_in, key_in, value_in, out_grad, key_blocks, block_count):
    half, x, core = (lax.axis_index(name) for name in ("half", "x", "core"))
    last = lax.axis_size("x") - 1
    packed = jnp.concatenate([key_blocks, block_count[:, :, None]], axis=2)
    ka, va, qda, kvb, qdb = split_heads(key_in, value_in, query_in, out_grad)

    keys = exchange(ka, WIDE)
    key_near = [shift(keys, "x", 1), shift(keys, "x", -1)]
    values = exchange(after(va, keys), WIDE)
    value_near = [shift(values, "x", 1), shift(values, "x", -1)]
    queries = exchange(after(qda, values, *key_near), WIDE)
    lists = lax.all_gather(packed[:4], ("half", "core"))
    lists = lax.dynamic_index_in_dim(lists, 2 * half + core, 1, False)
    own_b = exchange(after(kvb, queries, *key_near, *value_near), PAIR)
    near_b = [shift(own_b, CHIPS, 1), shift(own_b, CHIPS, -1)]
    queries_b = exchange(after(qdb, own_b), "group")

    def plain(lists, chip):
        lists = lists.reshape(-1, MAXK + 1)
        first_block = (chip - 1) * 2 * BPD
        return (lists[:, :MAXK] - first_block).reshape(-1), lists[:, MAXK]

    def third(t, i):
        return lambda ref, place: [(ref.at[pl.ds(pl.multiple_of(place[2 + i], 8), size)], t, i)]

    size = 2 * BPD
    fetches = [third(t, i) for t in range(2) for i in range(3)]
    sources = (key_near[0], keys, key_near[1], value_near[0], values, value_near[1])
    done = []
    for s in range(2):
        ids, counts = plain(lists[2 * s : 2 * s + 2], s * (last + 1) + x)
        left = jnp.where(x == 0, 1 - s, s) * size
        right = jnp.where(x == last, 1 - s, s) * size
        place = jnp.stack([jnp.int32(s * size), jnp.int32(0), left, jnp.int32(s * size), right])
        place = after(place, *[d[0] for d in done])
        dq, grads = attention(ids, counts, place, sources, fetches, queries, size, size)
        done.append((dq, grads, shift(grads[0], "x", -1), shift(grads[2], "x", 1)))

    def pair(i):
        return lambda ref, place: [(ref.at[:, t], t, i) for t in range(2)]

    ids, counts = plain(packed[4], half * (last + 1) + x)
    place = jnp.stack([jnp.int32(0), core * BPD])
    place = after(place, done[1][0], done[0][2], done[0][3])
    dq_b, grads_b = attention(
        ids, counts, place, (near_b[0], own_b, near_b[1]), [pair(i) for i in range(3)], queries_b, BPD, size
    )
    terms_b = [shift(grads_b[0], CHIPS, -1), shift(grads_b[2], CHIPS, 1)]

    dqa = jnp.concatenate([done[0][0], done[1][0]])
    dqa = exchange(after(dqa, *near_b), WIDE)
    dkva = both_halves(
        after(x, dq_b), last, [d[1][1] for d in done], [d[2] for d in done], [d[3] for d in done]
    )
    dkva = exchange(after(dkva, dqa), WIDE)
    back_b = exchange(after(total_grads(dq_b, grads_b[1], terms_b), dkva), PAIR)
    return tuple(join_heads(dqa, dkva, back_b))


def solution(mesh):
    chips = mesh.shape["frame"] // 4
    mesh = Mesh(mesh.devices.reshape(2, chips, 2, -1), ("half", "x", "core", "group"))
    runs = ("half", "x", "core")
    tokens = P((*runs, "group"), None)
    return jax.shard_map(
        shards,
        mesh=mesh,
        in_specs=(tokens,) * 4 + (P("group", runs, None), P("group", runs)),
        out_specs=(tokens,) * 3,
        check_vma=False,
    )
```

time: 385 us -> 312 us (0.81)
  waiting for transfers between devices: 168 us -> 77.9 us
  blocking collectives: 54.6 us -> 83.8 us
  starting transfers between devices: 65.9 us -> 48.3 us
    all_to_all x7 -> x5, waiting for transfers between devices: 143 us -> 11.7 us  [exchange(): return lax.all_to_all(x, axes, 0, 0, tiled=True)]
    ppermute x12, waiting for transfers between devices: 23.7 us -> 66.2 us  [shift(): lax.ppermute(value, axes, [(s, (s + steps) % count) for s in range(count)])]
    all_to_all x2 -> x3, blocking collectives: 54.6 us -> 76.7 us  [exchange(): return lax.all_to_all(x, axes, 0, 0, tiled=True)]
    all_to_all x7 -> x5, starting transfers between devices: 43.6 us -> 30.4 us  [exchange(): return lax.all_to_all(x, axes, 0, 0, tiled=True)]
    pallas_call x3 -> x1, Pallas kernels: 12.3 us -> 4.1 us  [total_grads(): pl.pallas_call(total_kernel, grid=(blocks // step,), out_shape=jax.ShapeD...]
    pallas_call x4 -> x5, Pallas kernels: 68.3 us -> 76.4 us  [the longest x3 65.7 us: attention(): pl.pallas_call(functools.partial(attention_kernel, size, n_query, fetches...]
    all_gather x0 -> x1, blocking collectives: none -> 7.08 us  [shards(): lists = lax.all_gather(packed[:4], ('half', 'core'))]
    ppermute x12, starting transfers between devices: 22.2 us -> 17.9 us  [shift(): lax.ppermute(value, axes, [(s, (s + steps) % count) for s in range(count)])]
  transfers between devices with their start and end apart: 20 -> 17, of which waited for: 11 -> 6; matrix products, arithmetic and copies ran while one was open for 1% -> 3% of each run, Pallas kernels for 18% -> 24%
where the time goes in v4:
time: 312 us; the launch traced here: 308 us
  Pallas kernels  85.4 us (27%)
  blocking collectives  83.8 us (27%)
  waiting for transfers between devices  77.9 us (25%)
  starting transfers between devices  48.3 us (15%)
  local copies, waits for them, and re-layouts  8.05 us (3%)
  other arithmetic  4.17 us (1%)
    all_to_all x3, blocking collectives, exchange(): return lax.all_to_all(x, axes, 0, 0, tiled=True)  76.7 us
    ppermute x12, waiting for transfers between devices, shift(): lax.ppermute(value, axes, [(s, (s + steps) % count) for s in range(count)])  66.2 us
    pallas_call x3, Pallas kernels, attention(): pl.pallas_call(functools.partial(attention_kernel, size, n_query, fetches...  65.7 us
    all_to_all x5, starting transfers between devices, exchange(): return lax.all_to_all(x, axes, 0, 0, tiled=True)  30.4 us
    ppermute x12, starting transfers between devices, shift(): lax.ppermute(value, axes, [(s, (s + steps) % count) for s in range(count)])  17.9 us
    all_to_all x5, waiting for transfers between devices, exchange(): return lax.all_to_all(x, axes, 0, 0, tiled=True)  11.7 us
    all_gather x1, blocking collectives, shards(): lists = lax.all_gather(packed[:4], ('half', 'core'))  7.08 us
  transfers between devices with their start and end apart: 17, of which 6 were waited for; matrix products, arithmetic and copies ran while one was open for 3% of the time, Pallas kernels for 24%

profile of v4, /device:TPU:8, one launch (start us, length us, event | category | flops | bytes accessed | tf_op | source)
XLA Modules:
  0.0 308.4 jit_solution(17485364726905143960)
XLA Ops:
  0.6 5.7 %split_heads.1 = (bf16[4,8,128,128]{3,2,1,0:T(8,128)(2,1)}, bf16[4,8,128,128]{3,2,1,0:T(8,128)(2,1)}, bf16[4,8,2,128,128]{4,3,2,1,0:T(8,128)(2,1)}, bf16[2,8,2,1...) custom-call(bf16[128,5120]{1,0:T(8,128)(2,1)} %k_ref.1, bf16[128,5120]{1,0:T(8,128)(2,1)} %v_ref.1, ...), custom_call_target="tpu_custom_call" | custom-call | bytes 10485760 | tf_op jit(solution)/shard_map/split_heads/pallas_call | solution.py:184
  6.3 25.4 %all_to_all.40.refs_1_ = bf16[32,128,128]{2,1,0:T(8,128)(2,1)S(1)} all-to-all(bf16[32,128,128]{2,1,0:T(8,128)(2,1)} %bitcast.29), channel_id=1, replica_groups=mesh['half'=2,'x'=4,'core'=2,'group'=8] {'half','core','group'}, dimensions={0} | all-to-all | bytes 2097152 | tf_op jit(solution)/shard_map/all_to_all | solution.py:301
  31.7 1.5 collective-permute-start
  33.2 1.7 collective-permute-start.1
  34.9 21.6 %all_to_all.41.refs_4_ = bf16[32,128,128]{2,1,0:T(8,128)(2,1)} all-to-all(bf16[32,128,128]{2,1,0:T(8,128)(2,1)S(1)} %bitcast.28), channel_id=1, replica_groups=mesh['half'=2,'x'=4,'core'=2,'group'=8] {'half','core','group'}, dimensions={0} | all-to-all | bytes 2097152 | tf_op jit(solution)/shard_map/all_to_all | solution.py:301
  56.6 0.9 collective-permute-done.refs_0_
  57.5 0.0 collective-permute-done.1.refs_2_
  57.5 1.0 copy-done.12
  58.4 1.0 copy-done.13
  59.4 5.1 %all-to-all-start.2 = ((bf16[32,2,128,128]{3,2,1,0:T(8,128)(2,1)}), bf16[32,2,128,128]{3,2,1,0:T(8,128)(2,1)S(1)}, u32[]{:S(2)}, u32[]{:S(2)}) async-start(bf16[32,2,128,128]{3,2,1,0:T(8,128)(2,1)} %bitcast.26), calls=%async_computation.2 | async-start | bytes 4194304 | tf_op jit(solution)/shard_map/all_to_all | solution.py:301
  64.5 0.0 copy-start.11
  64.5 0.0 copy-start.10
  64.5 0.6 collective-permute-start.2
  65.1 2.7 collective-permute-start.3
  67.9 23.4 %collective-permute-done.2.refs_3_ = bf16[32,128,128]{2,1,0:T(8,128)(2,1)S(1)} collective-permute-done((bf16[32,128,128]{2,1,0:T(8,128)(2,1)}, bf16[32,128,128]{2,1,0:T(8,128)(2,1)S(1)}, u32[]{:S(2)}, u32[]{:S(2)}) %collective-permute-start.2) | collective-permute-done | bytes 1048608 | tf_op jit(solution)/shard_map/ppermute | solution.py:297
  91.3 0.0 collective-permute-done.3.refs_5_
  91.3 2.4 all-to-all-done.2.refs_6_
  93.7 6.3 %all-to-all-start.3 = ((bf16[16,2,128,128]{3,2,1,0:T(8,128)(2,1)}), bf16[16,2,128,128]{3,2,1,0:T(8,128)(2,1)}, u32[]{:S(2)}, u32[]{:S(2)}) async-start(bf16[16,2,128,128]{3,2,1,0:T(8,128)(2,1)} %bitcast.27), calls=%async_computation.3 | async-start | bytes 2097152 | tf_op jit(solution)/shard_map/all_to_all | solution.py:301
  100.0 0.1 copy.14
  100.1 0.1 fusion
  100.2 7.1 %all-gather = s32[16,8,13]{2,1,0:T(8,128)S(1)} all-gather(s32[4,8,13]{2,1,0:T(8,128)S(1)} %fusion), channel_id=2, replica_groups=mesh['half'=2,'x'=4,'core'=2,'group'=8] {'half','core'}, dimensions={0}, use_global_device_ids=true | all-gather | bytes 8320 | tf_op jit(solution)/shard_map/all_gather | solution.py:319
  107.2 9.3 %all-to-all-done.3.refs_1_ = bf16[16,2,128,128]{3,2,1,0:T(8,128)(2,1)} async-done(((bf16[16,2,128,128]{3,2,1,0:T(8,128)(2,1)}), bf16[16,2,128,128]{3,2,1,0:T(8,128)(2,1)}, u32[]{:S(2)}, u32[]{:S(2)}) %all-to-all-start.3) | async-done | bytes 1048608 | tf_op jit(solution)/shard_map/all_to_all | solution.py:301
  116.5 0.5 collective-permute-start.4
  117.1 3.6 %collective-permute-start.5 = (bf16[16,2,128,128]{3,2,1,0:T(8,128)(2,1)}, bf16[16,2,128,128]{3,2,1,0:T(8,128)(2,1)}, u32[]{:S(2)}, u32[]{:S(2)}) collective-permute-start(bf16[16,2,128,128]{3,2,1,0:T(8,128)(2,1)} %all-to-all-done.3.refs_1_), channel_id=1, source_target_pairs={{0,112},{16,0},{32,16},{48,32},{64,48},{80,64},{96,80},{112,96},{1... | collective-permute-start | bytes 3145736 | tf_op jit(solution)/shard_map/ppermute | solution.py:297
  120.7 0.7 reshape.50.ids_ref
  121.3 0.6 pad_add_fusion.1.place_ref
  121.9 0.7 reshape.55.ids_ref
  122.6 0.7 stack.35.place_ref
  123.3 0.8 slice_reduce_fusion
  124.0 4.9 %all-to-all-start.5 = ((bf16[8,2,128,128]{3,2,1,0:T(8,128)(2,1)}), bf16[8,2,128,128]{3,2,1,0:T(8,128)(2,1)S(1)}, u32[]{:S(2)}, u32[]{:S(2)}) async-start(bf16[8,2,128,128]{3,2,1,0:T(8,128)(2,1)} %get-tuple-element.45), calls=%async_computation.5 | async-start | bytes 1048576 | tf_op jit(solution)/shard_map/all_to_all | solution.py:301
  128.9 24.7 %attention.3 = (bf16[16,128,128]{2,1,0:T(8,128)(2,1)}, bf16[16,2,128,128]{3,2,1,0:T(8,128)(2,1)}, bf16[16,2,128,128]{3,2,1,0:T(8,128)(2,1)}, bf16[16,2,128,128]{3,2,1,0:T(8,128)(2,1)}) custom-call(s32[192]{0:T(256)} %reshape.50.ids_ref, s32[16]{0:T(128)} %get-tuple-element.60.cnt_ref, s32[5]{0:T(128)} %pad_add_fusion.1.place_ref, ...), custom_call_target="tpu_custom_call" | custom-call | flops 2684354560 | bytes 7340032 | tf_op jit(solution)/shard_map/attention/pallas_call | solution.py:127
  153.6 0.6 collective-permute-start.6
  154.2 1.5 collective-permute-start.7
  155.7 25.4 %attention.4 = (bf16[16,128,128]{2,1,0:T(8,128)(2,1)}, bf16[16,2,128,128]{3,2,1,0:T(8,128)(2,1)}, bf16[16,2,128,128]{3,2,1,0:T(8,128)(2,1)}, bf16[16,2,128,128]{3,2,1,0:T(8,128)(2,1)}) custom-call(s32[192]{0:T(256)} %reshape.55.ids_ref, s32[16]{0:T(128)} %get-tuple-element.59.cnt_ref, s32[5]{0:T(128)} %stack.35.place_ref, bf16[32,128,128]{2,1,0:T(8,128)(2,1)} %copy-done.12, ...), custom_call_target="tpu_custom_call" | custom-call | flops 2684354560 | bytes 7340032 | tf_op jit(solution)/shard_map/attention/pallas_call | solution.py:127
  181.1 0.1 collective-permute-start.8
  181.2 0.0 collective-permute-done.4.refs_0_
  181.2 2.0 collective-permute-start.9
  183.2 2.1 pad_maximum_fusion
  185.3 0.0 collective-permute-done.5.refs_2_
  185.3 0.0 all-to-all-done.5.refs_3_
  185.3 0.8 copy-done.8
  186.1 7.5 %all-to-all-start.4 = ((bf16[32,128,128]{2,1,0:T(8,128)(2,1)}), bf16[32,128,128]{2,1,0:T(8,128)(2,1)S(1)}, u32[]{:S(2)}, u32[]{:S(2)}) async-start(bf16[32,128,128]{2,1,0:T(8,128)(2,1)} %pad_maximum_fusion), calls=%async_computation.4 | async-start | bytes 2097152 | tf_op jit(solution)/shard_map/all_to_all | solution.py:301
  193.6 0.1 fusion.1
  193.7 0.7 reshape.58.ids_ref
  194.4 0.6 pad_add_fusion.2.place_ref
  195.0 0.8 slice_reduce_fusion.2.cnt_ref
  195.8 0.0 collective-permute-done.6.right0
  195.8 0.0 collective-permute-done.7.left0
  195.8 15.6 %attention.5 = (bf16[16,128,128]{2,1,0:T(8,128)(2,1)}, bf16[16,2,128,128]{3,2,1,0:T(8,128)(2,1)}, bf16[16,2,128,128]{3,2,1,0:T(8,128)(2,1)}, bf16[16,2,128,128]{3,2,1,0:T(8,128)(2,1)}) custom-call(s32[96]{0:T(128)} %reshape.58.ids_ref, s32[8]{0:T(128)} %slice_reduce_fusion.2.cnt_ref, s32[2]{0:T(128)} %pad_add_fusion.2.place_ref, ...), custom_call_target="tpu_custom_call" | custom-call | flops 1342177280 | bytes 6815744 | tf_op jit(solution)/shard_map/attention/pallas_call | solution.py:127
  211.4 0.7 pad_add_fusion.3.x_ref
  212.1 0.0 collective-permute-done.8.right1
  212.1 0.0 collective-permute-done.9.left1
  212.1 5.0 %both_halves.1 = bf16[2,16,2,128,128]{4,3,2,1,0:T(8,128)(2,1)} custom-call(s32[2]{0:T(128)} %pad_add_fusion.3.x_ref, bf16[16,2,128,128]{3,2,1,0:T(8,128)(2,1)} %get-tuple-element.48.own0, bf16[16,2,128,128]{3,2,1,0:T(8,128)(2,1)} %get-tuple-element.49.own1, bf16[16,2,128,128]{3,2,1,0:T(8,128)(2,1)} %copy-done.3, ...), custom_call_target="tpu_custom_call" | custom-call | bytes 8388608 | tf_op jit(solution)/shard_map/both_halves/pallas_call | solution.py:278
  217.1 0.0 all-to-all-done.4
  217.1 1.0 copy-done.1
  218.1 6.7 %all-to-all-start.6 = ((bf16[32,2,128,128]{3,2,1,0:T(8,128)(2,1)}), bf16[32,2,128,128]{3,2,1,0:T(8,128)(2,1)S(1)}, u32[]{:S(2)}, u32[]{:S(2)}) async-start(bf16[32,2,128,128]{3,2,1,0:T(8,128)(2,1)} %bitcast.23), calls=%async_computation.6 | async-start | bytes 4194304 | tf_op jit(solution)/shard_map/all_to_all | solution.py:301
  224.8 3.0 collective-permute-start.10
  227.9 0.0 collective-permute-start.11
  227.9 38.0 %collective-permute-done.10.refs_0_ = bf16[16,2,128,128]{3,2,1,0:T(8,128)(2,1)S(1)} collective-permute-done((bf16[16,2,128,128]{3,2,1,0:T(8,128)(2,1)}, bf16[16,2,128,128]{3,2,1,0:T(8,128)(2,1)S(1)}, u32[]{:S(2)}, u32[]{:S(2)}) %collective-permute-start.10) | collective-permute-done | bytes 1048608 | tf_op jit(solution)/shard_map/ppermute | solution.py:297
  265.8 3.9 %collective-permute-done.11.refs_1_ = bf16[16,2,128,128]{3,2,1,0:T(8,128)(2,1)} collective-permute-done((bf16[16,2,128,128]{3,2,1,0:T(8,128)(2,1)}, bf16[16,2,128,128]{3,2,1,0:T(8,128)(2,1)}, u32[]{:S(2)}, u32[]{:S(2)}) %collective-permute-start.11) | collective-permute-done | bytes 1048608 | tf_op jit(solution)/shard_map/ppermute | solution.py:297
  269.8 4.1 %total_grads.1 = bf16[16,3,128,128]{3,2,1,0:T(8,128)(2,1)} custom-call(bf16[16,128,128]{2,1,0:T(8,128)(2,1)} %get-tuple-element.46.dq_ref, bf16[16,2,128,128]{3,2,1,0:T(8,128)(2,1)} %get-tuple-element.53.own_ref, bf16[16,2,128,128]{3,2,1,0:T(8,128)(2,1)} %copy-done.5, bf16[16,2,128,128]{3,2,1,0:T(8,128)(2,1)} %collective-permute-done.11.refs_1_), custom_call_target="tpu_custom_call" | custom-call | bytes 5242880 | tf_op jit(solution)/shard_map/total_grads/pallas_call | solution.py:253
  273.9 0.0 all-to-all-done.6
  273.9 29.7 %all_to_all.42 = bf16[16,3,128,128]{3,2,1,0:T(8,128)(2,1)} all-to-all(bf16[16,3,128,128]{3,2,1,0:T(8,128)(2,1)} %total_grads.1), channel_id=1, replica_groups=mesh['half'=2,'x'=4,'core'=2,'group'=8] {'core','group'}, dimensions={0} | all-to-all | bytes 3145728 | tf_op jit(solution)/shard_map/all_to_all | solution.py:301
  303.5 4.9 %join_heads.1 = (bf16[128,5120]{1,0:T(8,128)(2,1)}, bf16[128,5120]{1,0:T(8,128)(2,1)}, bf16[128,5120]{1,0:T(8,128)(2,1)}) custom-call(bf16[4,8,128,128]{3,2,1,0:T(8,128)(2,1)} %bitcast.25, bf16[4,8,2,128,128]{4,3,2,1,0:T(8,128)(2,1)} %bitcast.22, bf16[2,8,3,128,128]{4,3,2,1,0:T(8,128)(2,1)} %bitcast.24), custom_call_target="tpu_custom_call" | custom-call | bytes 7864320 | tf_op jit(solution)/shard_map/join_heads/pallas_call | solution.py:219
  (28 shorter events, 0.1 us)
Async XLA Ops:
  6.3 28.7 %copy-start.7 = (bf16[4,8,128,128]{3,2,1,0:T(8,128)(2,1)S(1)}, bf16[4,8,128,128]{3,2,1,0:T(8,128)(2,1)}, u32[]{:S(2)}) copy-start(bf16[4,8,128,128]{3,2,1,0:T(8,128)(2,1)} %get-tuple-element.31) | copy-start | bytes 3145732
  31.7 27.7 %copy-start.6 = (bf16[32,128,128]{2,1,0:T(8,128)(2,1)}, bf16[32,128,128]{2,1,0:T(8,128)(2,1)S(1)}, u32[]{:S(2)}) copy-start(bf16[32,128,128]{2,1,0:T(8,128)(2,1)S(1)} %all_to_all.40.refs_1_) | copy-start | bytes 3145732
  31.7 25.7 %collective-permute-start = (bf16[32,128,128]{2,1,0:T(8,128)(2,1)S(1)}, bf16[32,128,128]{2,1,0:T(8,128)(2,1)S(1)}, u32[]{:S(2)}, u32[]{:S(2)}) collective-permute-start(bf16[32,128,128]{2,1,0:T(8,128)(2,1)S(1)} %all_to_all.40.refs_1_), channel_id=1, source_target_pairs={{0,16},{16,32},{32,48},{48,0},{1,17},{17,33},{33,49},{49,1},{2,18}... | collective-permute-start | bytes 3145736 | tf_op jit(solution)/shard_map/ppermute | solution.py:297
  33.2 24.3 %collective-permute-start.1 = (bf16[32,128,128]{2,1,0:T(8,128)(2,1)S(1)}, bf16[32,128,128]{2,1,0:T(8,128)(2,1)S(1)}, u32[]{:S(2)}, u32[]{:S(2)}) collective-permute-start(bf16[32,128,128]{2,1,0:T(8,128)(2,1)S(1)} %all_to_all.40.refs_1_), channel_id=1, source_target_pairs={{0,48},{16,0},{32,16},{48,32},{1,49},{17,1},{33,17},{49,33},{2,50}... | collective-permute-start | bytes 3145736 | tf_op jit(solution)/shard_map/ppermute | solution.py:297
  57.5 1.0 copy-start.12
  58.4 1.0 copy-start.13
  59.4 34.3 %all-to-all-start.2 = ((bf16[32,2,128,128]{3,2,1,0:T(8,128)(2,1)}), bf16[32,2,128,128]{3,2,1,0:T(8,128)(2,1)S(1)}, u32[]{:S(2)}, u32[]{:S(2)}) async-start(bf16[32,2,128,128]{3,2,1,0:T(8,128)(2,1)} %bitcast.26), calls=%async_computation.2 | async-start | bytes 4194304 | tf_op jit(solution)/shard_map/all_to_all | solution.py:301
  64.5 35.4 %copy-start.11 = (s32[5,8]{1,0:T(8,128)S(1)}, s32[5,8]{1,0:T(8,128)}, u32[]{:S(2)}) copy-start(s32[5,8]{1,0:T(8,128)} %param.11) | copy-start | bytes 484
  64.5 35.5 %copy-start.10 = (s32[5,8,12]{2,1,0:T(8,128)S(1)}, s32[5,8,12]{2,1,0:T(8,128)}, u32[]{:S(2)}) copy-start(s32[5,8,12]{2,1,0:T(8,128)} %param.10) | copy-start | bytes 5764
  64.5 26.7 %collective-permute-start.2 = (bf16[32,128,128]{2,1,0:T(8,128)(2,1)}, bf16[32,128,128]{2,1,0:T(8,128)(2,1)S(1)}, u32[]{:S(2)}, u32[]{:S(2)}) collective-permute-start(bf16[32,128,128]{2,1,0:T(8,128)(2,1)} %all_to_all.41.refs_4_), channel_id=1, source_target_pairs={{0,16},{16,32},{32,48},{48,0},{1,17},{17,33},{33,49},{49,1},{2,18}... | collective-permute-start | bytes 3145736 | tf_op jit(solution)/shard_map/ppermute | solution.py:297
  65.1 26.1 %collective-permute-start.3 = (bf16[32,128,128]{2,1,0:T(8,128)(2,1)}, bf16[32,128,128]{2,1,0:T(8,128)(2,1)}, u32[]{:S(2)}, u32[]{:S(2)}) collective-permute-start(bf16[32,128,128]{2,1,0:T(8,128)(2,1)} %all_to_all.41.refs_4_), channel_id=1, source_target_pairs={{0,48},{16,0},{32,16},{48,32},{1,49},{17,1},{33,17},{49,33},{2,50}... | collective-permute-start | bytes 3145736 | tf_op jit(solution)/shard_map/ppermute | solution.py:297
  91.3 8.7 %copy-start.14 = (bf16[32,128,128]{2,1,0:T(8,128)(2,1)}, bf16[32,128,128]{2,1,0:T(8,128)(2,1)S(1)}, u32[]{:S(2)}) copy-start(bf16[32,128,128]{2,1,0:T(8,128)(2,1)S(1)} %collective-permute-done.2.refs_3_) | copy-start | bytes 3145732
  93.7 30.4 %copy-start.2 = (bf16[32,2,128,128]{3,2,1,0:T(8,128)(2,1)}, bf16[32,2,128,128]{3,2,1,0:T(8,128)(2,1)S(1)}, u32[]{:S(2)}) copy-start(bf16[32,2,128,128]{3,2,1,0:T(8,128)(2,1)S(1)} %all-to-all-done.2.refs_6_) | copy-start | bytes 6291460
  93.7 22.9 %all-to-all-start.3 = ((bf16[16,2,128,128]{3,2,1,0:T(8,128)(2,1)}), bf16[16,2,128,128]{3,2,1,0:T(8,128)(2,1)}, u32[]{:S(2)}, u32[]{:S(2)}) async-start(bf16[16,2,128,128]{3,2,1,0:T(8,128)(2,1)} %bitcast.27), calls=%async_computation.3 | async-start | bytes 2097152 | tf_op jit(solution)/shard_map/all_to_all | solution.py:301
  116.5 64.7 %collective-permute-start.4 = (bf16[16,2,128,128]{3,2,1,0:T(8,128)(2,1)}, bf16[16,2,128,128]{3,2,1,0:T(8,128)(2,1)}, u32[]{:S(2)}, u32[]{:S(2)}) collective-permute-start(bf16[16,2,128,128]{3,2,1,0:T(8,128)(2,1)} %all-to-all-done.3.refs_1_), channel_id=1, source_target_pairs={{0,16},{16,32},{32,48},{48,64},{64,80},{80,96},{96,112},{112,0},{1... | collective-permute-start | bytes 3145736 | tf_op jit(solution)/shard_map/ppermute | solution.py:297
  117.1 68.3 %collective-permute-start.5 = (bf16[16,2,128,128]{3,2,1,0:T(8,128)(2,1)}, bf16[16,2,128,128]{3,2,1,0:T(8,128)(2,1)}, u32[]{:S(2)}, u32[]{:S(2)}) collective-permute-start(bf16[16,2,128,128]{3,2,1,0:T(8,128)(2,1)} %all-to-all-done.3.refs_1_), channel_id=1, source_target_pairs={{0,112},{16,0},{32,16},{48,32},{64,48},{80,64},{96,80},{112,96},{1... | collective-permute-start | bytes 3145736 | tf_op jit(solution)/shard_map/ppermute | solution.py:297
  124.0 61.3 %all-to-all-start.5 = ((bf16[8,2,128,128]{3,2,1,0:T(8,128)(2,1)}), bf16[8,2,128,128]{3,2,1,0:T(8,128)(2,1)S(1)}, u32[]{:S(2)}, u32[]{:S(2)}) async-start(bf16[8,2,128,128]{3,2,1,0:T(8,128)(2,1)} %get-tuple-element.45), calls=%async_computation.5 | async-start | bytes 1048576 | tf_op jit(solution)/shard_map/all_to_all | solution.py:301
  153.6 42.1 %collective-permute-start.6 = (bf16[16,2,128,128]{3,2,1,0:T(8,128)(2,1)}, bf16[16,2,128,128]{3,2,1,0:T(8,128)(2,1)S(1)}, u32[]{:S(2)}, u32[]{:S(2)}) collective-permute-start(bf16[16,2,128,128]{3,2,1,0:T(8,128)(2,1)} %get-tuple-element.41), channel_id=1, source_target_pairs={{0,48},{16,0},{32,16},{48,32},{1,49},{17,1},{33,17},{49,33},{2,50}... | collective-permute-start | bytes 3145736 | tf_op jit(solution)/shard_map/ppermute | solution.py:297
  154.2 41.6 %collective-permute-start.7 = (bf16[16,2,128,128]{3,2,1,0:T(8,128)(2,1)}, bf16[16,2,128,128]{3,2,1,0:T(8,128)(2,1)S(1)}, u32[]{:S(2)}, u32[]{:S(2)}) collective-permute-start(bf16[16,2,128,128]{3,2,1,0:T(8,128)(2,1)} %get-tuple-element.42), channel_id=1, source_target_pairs={{0,16},{16,32},{32,48},{48,0},{1,17},{17,33},{33,49},{49,1},{2,18}... | collective-permute-start | bytes 3145736 | tf_op jit(solution)/shard_map/ppermute | solution.py:297
  155.7 27.5 %copy-start.9 = (bf16[16,128,128]{2,1,0:T(8,128)(2,1)S(1)}, bf16[16,128,128]{2,1,0:T(8,128)(2,1)}, u32[]{:S(2)}) copy-start(bf16[16,128,128]{2,1,0:T(8,128)(2,1)} %get-tuple-element.35) | copy-start | bytes 1572868
  181.1 31.0 %collective-permute-start.8 = (bf16[16,2,128,128]{3,2,1,0:T(8,128)(2,1)}, bf16[16,2,128,128]{3,2,1,0:T(8,128)(2,1)}, u32[]{:S(2)}, u32[]{:S(2)}) collective-permute-start(bf16[16,2,128,128]{3,2,1,0:T(8,128)(2,1)} %get-tuple-element.50), channel_id=1, source_target_pairs={{0,48},{16,0},{32,16},{48,32},{1,49},{17,1},{33,17},{49,33},{2,50}... | collective-permute-start | bytes 3145736 | tf_op jit(solution)/shard_map/ppermute | solution.py:297
  181.2 30.9 %collective-permute-start.9 = (bf16[16,2,128,128]{3,2,1,0:T(8,128)(2,1)}, bf16[16,2,128,128]{3,2,1,0:T(8,128)(2,1)}, u32[]{:S(2)}, u32[]{:S(2)}) collective-permute-start(bf16[16,2,128,128]{3,2,1,0:T(8,128)(2,1)} %get-tuple-element.51), channel_id=1, source_target_pairs={{0,16},{16,32},{32,48},{48,0},{1,17},{17,33},{33,49},{49,1},{2,18}... | collective-permute-start | bytes 3145736 | tf_op jit(solution)/shard_map/ppermute | solution.py:297
  185.3 0.8 copy-start.8
  186.1 31.0 %all-to-all-start.4 = ((bf16[32,128,128]{2,1,0:T(8,128)(2,1)}), bf16[32,128,128]{2,1,0:T(8,128)(2,1)S(1)}, u32[]{:S(2)}, u32[]{:S(2)}) async-start(bf16[32,128,128]{2,1,0:T(8,128)(2,1)} %pad_maximum_fusion), calls=%async_computation.4 | async-start | bytes 2097152 | tf_op jit(solution)/shard_map/all_to_all | solution.py:301
  195.8 15.7 %copy-start.3 = (bf16[16,2,128,128]{3,2,1,0:T(8,128)(2,1)}, bf16[16,2,128,128]{3,2,1,0:T(8,128)(2,1)S(1)}, u32[]{:S(2)}) copy-start(bf16[16,2,128,128]{3,2,1,0:T(8,128)(2,1)S(1)} %collective-permute-done.6.right0) | copy-start | bytes 3145732
  195.8 15.7 %copy-start.4 = (bf16[16,2,128,128]{3,2,1,0:T(8,128)(2,1)}, bf16[16,2,128,128]{3,2,1,0:T(8,128)(2,1)S(1)}, u32[]{:S(2)}) copy-start(bf16[16,2,128,128]{3,2,1,0:T(8,128)(2,1)S(1)} %collective-permute-done.7.left0) | copy-start | bytes 3145732
  217.1 1.0 copy-start.1
  218.1 55.8 %all-to-all-start.6 = ((bf16[32,2,128,128]{3,2,1,0:T(8,128)(2,1)}), bf16[32,2,128,128]{3,2,1,0:T(8,128)(2,1)S(1)}, u32[]{:S(2)}, u32[]{:S(2)}) async-start(bf16[32,2,128,128]{3,2,1,0:T(8,128)(2,1)} %bitcast.23), calls=%async_computation.6 | async-start | bytes 4194304 | tf_op jit(solution)/shard_map/all_to_all | solution.py:301
  224.8 41.0 %collective-permute-start.10 = (bf16[16,2,128,128]{3,2,1,0:T(8,128)(2,1)}, bf16[16,2,128,128]{3,2,1,0:T(8,128)(2,1)S(1)}, u32[]{:S(2)}, u32[]{:S(2)}) collective-permute-start(bf16[16,2,128,128]{3,2,1,0:T(8,128)(2,1)} %get-tuple-element.54), channel_id=1, source_target_pairs={{0,112},{16,0},{32,16},{48,32},{64,48},{80,64},{96,80},{112,96},{1... | collective-permute-start | bytes 3145736 | tf_op jit(solution)/shard_map/ppermute | solution.py:297
  227.9 41.9 %collective-permute-start.11 = (bf16[16,2,128,128]{3,2,1,0:T(8,128)(2,1)}, bf16[16,2,128,128]{3,2,1,0:T(8,128)(2,1)}, u32[]{:S(2)}, u32[]{:S(2)}) collective-permute-start(bf16[16,2,128,128]{3,2,1,0:T(8,128)(2,1)} %get-tuple-element.55), channel_id=1, source_target_pairs={{0,16},{16,32},{32,48},{48,64},{64,80},{80,96},{96,112},{112,0},{1... | collective-permute-start | bytes 3145736 | tf_op jit(solution)/shard_map/ppermute | solution.py:297
  265.8 3.9 %copy-start.5 = (bf16[16,2,128,128]{3,2,1,0:T(8,128)(2,1)}, bf16[16,2,128,128]{3,2,1,0:T(8,128)(2,1)S(1)}, u32[]{:S(2)}) copy-start(bf16[16,2,128,128]{3,2,1,0:T(8,128)(2,1)S(1)} %collective-permute-done.10.refs_0_) | copy-start | bytes 3145732
  273.9 29.7 %copy-start = (bf16[32,2,128,128]{3,2,1,0:T(8,128)(2,1)}, bf16[32,2,128,128]{3,2,1,0:T(8,128)(2,1)S(1)}, u32[]{:S(2)}) copy-start(bf16[32,2,128,128]{3,2,1,0:T(8,128)(2,1)S(1)} %all-to-all-done.6) | copy-start | bytes 6291460

commit v5 on v4

--- a/solution.py
+++ b/solution.py
@@ -72,7 +72,10 @@
 
 def attention_kernel(size, n_query, fetches, ids_ref, cnt_ref, place_ref, *refs):
     sources, refs = refs[: len(fetches)], refs[len(fetches) :]
-    qd_in, dq_out, left_out, own_out, right_out = refs[:5]
+    shared = n_query < size
+    qd_in, dq_out, targets = refs[0], refs[1], refs[2:5]
+    if shared:
+        give_out, refs = refs[5], refs[1:]
     keys, values, qd, acc, stage, dq, kcat, s_scr, dp_scr, ds_scr, in_sem, out_sem = refs[5:]
     copies = []
     for source, fetch in zip(sources, fetches):
@@ -84,9 +87,6 @@
     for copy in copies:
         copy.start()
     acc[...] = jnp.zeros_like(acc)
-    first = place_ref[1]
-    if n_query < size:
-        dq[...] = jnp.zeros_like(dq)
     for copy in copies:
         copy.wait()
 
@@ -97,7 +97,7 @@
             @pl.when((count > upto - GROUP) & (count <= upto))
             def _():
                 query_block(
-                    upto, b, ids_ref, count, qd, keys, values, acc, dq.at[first + b], kcat, s_scr, dp_scr, ds_scr
+                    upto, b, ids_ref, count, qd, keys, values, acc, dq.at[b], kcat, s_scr, dp_scr, ds_scr
                 )
 
         return carry
@@ -105,7 +105,7 @@
     lax.fori_loop(0, n_query, one, 0)
     puts = [pltpu.make_async_copy(dq, dq_out, out_sem.at[3])]
     puts[0].start()
-    for i, target in enumerate((left_out, own_out, right_out)):
+    for i, target in enumerate(targets):
 
         def convert(j, carry):
             stage[j, 0] = (acc[j, 0] * SCALE).astype(BF16)
@@ -113,7 +113,16 @@
             return carry
 
         lax.fori_loop(i * size, (i + 1) * size, convert, 0)
-        puts.append(pltpu.make_async_copy(stage.at[pl.ds(i * size, size)], target, out_sem.at[i]))
+        rows = pl.ds(i * size, size)
+        if shared:
+            keep = pl.multiple_of(i * size + place_ref[1], 8)
+            give = pl.multiple_of(i * size + n_query - place_ref[1], 8)
+            rows = pl.ds(keep, n_query)
+            puts.append(
+                pltpu.make_async_copy(stage.at[pl.ds(give, n_query)], give_out.at[i], out_sem.at[4 + i])
+            )
+            puts[-1].start()
+        puts.append(pltpu.make_async_copy(stage.at[rows], target, out_sem.at[i]))
         puts[-1].start()
     for copy in puts:
         copy.wait()
@@ -121,34 +130,36 @@
 
 def attention(ids, counts, place, sources, fetches, qd, n_query, size):
     window = 3 * size
+    shared = n_query < size
+    kept = jax.ShapeDtypeStruct((n_query, 2, BLK, HD), BF16)
+    given = [jax.ShapeDtypeStruct((3, n_query, 2, BLK, HD), BF16)] if shared else []
     smem = pl.BlockSpec(memory_space=pltpu.SMEM)
     hbm = pl.BlockSpec(memory_space=pl.ANY)
     pairs = n_query * 8
     out = pl.pallas_call(
         functools.partial(attention_kernel, size, n_query, fetches),
-        out_shape=[jax.ShapeDtypeStruct((size, BLK, HD), BF16)]
-        + [jax.ShapeDtypeStruct((size, 2, BLK, HD), BF16)] * 3,
+        out_shape=[jax.ShapeDtypeStruct((n_query, BLK, HD), BF16)] + [kept] * 3 + given,
         in_specs=[smem] * 3 + [hbm] * (len(sources) + 1),
-        out_specs=[hbm] * 4,
+        out_specs=[hbm] * (4 + len(given)),
         scratch_shapes=[
             pltpu.VMEM((window, BLK, HD), BF16),
             pltpu.VMEM((window, BLK, HD), BF16),
             pltpu.VMEM((n_query, 2, BLK, HD), BF16),
             pltpu.VMEM((window, 2, BLK, HD), F32),
             pltpu.VMEM((window, 2, BLK, HD), BF16),
-            pltpu.VMEM((size, BLK, HD), BF16),
+            pltpu.VMEM((n_query, BLK, HD), BF16),
             pltpu.VMEM((MAXK * BLK, HD), BF16),
             pltpu.VMEM((MAXK, BLK, HD), F32),
             pltpu.VMEM((MAXK, BLK, HD), F32),
             pltpu.VMEM((MAXK * BLK, HD), BF16),
             pltpu.SemaphoreType.DMA((7,)),
-            pltpu.SemaphoreType.DMA((4,)),
+            pltpu.SemaphoreType.DMA((7,)),
         ],
         compiler_params=pltpu.CompilerParams(vmem_limit_bytes=VMEM_LIMIT),
         cost_estimate=pl.CostEstimate(
-            flops=pairs * ATTENTION_COST * BLK * BLK * HD,
-            bytes_accessed=(2 * window + n_query) * 2 * BLK * HD * 2,
-            transcendentals=pairs * BLK * BLK,
+            flops=0 if shared else pairs * ATTENTION_COST * BLK * BLK * HD,
+            bytes_accessed=0 if shared else (2 * window + n_query) * 2 * BLK * HD * 2,
+            transcendentals=0 if shared else pairs * BLK * BLK,
         ),
         name="attention",
     )(ids, counts, place, *sources, qd)
@@ -201,29 +212,24 @@
     )
 
 
-def join_kernel(dqa_ref, dkva_ref, b_ref, *outs):
+def join_kernel(a_ref, b_ref, *outs):
     for t, ref in enumerate(outs):
-        for j in range(dqa_ref.shape[1]):
-
-            def put(m, value):
+        for j in range(b_ref.shape[0]):
+            for m in range(HPG):
+                value = a_ref[m, j, t] if m < 4 else b_ref[j, t]
                 ref[:, (j * HPG + m) * HD : (j * HPG + m + 1) * HD] = value
 
-            for m in range(4):
-                put(m, dqa_ref[m, j] if t == 0 else dkva_ref[m, j, t - 1])
-            put(4, (b_ref[0, j, t].astype(F32) + b_ref[1, j, t].astype(F32)).astype(BF16))
-
-
-def join_heads(dqa, dkva, back_b):
-    groups, step = dqa.shape[0] // 4, 2
+
+def join_heads(back_a, back_b):
+    groups, step = back_b.shape[0], 2
     out = jax.ShapeDtypeStruct((BLK, groups * HPG * HD), BF16)
     return pl.pallas_call(
         join_kernel,
         grid=(groups // step,),
         out_shape=(out,) * 3,
         in_specs=[
-            pl.BlockSpec((4, step, BLK, HD), lambda j: (0, j, 0, 0)),
-            pl.BlockSpec((4, step, 2, BLK, HD), lambda j: (0, j, 0, 0, 0)),
-            pl.BlockSpec((2, step, 3, BLK, HD), lambda j: (0, j, 0, 0, 0)),
+            pl.BlockSpec((4, step, 3, BLK, HD), lambda j: (0, j, 0, 0, 0)),
+            pl.BlockSpec((step, 3, BLK, HD), lambda j: (j, 0, 0, 0)),
         ],
         out_specs=(pl.BlockSpec((BLK, step * HPG * HD), lambda j: (0, j)),) * 3,
         compiler_params=pltpu.CompilerParams(vmem_limit_bytes=VMEM_LIMIT),
@@ -231,11 +237,7 @@
             flops=0, bytes_accessed=groups * HPG * 3 * BLK * HD * 4, transcendentals=0
         ),
         name="join_heads",
-    )(
-        dqa.reshape(4, groups, BLK, HD),
-        dkva.reshape(4, groups, 2, BLK, HD),
-        back_b.reshape(2, groups, 3, BLK, HD),
-    )
+    )(back_a.reshape(4, groups, 3, BLK, HD), back_b)
 
 
 def total_kernel(dq_ref, own_ref, *refs):
@@ -263,28 +265,31 @@
     )(dq, own, *terms)
 
 
-def both_halves_kernel(x_ref, own0, own1, right0, right1, left0, left1, out_ref):
+def both_halves_kernel(x_ref, dq0, dq1, own0, own1, right0, right1, left0, left1, out_ref):
     x = x_ref[0]
-    for s, own in enumerate((own0, own1)):
+    for s, (dq, own) in enumerate(((dq0, own0), (dq1, own1))):
         right = jnp.where(x == x_ref[1], (right1, right0)[s][...], (right0, right1)[s][...])
         left = jnp.where(x == 0, (left1, left0)[s][...], (left0, left1)[s][...])
         total = own[...].astype(F32) + right.astype(F32) + left.astype(F32)
-        out_ref[s] = total.astype(BF16)
-
-
-def both_halves(x, last, own, from_right, from_left):
+        out_ref[s, :, 0] = dq[...]
+        out_ref[s, :, 1:] = total.astype(BF16)
+
+
+def both_halves(x, last, dq, own, from_right, from_left):
     blocks, step = own[0].shape[0], 4
     spec = pl.BlockSpec((step, 2, BLK, HD), lambda i: (i, 0, 0, 0))
     out = pl.pallas_call(
         both_halves_kernel,
         grid=(blocks // step,),
-        out_shape=jax.ShapeDtypeStruct((2, blocks, 2, BLK, HD), BF16),
-        in_specs=[pl.BlockSpec(memory_space=pltpu.SMEM)] + [spec] * 6,
-        out_specs=pl.BlockSpec((2, step, 2, BLK, HD), lambda i: (0, i, 0, 0, 0)),
-        cost_estimate=pl.CostEstimate(flops=0, bytes_accessed=16 * own[0].size, transcendentals=0),
+        out_shape=jax.ShapeDtypeStruct((2, blocks, 3, BLK, HD), BF16),
+        in_specs=[pl.BlockSpec(memory_space=pltpu.SMEM)]
+        + [pl.BlockSpec((step, BLK, HD), lambda i: (i, 0, 0))] * 2
+        + [spec] * 6,
+        out_specs=pl.BlockSpec((2, step, 3, BLK, HD), lambda i: (0, i, 0, 0, 0)),
+        cost_estimate=pl.CostEstimate(flops=0, bytes_accessed=20 * own[0].size, transcendentals=0),
         name="both_halves",
-    )(jnp.stack([x, jnp.int32(last)]), *own, *from_right, *from_left)
-    return out.reshape(2 * blocks, 2, BLK, HD)
+    )(jnp.stack([x, jnp.int32(last)]), *dq, *own, *from_right, *from_left)
+    return out.reshape(2 * blocks, 3, BLK, HD)
 
 
 WIDE = ("half", "core", "group")
@@ -295,6 +300,10 @@
 def shift(value, axes, steps):
     count = lax.axis_size(axes)
     return lax.ppermute(value, axes, [(s, (s + steps) % count) for s in range(count)])
+
+
+def add(a, b):
+    return (a.astype(F32) + b.astype(F32)).astype(BF16)
 
 
 def exchange(x, axes):
@@ -319,8 +328,6 @@
     lists = lax.all_gather(packed[:4], ("half", "core"))
     lists = lax.dynamic_index_in_dim(lists, 2 * half + core, 1, False)
     own_b = exchange(after(kvb, queries, *key_near, *value_near), PAIR)
-    near_b = [shift(own_b, CHIPS, 1), shift(own_b, CHIPS, -1)]
-    queries_b = exchange(after(qdb, own_b), "group")
 
     def plain(lists, chip):
         lists = lists.reshape(-1, MAXK + 1)
@@ -342,6 +349,10 @@
         place = after(place, *[d[0] for d in done])
         dq, grads = attention(ids, counts, place, sources, fetches, queries, size, size)
         done.append((dq, grads, shift(grads[0], "x", -1), shift(grads[2], "x", 1)))
+        if s == 0:
+            own_b = after(own_b, dq)
+            near_b = [shift(own_b, CHIPS, 1), shift(own_b, CHIPS, -1)]
+            queries_b = exchange(after(qdb, own_b), "group")
 
     def pair(i):
         return lambda ref, place: [(ref.at[:, t], t, i) for t in range(2)]
@@ -349,19 +360,26 @@
     ids, counts = plain(packed[4], half * (last + 1) + x)
     place = jnp.stack([jnp.int32(0), core * BPD])
     place = after(place, done[1][0], done[0][2], done[0][3])
-    dq_b, grads_b = attention(
+    dq_b, (left_b, mine_b, right_b, give_b) = attention(
         ids, counts, place, (near_b[0], own_b, near_b[1]), [pair(i) for i in range(3)], queries_b, BPD, size
     )
-    terms_b = [shift(grads_b[0], CHIPS, -1), shift(grads_b[2], CHIPS, 1)]
-
-    dqa = jnp.concatenate([done[0][0], done[1][0]])
-    dqa = exchange(after(dqa, *near_b), WIDE)
-    dkva = both_halves(
-        after(x, dq_b), last, [d[1][1] for d in done], [d[2] for d in done], [d[3] for d in done]
+    got_b = [lax.ppermute(give_b[i], "core", [(0, 1), (1, 0)]) for i in range(3)]
+    terms_b = [
+        got_b[1],
+        shift(add(left_b, got_b[0]), CHIPS, -1),
+        shift(add(right_b, got_b[2]), CHIPS, 1),
+    ]
+    total_a = both_halves(
+        after(x, *terms_b[:1]),
+        last,
+        [d[0] for d in done],
+        [d[1][1] for d in done],
+        [d[2] for d in done],
+        [d[3] for d in done],
     )
-    dkva = exchange(after(dkva, dqa), WIDE)
-    back_b = exchange(after(total_grads(dq_b, grads_b[1], terms_b), dkva), PAIR)
-    return tuple(join_heads(dqa, dkva, back_b))
+    back_a = exchange(total_a, WIDE)
+    back_b = exchange(after(total_grads(dq_b, mine_b, terms_b), back_a), "group")
+    return tuple(join_heads(back_a, back_b))
 
 
 def solution(mesh):

time: 312 us -> 308 us (0.987)
  blocking collectives: 83.8 us -> 72.9 us
  starting transfers between devices: 48.3 us -> 55.7 us
  waiting for transfers between devices: 77.9 us -> 81.2 us
    all_to_all x3, blocking collectives: 76.7 us -> 66.2 us  [exchange(): return lax.all_to_all(x, axes, 0, 0, tiled=True)]
    ppermute x12, waiting for transfers between devices: 66.2 us -> 57.7 us  [shift(): lax.ppermute(value, axes, [(s, (s + steps) % count) for s in range(count)])]
    all_to_all x5 -> x4, waiting for transfers between devices: 11.7 us -> 19.8 us  [exchange(): return lax.all_to_all(x, axes, 0, 0, tiled=True)]
    all_to_all x5 -> x4, starting transfers between devices: 30.4 us -> 38.4 us  [exchange(): return lax.all_to_all(x, axes, 0, 0, tiled=True)]
    ppermute x0 -> x3, waiting for transfers between devices: none -> 3.65 us  [shards(): lax.ppermute(give_b[i], 'core', [(0, 1), (1, 0)])]
  transfers between devices with their start and end apart: 17 -> 19, of which waited for: 6 -> 11; matrix products, arithmetic and copies ran while one was open for 3% -> 3% of each run, Pallas kernels for 24% -> 22%
where the time goes in v5:
time: 308 us; the launch traced here: 306 us
  Pallas kernels  82.8 us (27%)
  waiting for transfers between devices  81.2 us (26%)
  blocking collectives  72.9 us (24%)
  starting transfers between devices  55.7 us (18%)
  local copies, waits for them, and re-layouts  9.13 us (3%)
  other arithmetic  3.27 us (1%)
    all_to_all x3, blocking collectives, exchange(): return lax.all_to_all(x, axes, 0, 0, tiled=True)  66.2 us
    pallas_call x3, Pallas kernels, attention(): pl.pallas_call(functools.partial(attention_kernel, size, n_query, fetches...  64.5 us
    ppermute x12, waiting for transfers between devices, shift(): lax.ppermute(value, axes, [(s, (s + steps) % count) for s in range(count)])  57.7 us
    all_to_all x4, starting transfers between devices, exchange(): return lax.all_to_all(x, axes, 0, 0, tiled=True)  38.4 us
    all_to_all x4, waiting for transfers between devices, exchange(): return lax.all_to_all(x, axes, 0, 0, tiled=True)  19.8 us
    ppermute x12, starting transfers between devices, shift(): lax.ppermute(value, axes, [(s, (s + steps) % count) for s in range(count)])  16.6 us
    all_gather x1, blocking collectives, shards(): lists = lax.all_gather(packed[:4], ('half', 'core'))  6.69 us
  transfers between devices with their start and end apart: 19, of which 11 were waited for; matrix products, arithmetic and copies ran while one was open for 3% of the time, Pallas kernels for 22%

profile of v5, /device:TPU:8, one launch (start us, length us, event | category | flops | bytes accessed | tf_op | source)
XLA Modules:
  0.0 305.8 jit_solution(10772328613052983095)
XLA Ops:
  0.6 5.7 %split_heads.1 = (bf16[4,8,128,128]{3,2,1,0:T(8,128)(2,1)}, bf16[4,8,128,128]{3,2,1,0:T(8,128)(2,1)}, bf16[4,8,2,128,128]{4,3,2,1,0:T(8,128)(2,1)}, bf16[2,8,2,1...) custom-call(bf16[128,5120]{1,0:T(8,128)(2,1)} %k_ref.1, bf16[128,5120]{1,0:T(8,128)(2,1)} %v_ref.1, ...), custom_call_target="tpu_custom_call" | custom-call | bytes 10485760 | tf_op jit(solution)/shard_map/split_heads/pallas_call | solution.py:195
  6.3 25.4 %all_to_all.35.refs_1_ = bf16[32,128,128]{2,1,0:T(8,128)(2,1)S(1)} all-to-all(bf16[32,128,128]{2,1,0:T(8,128)(2,1)} %bitcast.31), channel_id=1, replica_groups=mesh['half'=2,'x'=4,'core'=2,'group'=8] {'half','core','group'}, dimensions={0} | all-to-all | bytes 2097152 | tf_op jit(solution)/shard_map/all_to_all | solution.py:310
  31.7 2.8 collective-permute-start.1
  34.5 0.0 collective-permute-start
  34.5 21.5 %all_to_all.36.refs_4_ = bf16[32,128,128]{2,1,0:T(8,128)(2,1)S(1)} all-to-all(bf16[32,128,128]{2,1,0:T(8,128)(2,1)S(1)} %bitcast.30), channel_id=1, replica_groups=mesh['half'=2,'x'=4,'core'=2,'group'=8] {'half','core','group'}, dimensions={0} | all-to-all | bytes 2097152 | tf_op jit(solution)/shard_map/all_to_all | solution.py:310
  56.0 0.5 collective-permute-done.1.refs_2_
  56.5 3.4 %collective-permute-done.refs_0_ = bf16[32,128,128]{2,1,0:T(8,128)(2,1)S(1)} collective-permute-done((bf16[32,128,128]{2,1,0:T(8,128)(2,1)S(1)}, bf16[32,128,128]{2,1,0:T(8,128)(2,1)S(1)}, u32[]{:S(2)}, u32[]{:S(2)}) %collective-permute-start) | collective-permute-done | bytes 1048608 | tf_op jit(solution)/shard_map/ppermute | solution.py:302
  59.9 1.0 copy-done.14
  60.9 5.2 %all-to-all-start.2 = ((bf16[32,2,128,128]{3,2,1,0:T(8,128)(2,1)}), bf16[32,2,128,128]{3,2,1,0:T(8,128)(2,1)S(1)}, u32[]{:S(2)}, u32[]{:S(2)}) async-start(bf16[32,2,128,128]{3,2,1,0:T(8,128)(2,1)} %bitcast.28), calls=%async_computation.2 | async-start | bytes 4194304 | tf_op jit(solution)/shard_map/all_to_all | solution.py:310
  66.2 0.7 collective-permute-start.3
  66.9 1.4 collective-permute-start.2
  68.3 0.1 copy.17
  68.4 0.1 pad_add_fusion
  68.4 23.1 %collective-permute-done.3.refs_5_ = bf16[32,128,128]{2,1,0:T(8,128)(2,1)} collective-permute-done((bf16[32,128,128]{2,1,0:T(8,128)(2,1)S(1)}, bf16[32,128,128]{2,1,0:T(8,128)(2,1)}, u32[]{:S(2)}, u32[]{:S(2)}) %collective-permute-start.3) | collective-permute-done | bytes 1048608 | tf_op jit(solution)/shard_map/ppermute | solution.py:302
  91.5 1.6 collective-permute-done.2.refs_3_
  93.1 2.2 all-to-all-done.2.refs_6_
  95.3 6.3 %all-to-all-start.3 = ((bf16[16,2,128,128]{3,2,1,0:T(8,128)(2,1)}), bf16[16,2,128,128]{3,2,1,0:T(8,128)(2,1)S(1)}, u32[]{:S(2)}, u32[]{:S(2)}) async-start(bf16[16,2,128,128]{3,2,1,0:T(8,128)(2,1)} %bitcast.29), calls=%async_computation.3 | async-start | bytes 2097152 | tf_op jit(solution)/shard_map/all_to_all | solution.py:310
  101.6 0.6 pad_add_fusion.2.place_ref
  102.2 6.7 %all-gather = s32[16,8,13]{2,1,0:T(8,128)S(1)} all-gather(s32[4,8,13]{2,1,0:T(8,128)S(1)} %pad_add_fusion), channel_id=2, replica_groups=mesh['half'=2,'x'=4,'core'=2,'group'=8] {'half','core'}, dimensions={0}, use_global_device_ids=true | all-gather | bytes 8320 | tf_op jit(solution)/shard_map/all_gather | solution.py:328
  108.9 0.6 reshape.47.ids_ref
  109.5 0.8 slice_reduce_fusion
  110.3 24.0 %attention.3 = (bf16[16,128,128]{2,1,0:T(8,128)(2,1)}, bf16[16,2,128,128]{3,2,1,0:T(8,128)(2,1)}, bf16[16,2,128,128]{3,2,1,0:T(8,128)(2,1)}, bf16[16,2,128,128]{3,2,1,0:T(8,128)(2,1)}) custom-call(s32[192]{0:T(256)} %reshape.47.ids_ref, s32[16]{0:T(128)} %get-tuple-element.62.cnt_ref, s32[5]{0:T(128)} %pad_add_fusion.2.place_ref, ...), custom_call_target="tpu_custom_call" | custom-call | flops 2684354560 | bytes 7340032 | tf_op jit(solution)/shard_map/attention/pallas_call | solution.py:139
  134.3 1.1 collective-permute-start.4
  135.4 1.0 collective-permute-start.5
  136.4 0.0 all-to-all-done.3.refs_1_
  136.4 3.3 %collective-permute-start.7 = (bf16[16,2,128,128]{3,2,1,0:T(8,128)(2,1)S(1)}, bf16[16,2,128,128]{3,2,1,0:T(8,128)(2,1)S(1)}, u32[]{:S(2)}, u32[]{:S(2)}) collective-permute-start(bf16[16,2,128,128]{3,2,1,0:T(8,128)(2,1)S(1)} %all-to-all-done.3.refs_1_), channel_id=1, source_target_pairs={{0,112},{16,0},{32,16},{48,32},{64,48},{80,64},{96,80},{112,96},{1... | collective-permute-start | bytes 3145736 | tf_op jit(solution)/shard_map/ppermute | solution.py:302
  139.7 0.0 collective-permute-start.6
  139.7 0.7 reshape.45.ids_ref
  140.4 0.6 stack.34.place_ref
  141.0 0.1 add_bitcast_fusion
  141.1 13.7 %all-to-all-start.4 = ((bf16[8,2,128,128]{3,2,1,0:T(8,128)(2,1)}), bf16[8,2,128,128]{3,2,1,0:T(8,128)(2,1)S(1)}, u32[]{:S(2)}, u32[]{:S(2)}) async-start(bf16[8,2,128,128]{3,2,1,0:T(8,128)(2,1)} %get-tuple-element.45), calls=%async_computation.4 | async-start | bytes 1048576 | tf_op jit(solution)/shard_map/all_to_all | solution.py:310
  154.8 25.6 %attention.4 = (bf16[16,128,128]{2,1,0:T(8,128)(2,1)}, bf16[16,2,128,128]{3,2,1,0:T(8,128)(2,1)}, bf16[16,2,128,128]{3,2,1,0:T(8,128)(2,1)}, bf16[16,2,128,128]{3,2,1,0:T(8,128)(2,1)}) custom-call(s32[192]{0:T(256)} %reshape.45.ids_ref, s32[16]{0:T(128)} %get-tuple-element.63.cnt_ref, s32[5]{0:T(128)} %stack.34.place_ref, bf16[32,128,128]{2,1,0:T(8,128)(2,1)} %copy-done.14, ...), custom_call_target="tpu_custom_call" | custom-call | flops 2684354560 | bytes 7340032 | tf_op jit(solution)/shard_map/attention/pallas_call | solution.py:139
  180.4 1.9 collective-permute-start.9
  182.3 0.0 collective-permute-done.4.right0
  182.3 0.2 collective-permute-start.10
  182.5 0.6 pad_add_fusion.1.place_ref
  183.1 0.6 reshape.43.ids_ref
  183.6 0.7 slice_reduce_fusion.2.cnt_ref
  184.3 0.0 collective-permute-done.5.left0
  184.4 0.0 copy-start.4
  184.4 2.1 collective-permute-done.6.refs_0_
  186.5 14.9 %attention.5 = (bf16[8,128,128]{2,1,0:T(8,128)(2,1)}, bf16[8,2,128,128]{3,2,1,0:T(8,128)(2,1)}, bf16[8,2,128,128]{3,2,1,0:T(8,128)(2,1)}, bf16[8,2,128,128]{3,2,1,0:T(8,128)(2,1)}, bf16[3,8,2,128,128]{4,3,2,1,0:T(8,128)(2,1)}) custom-call(s32[96]{0:T(128)} %reshape.43.ids_ref, s32[8]{0:T(128)} %slice_reduce_fusion.2.cnt_ref, s32[2]{0:T(128)} %pad_add_fusion.1.place_ref, ...), custom_call_target="tpu_custom_call" | custom-call | tf_op jit(solution)/shard_map/attention/pallas_call | solution.py:139
  201.4 2.5 slice_bitcast_fusion
  203.9 2.0 collective-permute-done.8.refs_0_
  205.9 0.6 pad_add_fusion.3.x_ref
  206.5 0.0 collective-permute-done.9.right1
  206.5 1.7 collective-permute-done.10.left1
  208.2 5.5 %both_halves.1 = bf16[2,16,3,128,128]{4,3,2,1,0:T(8,128)(2,1)} custom-call(s32[2]{0:T(128)} %pad_add_fusion.3.x_ref, bf16[16,128,128]{2,1,0:T(8,128)(2,1)} %get-tuple-element.35.dq0, bf16[16,128,128]{2,1,0:T(8,128)(2,1)} %get-tuple-element.37.dq1, bf16[16,2,128,128]{3,2,1,0:T(8,128)(2,1)} %get-tuple-element.48.own0, ...), custom_call_target="tpu_custom_call" | custom-call | bytes 10485760 | tf_op jit(solution)/shard_map/both_halves/pallas_call | solution.py:281
  213.7 13.2 %all-to-all-start.5 = ((bf16[32,3,128,128]{3,2,1,0:T(8,128)(2,1)}), bf16[32,3,128,128]{3,2,1,0:T(8,128)(2,1)S(1)}, u32[]{:S(2)}, u32[]{:S(2)}) async-start(bf16[32,3,128,128]{3,2,1,0:T(8,128)(2,1)} %bitcast.27), calls=%async_computation.5 | async-start | bytes 6291456 | tf_op jit(solution)/shard_map/all_to_all | solution.py:310
  226.9 0.2 collective-permute-start.13
  227.2 0.4 collective-permute-start.11
  227.5 1.6 collective-permute-done.13
  229.1 1.2 add_convert_fusion
  230.3 0.9 collective-permute-start.14
  231.2 0.0 collective-permute-done.11
  231.2 0.1 add_convert_fusion.1
  231.4 3.4 %collective-permute-start.12 = (bf16[8,2,128,128]{3,2,1,0:T(8,128)(2,1)S(1)}, bf16[8,2,128,128]{3,2,1,0:T(8,128)(2,1)S(1)}, u32[]{:S(2)}, u32[]{:S(2)}) collective-permute-start(bf16[8,2,128,128]{3,2,1,0:T(8,128)(2,1)S(1)} %add_convert_fusion.1), channel_id=1, source_target_pairs={{0,112},{16,0},{32,16},{48,32},{64,48},{80,64},{96,80},{112,96},{1... | collective-permute-start | bytes 1572872 | tf_op jit(solution)/shard_map/ppermute | solution.py:302
  234.7 25.4 %collective-permute-done.14.refs_2_ = bf16[8,2,128,128]{3,2,1,0:T(8,128)(2,1)S(1)} collective-permute-done((bf16[8,2,128,128]{3,2,1,0:T(8,128)(2,1)S(1)}, bf16[8,2,128,128]{3,2,1,0:T(8,128)(2,1)S(1)}, u32[]{:S(2)}, u32[]{:S(2)}) %collective-permute-start.14) | collective-permute-done | bytes 524320 | tf_op jit(solution)/shard_map/ppermute | solution.py:302
  260.1 0.8 copy-done.9
  260.9 0.8 copy-done.10
  261.7 2.5 total_grads.1
  264.2 17.6 %all-to-all-done.5 = bf16[32,3,128,128]{3,2,1,0:T(8,128)(2,1)S(1)} async-done(((bf16[32,3,128,128]{3,2,1,0:T(8,128)(2,1)}), bf16[32,3,128,128]{3,2,1,0:T(8,128)(2,1)S(1)}, u32[]{:S(2)}, u32[]{:S(2)}) %all-to-all-start.5) | async-done | bytes 3145760 | tf_op jit(solution)/shard_map/all_to_all | solution.py:310
  281.8 19.3 %all_to_all.37.b_ref = bf16[8,3,128,128]{3,2,1,0:T(8,128)(2,1)} all-to-all(bf16[8,3,128,128]{3,2,1,0:T(8,128)(2,1)} %total_grads.1), channel_id=1, replica_groups=mesh['half'=2,'x'=4,'core'=2,'group'=8] {'group'}, dimensions={0} | all-to-all | bytes 1572864 | tf_op jit(solution)/shard_map/all_to_all | solution.py:310
  301.1 4.7 %join_heads.1 = (bf16[128,5120]{1,0:T(8,128)(2,1)}, bf16[128,5120]{1,0:T(8,128)(2,1)}, bf16[128,5120]{1,0:T(8,128)(2,1)}) custom-call(bf16[4,8,3,128,128]{4,3,2,1,0:T(8,128)(2,1)} %bitcast.26, bf16[8,3,128,128]{3,2,1,0:T(8,128)(2,1)} %all_to_all.37.b_ref), custom_call_target="tpu_custom_call" | custom-call | bytes 7864320 | tf_op jit(solution)/shard_map/join_heads/pallas_call | solution.py:226
  (34 shorter events, 0.1 us)
Async XLA Ops:
  6.3 28.2 %copy-start.7 = (bf16[4,8,128,128]{3,2,1,0:T(8,128)(2,1)S(1)}, bf16[4,8,128,128]{3,2,1,0:T(8,128)(2,1)}, u32[]{:S(2)}) copy-start(bf16[4,8,128,128]{3,2,1,0:T(8,128)(2,1)} %get-tuple-element.31) | copy-start | bytes 3145732
  31.7 2.8 copy-start.5
  31.7 24.8 %collective-permute-start.1 = (bf16[32,128,128]{2,1,0:T(8,128)(2,1)S(1)}, bf16[32,128,128]{2,1,0:T(8,128)(2,1)S(1)}, u32[]{:S(2)}, u32[]{:S(2)}) collective-permute-start(bf16[32,128,128]{2,1,0:T(8,128)(2,1)S(1)} %all_to_all.35.refs_1_), channel_id=1, source_target_pairs={{0,48},{16,0},{32,16},{48,32},{1,49},{17,1},{33,17},{49,33},{2,50}... | collective-permute-start | bytes 3145736 | tf_op jit(solution)/shard_map/ppermute | solution.py:302
  34.5 25.5 %collective-permute-start = (bf16[32,128,128]{2,1,0:T(8,128)(2,1)S(1)}, bf16[32,128,128]{2,1,0:T(8,128)(2,1)S(1)}, u32[]{:S(2)}, u32[]{:S(2)}) collective-permute-start(bf16[32,128,128]{2,1,0:T(8,128)(2,1)S(1)} %all_to_all.35.refs_1_), channel_id=1, source_target_pairs={{0,16},{16,32},{32,48},{48,0},{1,17},{17,33},{33,49},{49,1},{2,18}... | collective-permute-start | bytes 3145736 | tf_op jit(solution)/shard_map/ppermute | solution.py:302
  56.0 10.9 %copy-start.6 = (bf16[32,128,128]{2,1,0:T(8,128)(2,1)}, bf16[32,128,128]{2,1,0:T(8,128)(2,1)S(1)}, u32[]{:S(2)}) copy-start(bf16[32,128,128]{2,1,0:T(8,128)(2,1)S(1)} %all_to_all.36.refs_4_) | copy-start | bytes 3145732
  56.5 3.4 %copy-start.13 = (bf16[32,128,128]{2,1,0:T(8,128)(2,1)}, bf16[32,128,128]{2,1,0:T(8,128)(2,1)S(1)}, u32[]{:S(2)}) copy-start(bf16[32,128,128]{2,1,0:T(8,128)(2,1)S(1)} %collective-permute-done.1.refs_2_) | copy-start | bytes 3145732
  59.9 1.0 copy-start.14
  60.9 7.4 %copy-start.12 = (s32[5,8]{1,0:T(8,128)S(1)}, s32[5,8]{1,0:T(8,128)}, u32[]{:S(2)}) copy-start(s32[5,8]{1,0:T(8,128)} %param.11) | copy-start | bytes 484
  60.9 7.5 %copy-start.11 = (s32[5,8,12]{2,1,0:T(8,128)S(1)}, s32[5,8,12]{2,1,0:T(8,128)}, u32[]{:S(2)}) copy-start(s32[5,8,12]{2,1,0:T(8,128)} %param.10) | copy-start | bytes 5764
  60.9 34.4 %all-to-all-start.2 = ((bf16[32,2,128,128]{3,2,1,0:T(8,128)(2,1)}), bf16[32,2,128,128]{3,2,1,0:T(8,128)(2,1)S(1)}, u32[]{:S(2)}, u32[]{:S(2)}) async-start(bf16[32,2,128,128]{3,2,1,0:T(8,128)(2,1)} %bitcast.28), calls=%async_computation.2 | async-start | bytes 4194304 | tf_op jit(solution)/shard_map/all_to_all | solution.py:310
  66.2 25.4 %collective-permute-start.3 = (bf16[32,128,128]{2,1,0:T(8,128)(2,1)S(1)}, bf16[32,128,128]{2,1,0:T(8,128)(2,1)}, u32[]{:S(2)}, u32[]{:S(2)}) collective-permute-start(bf16[32,128,128]{2,1,0:T(8,128)(2,1)S(1)} %all_to_all.36.refs_4_), channel_id=1, source_target_pairs={{0,48},{16,0},{32,16},{48,32},{1,49},{17,1},{33,17},{49,33},{2,50}... | collective-permute-start | bytes 3145736 | tf_op jit(solution)/shard_map/ppermute | solution.py:302
  66.9 26.2 %collective-permute-start.2 = (bf16[32,128,128]{2,1,0:T(8,128)(2,1)S(1)}, bf16[32,128,128]{2,1,0:T(8,128)(2,1)}, u32[]{:S(2)}, u32[]{:S(2)}) collective-permute-start(bf16[32,128,128]{2,1,0:T(8,128)(2,1)S(1)} %all_to_all.36.refs_4_), channel_id=1, source_target_pairs={{0,16},{16,32},{32,48},{48,0},{1,17},{17,33},{33,49},{49,1},{2,18}... | collective-permute-start | bytes 3145736 | tf_op jit(solution)/shard_map/ppermute | solution.py:302
  95.3 15.0 %copy-start.2 = (bf16[32,2,128,128]{3,2,1,0:T(8,128)(2,1)}, bf16[32,2,128,128]{3,2,1,0:T(8,128)(2,1)S(1)}, u32[]{:S(2)}) copy-start(bf16[32,2,128,128]{3,2,1,0:T(8,128)(2,1)S(1)} %all-to-all-done.2.refs_6_) | copy-start | bytes 6291460
  95.3 41.1 %all-to-all-start.3 = ((bf16[16,2,128,128]{3,2,1,0:T(8,128)(2,1)}), bf16[16,2,128,128]{3,2,1,0:T(8,128)(2,1)S(1)}, u32[]{:S(2)}, u32[]{:S(2)}) async-start(bf16[16,2,128,128]{3,2,1,0:T(8,128)(2,1)} %bitcast.29), calls=%async_computation.3 | async-start | bytes 2097152 | tf_op jit(solution)/shard_map/all_to_all | solution.py:310
  134.3 48.0 %collective-permute-start.4 = (bf16[16,2,128,128]{3,2,1,0:T(8,128)(2,1)}, bf16[16,2,128,128]{3,2,1,0:T(8,128)(2,1)}, u32[]{:S(2)}, u32[]{:S(2)}) collective-permute-start(bf16[16,2,128,128]{3,2,1,0:T(8,128)(2,1)} %get-tuple-element.38), channel_id=1, source_target_pairs={{0,48},{16,0},{32,16},{48,32},{1,49},{17,1},{33,17},{49,33},{2,50}... | collective-permute-start | bytes 3145736 | tf_op jit(solution)/shard_map/ppermute | solution.py:302
  135.4 49.0 %collective-permute-start.5 = (bf16[16,2,128,128]{3,2,1,0:T(8,128)(2,1)}, bf16[16,2,128,128]{3,2,1,0:T(8,128)(2,1)}, u32[]{:S(2)}, u32[]{:S(2)}) collective-permute-start(bf16[16,2,128,128]{3,2,1,0:T(8,128)(2,1)} %get-tuple-element.39), channel_id=1, source_target_pairs={{0,16},{16,32},{32,48},{48,0},{1,17},{17,33},{33,49},{49,1},{2,18}... | collective-permute-start | bytes 3145736 | tf_op jit(solution)/shard_map/ppermute | solution.py:302
  136.4 44.0 %copy-start.1 = (bf16[16,2,128,128]{3,2,1,0:T(8,128)(2,1)}, bf16[16,2,128,128]{3,2,1,0:T(8,128)(2,1)S(1)}, u32[]{:S(2)}) copy-start(bf16[16,2,128,128]{3,2,1,0:T(8,128)(2,1)S(1)} %all-to-all-done.3.refs_1_) | copy-start | bytes 3145732
  136.4 48.0 %collective-permute-start.7 = (bf16[16,2,128,128]{3,2,1,0:T(8,128)(2,1)S(1)}, bf16[16,2,128,128]{3,2,1,0:T(8,128)(2,1)S(1)}, u32[]{:S(2)}, u32[]{:S(2)}) collective-permute-start(bf16[16,2,128,128]{3,2,1,0:T(8,128)(2,1)S(1)} %all-to-all-done.3.refs_1_), channel_id=1, source_target_pairs={{0,112},{16,0},{32,16},{48,32},{64,48},{80,64},{96,80},{112,96},{1... | collective-permute-start | bytes 3145736 | tf_op jit(solution)/shard_map/ppermute | solution.py:302
  139.7 46.8 %collective-permute-start.6 = (bf16[16,2,128,128]{3,2,1,0:T(8,128)(2,1)S(1)}, bf16[16,2,128,128]{3,2,1,0:T(8,128)(2,1)}, u32[]{:S(2)}, u32[]{:S(2)}) collective-permute-start(bf16[16,2,128,128]{3,2,1,0:T(8,128)(2,1)S(1)} %all-to-all-done.3.refs_1_), channel_id=1, source_target_pairs={{0,16},{16,32},{32,48},{48,64},{64,80},{80,96},{96,112},{112,0},{1... | collective-permute-start | bytes 3145736 | tf_op jit(solution)/shard_map/ppermute | solution.py:302
  141.1 43.3 %all-to-all-start.4 = ((bf16[8,2,128,128]{3,2,1,0:T(8,128)(2,1)}), bf16[8,2,128,128]{3,2,1,0:T(8,128)(2,1)S(1)}, u32[]{:S(2)}, u32[]{:S(2)}) async-start(bf16[8,2,128,128]{3,2,1,0:T(8,128)(2,1)} %get-tuple-element.45), calls=%async_computation.4 | async-start | bytes 1048576 | tf_op jit(solution)/shard_map/all_to_all | solution.py:310
  180.4 26.2 %collective-permute-start.9 = (bf16[16,2,128,128]{3,2,1,0:T(8,128)(2,1)}, bf16[16,2,128,128]{3,2,1,0:T(8,128)(2,1)}, u32[]{:S(2)}, u32[]{:S(2)}) collective-permute-start(bf16[16,2,128,128]{3,2,1,0:T(8,128)(2,1)} %get-tuple-element.50), channel_id=1, source_target_pairs={{0,48},{16,0},{32,16},{48,32},{1,49},{17,1},{33,17},{49,33},{2,50}... | collective-permute-start | bytes 3145736 | tf_op jit(solution)/shard_map/ppermute | solution.py:302
  182.3 25.9 %collective-permute-start.10 = (bf16[16,2,128,128]{3,2,1,0:T(8,128)(2,1)}, bf16[16,2,128,128]{3,2,1,0:T(8,128)(2,1)}, u32[]{:S(2)}, u32[]{:S(2)}) collective-permute-start(bf16[16,2,128,128]{3,2,1,0:T(8,128)(2,1)} %get-tuple-element.51), channel_id=1, source_target_pairs={{0,16},{16,32},{32,48},{48,0},{1,17},{17,33},{33,49},{49,1},{2,18}... | collective-permute-start | bytes 3145736 | tf_op jit(solution)/shard_map/ppermute | solution.py:302
  184.4 2.1 copy-start.3
  184.4 2.1 copy-start.4
  203.9 2.0 collective-permute-start.8
  213.7 68.1 %all-to-all-start.5 = ((bf16[32,3,128,128]{3,2,1,0:T(8,128)(2,1)}), bf16[32,3,128,128]{3,2,1,0:T(8,128)(2,1)S(1)}, u32[]{:S(2)}, u32[]{:S(2)}) async-start(bf16[32,3,128,128]{3,2,1,0:T(8,128)(2,1)} %bitcast.27), calls=%async_computation.5 | async-start | bytes 6291456 | tf_op jit(solution)/shard_map/all_to_all | solution.py:310
  226.9 4.3 %copy-start.8 = (bf16[8,2,128,128]{3,2,1,0:T(8,128)(2,1)S(1)}, bf16[8,2,128,128]{3,2,1,0:T(8,128)(2,1)}, u32[]{:S(2)}) copy-start(bf16[8,2,128,128]{3,2,1,0:T(8,128)(2,1)} %get-tuple-element.54) | copy-start | bytes 1572868
  226.9 2.2 collective-permute-start.13
  227.2 4.1 %collective-permute-start.11 = (bf16[8,2,128,128]{3,2,1,0:T(8,128)(2,1)}, bf16[8,2,128,128]{3,2,1,0:T(8,128)(2,1)S(1)}, u32[]{:S(2)}, u32[]{:S(2)}) collective-permute-start(bf16[8,2,128,128]{3,2,1,0:T(8,128)(2,1)} %get-tuple-element.58), channel_id=1, source_target_pairs={{0,8},{8,0},{1,9},{9,1},{2,10},{10,2},{3,11},{11,3},{4,12},{12,4},... | collective-permute-start | bytes 1572872 | tf_op jit(solution)/shard_map/ppermute | solution.py:366
  230.3 29.8 %collective-permute-start.14 = (bf16[8,2,128,128]{3,2,1,0:T(8,128)(2,1)S(1)}, bf16[8,2,128,128]{3,2,1,0:T(8,128)(2,1)S(1)}, u32[]{:S(2)}, u32[]{:S(2)}) collective-permute-start(bf16[8,2,128,128]{3,2,1,0:T(8,128)(2,1)S(1)} %add_convert_fusion), channel_id=1, source_target_pairs={{0,16},{16,32},{32,48},{48,64},{64,80},{80,96},{96,112},{112,0},{1... | collective-permute-start | bytes 1572872 | tf_op jit(solution)/shard_map/ppermute | solution.py:302
  231.4 28.7 %collective-permute-start.12 = (bf16[8,2,128,128]{3,2,1,0:T(8,128)(2,1)S(1)}, bf16[8,2,128,128]{3,2,1,0:T(8,128)(2,1)S(1)}, u32[]{:S(2)}, u32[]{:S(2)}) collective-permute-start(bf16[8,2,128,128]{3,2,1,0:T(8,128)(2,1)S(1)} %add_convert_fusion.1), channel_id=1, source_target_pairs={{0,112},{16,0},{32,16},{48,32},{64,48},{80,64},{96,80},{112,96},{1... | collective-permute-start | bytes 1572872 | tf_op jit(solution)/shard_map/ppermute | solution.py:302
  260.1 0.8 copy-start.9
  260.9 0.8 copy-start.10
  281.8 19.3 %copy-start = (bf16[32,3,128,128]{3,2,1,0:T(8,128)(2,1)}, bf16[32,3,128,128]{3,2,1,0:T(8,128)(2,1)S(1)}, u32[]{:S(2)}) copy-start(bf16[32,3,128,128]{3,2,1,0:T(8,128)(2,1)S(1)} %all-to-all-done.5) | copy-start | bytes 9437188

commit v6 on v5

--- a/solution.py
+++ b/solution.py
@@ -79,10 +79,10 @@
     keys, values, qd, acc, stage, dq, kcat, s_scr, dp_scr, ds_scr, in_sem, out_sem = refs[5:]
     copies = []
     for source, fetch in zip(sources, fetches):
-        for src, t, i in fetch(source, place_ref):
-            dst = (keys, values)[t].at[pl.ds(i * size, size)]
+        for src, t, row in fetch(source, place_ref):
+            dst = (keys, values)[t].at[pl.ds(row, src.shape[0])]
             copies.append(pltpu.make_async_copy(src, dst, in_sem.at[len(copies)]))
-    q_rows = qd_in.at[pl.ds(pl.multiple_of(place_ref[0], 8), n_query)]
+    q_rows = qd_in.at[pl.ds(pl.multiple_of(place_ref[0], 8), n_query), pl.ds(qd_in.shape[1] - 2, 2)]
     copies.append(pltpu.make_async_copy(q_rows, qd, in_sem.at[len(copies)]))
     for copy in copies:
         copy.start()
@@ -152,7 +152,7 @@
             pltpu.VMEM((MAXK, BLK, HD), F32),
             pltpu.VMEM((MAXK, BLK, HD), F32),
             pltpu.VMEM((MAXK * BLK, HD), BF16),
-            pltpu.SemaphoreType.DMA((7,)),
+            pltpu.SemaphoreType.DMA((13,)),
             pltpu.SemaphoreType.DMA((7,)),
         ],
         compiler_params=pltpu.CompilerParams(vmem_limit_bytes=VMEM_LIMIT),
@@ -166,7 +166,7 @@
     return out[0], out[1:]
 
 
-def split_kernel(k_ref, v_ref, q_ref, g_ref, ka_ref, va_ref, qda_ref, kvb_ref, qdb_ref):
+def split_kernel(k_ref, v_ref, q_ref, g_ref, ka_ref, va_ref, qda_ref, b_ref):
     for j in range(ka_ref.shape[1]):
 
         def head(ref, m):
@@ -177,50 +177,42 @@
             va_ref[m, j] = head(v_ref, m)
             qda_ref[m, j, 0] = head(q_ref, m)
             qda_ref[m, j, 1] = head(g_ref, m)
-        for core in range(2):
-            kvb_ref[core, j, 0] = head(k_ref, 4)
-            kvb_ref[core, j, 1] = head(v_ref, 4)
-        qdb_ref[j, 0] = head(q_ref, 4)
-        qdb_ref[j, 1] = head(g_ref, 4)
+        for t, ref in enumerate((k_ref, v_ref, q_ref, g_ref)):
+            b_ref[j, t] = head(ref, 4)
 
 
 def split_heads(key_in, value_in, query_in, out_grad):
     groups, step = key_in.shape[1] // (HPG * HD), 2
-
     one = pl.BlockSpec((4, step, BLK, HD), lambda j: (0, j, 0, 0))
     two = pl.BlockSpec((4, step, 2, BLK, HD), lambda j: (0, j, 0, 0, 0))
-    kvb = pl.BlockSpec((2, step, 2, BLK, HD), lambda j: (0, j, 0, 0, 0))
-    qdb = pl.BlockSpec((step, 2, BLK, HD), lambda j: (j, 0, 0, 0))
-    shapes = ((4, groups), (4, groups), (4, groups, 2), (2, groups, 2), (groups, 2))
-    ka, va, qda, kvb_out, qdb_out = pl.pallas_call(
+    four = pl.BlockSpec((step, 4, BLK, HD), lambda j: (j, 0, 0, 0))
+    shapes = ((4, groups), (4, groups), (4, groups, 2), (groups, 4))
+    ka, va, qda, b = pl.pallas_call(
         split_kernel,
         grid=(groups // step,),
         out_shape=tuple(jax.ShapeDtypeStruct((*x, BLK, HD), BF16) for x in shapes),
         in_specs=[pl.BlockSpec((BLK, step * HPG * HD), lambda j: (0, j))] * 4,
-        out_specs=(one, one, two, kvb, qdb),
+        out_specs=(one, one, two, four),
         compiler_params=pltpu.CompilerParams(vmem_limit_bytes=VMEM_LIMIT),
         cost_estimate=pl.CostEstimate(flops=0, bytes_accessed=16 * key_in.size, transcendentals=0),
         name="split_heads",
     )(key_in, value_in, query_in, out_grad)
     flat = 4 * groups
-    return (
-        ka.reshape(flat, BLK, HD),
-        va.reshape(flat, BLK, HD),
-        qda.reshape(flat, 2, BLK, HD),
-        kvb_out.reshape(2 * groups, 2, BLK, HD),
-        qdb_out,
-    )
-
-
-def join_kernel(a_ref, b_ref, *outs):
+    return ka.reshape(flat, BLK, HD), va.reshape(flat, BLK, HD), qda.reshape(flat, 2, BLK, HD), b
+
+
+def join_kernel(dqa_ref, dkva_ref, b_ref, *outs):
     for t, ref in enumerate(outs):
         for j in range(b_ref.shape[0]):
             for m in range(HPG):
-                value = a_ref[m, j, t] if m < 4 else b_ref[j, t]
+                if m == 4:
+                    value = b_ref[j, t]
+                else:
+                    value = dqa_ref[m, j] if t == 0 else dkva_ref[m, j, t - 1]
                 ref[:, (j * HPG + m) * HD : (j * HPG + m + 1) * HD] = value
 
 
-def join_heads(back_a, back_b):
+def join_heads(dqa, dkva, back_b):
     groups, step = back_b.shape[0], 2
     out = jax.ShapeDtypeStruct((BLK, groups * HPG * HD), BF16)
     return pl.pallas_call(
@@ -228,7 +220,8 @@
         grid=(groups // step,),
         out_shape=(out,) * 3,
         in_specs=[
-            pl.BlockSpec((4, step, 3, BLK, HD), lambda j: (0, j, 0, 0, 0)),
+            pl.BlockSpec((4, step, BLK, HD), lambda j: (0, j, 0, 0)),
+            pl.BlockSpec((4, step, 2, BLK, HD), lambda j: (0, j, 0, 0, 0)),
             pl.BlockSpec((step, 3, BLK, HD), lambda j: (j, 0, 0, 0)),
         ],
         out_specs=(pl.BlockSpec((BLK, step * HPG * HD), lambda j: (0, j)),) * 3,
@@ -237,7 +230,7 @@
             flops=0, bytes_accessed=groups * HPG * 3 * BLK * HD * 4, transcendentals=0
         ),
         name="join_heads",
-    )(back_a.reshape(4, groups, 3, BLK, HD), back_b)
+    )(dqa.reshape(4, groups, BLK, HD), dkva.reshape(4, groups, 2, BLK, HD), back_b)
 
 
 def total_kernel(dq_ref, own_ref, *refs):
@@ -265,31 +258,28 @@
     )(dq, own, *terms)
 
 
-def both_halves_kernel(x_ref, dq0, dq1, own0, own1, right0, right1, left0, left1, out_ref):
+def both_halves_kernel(x_ref, own0, own1, right0, right1, left0, left1, out_ref):
     x = x_ref[0]
-    for s, (dq, own) in enumerate(((dq0, own0), (dq1, own1))):
+    for s, own in enumerate((own0, own1)):
         right = jnp.where(x == x_ref[1], (right1, right0)[s][...], (right0, right1)[s][...])
         left = jnp.where(x == 0, (left1, left0)[s][...], (left0, left1)[s][...])
         total = own[...].astype(F32) + right.astype(F32) + left.astype(F32)
-        out_ref[s, :, 0] = dq[...]
-        out_ref[s, :, 1:] = total.astype(BF16)
-
-
-def both_halves(x, last, dq, own, from_right, from_left):
+        out_ref[s] = total.astype(BF16)
+
+
+def both_halves(x, last, own, from_right, from_left):
     blocks, step = own[0].shape[0], 4
     spec = pl.BlockSpec((step, 2, BLK, HD), lambda i: (i, 0, 0, 0))
     out = pl.pallas_call(
         both_halves_kernel,
         grid=(blocks // step,),
-        out_shape=jax.ShapeDtypeStruct((2, blocks, 3, BLK, HD), BF16),
-        in_specs=[pl.BlockSpec(memory_space=pltpu.SMEM)]
-        + [pl.BlockSpec((step, BLK, HD), lambda i: (i, 0, 0))] * 2
-        + [spec] * 6,
-        out_specs=pl.BlockSpec((2, step, 3, BLK, HD), lambda i: (0, i, 0, 0, 0)),
-        cost_estimate=pl.CostEstimate(flops=0, bytes_accessed=20 * own[0].size, transcendentals=0),
+        out_shape=jax.ShapeDtypeStruct((2, blocks, 2, BLK, HD), BF16),
+        in_specs=[pl.BlockSpec(memory_space=pltpu.SMEM)] + [spec] * 6,
+        out_specs=pl.BlockSpec((2, step, 2, BLK, HD), lambda i: (0, i, 0, 0, 0)),
+        cost_estimate=pl.CostEstimate(flops=0, bytes_accessed=16 * own[0].size, transcendentals=0),
         name="both_halves",
-    )(jnp.stack([x, jnp.int32(last)]), *dq, *own, *from_right, *from_left)
-    return out.reshape(2 * blocks, 3, BLK, HD)
+    )(jnp.stack([x, jnp.int32(last)]), *own, *from_right, *from_left)
+    return out.reshape(2 * blocks, 2, BLK, HD)
 
 
 WIDE = ("half", "core", "group")
@@ -314,72 +304,73 @@
     return lax.optimization_barrier((x, *done))[0]
 
 
+def swap(value):
+    return lax.ppermute(value, "core", [(0, 1), (1, 0)])
+
+
 def shards(query_in, key_in, value_in, out_grad, key_blocks, block_count):
     half, x, core = (lax.axis_index(name) for name in ("half", "x", "core"))
-    last = lax.axis_size("x") - 1
+    last, size = lax.axis_size("x") - 1, 2 * BPD
     packed = jnp.concatenate([key_blocks, block_count[:, :, None]], axis=2)
-    ka, va, qda, kvb, qdb = split_heads(key_in, value_in, query_in, out_grad)
-
-    keys = exchange(ka, WIDE)
-    key_near = [shift(keys, "x", 1), shift(keys, "x", -1)]
-    values = exchange(after(va, keys), WIDE)
-    value_near = [shift(values, "x", 1), shift(values, "x", -1)]
-    queries = exchange(after(qda, values, *key_near), WIDE)
     lists = lax.all_gather(packed[:4], ("half", "core"))
     lists = lax.dynamic_index_in_dim(lists, 2 * half + core, 1, False)
-    own_b = exchange(after(kvb, queries, *key_near, *value_near), PAIR)
+    ka, va, qda, b = split_heads(key_in, value_in, query_in, out_grad)
 
     def plain(lists, chip):
         lists = lists.reshape(-1, MAXK + 1)
         first_block = (chip - 1) * 2 * BPD
         return (lists[:, :MAXK] - first_block).reshape(-1), lists[:, MAXK]
 
+    own_b = exchange(b, "group")
+    pairs_b = own_b[:, :2]
+    mine = (shift(pairs_b, CHIPS, 1), pairs_b, shift(pairs_b, CHIPS, -1))
+    theirs = tuple(swap(pairs) for pairs in mine)
+
+    keys = exchange(after(ka, own_b), WIDE)
+    key_near = [shift(keys, "x", 1), shift(keys, "x", -1)]
+    values = exchange(after(va, keys, *mine), WIDE)
+    value_near = [shift(values, "x", 1), shift(values, "x", -1)]
+
+    def run(i, other):
+        def fetch(ref, place):
+            at = i * size + (BPD - place[1] if other else place[1])
+            return [(ref.at[:, t], t, pl.multiple_of(at, 8)) for t in range(2)]
+
+        return fetch
+
+    ids, counts = plain(packed[4], half * (last + 1) + x)
+    place = after(jnp.stack([jnp.int32(0), core * BPD]), keys, lists)
+    fetches = [run(i, other) for other in range(2) for i in range(3)]
+    dq_b, (left_b, mine_b, right_b, give_b) = attention(
+        ids, counts, place, mine + theirs, fetches, own_b, BPD, size
+    )
+    got_b = [swap(give_b[i]) for i in range(3)]
+    out_b = lax.optimization_barrier((add(left_b, got_b[0]), add(right_b, got_b[2]), *value_near))
+    terms_b = [got_b[1], shift(out_b[0], CHIPS, -1), shift(out_b[1], CHIPS, 1)]
+
+    queries = exchange(after(qda, values, dq_b, *key_near), WIDE)
+
     def third(t, i):
-        return lambda ref, place: [(ref.at[pl.ds(pl.multiple_of(place[2 + i], 8), size)], t, i)]
-
-    size = 2 * BPD
+        return lambda ref, place: [(ref.at[pl.ds(pl.multiple_of(place[1 + i], 8), size)], t, i * size)]
+
     fetches = [third(t, i) for t in range(2) for i in range(3)]
     sources = (key_near[0], keys, key_near[1], value_near[0], values, value_near[1])
-    done = []
+    done, back_b = [], ()
     for s in range(2):
         ids, counts = plain(lists[2 * s : 2 * s + 2], s * (last + 1) + x)
         left = jnp.where(x == 0, 1 - s, s) * size
         right = jnp.where(x == last, 1 - s, s) * size
-        place = jnp.stack([jnp.int32(s * size), jnp.int32(0), left, jnp.int32(s * size), right])
-        place = after(place, *[d[0] for d in done])
+        place = after(jnp.stack([jnp.int32(s * size), left, jnp.int32(s * size), right]), *back_b)
         dq, grads = attention(ids, counts, place, sources, fetches, queries, size, size)
         done.append((dq, grads, shift(grads[0], "x", -1), shift(grads[2], "x", 1)))
         if s == 0:
-            own_b = after(own_b, dq)
-            near_b = [shift(own_b, CHIPS, 1), shift(own_b, CHIPS, -1)]
-            queries_b = exchange(after(qdb, own_b), "group")
-
-    def pair(i):
-        return lambda ref, place: [(ref.at[:, t], t, i) for t in range(2)]
-
-    ids, counts = plain(packed[4], half * (last + 1) + x)
-    place = jnp.stack([jnp.int32(0), core * BPD])
-    place = after(place, done[1][0], done[0][2], done[0][3])
-    dq_b, (left_b, mine_b, right_b, give_b) = attention(
-        ids, counts, place, (near_b[0], own_b, near_b[1]), [pair(i) for i in range(3)], queries_b, BPD, size
-    )
-    got_b = [lax.ppermute(give_b[i], "core", [(0, 1), (1, 0)]) for i in range(3)]
-    terms_b = [
-        got_b[1],
-        shift(add(left_b, got_b[0]), CHIPS, -1),
-        shift(add(right_b, got_b[2]), CHIPS, 1),
-    ]
-    total_a = both_halves(
-        after(x, *terms_b[:1]),
-        last,
-        [d[0] for d in done],
-        [d[1][1] for d in done],
-        [d[2] for d in done],
-        [d[3] for d in done],
-    )
-    back_a = exchange(total_a, WIDE)
-    back_b = exchange(after(total_grads(dq_b, mine_b, terms_b), back_a), "group")
-    return tuple(join_heads(back_a, back_b))
+            total_b = total_grads(after(dq_b, dq), mine_b, terms_b)
+            back_b = (total_b,)
+    back_b = exchange(total_b, "group")
+    dqa = exchange(after(jnp.concatenate([d[0] for d in done]), *done[0][2:], back_b), WIDE)
+    dkva = both_halves(x, last, [d[1][1] for d in done], [d[2] for d in done], [d[3] for d in done])
+    dkva = exchange(after(dkva, dqa), WIDE)
+    return tuple(join_heads(dqa, dkva, back_b))
 
 
 def solution(mesh):

time: 308 us -> 280 us (0.909)
  waiting for transfers between devices: 81.2 us -> 37.1 us
  blocking collectives: 72.9 us -> 84.8 us
  other arithmetic: 3.27 us -> 8.9 us
  Pallas kernels: 82.8 us -> 79 us
    ppermute x12, waiting for transfers between devices: 57.7 us -> 13.9 us  [shift(): lax.ppermute(value, axes, [(s, (s + steps) % count) for s in range(count)])]
    all_gather x1, blocking collectives: 6.69 us -> 23 us  [shards(): lists = lax.all_gather(packed[:4], ('half', 'core'))]
    all_to_all x3 -> x2, blocking collectives: 66.2 us -> 61.8 us  [exchange(): return lax.all_to_all(x, axes, 0, 0, tiled=True)]
    pallas_call x3, Pallas kernels: 64.5 us -> 61.3 us  [attention(): pl.pallas_call(functools.partial(attention_kernel, size, n_query, fetches...]
    all_to_all x4 -> x5, waiting for transfers between devices: 19.8 us -> 22.1 us  [exchange(): return lax.all_to_all(x, axes, 0, 0, tiled=True)]
    all_to_all x4 -> x5, starting transfers between devices: 38.4 us -> 37.9 us  [exchange(): return lax.all_to_all(x, axes, 0, 0, tiled=True)]
  transfers between devices with their start and end apart: 19 -> 23, of which waited for: 11 -> 6; matrix products, arithmetic and copies ran while one was open for 3% -> 5% of each run, Pallas kernels for 22% -> 25%
where the time goes in v6:
time: 280 us; the launch traced here: 279 us
  blocking collectives  84.8 us (30%)
  Pallas kernels  79 us (28%)
  starting transfers between devices  57.2 us (20%)
  waiting for transfers between devices  37.1 us (13%)
  local copies, waits for them, and re-layouts  11 us (4%)
  other arithmetic  8.9 us (3%)
    all_to_all x2, blocking collectives, exchange(): return lax.all_to_all(x, axes, 0, 0, tiled=True)  61.8 us
    pallas_call x3, Pallas kernels, attention(): pl.pallas_call(functools.partial(attention_kernel, size, n_query, fetches...  61.3 us
    all_to_all x5, starting transfers between devices, exchange(): return lax.all_to_all(x, axes, 0, 0, tiled=True)  37.9 us
    all_gather x1, blocking collectives, shards(): lists = lax.all_gather(packed[:4], ('half', 'core'))  23 us
    all_to_all x5, waiting for transfers between devices, exchange(): return lax.all_to_all(x, axes, 0, 0, tiled=True)  22.1 us
    ppermute x12, starting transfers between devices, shift(): lax.ppermute(value, axes, [(s, (s + steps) % count) for s in range(count)])  17.9 us
    ppermute x12, waiting for transfers between devices, shift(): lax.ppermute(value, axes, [(s, (s + steps) % count) for s in range(count)])  13.9 us
  transfers between devices with their start and end apart: 23, of which 6 were waited for; matrix products, arithmetic and copies ran while one was open for 5% of the time, Pallas kernels for 25%

profile of v6, /device:TPU:8, one launch (start us, length us, event | category | flops | bytes accessed | tf_op | source)
XLA Modules:
  0.0 278.8 jit_solution(5676356184974397532)
XLA Ops:
  0.6 5.5 %split_heads.1 = (bf16[4,8,128,128]{3,2,1,0:T(8,128)(2,1)}, bf16[4,8,128,128]{3,2,1,0:T(8,128)(2,1)}, bf16[4,8,2,128,128]{4,3,2,1,0:T(8,128)(2,1)}, bf16[8,4,128,128]{3,2,1,0:T(8,128)(2,1)}) custom-call(bf16[128,5120]{1,0:T(8,128)(2,1)} %k_ref.1, bf16[128,5120]{1,0:T(8,128)(2,1)} %v_ref.1, bf16[128,5120]{1,0:T(8,128)(2,1)} %q_ref.1, bf16[128,5120]{1,0:T(8,128)(2,1)} %g_ref.1), custom_call_target="tpu_custom_call" | custom-call | bytes 10485760 | tf_op jit(solution)/shard_map/split_heads/pallas_call | solution.py:190
  6.1 24.4 %all_to_all.35.refs_6_ = bf16[8,4,128,128]{3,2,1,0:T(8,128)(2,1)S(1)} all-to-all(bf16[8,4,128,128]{3,2,1,0:T(8,128)(2,1)} %get-tuple-element.31), channel_id=1, replica_groups=mesh['half'=2,'x'=4,'core'=2,'group'=8] {'group'}, dimensions={0} | all-to-all | bytes 2097152 | tf_op jit(solution)/shard_map/all_to_all | solution.py:300
  30.5 4.7 %all-to-all-start.1 = ((bf16[32,128,128]{2,1,0:T(8,128)(2,1)}), bf16[32,128,128]{2,1,0:T(8,128)(2,1)S(1)}, u32[]{:S(2)}, u32[]{:S(2)}) async-start(bf16[32,128,128]{2,1,0:T(8,128)(2,1)} %bitcast.30), calls=%async_computation.1 | async-start | bytes 2097152 | tf_op jit(solution)/shard_map/all_to_all | solution.py:300
  35.2 0.0 copy-start.17
  35.2 0.0 copy-start.16
  35.2 3.8 %collective-permute-start.3 = (bf16[8,2,128,128]{3,2,1,0:T(8,128)(2,1)S(1)}, bf16[8,2,128,128]{3,2,1,0:T(8,128)(2,1)S(1)}, u32[]{:S(2)}, u32[]{:S(2)}) collective-permute-start(bf16[8,2,128,128]{3,2,1,0:T(8,128)(2,1)S(1)} %slice.62.refs_1_), channel_id=1, source_target_pairs={{0,112},{16,0},{32,16},{48,32},{64,48},{80,64},{96,80},{112,96},{1... | collective-permute-start | bytes 1572872 | tf_op jit(solution)/shard_map/ppermute | solution.py:292
  39.1 0.0 collective-permute-start.2
  39.1 22.1 %all-to-all-done.1.refs_1_ = bf16[32,128,128]{2,1,0:T(8,128)(2,1)S(1)} async-done(((bf16[32,128,128]{2,1,0:T(8,128)(2,1)}), bf16[32,128,128]{2,1,0:T(8,128)(2,1)S(1)}, u32[]{:S(2)}, u32[]{:S(2)}) %all-to-all-start.1) | async-done | bytes 1048608 | tf_op jit(solution)/shard_map/all_to_all | solution.py:300
  61.2 2.8 collective-permute-start.1
  64.0 0.0 collective-permute-done.2.refs_0_
  64.0 0.9 copy-done.12
  64.9 6.6 %all-to-all-start.2 = ((bf16[32,128,128]{2,1,0:T(8,128)(2,1)}), bf16[32,128,128]{2,1,0:T(8,128)(2,1)S(1)}, u32[]{:S(2)}, u32[]{:S(2)}) async-start(bf16[32,128,128]{2,1,0:T(8,128)(2,1)} %bitcast.29), calls=%async_computation.2 | async-start | bytes 2097152 | tf_op jit(solution)/shard_map/all_to_all | solution.py:300
  71.4 0.1 copy.14
  71.6 0.2 collective-permute-start.7
  71.7 0.4 collective-permute-start.8
  72.1 0.1 collective-permute-start.6
  72.2 0.1 fusion.1
  72.3 0.6 reshape.48.ids_ref
  72.9 0.6 pad_add_fusion.2.place_ref
  73.6 0.8 slice_reduce_fusion.2.cnt_ref
  74.3 0.8 collective-permute-done.8.refs_5_
  75.1 0.2 collective-permute-done.6.refs_3_
  75.3 13.3 %attention.3 = (bf16[8,128,128]{2,1,0:T(8,128)(2,1)}, bf16[8,2,128,128]{3,2,1,0:T(8,128)(2,1)}, bf16[8,2,128,128]{3,2,1,0:T(8,128)(2,1)}, bf16[8,2,128,128]{3,2,1,0:T(8,128)(2,1)}, bf16[3,8,2,128,128]{4,3,2,1,0:T(8,128)(2,1)}) custom-call(s32[96]{0:T(128)} %reshape.48.ids_ref, s32[8]{0:T(128)} %slice_reduce_fusion.2.cnt_ref, s32[2]{0:T(128)} %pad_add_fusion.2.place_ref, ...), custom_call_target="tpu_custom_call" | custom-call | tf_op jit(solution)/shard_map/attention/pallas_call | solution.py:139
  88.6 0.0 all-to-all-done.2.refs_4_
  88.7 0.0 copy-start.8
  88.7 0.5 collective-permute-done.refs_0_
  89.2 0.5 copy-done.8
  89.6 8.9 %all-to-all-start.3 = ((bf16[32,2,128,128]{3,2,1,0:T(8,128)(2,1)}), bf16[32,2,128,128]{3,2,1,0:T(8,128)(2,1)S(1)}, u32[]{:S(2)}, u32[]{:S(2)}) async-start(bf16[32,2,128,128]{3,2,1,0:T(8,128)(2,1)} %bitcast.7), calls=%async_computation.3 | async-start | bytes 4194304 | tf_op jit(solution)/shard_map/all_to_all | solution.py:300
  98.6 0.7 pad_add_fusion.1.place_ref
  99.3 2.6 slice_bitcast_fusion
  101.9 0.1 collective-permute-start.11
  102.0 3.4 %collective-permute-start.5 = (bf16[32,128,128]{2,1,0:T(8,128)(2,1)S(1)}, bf16[32,128,128]{2,1,0:T(8,128)(2,1)}, u32[]{:S(2)}, u32[]{:S(2)}) collective-permute-start(bf16[32,128,128]{2,1,0:T(8,128)(2,1)S(1)} %copy-done.9), channel_id=1, source_target_pairs={{0,48},{16,0},{32,16},{48,32},{1,49},{17,1},{33,17},{49,33},{2,50}... | collective-permute-start | bytes 3145736 | tf_op jit(solution)/shard_map/ppermute | solution.py:292
  105.4 0.1 fusion
  105.5 23.0 %all-gather = s32[16,8,13]{2,1,0:T(8,128)S(1)} all-gather(s32[4,8,13]{2,1,0:T(8,128)S(1)} %fusion), channel_id=2, replica_groups=mesh['half'=2,'x'=4,'core'=2,'group'=8] {'half','core'}, dimensions={0}, use_global_device_ids=true | all-gather | bytes 8320 | tf_op jit(solution)/shard_map/all_gather | solution.py:315
  128.4 0.4 collective-permute-start.10
  128.8 0.7 reshape.44.ids_ref
  129.5 0.8 slice_reduce_fusion
  130.3 0.1 collective-permute-start.9
  130.4 2.2 add_convert_fusion
  132.6 2.0 add_convert_fusion.1
  134.6 1.5 collective-permute-start.12
  136.1 0.5 collective-permute-start.13
  136.6 1.3 copy-done.4
  137.9 23.8 %attention.4 = (bf16[16,128,128]{2,1,0:T(8,128)(2,1)}, bf16[16,2,128,128]{3,2,1,0:T(8,128)(2,1)}, bf16[16,2,128,128]{3,2,1,0:T(8,128)(2,1)}, bf16[16,2,128,128]{3,2,1,0:T(8,128)(2,1)}) custom-call(s32[192]{0:T(256)} %reshape.44.ids_ref, s32[16]{0:T(128)} %get-tuple-element.63.cnt_ref, s32[4]{0:T(128)} %pad_add_fusion.1.place_ref, ...), custom_call_target="tpu_custom_call" | custom-call | flops 2684354560 | bytes 7340032 | tf_op jit(solution)/shard_map/attention/pallas_call | solution.py:139
  161.8 3.6 %collective-permute-start.14 = (bf16[16,2,128,128]{3,2,1,0:T(8,128)(2,1)}, bf16[16,2,128,128]{3,2,1,0:T(8,128)(2,1)S(1)}, u32[]{:S(2)}, u32[]{:S(2)}) collective-permute-start(bf16[16,2,128,128]{3,2,1,0:T(8,128)(2,1)} %get-tuple-element.49), channel_id=1, source_target_pairs={{0,48},{16,0},{32,16},{48,32},{1,49},{17,1},{33,17},{49,33},{2,50}... | collective-permute-start | bytes 3145736 | tf_op jit(solution)/shard_map/ppermute | solution.py:292
  165.3 0.0 copy-start.14
  165.4 0.8 copy-done.14
  166.1 0.2 copy-done.15
  166.3 2.5 total_grads.1
  168.8 7.8 %all-to-all-start.4 = ((bf16[8,3,128,128]{3,2,1,0:T(8,128)(2,1)}), bf16[8,3,128,128]{3,2,1,0:T(8,128)(2,1)S(1)}, u32[]{:S(2)}, u32[]{:S(2)}) async-start(bf16[8,3,128,128]{3,2,1,0:T(8,128)(2,1)} %total_grads.1), calls=%async_computation.4 | async-start | bytes 1572864 | tf_op jit(solution)/shard_map/all_to_all | solution.py:300
  176.6 0.7 reshape.50.ids_ref
  177.2 0.6 pad_add_fusion.3.place_ref
  177.8 24.2 %attention.5 = (bf16[16,128,128]{2,1,0:T(8,128)(2,1)}, bf16[16,2,128,128]{3,2,1,0:T(8,128)(2,1)}, bf16[16,2,128,128]{3,2,1,0:T(8,128)(2,1)}, bf16[16,2,128,128]{3,2,1,0:T(8,128)(2,1)}) custom-call(s32[192]{0:T(256)} %reshape.50.ids_ref, s32[16]{0:T(128)} %get-tuple-element.62.cnt_ref, s32[4]{0:T(128)} %pad_add_fusion.3.place_ref, ...), custom_call_target="tpu_custom_call" | custom-call | flops 2684354560 | bytes 7340032 | tf_op jit(solution)/shard_map/attention/pallas_call | solution.py:139
  202.0 2.3 collective-permute-start.16
  204.4 2.1 pad_maximum_fusion
  206.5 0.0 copy-start.5
  206.5 1.0 copy-done.6
  207.5 10.0 %all-to-all-start.5 = ((bf16[32,128,128]{2,1,0:T(8,128)(2,1)}), bf16[32,128,128]{2,1,0:T(8,128)(2,1)S(1)}, u32[]{:S(2)}, u32[]{:S(2)}) async-start(bf16[32,128,128]{2,1,0:T(8,128)(2,1)} %pad_maximum_fusion), calls=%async_computation.5 | async-start | bytes 2097152 | tf_op jit(solution)/shard_map/all_to_all | solution.py:300
  217.5 0.7 pad_add_fusion.4.x_ref
  218.2 10.0 %collective-permute-done.16.right1 = bf16[16,2,128,128]{3,2,1,0:T(8,128)(2,1)} collective-permute-done((bf16[16,2,128,128]{3,2,1,0:T(8,128)(2,1)}, bf16[16,2,128,128]{3,2,1,0:T(8,128)(2,1)}, u32[]{:S(2)}, u32[]{:S(2)}) %collective-permute-start.16) | collective-permute-done | bytes 1048608 | tf_op jit(solution)/shard_map/ppermute | solution.py:292
  228.2 3.4 %collective-permute-done.17.left1 = bf16[16,2,128,128]{3,2,1,0:T(8,128)(2,1)} collective-permute-done((bf16[16,2,128,128]{3,2,1,0:T(8,128)(2,1)}, bf16[16,2,128,128]{3,2,1,0:T(8,128)(2,1)}, u32[]{:S(2)}, u32[]{:S(2)}) %collective-permute-start.17) | collective-permute-done | bytes 1048608 | tf_op jit(solution)/shard_map/ppermute | solution.py:292
  231.6 5.0 %both_halves.1 = bf16[2,16,2,128,128]{4,3,2,1,0:T(8,128)(2,1)} custom-call(s32[2]{0:T(128)} %pad_add_fusion.4.x_ref, bf16[16,2,128,128]{3,2,1,0:T(8,128)(2,1)} %get-tuple-element.52.own0, bf16[16,2,128,128]{3,2,1,0:T(8,128)(2,1)} %get-tuple-element.53.own1, bf16[16,2,128,128]{3,2,1,0:T(8,128)(2,1)} %copy-done.5, ...), custom_call_target="tpu_custom_call" | custom-call | bytes 8388608 | tf_op jit(solution)/shard_map/both_halves/pallas_call | solution.py:273
  236.6 37.5 %all_to_all.36 = bf16[32,2,128,128]{3,2,1,0:T(8,128)(2,1)} all-to-all(bf16[32,2,128,128]{3,2,1,0:T(8,128)(2,1)} %bitcast.27), channel_id=1, replica_groups=mesh['half'=2,'x'=4,'core'=2,'group'=8] {'half','core','group'}, dimensions={0} | all-to-all | bytes 4194304 | tf_op jit(solution)/shard_map/all_to_all | solution.py:300
  274.1 4.7 %join_heads.1 = (bf16[128,5120]{1,0:T(8,128)(2,1)}, bf16[128,5120]{1,0:T(8,128)(2,1)}, bf16[128,5120]{1,0:T(8,128)(2,1)}) custom-call(bf16[4,8,128,128]{3,2,1,0:T(8,128)(2,1)} %bitcast.28, bf16[4,8,2,128,128]{4,3,2,1,0:T(8,128)(2,1)} %bitcast.26, bf16[8,3,128,128]{3,2,1,0:T(8,128)(2,1)} %copy-done.2), custom_call_target="tpu_custom_call" | custom-call | bytes 7864320 | tf_op jit(solution)/shard_map/join_heads/pallas_call | solution.py:218
  (48 shorter events, 0.2 us)
Async XLA Ops:
  30.5 4.7 %copy-start = (bf16[8,4,128,128]{3,2,1,0:T(8,128)(2,1)}, bf16[8,4,128,128]{3,2,1,0:T(8,128)(2,1)S(1)}, u32[]{:S(2)}) copy-start(bf16[8,4,128,128]{3,2,1,0:T(8,128)(2,1)S(1)} %all_to_all.35.refs_6_) | copy-start | bytes 3145732
  30.5 30.7 %all-to-all-start.1 = ((bf16[32,128,128]{2,1,0:T(8,128)(2,1)}), bf16[32,128,128]{2,1,0:T(8,128)(2,1)S(1)}, u32[]{:S(2)}, u32[]{:S(2)}) async-start(bf16[32,128,128]{2,1,0:T(8,128)(2,1)} %bitcast.30), calls=%async_computation.1 | async-start | bytes 2097152 | tf_op jit(solution)/shard_map/all_to_all | solution.py:300
  35.2 40.1 %copy-start.3 = (bf16[8,2,128,128]{3,2,1,0:T(8,128)(2,1)}, bf16[8,2,128,128]{3,2,1,0:T(8,128)(2,1)S(1)}, u32[]{:S(2)}) copy-start(bf16[8,2,128,128]{3,2,1,0:T(8,128)(2,1)S(1)} %slice.62.refs_1_) | copy-start | bytes 1572868
  35.2 36.2 %copy-start.17 = (s32[5,8]{1,0:T(8,128)S(1)}, s32[5,8]{1,0:T(8,128)}, u32[]{:S(2)}) copy-start(s32[5,8]{1,0:T(8,128)} %param.11) | copy-start | bytes 484
  35.2 37.0 %copy-start.16 = (s32[5,8,12]{2,1,0:T(8,128)S(1)}, s32[5,8,12]{2,1,0:T(8,128)}, u32[]{:S(2)}) copy-start(s32[5,8,12]{2,1,0:T(8,128)} %param.10) | copy-start | bytes 5764
  35.2 28.7 %collective-permute-start.3 = (bf16[8,2,128,128]{3,2,1,0:T(8,128)(2,1)S(1)}, bf16[8,2,128,128]{3,2,1,0:T(8,128)(2,1)S(1)}, u32[]{:S(2)}, u32[]{:S(2)}) collective-permute-start(bf16[8,2,128,128]{3,2,1,0:T(8,128)(2,1)S(1)} %slice.62.refs_1_), channel_id=1, source_target_pairs={{0,112},{16,0},{32,16},{48,32},{64,48},{80,64},{96,80},{112,96},{1... | collective-permute-start | bytes 1572872 | tf_op jit(solution)/shard_map/ppermute | solution.py:292
  39.1 24.9 %collective-permute-start.2 = (bf16[8,2,128,128]{3,2,1,0:T(8,128)(2,1)S(1)}, bf16[8,2,128,128]{3,2,1,0:T(8,128)(2,1)S(1)}, u32[]{:S(2)}, u32[]{:S(2)}) collective-permute-start(bf16[8,2,128,128]{3,2,1,0:T(8,128)(2,1)S(1)} %slice.62.refs_1_), channel_id=1, source_target_pairs={{0,16},{16,32},{32,48},{48,64},{64,80},{80,96},{96,112},{112,0},{1... | collective-permute-start | bytes 1572872 | tf_op jit(solution)/shard_map/ppermute | solution.py:292
  61.2 27.5 %copy-start.7 = (bf16[32,128,128]{2,1,0:T(8,128)(2,1)}, bf16[32,128,128]{2,1,0:T(8,128)(2,1)S(1)}, u32[]{:S(2)}) copy-start(bf16[32,128,128]{2,1,0:T(8,128)(2,1)S(1)} %all-to-all-done.1.refs_1_) | copy-start | bytes 3145732
  61.2 27.5 %collective-permute-start.1 = (bf16[32,128,128]{2,1,0:T(8,128)(2,1)S(1)}, bf16[32,128,128]{2,1,0:T(8,128)(2,1)}, u32[]{:S(2)}, u32[]{:S(2)}) collective-permute-start(bf16[32,128,128]{2,1,0:T(8,128)(2,1)S(1)} %all-to-all-done.1.refs_1_), channel_id=1, source_target_pairs={{0,48},{16,0},{32,16},{48,32},{1,49},{17,1},{33,17},{49,33},{2,50}... | collective-permute-start | bytes 3145736 | tf_op jit(solution)/shard_map/ppermute | solution.py:292
  63.9 25.2 %collective-permute-start = (bf16[32,128,128]{2,1,0:T(8,128)(2,1)S(1)}, bf16[32,128,128]{2,1,0:T(8,128)(2,1)}, u32[]{:S(2)}, u32[]{:S(2)}) collective-permute-start(bf16[32,128,128]{2,1,0:T(8,128)(2,1)S(1)} %all-to-all-done.1.refs_1_), channel_id=1, source_target_pairs={{0,16},{16,32},{32,48},{48,0},{1,17},{17,33},{33,49},{49,1},{2,18}... | collective-permute-start | bytes 3145736 | tf_op jit(solution)/shard_map/ppermute | solution.py:292
  63.9 11.4 %copy-start.11 = (bf16[8,2,128,128]{3,2,1,0:T(8,128)(2,1)}, bf16[8,2,128,128]{3,2,1,0:T(8,128)(2,1)S(1)}, u32[]{:S(2)}) copy-start(bf16[8,2,128,128]{3,2,1,0:T(8,128)(2,1)S(1)} %collective-permute-done.3.refs_2_) | copy-start | bytes 1572868
  64.0 0.9 copy-start.12
  64.9 23.8 %all-to-all-start.2 = ((bf16[32,128,128]{2,1,0:T(8,128)(2,1)}), bf16[32,128,128]{2,1,0:T(8,128)(2,1)S(1)}, u32[]{:S(2)}, u32[]{:S(2)}) async-start(bf16[32,128,128]{2,1,0:T(8,128)(2,1)} %bitcast.29), calls=%async_computation.2 | async-start | bytes 2097152 | tf_op jit(solution)/shard_map/all_to_all | solution.py:300
  71.6 2.8 collective-permute-start.7
  71.7 3.4 %collective-permute-start.8 = (bf16[8,2,128,128]{3,2,1,0:T(8,128)(2,1)S(1)}, bf16[8,2,128,128]{3,2,1,0:T(8,128)(2,1)}, u32[]{:S(2)}, u32[]{:S(2)}) collective-permute-start(bf16[8,2,128,128]{3,2,1,0:T(8,128)(2,1)S(1)} %collective-permute-done.3.refs_2_), channel_id=1, source_target_pairs={{0,8},{8,0},{1,9},{9,1},{2,10},{10,2},{3,11},{11,3},{4,12},{12,4},... | collective-permute-start | bytes 1572872 | tf_op jit(solution)/shard_map/ppermute | solution.py:308
  72.1 3.2 %collective-permute-start.6 = (bf16[8,2,128,128]{3,2,1,0:T(8,128)(2,1)}, bf16[8,2,128,128]{3,2,1,0:T(8,128)(2,1)}, u32[]{:S(2)}, u32[]{:S(2)}) collective-permute-start(bf16[8,2,128,128]{3,2,1,0:T(8,128)(2,1)} %copy-done.12), channel_id=1, source_target_pairs={{0,8},{8,0},{1,9},{9,1},{2,10},{10,2},{3,11},{11,3},{4,12},{12,4},... | collective-permute-start | bytes 1572872 | tf_op jit(solution)/shard_map/ppermute | solution.py:308
  88.7 1.0 copy-start.8
  89.6 47.0 %all-to-all-start.3 = ((bf16[32,2,128,128]{3,2,1,0:T(8,128)(2,1)}), bf16[32,2,128,128]{3,2,1,0:T(8,128)(2,1)S(1)}, u32[]{:S(2)}, u32[]{:S(2)}) async-start(bf16[32,2,128,128]{3,2,1,0:T(8,128)(2,1)} %bitcast.7), calls=%async_computation.3 | async-start | bytes 4194304 | tf_op jit(solution)/shard_map/all_to_all | solution.py:300
  99.3 2.8 copy-start.9
  101.9 28.5 %collective-permute-start.11 = (bf16[8,2,128,128]{3,2,1,0:T(8,128)(2,1)}, bf16[8,2,128,128]{3,2,1,0:T(8,128)(2,1)}, u32[]{:S(2)}, u32[]{:S(2)}) collective-permute-start(bf16[8,2,128,128]{3,2,1,0:T(8,128)(2,1)} %get-tuple-element.57), channel_id=1, source_target_pairs={{0,8},{8,0},{1,9},{9,1},{2,10},{10,2},{3,11},{11,3},{4,12},{12,4},... | collective-permute-start | bytes 1572872 | tf_op jit(solution)/shard_map/ppermute | solution.py:308
  102.0 32.5 %collective-permute-start.5 = (bf16[32,128,128]{2,1,0:T(8,128)(2,1)S(1)}, bf16[32,128,128]{2,1,0:T(8,128)(2,1)}, u32[]{:S(2)}, u32[]{:S(2)}) collective-permute-start(bf16[32,128,128]{2,1,0:T(8,128)(2,1)S(1)} %copy-done.9), channel_id=1, source_target_pairs={{0,48},{16,0},{32,16},{48,32},{1,49},{17,1},{33,17},{49,33},{2,50}... | collective-permute-start | bytes 3145736 | tf_op jit(solution)/shard_map/ppermute | solution.py:292
  105.4 29.2 %collective-permute-start.4 = (bf16[32,128,128]{2,1,0:T(8,128)(2,1)S(1)}, bf16[32,128,128]{2,1,0:T(8,128)(2,1)}, u32[]{:S(2)}, u32[]{:S(2)}) collective-permute-start(bf16[32,128,128]{2,1,0:T(8,128)(2,1)S(1)} %copy-done.9), channel_id=1, source_target_pairs={{0,16},{16,32},{32,48},{48,0},{1,17},{17,33},{33,49},{49,1},{2,18}... | collective-permute-start | bytes 3145736 | tf_op jit(solution)/shard_map/ppermute | solution.py:292
  128.4 4.1 %collective-permute-start.10 = (bf16[8,2,128,128]{3,2,1,0:T(8,128)(2,1)}, bf16[8,2,128,128]{3,2,1,0:T(8,128)(2,1)}, u32[]{:S(2)}, u32[]{:S(2)}) collective-permute-start(bf16[8,2,128,128]{3,2,1,0:T(8,128)(2,1)} %get-tuple-element.58), channel_id=1, source_target_pairs={{0,8},{8,0},{1,9},{9,1},{2,10},{10,2},{3,11},{11,3},{4,12},{12,4},... | collective-permute-start | bytes 1572872 | tf_op jit(solution)/shard_map/ppermute | solution.py:308
  129.5 3.1 %copy-start.10 = (bf16[8,2,128,128]{3,2,1,0:T(8,128)(2,1)S(1)}, bf16[8,2,128,128]{3,2,1,0:T(8,128)(2,1)}, u32[]{:S(2)}) copy-start(bf16[8,2,128,128]{3,2,1,0:T(8,128)(2,1)} %get-tuple-element.43) | copy-start | bytes 1572868
  130.3 35.1 %collective-permute-start.9 = (bf16[8,2,128,128]{3,2,1,0:T(8,128)(2,1)}, bf16[8,2,128,128]{3,2,1,0:T(8,128)(2,1)}, u32[]{:S(2)}, u32[]{:S(2)}) collective-permute-start(bf16[8,2,128,128]{3,2,1,0:T(8,128)(2,1)} %get-tuple-element.59), channel_id=1, source_target_pairs={{0,8},{8,0},{1,9},{9,1},{2,10},{10,2},{3,11},{11,3},{4,12},{12,4},... | collective-permute-start | bytes 1572872 | tf_op jit(solution)/shard_map/ppermute | solution.py:308
  134.6 30.8 %collective-permute-start.12 = (bf16[8,2,128,128]{3,2,1,0:T(8,128)(2,1)}, bf16[8,2,128,128]{3,2,1,0:T(8,128)(2,1)S(1)}, u32[]{:S(2)}, u32[]{:S(2)}) collective-permute-start(bf16[8,2,128,128]{3,2,1,0:T(8,128)(2,1)} %add_convert_fusion.1), channel_id=1, source_target_pairs={{0,112},{16,0},{32,16},{48,32},{64,48},{80,64},{96,80},{112,96},{1... | collective-permute-start | bytes 1572872 | tf_op jit(solution)/shard_map/ppermute | solution.py:292
  136.1 29.3 %collective-permute-start.13 = (bf16[8,2,128,128]{3,2,1,0:T(8,128)(2,1)}, bf16[8,2,128,128]{3,2,1,0:T(8,128)(2,1)S(1)}, u32[]{:S(2)}, u32[]{:S(2)}) collective-permute-start(bf16[8,2,128,128]{3,2,1,0:T(8,128)(2,1)} %add_convert_fusion), channel_id=1, source_target_pairs={{0,16},{16,32},{32,48},{48,64},{64,80},{80,96},{96,112},{112,0},{1... | collective-permute-start | bytes 1572872 | tf_op jit(solution)/shard_map/ppermute | solution.py:292
  136.6 1.3 copy-start.4
  161.8 44.7 %collective-permute-start.14 = (bf16[16,2,128,128]{3,2,1,0:T(8,128)(2,1)}, bf16[16,2,128,128]{3,2,1,0:T(8,128)(2,1)S(1)}, u32[]{:S(2)}, u32[]{:S(2)}) collective-permute-start(bf16[16,2,128,128]{3,2,1,0:T(8,128)(2,1)} %get-tuple-element.49), channel_id=1, source_target_pairs={{0,48},{16,0},{32,16},{48,32},{1,49},{17,1},{33,17},{49,33},{2,50}... | collective-permute-start | bytes 3145736 | tf_op jit(solution)/shard_map/ppermute | solution.py:292
  165.3 41.2 %collective-permute-start.15 = (bf16[16,2,128,128]{3,2,1,0:T(8,128)(2,1)}, bf16[16,2,128,128]{3,2,1,0:T(8,128)(2,1)S(1)}, u32[]{:S(2)}, u32[]{:S(2)}) collective-permute-start(bf16[16,2,128,128]{3,2,1,0:T(8,128)(2,1)} %get-tuple-element.50), channel_id=1, source_target_pairs={{0,16},{16,32},{32,48},{48,0},{1,17},{17,33},{33,49},{49,1},{2,18}... | collective-permute-start | bytes 3145736 | tf_op jit(solution)/shard_map/ppermute | solution.py:292
  165.3 0.8 copy-start.14
  165.4 1.0 copy-start.15
  168.8 37.6 %all-to-all-start.4 = ((bf16[8,3,128,128]{3,2,1,0:T(8,128)(2,1)}), bf16[8,3,128,128]{3,2,1,0:T(8,128)(2,1)S(1)}, u32[]{:S(2)}, u32[]{:S(2)}) async-start(bf16[8,3,128,128]{3,2,1,0:T(8,128)(2,1)} %total_grads.1), calls=%async_computation.4 | async-start | bytes 1572864 | tf_op jit(solution)/shard_map/all_to_all | solution.py:300
  177.8 26.6 %copy-start.13 = (bf16[16,128,128]{2,1,0:T(8,128)(2,1)S(1)}, bf16[16,128,128]{2,1,0:T(8,128)(2,1)}, u32[]{:S(2)}) copy-start(bf16[16,128,128]{2,1,0:T(8,128)(2,1)} %get-tuple-element.39) | copy-start | bytes 1572868
  202.0 26.2 %collective-permute-start.16 = (bf16[16,2,128,128]{3,2,1,0:T(8,128)(2,1)}, bf16[16,2,128,128]{3,2,1,0:T(8,128)(2,1)}, u32[]{:S(2)}, u32[]{:S(2)}) collective-permute-start(bf16[16,2,128,128]{3,2,1,0:T(8,128)(2,1)} %get-tuple-element.54), channel_id=1, source_target_pairs={{0,48},{16,0},{32,16},{48,32},{1,49},{17,1},{33,17},{49,33},{2,50}... | collective-permute-start | bytes 3145736 | tf_op jit(solution)/shard_map/ppermute | solution.py:292
  204.4 27.3 %collective-permute-start.17 = (bf16[16,2,128,128]{3,2,1,0:T(8,128)(2,1)}, bf16[16,2,128,128]{3,2,1,0:T(8,128)(2,1)}, u32[]{:S(2)}, u32[]{:S(2)}) collective-permute-start(bf16[16,2,128,128]{3,2,1,0:T(8,128)(2,1)} %get-tuple-element.55), channel_id=1, source_target_pairs={{0,16},{16,32},{32,48},{48,0},{1,17},{17,33},{33,49},{49,1},{2,18}... | collective-permute-start | bytes 3145736 | tf_op jit(solution)/shard_map/ppermute | solution.py:292
  206.5 30.2 %copy-start.2 = (bf16[8,3,128,128]{3,2,1,0:T(8,128)(2,1)}, bf16[8,3,128,128]{3,2,1,0:T(8,128)(2,1)S(1)}, u32[]{:S(2)}) copy-start(bf16[8,3,128,128]{3,2,1,0:T(8,128)(2,1)S(1)} %all-to-all-done.4.b_ref) | copy-start | bytes 2359300
  206.5 25.1 %copy-start.5 = (bf16[16,2,128,128]{3,2,1,0:T(8,128)(2,1)}, bf16[16,2,128,128]{3,2,1,0:T(8,128)(2,1)S(1)}, u32[]{:S(2)}) copy-start(bf16[16,2,128,128]{3,2,1,0:T(8,128)(2,1)S(1)} %collective-permute-done.14.right0) | copy-start | bytes 3145732
  206.5 1.0 copy-start.6
  207.5 29.1 %all-to-all-start.5 = ((bf16[32,128,128]{2,1,0:T(8,128)(2,1)}), bf16[32,128,128]{2,1,0:T(8,128)(2,1)S(1)}, u32[]{:S(2)}, u32[]{:S(2)}) async-start(bf16[32,128,128]{2,1,0:T(8,128)(2,1)} %pad_maximum_fusion), calls=%async_computation.5 | async-start | bytes 2097152 | tf_op jit(solution)/shard_map/all_to_all | solution.py:300
  236.6 37.5 %copy-start.1 = (bf16[32,128,128]{2,1,0:T(8,128)(2,1)}, bf16[32,128,128]{2,1,0:T(8,128)(2,1)S(1)}, u32[]{:S(2)}) copy-start(bf16[32,128,128]{2,1,0:T(8,128)(2,1)S(1)} %all-to-all-done.5) | copy-start | bytes 3145732

commit v7 on v6

--- a/solution.py
+++ b/solution.py
@@ -312,7 +312,8 @@
     half, x, core = (lax.axis_index(name) for name in ("half", "x", "core"))
     last, size = lax.axis_size("x") - 1, 2 * BPD
     packed = jnp.concatenate([key_blocks, block_count[:, :, None]], axis=2)
-    lists = lax.all_gather(packed[:4], ("half", "core"))
+    lists = lax.all_gather(packed, ("half", "core"))
+    list_b = lists[2 * half + core, 4]
     lists = lax.dynamic_index_in_dim(lists, 2 * half + core, 1, False)
     ka, va, qda, b = split_heads(key_in, value_in, query_in, out_grad)
 
@@ -338,17 +339,17 @@
 
         return fetch
 
-    ids, counts = plain(packed[4], half * (last + 1) + x)
-    place = after(jnp.stack([jnp.int32(0), core * BPD]), keys, lists)
+    ids, counts = plain(list_b, half * (last + 1) + x)
+    place = jnp.stack([jnp.int32(0), core * BPD])
     fetches = [run(i, other) for other in range(2) for i in range(3)]
     dq_b, (left_b, mine_b, right_b, give_b) = attention(
-        ids, counts, place, mine + theirs, fetches, own_b, BPD, size
+        ids, counts, place, mine + theirs, fetches, after(own_b, values, *key_near), BPD, size
     )
     got_b = [swap(give_b[i]) for i in range(3)]
     out_b = lax.optimization_barrier((add(left_b, got_b[0]), add(right_b, got_b[2]), *value_near))
     terms_b = [got_b[1], shift(out_b[0], CHIPS, -1), shift(out_b[1], CHIPS, 1)]
 
-    queries = exchange(after(qda, values, dq_b, *key_near), WIDE)
+    queries = exchange(after(qda, values), WIDE)
 
     def third(t, i):
         return lambda ref, place: [(ref.at[pl.ds(pl.multiple_of(place[1 + i], 8), size)], t, i * size)]

time: 280 us -> 310 us (1.11)
  waiting for transfers between devices: 37.1 us -> 72.5 us
  local copies, waits for them, and re-layouts: 11 us -> 7.84 us
    ppermute x12, waiting for transfers between devices: 13.9 us -> 55.5 us  [shift(): lax.ppermute(value, axes, [(s, (s + steps) % count) for s in range(count)])]
    all_to_all x5, waiting for transfers between devices: 22.1 us -> 15.9 us  [exchange(): return lax.all_to_all(x, axes, 0, 0, tiled=True)]
  transfers between devices with their start and end apart: 23 -> 23, of which waited for: 6 -> 10; matrix products, arithmetic and copies ran while one was open for 5% -> 4% of each run, Pallas kernels for 25% -> 23%
where the time goes in v7:
time: 310 us; the launch traced here: 309 us
  blocking collectives  85.9 us (28%)
  Pallas kernels  81.3 us (26%)
  waiting for transfers between devices  72.5 us (23%)
  starting transfers between devices  54.2 us (17%)
  local copies, waits for them, and re-layouts  7.84 us (3%)
  other arithmetic  5.94 us (2%)
    pallas_call x3, Pallas kernels, attention(): pl.pallas_call(functools.partial(attention_kernel, size, n_query, fetches...  63.6 us
    all_to_all x2, blocking collectives, exchange(): return lax.all_to_all(x, axes, 0, 0, tiled=True)  60.1 us
    ppermute x12, waiting for transfers between devices, shift(): lax.ppermute(value, axes, [(s, (s + steps) % count) for s in range(count)])  55.5 us
    all_to_all x5, starting transfers between devices, exchange(): return lax.all_to_all(x, axes, 0, 0, tiled=True)  36.8 us
    all_gather x1, blocking collectives, shards(): lists = lax.all_gather(packed, ('half', 'core'))  25.8 us
    ppermute x12, starting transfers between devices, shift(): lax.ppermute(value, axes, [(s, (s + steps) % count) for s in range(count)])  16 us
    all_to_all x5, waiting for transfers between devices, exchange(): return lax.all_to_all(x, axes, 0, 0, tiled=True)  15.9 us
  transfers between devices with their start and end apart: 23, of which 10 were waited for; matrix products, arithmetic and copies ran while one was open for 4% of the time, Pallas kernels for 23%

profile of v7, /device:TPU:8, one launch (start us, length us, event | category | flops | bytes accessed | tf_op | source)
XLA Modules:
  0.0 308.6 jit_solution(12792101392052719400)
XLA Ops:
  0.6 5.5 %split_heads.1 = (bf16[4,8,128,128]{3,2,1,0:T(8,128)(2,1)}, bf16[4,8,128,128]{3,2,1,0:T(8,128)(2,1)}, bf16[4,8,2,128,128]{4,3,2,1,0:T(8,128)(2,1)}, bf16[8,4,128,128]{3,2,1,0:T(8,128)(2,1)}) custom-call(bf16[128,5120]{1,0:T(8,128)(2,1)} %k_ref.1, bf16[128,5120]{1,0:T(8,128)(2,1)} %v_ref.1, bf16[128,5120]{1,0:T(8,128)(2,1)} %q_ref.1, bf16[128,5120]{1,0:T(8,128)(2,1)} %g_ref.1), custom_call_target="tpu_custom_call" | custom-call | bytes 10485760 | tf_op jit(solution)/shard_map/split_heads/pallas_call | solution.py:190
  6.1 24.4 %all_to_all.35.refs_6_ = bf16[8,4,128,128]{3,2,1,0:T(8,128)(2,1)S(1)} all-to-all(bf16[8,4,128,128]{3,2,1,0:T(8,128)(2,1)} %get-tuple-element.31), channel_id=1, replica_groups=mesh['half'=2,'x'=4,'core'=2,'group'=8] {'group'}, dimensions={0} | all-to-all | bytes 2097152 | tf_op jit(solution)/shard_map/all_to_all | solution.py:300
  30.5 4.7 %all-to-all-start.1 = ((bf16[32,128,128]{2,1,0:T(8,128)(2,1)}), bf16[32,128,128]{2,1,0:T(8,128)(2,1)S(1)}, u32[]{:S(2)}, u32[]{:S(2)}) async-start(bf16[32,128,128]{2,1,0:T(8,128)(2,1)} %bitcast.6), calls=%async_computation.1 | async-start | bytes 2097152 | tf_op jit(solution)/shard_map/all_to_all | solution.py:300
  35.2 3.8 %collective-permute-start.3 = (bf16[8,2,128,128]{3,2,1,0:T(8,128)(2,1)S(1)}, bf16[8,2,128,128]{3,2,1,0:T(8,128)(2,1)S(1)}, u32[]{:S(2)}, u32[]{:S(2)}) collective-permute-start(bf16[8,2,128,128]{3,2,1,0:T(8,128)(2,1)S(1)} %slice.52.refs_1_), channel_id=1, source_target_pairs={{0,112},{16,0},{32,16},{48,32},{64,48},{80,64},{96,80},{112,96},{1... | collective-permute-start | bytes 1572872 | tf_op jit(solution)/shard_map/ppermute | solution.py:292
  39.1 18.0 %collective-permute-done.3.refs_2_ = bf16[8,2,128,128]{3,2,1,0:T(8,128)(2,1)S(1)} collective-permute-done((bf16[8,2,128,128]{3,2,1,0:T(8,128)(2,1)S(1)}, bf16[8,2,128,128]{3,2,1,0:T(8,128)(2,1)S(1)}, u32[]{:S(2)}, u32[]{:S(2)}) %collective-permute-start.3) | collective-permute-done | bytes 524320 | tf_op jit(solution)/shard_map/ppermute | solution.py:292
  57.0 2.5 collective-permute-done.2.refs_0_
  59.6 1.6 all-to-all-done.1.refs_1_
  61.2 7.0 %all-to-all-start.2 = ((bf16[32,128,128]{2,1,0:T(8,128)(2,1)}), bf16[32,128,128]{2,1,0:T(8,128)(2,1)S(1)}, u32[]{:S(2)}, u32[]{:S(2)}) async-start(bf16[32,128,128]{2,1,0:T(8,128)(2,1)} %bitcast.31), calls=%async_computation.2 | async-start | bytes 2097152 | tf_op jit(solution)/shard_map/all_to_all | solution.py:300
  68.2 2.4 collective-permute-start.1
  70.6 14.3 %all-to-all-done.2.refs_4_ = bf16[32,128,128]{2,1,0:T(8,128)(2,1)S(1)} async-done(((bf16[32,128,128]{2,1,0:T(8,128)(2,1)}), bf16[32,128,128]{2,1,0:T(8,128)(2,1)S(1)}, u32[]{:S(2)}, u32[]{:S(2)}) %all-to-all-start.2) | async-done | bytes 1048608 | tf_op jit(solution)/shard_map/all_to_all | solution.py:300
  84.9 5.8 %all-to-all-start.3 = ((bf16[32,2,128,128]{3,2,1,0:T(8,128)(2,1)}), bf16[32,2,128,128]{3,2,1,0:T(8,128)(2,1)}, u32[]{:S(2)}, u32[]{:S(2)}) async-start(bf16[32,2,128,128]{3,2,1,0:T(8,128)(2,1)} %bitcast.8), calls=%async_computation.3 | async-start | bytes 4194304 | tf_op jit(solution)/shard_map/all_to_all | solution.py:300
  90.7 0.1 copy.15
  90.8 0.1 pad_add_fusion
  90.9 25.8 %all-gather = s32[20,8,13]{2,1,0:T(8,128)S(1)} all-gather(s32[5,8,13]{2,1,0:T(8,128)S(1)} %pad_add_fusion), channel_id=2, replica_groups=mesh['half'=2,'x'=4,'core'=2,'group'=8] {'half','core'}, dimensions={0}, use_global_device_ids=true | all-gather | bytes 10400 | tf_op jit(solution)/shard_map/all_gather | solution.py:315
  116.7 0.3 collective-permute-start.7
  117.0 0.2 collective-permute-start.8
  117.2 0.3 collective-permute-start.6
  117.5 0.6 reshape.50.ids_ref
  118.1 0.6 pad_add_fusion.3.place_ref
  118.7 0.7 slice_reduce_fusion.cnt_ref
  119.4 0.0 collective-permute-done.7.refs_4_
  119.4 0.8 collective-permute-done.8.refs_5_
  120.2 0.2 collective-permute-done.6.refs_3_
  120.4 14.5 %attention.4 = (bf16[8,128,128]{2,1,0:T(8,128)(2,1)}, bf16[8,2,128,128]{3,2,1,0:T(8,128)(2,1)}, bf16[8,2,128,128]{3,2,1,0:T(8,128)(2,1)}, bf16[8,2,128,128]{3,2,1,0:T(8,128)(2,1)}, bf16[3,8,2,128,128]{4,3,2,1,0:T(8,128)(2,1)}) custom-call(s32[96]{0:T(128)} %reshape.50.ids_ref, s32[8]{0:T(128)} %slice_reduce_fusion.cnt_ref, s32[2]{0:T(128)} %pad_add_fusion.3.place_ref, ...), custom_call_target="tpu_custom_call" | custom-call | tf_op jit(solution)/shard_map/attention/pallas_call | solution.py:139
  134.9 2.5 slice_bitcast_fusion
  137.4 0.0 collective-permute-start.11
  137.4 2.3 collective-permute-start.5
  139.8 0.1 collective-permute-start.10
  139.8 0.7 pad_add_fusion.1.place_ref
  140.5 0.1 slice.51
  140.6 0.7 copy.18
  141.3 0.7 reshape.44.ids_ref
  141.9 0.5 collective-permute-start.9
  142.4 0.0 collective-permute-done.11
  142.4 0.1 add_convert_fusion
  142.6 1.2 add_convert_fusion.1
  143.8 19.3 %collective-permute-done.5.refs_5_ = bf16[32,128,128]{2,1,0:T(8,128)(2,1)} collective-permute-done((bf16[32,128,128]{2,1,0:T(8,128)(2,1)S(1)}, bf16[32,128,128]{2,1,0:T(8,128)(2,1)}, u32[]{:S(2)}, u32[]{:S(2)}) %collective-permute-start.5) | collective-permute-done | bytes 1048608 | tf_op jit(solution)/shard_map/ppermute | solution.py:292
  163.1 2.8 collective-permute-done.4.refs_3_
  165.8 0.2 collective-permute-start.12
  166.1 1.8 collective-permute-start.13
  167.9 0.0 all-to-all-done.3.refs_6_
  167.9 25.3 %attention.3 = (bf16[16,128,128]{2,1,0:T(8,128)(2,1)}, bf16[16,2,128,128]{3,2,1,0:T(8,128)(2,1)}, bf16[16,2,128,128]{3,2,1,0:T(8,128)(2,1)}, bf16[16,2,128,128]{3,2,1,0:T(8,128)(2,1)}) custom-call(s32[192]{0:T(256)} %reshape.44.ids_ref, s32[16]{0:T(128)} %bitcast.35, s32[4]{0:T(128)} %pad_add_fusion.1.place_ref, ...), custom_call_target="tpu_custom_call" | custom-call | flops 2684354560 | bytes 7340032 | tf_op jit(solution)/shard_map/attention/pallas_call | solution.py:139
  193.2 0.9 collective-permute-start.14
  194.1 1.2 collective-permute-start.15
  195.3 2.5 total_grads.1
  197.8 10.8 %all-to-all-start.4 = ((bf16[8,3,128,128]{3,2,1,0:T(8,128)(2,1)}), bf16[8,3,128,128]{3,2,1,0:T(8,128)(2,1)S(1)}, u32[]{:S(2)}, u32[]{:S(2)}) async-start(bf16[8,3,128,128]{3,2,1,0:T(8,128)(2,1)} %total_grads.1), calls=%async_computation.4 | async-start | bytes 1572864 | tf_op jit(solution)/shard_map/all_to_all | solution.py:300
  208.6 0.1 slice.54
  208.7 0.6 copy.19
  209.3 0.7 reshape.49.ids_ref
  210.0 0.6 pad_add_fusion.2.place_ref
  210.5 23.8 %attention.5 = (bf16[16,128,128]{2,1,0:T(8,128)(2,1)}, bf16[16,2,128,128]{3,2,1,0:T(8,128)(2,1)}, bf16[16,2,128,128]{3,2,1,0:T(8,128)(2,1)}, bf16[16,2,128,128]{3,2,1,0:T(8,128)(2,1)}) custom-call(s32[192]{0:T(256)} %reshape.49.ids_ref, s32[16]{0:T(128)} %bitcast.36, s32[4]{0:T(128)} %pad_add_fusion.2.place_ref, ...), custom_call_target="tpu_custom_call" | custom-call | flops 2684354560 | bytes 7340032 | tf_op jit(solution)/shard_map/attention/pallas_call | solution.py:139
  234.4 2.9 collective-permute-start.16
  237.3 0.4 collective-permute-start.17
  237.7 2.1 pad_maximum_fusion
  239.8 0.0 collective-permute-done.14.right0
  239.8 0.0 copy-start.4
  239.8 1.0 copy-done.5
  240.8 8.7 %all-to-all-start.5 = ((bf16[32,128,128]{2,1,0:T(8,128)(2,1)}), bf16[32,128,128]{2,1,0:T(8,128)(2,1)S(1)}, u32[]{:S(2)}, u32[]{:S(2)}) async-start(bf16[32,128,128]{2,1,0:T(8,128)(2,1)} %pad_maximum_fusion), calls=%async_computation.5 | async-start | bytes 2097152 | tf_op jit(solution)/shard_map/all_to_all | solution.py:300
  249.5 0.7 pad_add_fusion.4.x_ref
  250.1 9.6 %collective-permute-done.16.right1 = bf16[16,2,128,128]{3,2,1,0:T(8,128)(2,1)} collective-permute-done((bf16[16,2,128,128]{3,2,1,0:T(8,128)(2,1)}, bf16[16,2,128,128]{3,2,1,0:T(8,128)(2,1)}, u32[]{:S(2)}, u32[]{:S(2)}) %collective-permute-start.16) | collective-permute-done | bytes 1048608 | tf_op jit(solution)/shard_map/ppermute | solution.py:292
  259.7 3.4 %collective-permute-done.17.left1 = bf16[16,2,128,128]{3,2,1,0:T(8,128)(2,1)} collective-permute-done((bf16[16,2,128,128]{3,2,1,0:T(8,128)(2,1)}, bf16[16,2,128,128]{3,2,1,0:T(8,128)(2,1)}, u32[]{:S(2)}, u32[]{:S(2)}) %collective-permute-start.17) | collective-permute-done | bytes 1048608 | tf_op jit(solution)/shard_map/ppermute | solution.py:292
  263.1 5.0 %both_halves.1 = bf16[2,16,2,128,128]{4,3,2,1,0:T(8,128)(2,1)} custom-call(s32[2]{0:T(128)} %pad_add_fusion.4.x_ref, bf16[16,2,128,128]{3,2,1,0:T(8,128)(2,1)} %get-tuple-element.52.own0, bf16[16,2,128,128]{3,2,1,0:T(8,128)(2,1)} %get-tuple-element.53.own1, bf16[16,2,128,128]{3,2,1,0:T(8,128)(2,1)} %copy-done.4, ...), custom_call_target="tpu_custom_call" | custom-call | bytes 8388608 | tf_op jit(solution)/shard_map/both_halves/pallas_call | solution.py:273
  268.1 35.8 %all_to_all.36 = bf16[32,2,128,128]{3,2,1,0:T(8,128)(2,1)} all-to-all(bf16[32,2,128,128]{3,2,1,0:T(8,128)(2,1)} %bitcast.29), channel_id=1, replica_groups=mesh['half'=2,'x'=4,'core'=2,'group'=8] {'half','core','group'}, dimensions={0} | all-to-all | bytes 4194304 | tf_op jit(solution)/shard_map/all_to_all | solution.py:300
  303.9 4.7 %join_heads.1 = (bf16[128,5120]{1,0:T(8,128)(2,1)}, bf16[128,5120]{1,0:T(8,128)(2,1)}, bf16[128,5120]{1,0:T(8,128)(2,1)}) custom-call(bf16[4,8,128,128]{3,2,1,0:T(8,128)(2,1)} %bitcast.30, bf16[4,8,2,128,128]{4,3,2,1,0:T(8,128)(2,1)} %bitcast.28, bf16[8,3,128,128]{3,2,1,0:T(8,128)(2,1)} %copy-done.2), custom_call_target="tpu_custom_call" | custom-call | bytes 7864320 | tf_op jit(solution)/shard_map/join_heads/pallas_call | solution.py:218
  (43 shorter events, 0.1 us)
Async XLA Ops:
  30.5 4.7 %copy-start = (bf16[8,4,128,128]{3,2,1,0:T(8,128)(2,1)}, bf16[8,4,128,128]{3,2,1,0:T(8,128)(2,1)S(1)}, u32[]{:S(2)}) copy-start(bf16[8,4,128,128]{3,2,1,0:T(8,128)(2,1)S(1)} %all_to_all.35.refs_6_) | copy-start | bytes 3145732
  30.5 30.7 %all-to-all-start.1 = ((bf16[32,128,128]{2,1,0:T(8,128)(2,1)}), bf16[32,128,128]{2,1,0:T(8,128)(2,1)S(1)}, u32[]{:S(2)}, u32[]{:S(2)}) async-start(bf16[32,128,128]{2,1,0:T(8,128)(2,1)} %bitcast.6), calls=%async_computation.1 | async-start | bytes 2097152 | tf_op jit(solution)/shard_map/all_to_all | solution.py:300
  35.2 81.4 %copy-start.3 = (bf16[8,2,128,128]{3,2,1,0:T(8,128)(2,1)}, bf16[8,2,128,128]{3,2,1,0:T(8,128)(2,1)S(1)}, u32[]{:S(2)}) copy-start(bf16[8,2,128,128]{3,2,1,0:T(8,128)(2,1)S(1)} %slice.52.refs_1_) | copy-start | bytes 1572868
  35.2 21.8 %collective-permute-start.3 = (bf16[8,2,128,128]{3,2,1,0:T(8,128)(2,1)S(1)}, bf16[8,2,128,128]{3,2,1,0:T(8,128)(2,1)S(1)}, u32[]{:S(2)}, u32[]{:S(2)}) collective-permute-start(bf16[8,2,128,128]{3,2,1,0:T(8,128)(2,1)S(1)} %slice.52.refs_1_), channel_id=1, source_target_pairs={{0,112},{16,0},{32,16},{48,32},{64,48},{80,64},{96,80},{112,96},{1... | collective-permute-start | bytes 1572872 | tf_op jit(solution)/shard_map/ppermute | solution.py:292
  39.0 20.5 %collective-permute-start.2 = (bf16[8,2,128,128]{3,2,1,0:T(8,128)(2,1)S(1)}, bf16[8,2,128,128]{3,2,1,0:T(8,128)(2,1)}, u32[]{:S(2)}, u32[]{:S(2)}) collective-permute-start(bf16[8,2,128,128]{3,2,1,0:T(8,128)(2,1)S(1)} %slice.52.refs_1_), channel_id=1, source_target_pairs={{0,16},{16,32},{32,48},{48,64},{64,80},{80,96},{96,112},{112,0},{1... | collective-permute-start | bytes 1572872 | tf_op jit(solution)/shard_map/ppermute | solution.py:292
  57.0 60.0 %copy-start.8 = (bf16[8,2,128,128]{3,2,1,0:T(8,128)(2,1)}, bf16[8,2,128,128]{3,2,1,0:T(8,128)(2,1)S(1)}, u32[]{:S(2)}) copy-start(bf16[8,2,128,128]{3,2,1,0:T(8,128)(2,1)S(1)} %collective-permute-done.3.refs_2_) | copy-start | bytes 1572868
  61.2 23.7 %copy-start.6 = (bf16[32,128,128]{2,1,0:T(8,128)(2,1)}, bf16[32,128,128]{2,1,0:T(8,128)(2,1)S(1)}, u32[]{:S(2)}) copy-start(bf16[32,128,128]{2,1,0:T(8,128)(2,1)S(1)} %all-to-all-done.1.refs_1_) | copy-start | bytes 3145732
  61.2 23.7 %all-to-all-start.2 = ((bf16[32,128,128]{2,1,0:T(8,128)(2,1)}), bf16[32,128,128]{2,1,0:T(8,128)(2,1)S(1)}, u32[]{:S(2)}, u32[]{:S(2)}) async-start(bf16[32,128,128]{2,1,0:T(8,128)(2,1)} %bitcast.31), calls=%async_computation.2 | async-start | bytes 2097152 | tf_op jit(solution)/shard_map/all_to_all | solution.py:300
  68.2 51.2 %collective-permute-start.1 = (bf16[32,128,128]{2,1,0:T(8,128)(2,1)S(1)}, bf16[32,128,128]{2,1,0:T(8,128)(2,1)}, u32[]{:S(2)}, u32[]{:S(2)}) collective-permute-start(bf16[32,128,128]{2,1,0:T(8,128)(2,1)S(1)} %all-to-all-done.1.refs_1_), channel_id=1, source_target_pairs={{0,48},{16,0},{32,16},{48,32},{1,49},{17,1},{33,17},{49,33},{2,50}... | collective-permute-start | bytes 3145736 | tf_op jit(solution)/shard_map/ppermute | solution.py:292
  70.6 48.8 %collective-permute-start = (bf16[32,128,128]{2,1,0:T(8,128)(2,1)S(1)}, bf16[32,128,128]{2,1,0:T(8,128)(2,1)}, u32[]{:S(2)}, u32[]{:S(2)}) collective-permute-start(bf16[32,128,128]{2,1,0:T(8,128)(2,1)S(1)} %all-to-all-done.1.refs_1_), channel_id=1, source_target_pairs={{0,16},{16,32},{32,48},{48,0},{1,17},{17,33},{33,49},{49,1},{2,18}... | collective-permute-start | bytes 3145736 | tf_op jit(solution)/shard_map/ppermute | solution.py:292
  84.9 54.9 %copy-start.7 = (bf16[32,128,128]{2,1,0:T(8,128)(2,1)}, bf16[32,128,128]{2,1,0:T(8,128)(2,1)S(1)}, u32[]{:S(2)}) copy-start(bf16[32,128,128]{2,1,0:T(8,128)(2,1)S(1)} %all-to-all-done.2.refs_4_) | copy-start | bytes 3145732
  84.9 5.8 %copy-start.13 = (s32[5,8]{1,0:T(8,128)S(1)}, s32[5,8]{1,0:T(8,128)}, u32[]{:S(2)}) copy-start(s32[5,8]{1,0:T(8,128)} %param.11) | copy-start | bytes 484
  84.9 5.9 %copy-start.12 = (s32[5,8,12]{2,1,0:T(8,128)S(1)}, s32[5,8,12]{2,1,0:T(8,128)}, u32[]{:S(2)}) copy-start(s32[5,8,12]{2,1,0:T(8,128)} %param.10) | copy-start | bytes 5764
  84.9 83.0 %all-to-all-start.3 = ((bf16[32,2,128,128]{3,2,1,0:T(8,128)(2,1)}), bf16[32,2,128,128]{3,2,1,0:T(8,128)(2,1)}, u32[]{:S(2)}, u32[]{:S(2)}) async-start(bf16[32,2,128,128]{3,2,1,0:T(8,128)(2,1)} %bitcast.8), calls=%async_computation.3 | async-start | bytes 4194304 | tf_op jit(solution)/shard_map/all_to_all | solution.py:300
  116.7 2.7 collective-permute-start.7
  117.0 3.2 %collective-permute-start.8 = (bf16[8,2,128,128]{3,2,1,0:T(8,128)(2,1)S(1)}, bf16[8,2,128,128]{3,2,1,0:T(8,128)(2,1)}, u32[]{:S(2)}, u32[]{:S(2)}) collective-permute-start(bf16[8,2,128,128]{3,2,1,0:T(8,128)(2,1)S(1)} %collective-permute-done.3.refs_2_), channel_id=1, source_target_pairs={{0,8},{8,0},{1,9},{9,1},{2,10},{10,2},{3,11},{11,3},{4,12},{12,4},... | collective-permute-start | bytes 1572872 | tf_op jit(solution)/shard_map/ppermute | solution.py:308
  117.2 3.2 %collective-permute-start.6 = (bf16[8,2,128,128]{3,2,1,0:T(8,128)(2,1)}, bf16[8,2,128,128]{3,2,1,0:T(8,128)(2,1)}, u32[]{:S(2)}, u32[]{:S(2)}) collective-permute-start(bf16[8,2,128,128]{3,2,1,0:T(8,128)(2,1)} %collective-permute-done.2.refs_0_), channel_id=1, source_target_pairs={{0,8},{8,0},{1,9},{9,1},{2,10},{10,2},{3,11},{11,3},{4,12},{12,4},... | collective-permute-start | bytes 1572872 | tf_op jit(solution)/shard_map/ppermute | solution.py:308
  134.9 7.6 %copy-start.10 = (bf16[8,2,128,128]{3,2,1,0:T(8,128)(2,1)S(1)}, bf16[8,2,128,128]{3,2,1,0:T(8,128)(2,1)}, u32[]{:S(2)}) copy-start(bf16[8,2,128,128]{3,2,1,0:T(8,128)(2,1)} %get-tuple-element.44) | copy-start | bytes 1572868
  137.4 5.2 %copy-start.9 = (bf16[8,2,128,128]{3,2,1,0:T(8,128)(2,1)S(1)}, bf16[8,2,128,128]{3,2,1,0:T(8,128)(2,1)}, u32[]{:S(2)}) copy-start(bf16[8,2,128,128]{3,2,1,0:T(8,128)(2,1)} %get-tuple-element.43) | copy-start | bytes 1572868
  137.4 5.0 %collective-permute-start.11 = (bf16[8,2,128,128]{3,2,1,0:T(8,128)(2,1)S(1)}, bf16[8,2,128,128]{3,2,1,0:T(8,128)(2,1)S(1)}, u32[]{:S(2)}, u32[]{:S(2)}) collective-permute-start(bf16[8,2,128,128]{3,2,1,0:T(8,128)(2,1)S(1)} %get-tuple-element.57), channel_id=1, source_target_pairs={{0,8},{8,0},{1,9},{9,1},{2,10},{10,2},{3,11},{11,3},{4,12},{12,4},... | collective-permute-start | bytes 1572872 | tf_op jit(solution)/shard_map/ppermute | solution.py:308
  137.4 25.7 %collective-permute-start.5 = (bf16[32,128,128]{2,1,0:T(8,128)(2,1)S(1)}, bf16[32,128,128]{2,1,0:T(8,128)(2,1)}, u32[]{:S(2)}, u32[]{:S(2)}) collective-permute-start(bf16[32,128,128]{2,1,0:T(8,128)(2,1)S(1)} %all-to-all-done.2.refs_4_), channel_id=1, source_target_pairs={{0,48},{16,0},{32,16},{48,32},{1,49},{17,1},{33,17},{49,33},{2,50}... | collective-permute-start | bytes 3145736 | tf_op jit(solution)/shard_map/ppermute | solution.py:292
  139.7 26.1 %collective-permute-start.4 = (bf16[32,128,128]{2,1,0:T(8,128)(2,1)S(1)}, bf16[32,128,128]{2,1,0:T(8,128)(2,1)}, u32[]{:S(2)}, u32[]{:S(2)}) collective-permute-start(bf16[32,128,128]{2,1,0:T(8,128)(2,1)S(1)} %all-to-all-done.2.refs_4_), channel_id=1, source_target_pairs={{0,16},{16,32},{32,48},{48,0},{1,17},{17,33},{33,49},{49,1},{2,18}... | collective-permute-start | bytes 3145736 | tf_op jit(solution)/shard_map/ppermute | solution.py:292
  139.8 2.8 collective-permute-start.10
  141.9 53.4 %collective-permute-start.9 = (bf16[8,2,128,128]{3,2,1,0:T(8,128)(2,1)}, bf16[8,2,128,128]{3,2,1,0:T(8,128)(2,1)}, u32[]{:S(2)}, u32[]{:S(2)}) collective-permute-start(bf16[8,2,128,128]{3,2,1,0:T(8,128)(2,1)} %get-tuple-element.59), channel_id=1, source_target_pairs={{0,8},{8,0},{1,9},{9,1},{2,10},{10,2},{3,11},{11,3},{4,12},{12,4},... | collective-permute-start | bytes 1572872 | tf_op jit(solution)/shard_map/ppermute | solution.py:308
  165.8 29.5 %collective-permute-start.12 = (bf16[8,2,128,128]{3,2,1,0:T(8,128)(2,1)S(1)}, bf16[8,2,128,128]{3,2,1,0:T(8,128)(2,1)}, u32[]{:S(2)}, u32[]{:S(2)}) collective-permute-start(bf16[8,2,128,128]{3,2,1,0:T(8,128)(2,1)S(1)} %add_convert_fusion.1), channel_id=1, source_target_pairs={{0,112},{16,0},{32,16},{48,32},{64,48},{80,64},{96,80},{112,96},{1... | collective-permute-start | bytes 1572872 | tf_op jit(solution)/shard_map/ppermute | solution.py:292
  166.1 29.2 %collective-permute-start.13 = (bf16[8,2,128,128]{3,2,1,0:T(8,128)(2,1)S(1)}, bf16[8,2,128,128]{3,2,1,0:T(8,128)(2,1)}, u32[]{:S(2)}, u32[]{:S(2)}) collective-permute-start(bf16[8,2,128,128]{3,2,1,0:T(8,128)(2,1)S(1)} %add_convert_fusion), channel_id=1, source_target_pairs={{0,16},{16,32},{32,48},{48,64},{64,80},{80,96},{96,112},{112,0},{1... | collective-permute-start | bytes 1572872 | tf_op jit(solution)/shard_map/ppermute | solution.py:292
  193.2 46.6 %collective-permute-start.14 = (bf16[16,2,128,128]{3,2,1,0:T(8,128)(2,1)}, bf16[16,2,128,128]{3,2,1,0:T(8,128)(2,1)S(1)}, u32[]{:S(2)}, u32[]{:S(2)}) collective-permute-start(bf16[16,2,128,128]{3,2,1,0:T(8,128)(2,1)} %get-tuple-element.49), channel_id=1, source_target_pairs={{0,48},{16,0},{32,16},{48,32},{1,49},{17,1},{33,17},{49,33},{2,50}... | collective-permute-start | bytes 3145736 | tf_op jit(solution)/shard_map/ppermute | solution.py:292
  194.1 45.7 %collective-permute-start.15 = (bf16[16,2,128,128]{3,2,1,0:T(8,128)(2,1)}, bf16[16,2,128,128]{3,2,1,0:T(8,128)(2,1)S(1)}, u32[]{:S(2)}, u32[]{:S(2)}) collective-permute-start(bf16[16,2,128,128]{3,2,1,0:T(8,128)(2,1)} %get-tuple-element.50), channel_id=1, source_target_pairs={{0,16},{16,32},{32,48},{48,0},{1,17},{17,33},{33,49},{49,1},{2,18}... | collective-permute-start | bytes 3145736 | tf_op jit(solution)/shard_map/ppermute | solution.py:292
  197.8 41.9 %all-to-all-start.4 = ((bf16[8,3,128,128]{3,2,1,0:T(8,128)(2,1)}), bf16[8,3,128,128]{3,2,1,0:T(8,128)(2,1)S(1)}, u32[]{:S(2)}, u32[]{:S(2)}) async-start(bf16[8,3,128,128]{3,2,1,0:T(8,128)(2,1)} %total_grads.1), calls=%async_computation.4 | async-start | bytes 1572864 | tf_op jit(solution)/shard_map/all_to_all | solution.py:300
  210.5 27.1 %copy-start.11 = (bf16[16,128,128]{2,1,0:T(8,128)(2,1)S(1)}, bf16[16,128,128]{2,1,0:T(8,128)(2,1)}, u32[]{:S(2)}) copy-start(bf16[16,128,128]{2,1,0:T(8,128)(2,1)} %get-tuple-element.37) | copy-start | bytes 1572868
  234.4 25.3 %collective-permute-start.16 = (bf16[16,2,128,128]{3,2,1,0:T(8,128)(2,1)}, bf16[16,2,128,128]{3,2,1,0:T(8,128)(2,1)}, u32[]{:S(2)}, u32[]{:S(2)}) collective-permute-start(bf16[16,2,128,128]{3,2,1,0:T(8,128)(2,1)} %get-tuple-element.54), channel_id=1, source_target_pairs={{0,48},{16,0},{32,16},{48,32},{1,49},{17,1},{33,17},{49,33},{2,50}... | collective-permute-start | bytes 3145736 | tf_op jit(solution)/shard_map/ppermute | solution.py:292
  237.3 25.8 %collective-permute-start.17 = (bf16[16,2,128,128]{3,2,1,0:T(8,128)(2,1)}, bf16[16,2,128,128]{3,2,1,0:T(8,128)(2,1)}, u32[]{:S(2)}, u32[]{:S(2)}) collective-permute-start(bf16[16,2,128,128]{3,2,1,0:T(8,128)(2,1)} %get-tuple-element.55), channel_id=1, source_target_pairs={{0,16},{16,32},{32,48},{48,0},{1,17},{17,33},{33,49},{49,1},{2,18}... | collective-permute-start | bytes 3145736 | tf_op jit(solution)/shard_map/ppermute | solution.py:292
  239.8 28.4 %copy-start.2 = (bf16[8,3,128,128]{3,2,1,0:T(8,128)(2,1)}, bf16[8,3,128,128]{3,2,1,0:T(8,128)(2,1)S(1)}, u32[]{:S(2)}) copy-start(bf16[8,3,128,128]{3,2,1,0:T(8,128)(2,1)S(1)} %all-to-all-done.4.b_ref) | copy-start | bytes 2359300
  239.8 23.3 %copy-start.4 = (bf16[16,2,128,128]{3,2,1,0:T(8,128)(2,1)}, bf16[16,2,128,128]{3,2,1,0:T(8,128)(2,1)S(1)}, u32[]{:S(2)}) copy-start(bf16[16,2,128,128]{3,2,1,0:T(8,128)(2,1)S(1)} %collective-permute-done.14.right0) | copy-start | bytes 3145732
  239.8 1.0 copy-start.5
  240.8 27.3 %all-to-all-start.5 = ((bf16[32,128,128]{2,1,0:T(8,128)(2,1)}), bf16[32,128,128]{2,1,0:T(8,128)(2,1)S(1)}, u32[]{:S(2)}, u32[]{:S(2)}) async-start(bf16[32,128,128]{2,1,0:T(8,128)(2,1)} %pad_maximum_fusion), calls=%async_computation.5 | async-start | bytes 2097152 | tf_op jit(solution)/shard_map/all_to_all | solution.py:300
  268.1 35.8 %copy-start.1 = (bf16[32,128,128]{2,1,0:T(8,128)(2,1)}, bf16[32,128,128]{2,1,0:T(8,128)(2,1)S(1)}, u32[]{:S(2)}) copy-start(bf16[32,128,128]{2,1,0:T(8,128)(2,1)S(1)} %all-to-all-done.5) | copy-start | bytes 3145732

commit v8 on v7

--- a/solution.py
+++ b/solution.py
@@ -312,9 +312,9 @@
     half, x, core = (lax.axis_index(name) for name in ("half", "x", "core"))
     last, size = lax.axis_size("x") - 1, 2 * BPD
     packed = jnp.concatenate([key_blocks, block_count[:, :, None]], axis=2)
-    lists = lax.all_gather(packed, ("half", "core"))
-    list_b = lists[2 * half + core, 4]
-    lists = lax.dynamic_index_in_dim(lists, 2 * half + core, 1, False)
+    gathered = lax.all_gather(packed, ("half", "core"))
+    list_b = gathered[2 * half + core, 4]
+    lists = lax.dynamic_index_in_dim(gathered, 2 * half + core, 1, False)
     ka, va, qda, b = split_heads(key_in, value_in, query_in, out_grad)
 
     def plain(lists, chip):
@@ -322,7 +322,7 @@
         first_block = (chip - 1) * 2 * BPD
         return (lists[:, :MAXK] - first_block).reshape(-1), lists[:, MAXK]
 
-    own_b = exchange(b, "group")
+    own_b = exchange(after(b, gathered), "group")
     pairs_b = own_b[:, :2]
     mine = (shift(pairs_b, CHIPS, 1), pairs_b, shift(pairs_b, CHIPS, -1))
     theirs = tuple(swap(pairs) for pairs in mine)
@@ -345,8 +345,9 @@
     dq_b, (left_b, mine_b, right_b, give_b) = attention(
         ids, counts, place, mine + theirs, fetches, after(own_b, values, *key_near), BPD, size
     )
+    give_b = after(give_b, *value_near)
     got_b = [swap(give_b[i]) for i in range(3)]
-    out_b = lax.optimization_barrier((add(left_b, got_b[0]), add(right_b, got_b[2]), *value_near))
+    out_b = lax.optimization_barrier((add(left_b, got_b[0]), add(right_b, got_b[2])))
     terms_b = [got_b[1], shift(out_b[0], CHIPS, -1), shift(out_b[1], CHIPS, 1)]
 
     queries = exchange(after(qda, values), WIDE)

time: 310 us -> 274 us (0.88)
  blocking collectives: 85.9 us -> 68.2 us
  waiting for transfers between devices: 72.5 us -> 56.5 us
    all_gather x1, blocking collectives: 25.8 us -> 5.28 us  [shards(): gathered = lax.all_gather(packed, ('half', 'core'))]
    ppermute x12, waiting for transfers between devices: 55.5 us -> 40.3 us  [shift(): lax.ppermute(value, axes, [(s, (s + steps) % count) for s in range(count)])]
  transfers between devices with their start and end apart: 23 -> 23, of which waited for: 10 -> 11; matrix products, arithmetic and copies ran while one was open for 4% -> 4% of each run, Pallas kernels for 23% -> 25%
where the time goes in v8:
time: 274 us; the launch traced here: 272 us
  Pallas kernels  78.6 us (29%)
  blocking collectives  68.2 us (25%)
  waiting for transfers between devices  56.5 us (21%)
  starting transfers between devices  53.4 us (19%)
  local copies, waits for them, and re-layouts  8.99 us (3%)
  other arithmetic  5.77 us (2%)
    all_to_all x2, blocking collectives, exchange(): return lax.all_to_all(x, axes, 0, 0, tiled=True)  62.9 us
    pallas_call x3, Pallas kernels, attention(): pl.pallas_call(functools.partial(attention_kernel, size, n_query, fetches...  60.9 us
    ppermute x12, waiting for transfers between devices, shift(): lax.ppermute(value, axes, [(s, (s + steps) % count) for s in range(count)])  40.3 us
    all_to_all x5, starting transfers between devices, exchange(): return lax.all_to_all(x, axes, 0, 0, tiled=True)  34.1 us
    ppermute x12, starting transfers between devices, shift(): lax.ppermute(value, axes, [(s, (s + steps) % count) for s in range(count)])  18.4 us
    all_to_all x5, waiting for transfers between devices, exchange(): return lax.all_to_all(x, axes, 0, 0, tiled=True)  16 us
  transfers between devices with their start and end apart: 23, of which 11 were waited for; matrix products, arithmetic and copies ran while one was open for 4% of the time, Pallas kernels for 25%

profile of v8, /device:TPU:8, one launch (start us, length us, event | category | flops | bytes accessed | tf_op | source)
XLA Modules:
  0.0 272.3 jit_solution(9333255422214372327)
XLA Ops:
  0.6 0.8 copy.15
  1.4 0.8 pad_add_fusion
  2.2 5.3 %all-gather = s32[20,8,13]{2,1,0:T(8,128)S(1)} all-gather(s32[5,8,13]{2,1,0:T(8,128)S(1)} %pad_add_fusion), channel_id=2, replica_groups=mesh['half'=2,'x'=4,'core'=2,'group'=8] {'half','core'}, dimensions={0}, use_global_device_ids=true | all-gather | bytes 10400 | tf_op jit(solution)/shard_map/all_gather | solution.py:315
  7.5 5.5 %split_heads.1 = (bf16[4,8,128,128]{3,2,1,0:T(8,128)(2,1)}, bf16[4,8,128,128]{3,2,1,0:T(8,128)(2,1)}, bf16[4,8,2,128,128]{4,3,2,1,0:T(8,128)(2,1)}, bf16[8,4,128,128]{3,2,1,0:T(8,128)(2,1)}) custom-call(bf16[128,5120]{1,0:T(8,128)(2,1)} %k_ref.1, bf16[128,5120]{1,0:T(8,128)(2,1)} %v_ref.1, bf16[128,5120]{1,0:T(8,128)(2,1)} %q_ref.1, bf16[128,5120]{1,0:T(8,128)(2,1)} %g_ref.1), custom_call_target="tpu_custom_call" | custom-call | bytes 10485760 | tf_op jit(solution)/shard_map/split_heads/pallas_call | solution.py:190
  13.0 24.8 %all_to_all.35.refs_6_ = bf16[8,4,128,128]{3,2,1,0:T(8,128)(2,1)S(1)} all-to-all(bf16[8,4,128,128]{3,2,1,0:T(8,128)(2,1)} %get-tuple-element.34), channel_id=1, replica_groups=mesh['half'=2,'x'=4,'core'=2,'group'=8] {'group'}, dimensions={0} | all-to-all | bytes 2097152 | tf_op jit(solution)/shard_map/all_to_all | solution.py:300
  37.7 4.8 %all-to-all-start.1 = ((bf16[32,128,128]{2,1,0:T(8,128)(2,1)}), bf16[32,128,128]{2,1,0:T(8,128)(2,1)S(1)}, u32[]{:S(2)}, u32[]{:S(2)}) async-start(bf16[32,128,128]{2,1,0:T(8,128)(2,1)} %bitcast.32), calls=%async_computation.1 | async-start | bytes 2097152 | tf_op jit(solution)/shard_map/all_to_all | solution.py:300
  42.6 3.8 %collective-permute-start.3 = (bf16[8,2,128,128]{3,2,1,0:T(8,128)(2,1)S(1)}, bf16[8,2,128,128]{3,2,1,0:T(8,128)(2,1)S(1)}, u32[]{:S(2)}, u32[]{:S(2)}) collective-permute-start(bf16[8,2,128,128]{3,2,1,0:T(8,128)(2,1)S(1)} %slice.52.refs_1_), channel_id=1, source_target_pairs={{0,112},{16,0},{32,16},{48,32},{64,48},{80,64},{96,80},{112,96},{1... | collective-permute-start | bytes 1572872 | tf_op jit(solution)/shard_map/ppermute | solution.py:292
  46.4 0.0 collective-permute-start.2
  46.4 18.0 %collective-permute-done.3.refs_2_ = bf16[8,2,128,128]{3,2,1,0:T(8,128)(2,1)S(1)} collective-permute-done((bf16[8,2,128,128]{3,2,1,0:T(8,128)(2,1)S(1)}, bf16[8,2,128,128]{3,2,1,0:T(8,128)(2,1)S(1)}, u32[]{:S(2)}, u32[]{:S(2)}) %collective-permute-start.3) | collective-permute-done | bytes 524320 | tf_op jit(solution)/shard_map/ppermute | solution.py:292
  64.4 2.4 collective-permute-done.2.refs_0_
  66.8 1.7 all-to-all-done.1.refs_1_
  68.5 7.0 %all-to-all-start.2 = ((bf16[32,128,128]{2,1,0:T(8,128)(2,1)}), bf16[32,128,128]{2,1,0:T(8,128)(2,1)S(1)}, u32[]{:S(2)}, u32[]{:S(2)}) async-start(bf16[32,128,128]{2,1,0:T(8,128)(2,1)} %bitcast.31), calls=%async_computation.2 | async-start | bytes 2097152 | tf_op jit(solution)/shard_map/all_to_all | solution.py:300
  75.5 2.4 collective-permute-start.1
  77.9 14.3 %all-to-all-done.2.refs_4_ = bf16[32,128,128]{2,1,0:T(8,128)(2,1)S(1)} async-done(((bf16[32,128,128]{2,1,0:T(8,128)(2,1)}), bf16[32,128,128]{2,1,0:T(8,128)(2,1)S(1)}, u32[]{:S(2)}, u32[]{:S(2)}) %all-to-all-start.2) | async-done | bytes 1048608 | tf_op jit(solution)/shard_map/all_to_all | solution.py:300
  92.2 2.4 collective-permute-start.5
  94.6 5.6 %all-to-all-start.3 = ((bf16[32,2,128,128]{3,2,1,0:T(8,128)(2,1)}), bf16[32,2,128,128]{3,2,1,0:T(8,128)(2,1)}, u32[]{:S(2)}, u32[]{:S(2)}) async-start(bf16[32,2,128,128]{3,2,1,0:T(8,128)(2,1)} %bitcast.8), calls=%async_computation.3 | async-start | bytes 4194304 | tf_op jit(solution)/shard_map/all_to_all | solution.py:300
  100.3 0.2 collective-permute-start.7
  100.5 1.2 collective-permute-done.1.refs_2_
  101.7 3.6 %collective-permute-done.refs_0_ = bf16[32,128,128]{2,1,0:T(8,128)(2,1)} collective-permute-done((bf16[32,128,128]{2,1,0:T(8,128)(2,1)S(1)}, bf16[32,128,128]{2,1,0:T(8,128)(2,1)}, u32[]{:S(2)}, u32[]{:S(2)}) %collective-permute-start) | collective-permute-done | bytes 1048608 | tf_op jit(solution)/shard_map/ppermute | solution.py:292
  105.3 0.0 collective-permute-start.6
  105.3 0.6 reshape.50.ids_ref
  105.9 0.7 pad_add_fusion.3.place_ref
  106.6 0.7 slice_reduce_fusion.cnt_ref
  107.2 0.0 collective-permute-done.7.refs_4_
  107.3 0.0 collective-permute-done.8.refs_5_
  107.3 0.2 collective-permute-done.6.refs_3_
  107.4 0.8 copy-done.12
  108.2 14.9 %attention.4 = (bf16[8,128,128]{2,1,0:T(8,128)(2,1)}, bf16[8,2,128,128]{3,2,1,0:T(8,128)(2,1)}, bf16[8,2,128,128]{3,2,1,0:T(8,128)(2,1)}, bf16[8,2,128,128]{3,2,1,0:T(8,128)(2,1)}, bf16[3,8,2,128,128]{4,3,2,1,0:T(8,128)(2,1)}) custom-call(s32[96]{0:T(128)} %reshape.50.ids_ref, s32[8]{0:T(128)} %slice_reduce_fusion.cnt_ref, s32[2]{0:T(128)} %pad_add_fusion.3.place_ref, ...), custom_call_target="tpu_custom_call" | custom-call | tf_op jit(solution)/shard_map/attention/pallas_call | solution.py:139
  123.2 0.2 collective-permute-done.5.refs_5_
  123.4 3.3 %collective-permute-done.4.refs_3_ = bf16[32,128,128]{2,1,0:T(8,128)(2,1)} collective-permute-done((bf16[32,128,128]{2,1,0:T(8,128)(2,1)S(1)}, bf16[32,128,128]{2,1,0:T(8,128)(2,1)}, u32[]{:S(2)}, u32[]{:S(2)}) %collective-permute-start.4) | collective-permute-done | bytes 1048608 | tf_op jit(solution)/shard_map/ppermute | solution.py:292
  126.7 2.3 slice_bitcast_fusion
  129.0 0.0 collective-permute-start.11
  129.0 0.5 collective-permute-start.10
  129.5 0.7 pad_add_fusion.1.place_ref
  130.2 0.1 slice.51
  130.2 0.7 copy.18
  130.9 0.6 reshape.44.ids_ref
  131.5 0.1 collective-permute-start.9
  131.6 0.1 add_convert_fusion
  131.8 0.0 collective-permute-done.10
  131.8 0.1 add_convert_fusion.1
  131.9 1.3 collective-permute-start.12
  133.2 0.8 collective-permute-start.13
  134.0 22.9 %attention.3 = (bf16[16,128,128]{2,1,0:T(8,128)(2,1)}, bf16[16,2,128,128]{3,2,1,0:T(8,128)(2,1)}, bf16[16,2,128,128]{3,2,1,0:T(8,128)(2,1)}, bf16[16,2,128,128]{3,2,1,0:T(8,128)(2,1)}) custom-call(s32[192]{0:T(256)} %reshape.44.ids_ref, s32[16]{0:T(128)} %bitcast.36, s32[4]{0:T(128)} %pad_add_fusion.1.place_ref, ...), custom_call_target="tpu_custom_call" | custom-call | flops 2684354560 | bytes 7340032 | tf_op jit(solution)/shard_map/attention/pallas_call | solution.py:139
  157.0 4.4 %collective-permute-start.14 = (bf16[16,2,128,128]{3,2,1,0:T(8,128)(2,1)}, bf16[16,2,128,128]{3,2,1,0:T(8,128)(2,1)S(1)}, u32[]{:S(2)}, u32[]{:S(2)}) collective-permute-start(bf16[16,2,128,128]{3,2,1,0:T(8,128)(2,1)} %get-tuple-element.53), channel_id=1, source_target_pairs={{0,48},{16,0},{32,16},{48,32},{1,49},{17,1},{33,17},{49,33},{2,50}... | collective-permute-start | bytes 3145736 | tf_op jit(solution)/shard_map/ppermute | solution.py:292
  161.4 0.0 collective-permute-start.15
  161.4 2.5 total_grads.1
  163.9 6.2 %all-to-all-start.4 = ((bf16[8,3,128,128]{3,2,1,0:T(8,128)(2,1)}), bf16[8,3,128,128]{3,2,1,0:T(8,128)(2,1)S(1)}, u32[]{:S(2)}, u32[]{:S(2)}) async-start(bf16[8,3,128,128]{3,2,1,0:T(8,128)(2,1)} %total_grads.1), calls=%async_computation.4 | async-start | bytes 1572864 | tf_op jit(solution)/shard_map/all_to_all | solution.py:300
  170.1 0.1 slice.54
  170.2 0.6 copy.19
  170.8 0.6 reshape.49.ids_ref
  171.4 0.6 pad_add_fusion.2.place_ref
  172.0 23.1 %attention.5 = (bf16[16,128,128]{2,1,0:T(8,128)(2,1)}, bf16[16,2,128,128]{3,2,1,0:T(8,128)(2,1)}, bf16[16,2,128,128]{3,2,1,0:T(8,128)(2,1)}, bf16[16,2,128,128]{3,2,1,0:T(8,128)(2,1)}) custom-call(s32[192]{0:T(256)} %reshape.49.ids_ref, s32[16]{0:T(128)} %bitcast.37, s32[4]{0:T(128)} %pad_add_fusion.2.place_ref, ...), custom_call_target="tpu_custom_call" | custom-call | flops 2684354560 | bytes 7340032 | tf_op jit(solution)/shard_map/attention/pallas_call | solution.py:139
  195.1 3.3 %collective-permute-start.16 = (bf16[16,2,128,128]{3,2,1,0:T(8,128)(2,1)}, bf16[16,2,128,128]{3,2,1,0:T(8,128)(2,1)}, u32[]{:S(2)}, u32[]{:S(2)}) collective-permute-start(bf16[16,2,128,128]{3,2,1,0:T(8,128)(2,1)} %get-tuple-element.58), channel_id=1, source_target_pairs={{0,48},{16,0},{32,16},{48,32},{1,49},{17,1},{33,17},{49,33},{2,50}... | collective-permute-start | bytes 3145736 | tf_op jit(solution)/shard_map/ppermute | solution.py:292
  198.4 2.1 pad_maximum_fusion
  200.5 0.0 copy-start.4
  200.5 1.0 copy-done.5
  201.5 10.6 %all-to-all-start.5 = ((bf16[32,128,128]{2,1,0:T(8,128)(2,1)}), bf16[32,128,128]{2,1,0:T(8,128)(2,1)S(1)}, u32[]{:S(2)}, u32[]{:S(2)}) async-start(bf16[32,128,128]{2,1,0:T(8,128)(2,1)} %pad_maximum_fusion), calls=%async_computation.5 | async-start | bytes 2097152 | tf_op jit(solution)/shard_map/all_to_all | solution.py:300
  212.2 0.7 pad_add_fusion.4.x_ref
  212.8 8.3 %collective-permute-done.16.right1 = bf16[16,2,128,128]{3,2,1,0:T(8,128)(2,1)} collective-permute-done((bf16[16,2,128,128]{3,2,1,0:T(8,128)(2,1)}, bf16[16,2,128,128]{3,2,1,0:T(8,128)(2,1)}, u32[]{:S(2)}, u32[]{:S(2)}) %collective-permute-start.16) | collective-permute-done | bytes 1048608 | tf_op jit(solution)/shard_map/ppermute | solution.py:292
  221.1 3.3 %collective-permute-done.17.left1 = bf16[16,2,128,128]{3,2,1,0:T(8,128)(2,1)} collective-permute-done((bf16[16,2,128,128]{3,2,1,0:T(8,128)(2,1)}, bf16[16,2,128,128]{3,2,1,0:T(8,128)(2,1)}, u32[]{:S(2)}, u32[]{:S(2)}) %collective-permute-start.17) | collective-permute-done | bytes 1048608 | tf_op jit(solution)/shard_map/ppermute | solution.py:292
  224.4 5.0 %both_halves.1 = bf16[2,16,2,128,128]{4,3,2,1,0:T(8,128)(2,1)} custom-call(s32[2]{0:T(128)} %pad_add_fusion.4.x_ref, bf16[16,2,128,128]{3,2,1,0:T(8,128)(2,1)} %get-tuple-element.56.own0, bf16[16,2,128,128]{3,2,1,0:T(8,128)(2,1)} %get-tuple-element.57.own1, bf16[16,2,128,128]{3,2,1,0:T(8,128)(2,1)} %copy-done.4, ...), custom_call_target="tpu_custom_call" | custom-call | bytes 8388608 | tf_op jit(solution)/shard_map/both_halves/pallas_call | solution.py:273
  229.5 38.2 %all_to_all.36 = bf16[32,2,128,128]{3,2,1,0:T(8,128)(2,1)} all-to-all(bf16[32,2,128,128]{3,2,1,0:T(8,128)(2,1)} %bitcast.29), channel_id=1, replica_groups=mesh['half'=2,'x'=4,'core'=2,'group'=8] {'half','core','group'}, dimensions={0} | all-to-all | bytes 4194304 | tf_op jit(solution)/shard_map/all_to_all | solution.py:300
  267.6 4.7 %join_heads.1 = (bf16[128,5120]{1,0:T(8,128)(2,1)}, bf16[128,5120]{1,0:T(8,128)(2,1)}, bf16[128,5120]{1,0:T(8,128)(2,1)}) custom-call(bf16[4,8,128,128]{3,2,1,0:T(8,128)(2,1)} %bitcast.30, bf16[4,8,2,128,128]{4,3,2,1,0:T(8,128)(2,1)} %bitcast.28, bf16[8,3,128,128]{3,2,1,0:T(8,128)(2,1)} %copy-done.2), custom_call_target="tpu_custom_call" | custom-call | bytes 7864320 | tf_op jit(solution)/shard_map/join_heads/pallas_call | solution.py:218
  (43 shorter events, 0.1 us)
Async XLA Ops:
  37.7 4.8 %copy-start = (bf16[8,4,128,128]{3,2,1,0:T(8,128)(2,1)}, bf16[8,4,128,128]{3,2,1,0:T(8,128)(2,1)S(1)}, u32[]{:S(2)}) copy-start(bf16[8,4,128,128]{3,2,1,0:T(8,128)(2,1)S(1)} %all_to_all.35.refs_6_) | copy-start | bytes 3145732
  37.7 30.8 %all-to-all-start.1 = ((bf16[32,128,128]{2,1,0:T(8,128)(2,1)}), bf16[32,128,128]{2,1,0:T(8,128)(2,1)S(1)}, u32[]{:S(2)}, u32[]{:S(2)}) async-start(bf16[32,128,128]{2,1,0:T(8,128)(2,1)} %bitcast.32), calls=%async_computation.1 | async-start | bytes 2097152 | tf_op jit(solution)/shard_map/all_to_all | solution.py:300
  42.6 57.7 %copy-start.3 = (bf16[8,2,128,128]{3,2,1,0:T(8,128)(2,1)}, bf16[8,2,128,128]{3,2,1,0:T(8,128)(2,1)S(1)}, u32[]{:S(2)}) copy-start(bf16[8,2,128,128]{3,2,1,0:T(8,128)(2,1)S(1)} %slice.52.refs_1_) | copy-start | bytes 1572868
  42.6 21.8 %collective-permute-start.3 = (bf16[8,2,128,128]{3,2,1,0:T(8,128)(2,1)S(1)}, bf16[8,2,128,128]{3,2,1,0:T(8,128)(2,1)S(1)}, u32[]{:S(2)}, u32[]{:S(2)}) collective-permute-start(bf16[8,2,128,128]{3,2,1,0:T(8,128)(2,1)S(1)} %slice.52.refs_1_), channel_id=1, source_target_pairs={{0,112},{16,0},{32,16},{48,32},{64,48},{80,64},{96,80},{112,96},{1... | collective-permute-start | bytes 1572872 | tf_op jit(solution)/shard_map/ppermute | solution.py:292
  46.4 20.4 %collective-permute-start.2 = (bf16[8,2,128,128]{3,2,1,0:T(8,128)(2,1)S(1)}, bf16[8,2,128,128]{3,2,1,0:T(8,128)(2,1)S(1)}, u32[]{:S(2)}, u32[]{:S(2)}) collective-permute-start(bf16[8,2,128,128]{3,2,1,0:T(8,128)(2,1)S(1)} %slice.52.refs_1_), channel_id=1, source_target_pairs={{0,16},{16,32},{32,48},{48,64},{64,80},{80,96},{96,112},{112,0},{1... | collective-permute-start | bytes 1572872 | tf_op jit(solution)/shard_map/ppermute | solution.py:292
  64.4 37.3 %copy-start.8 = (bf16[8,2,128,128]{3,2,1,0:T(8,128)(2,1)}, bf16[8,2,128,128]{3,2,1,0:T(8,128)(2,1)S(1)}, u32[]{:S(2)}) copy-start(bf16[8,2,128,128]{3,2,1,0:T(8,128)(2,1)S(1)} %collective-permute-done.3.refs_2_) | copy-start | bytes 1572868
  66.8 1.7 copy-start.9
  68.5 26.1 %copy-start.6 = (bf16[32,128,128]{2,1,0:T(8,128)(2,1)}, bf16[32,128,128]{2,1,0:T(8,128)(2,1)S(1)}, u32[]{:S(2)}) copy-start(bf16[32,128,128]{2,1,0:T(8,128)(2,1)S(1)} %all-to-all-done.1.refs_1_) | copy-start | bytes 3145732
  68.5 23.7 %all-to-all-start.2 = ((bf16[32,128,128]{2,1,0:T(8,128)(2,1)}), bf16[32,128,128]{2,1,0:T(8,128)(2,1)S(1)}, u32[]{:S(2)}, u32[]{:S(2)}) async-start(bf16[32,128,128]{2,1,0:T(8,128)(2,1)} %bitcast.31), calls=%async_computation.2 | async-start | bytes 2097152 | tf_op jit(solution)/shard_map/all_to_all | solution.py:300
  75.5 26.2 %collective-permute-start.1 = (bf16[32,128,128]{2,1,0:T(8,128)(2,1)S(1)}, bf16[32,128,128]{2,1,0:T(8,128)(2,1)}, u32[]{:S(2)}, u32[]{:S(2)}) collective-permute-start(bf16[32,128,128]{2,1,0:T(8,128)(2,1)S(1)} %all-to-all-done.1.refs_1_), channel_id=1, source_target_pairs={{0,48},{16,0},{32,16},{48,32},{1,49},{17,1},{33,17},{49,33},{2,50}... | collective-permute-start | bytes 3145736 | tf_op jit(solution)/shard_map/ppermute | solution.py:292
  77.9 27.4 %collective-permute-start = (bf16[32,128,128]{2,1,0:T(8,128)(2,1)S(1)}, bf16[32,128,128]{2,1,0:T(8,128)(2,1)}, u32[]{:S(2)}, u32[]{:S(2)}) collective-permute-start(bf16[32,128,128]{2,1,0:T(8,128)(2,1)S(1)} %all-to-all-done.1.refs_1_), channel_id=1, source_target_pairs={{0,16},{16,32},{32,48},{48,0},{1,17},{17,33},{33,49},{49,1},{2,18}... | collective-permute-start | bytes 3145736 | tf_op jit(solution)/shard_map/ppermute | solution.py:292
  92.2 2.4 copy-start.7
  92.2 31.1 %collective-permute-start.5 = (bf16[32,128,128]{2,1,0:T(8,128)(2,1)S(1)}, bf16[32,128,128]{2,1,0:T(8,128)(2,1)}, u32[]{:S(2)}, u32[]{:S(2)}) collective-permute-start(bf16[32,128,128]{2,1,0:T(8,128)(2,1)S(1)} %all-to-all-done.2.refs_4_), channel_id=1, source_target_pairs={{0,48},{16,0},{32,16},{48,32},{1,49},{17,1},{33,17},{49,33},{2,50}... | collective-permute-start | bytes 3145736 | tf_op jit(solution)/shard_map/ppermute | solution.py:292
  94.6 32.1 %collective-permute-start.4 = (bf16[32,128,128]{2,1,0:T(8,128)(2,1)S(1)}, bf16[32,128,128]{2,1,0:T(8,128)(2,1)}, u32[]{:S(2)}, u32[]{:S(2)}) collective-permute-start(bf16[32,128,128]{2,1,0:T(8,128)(2,1)S(1)} %all-to-all-done.2.refs_4_), channel_id=1, source_target_pairs={{0,16},{16,32},{32,48},{48,0},{1,17},{17,33},{33,49},{49,1},{2,18}... | collective-permute-start | bytes 3145736 | tf_op jit(solution)/shard_map/ppermute | solution.py:292
  94.6 39.4 %all-to-all-start.3 = ((bf16[32,2,128,128]{3,2,1,0:T(8,128)(2,1)}), bf16[32,2,128,128]{3,2,1,0:T(8,128)(2,1)}, u32[]{:S(2)}, u32[]{:S(2)}) async-start(bf16[32,2,128,128]{3,2,1,0:T(8,128)(2,1)} %bitcast.8), calls=%async_computation.3 | async-start | bytes 4194304 | tf_op jit(solution)/shard_map/all_to_all | solution.py:300
  100.3 7.0 %collective-permute-start.7 = (bf16[8,2,128,128]{3,2,1,0:T(8,128)(2,1)S(1)}, bf16[8,2,128,128]{3,2,1,0:T(8,128)(2,1)}, u32[]{:S(2)}, u32[]{:S(2)}) collective-permute-start(bf16[8,2,128,128]{3,2,1,0:T(8,128)(2,1)S(1)} %slice.52.refs_1_), channel_id=1, source_target_pairs={{0,8},{8,0},{1,9},{9,1},{2,10},{10,2},{3,11},{11,3},{4,12},{12,4},... | collective-permute-start | bytes 1572872 | tf_op jit(solution)/shard_map/ppermute | solution.py:308
  101.7 5.6 %collective-permute-start.8 = (bf16[8,2,128,128]{3,2,1,0:T(8,128)(2,1)S(1)}, bf16[8,2,128,128]{3,2,1,0:T(8,128)(2,1)}, u32[]{:S(2)}, u32[]{:S(2)}) collective-permute-start(bf16[8,2,128,128]{3,2,1,0:T(8,128)(2,1)S(1)} %collective-permute-done.3.refs_2_), channel_id=1, source_target_pairs={{0,8},{8,0},{1,9},{9,1},{2,10},{10,2},{3,11},{11,3},{4,12},{12,4},... | collective-permute-start | bytes 1572872 | tf_op jit(solution)/shard_map/ppermute | solution.py:308
  105.3 2.1 collective-permute-start.6
  107.4 0.8 copy-start.12
  126.7 5.0 %copy-start.11 = (bf16[8,2,128,128]{3,2,1,0:T(8,128)(2,1)S(1)}, bf16[8,2,128,128]{3,2,1,0:T(8,128)(2,1)}, u32[]{:S(2)}) copy-start(bf16[8,2,128,128]{3,2,1,0:T(8,128)(2,1)} %get-tuple-element.48) | copy-start | bytes 1572868
  129.0 2.8 %copy-start.10 = (bf16[8,2,128,128]{3,2,1,0:T(8,128)(2,1)S(1)}, bf16[8,2,128,128]{3,2,1,0:T(8,128)(2,1)}, u32[]{:S(2)}) copy-start(bf16[8,2,128,128]{3,2,1,0:T(8,128)(2,1)} %get-tuple-element.47) | copy-start | bytes 1572868
  129.0 2.6 collective-permute-start.11
  129.0 2.8 %collective-permute-start.10 = (bf16[8,2,128,128]{3,2,1,0:T(8,128)(2,1)S(1)}, bf16[8,2,128,128]{3,2,1,0:T(8,128)(2,1)S(1)}, u32[]{:S(2)}, u32[]{:S(2)}) collective-permute-start(bf16[8,2,128,128]{3,2,1,0:T(8,128)(2,1)S(1)} %get-tuple-element.62), channel_id=1, source_target_pairs={{0,8},{8,0},{1,9},{9,1},{2,10},{10,2},{3,11},{11,3},{4,12},{12,4},... | collective-permute-start | bytes 1572872 | tf_op jit(solution)/shard_map/ppermute | solution.py:308
  131.5 29.8 %collective-permute-start.9 = (bf16[8,2,128,128]{3,2,1,0:T(8,128)(2,1)}, bf16[8,2,128,128]{3,2,1,0:T(8,128)(2,1)}, u32[]{:S(2)}, u32[]{:S(2)}) collective-permute-start(bf16[8,2,128,128]{3,2,1,0:T(8,128)(2,1)} %get-tuple-element.63), channel_id=1, source_target_pairs={{0,8},{8,0},{1,9},{9,1},{2,10},{10,2},{3,11},{11,3},{4,12},{12,4},... | collective-permute-start | bytes 1572872 | tf_op jit(solution)/shard_map/ppermute | solution.py:308
  131.9 29.4 %collective-permute-start.12 = (bf16[8,2,128,128]{3,2,1,0:T(8,128)(2,1)S(1)}, bf16[8,2,128,128]{3,2,1,0:T(8,128)(2,1)}, u32[]{:S(2)}, u32[]{:S(2)}) collective-permute-start(bf16[8,2,128,128]{3,2,1,0:T(8,128)(2,1)S(1)} %add_convert_fusion.1), channel_id=1, source_target_pairs={{0,112},{16,0},{32,16},{48,32},{64,48},{80,64},{96,80},{112,96},{1... | collective-permute-start | bytes 1572872 | tf_op jit(solution)/shard_map/ppermute | solution.py:292
  133.2 28.2 %collective-permute-start.13 = (bf16[8,2,128,128]{3,2,1,0:T(8,128)(2,1)S(1)}, bf16[8,2,128,128]{3,2,1,0:T(8,128)(2,1)}, u32[]{:S(2)}, u32[]{:S(2)}) collective-permute-start(bf16[8,2,128,128]{3,2,1,0:T(8,128)(2,1)S(1)} %add_convert_fusion), channel_id=1, source_target_pairs={{0,16},{16,32},{32,48},{48,64},{64,80},{80,96},{96,112},{112,0},{1... | collective-permute-start | bytes 1572872 | tf_op jit(solution)/shard_map/ppermute | solution.py:292
  157.0 43.5 %collective-permute-start.14 = (bf16[16,2,128,128]{3,2,1,0:T(8,128)(2,1)}, bf16[16,2,128,128]{3,2,1,0:T(8,128)(2,1)S(1)}, u32[]{:S(2)}, u32[]{:S(2)}) collective-permute-start(bf16[16,2,128,128]{3,2,1,0:T(8,128)(2,1)} %get-tuple-element.53), channel_id=1, source_target_pairs={{0,48},{16,0},{32,16},{48,32},{1,49},{17,1},{33,17},{49,33},{2,50}... | collective-permute-start | bytes 3145736 | tf_op jit(solution)/shard_map/ppermute | solution.py:292
  161.4 39.1 %collective-permute-start.15 = (bf16[16,2,128,128]{3,2,1,0:T(8,128)(2,1)}, bf16[16,2,128,128]{3,2,1,0:T(8,128)(2,1)S(1)}, u32[]{:S(2)}, u32[]{:S(2)}) collective-permute-start(bf16[16,2,128,128]{3,2,1,0:T(8,128)(2,1)} %get-tuple-element.54), channel_id=1, source_target_pairs={{0,16},{16,32},{32,48},{48,0},{1,17},{17,33},{33,49},{49,1},{2,18}... | collective-permute-start | bytes 3145736 | tf_op jit(solution)/shard_map/ppermute | solution.py:292
  163.9 36.6 %all-to-all-start.4 = ((bf16[8,3,128,128]{3,2,1,0:T(8,128)(2,1)}), bf16[8,3,128,128]{3,2,1,0:T(8,128)(2,1)S(1)}, u32[]{:S(2)}, u32[]{:S(2)}) async-start(bf16[8,3,128,128]{3,2,1,0:T(8,128)(2,1)} %total_grads.1), calls=%async_computation.4 | async-start | bytes 1572864 | tf_op jit(solution)/shard_map/all_to_all | solution.py:300
  172.0 26.4 %copy-start.13 = (bf16[16,128,128]{2,1,0:T(8,128)(2,1)S(1)}, bf16[16,128,128]{2,1,0:T(8,128)(2,1)}, u32[]{:S(2)}) copy-start(bf16[16,128,128]{2,1,0:T(8,128)(2,1)} %get-tuple-element.40) | copy-start | bytes 1572868
  195.1 26.1 %collective-permute-start.16 = (bf16[16,2,128,128]{3,2,1,0:T(8,128)(2,1)}, bf16[16,2,128,128]{3,2,1,0:T(8,128)(2,1)}, u32[]{:S(2)}, u32[]{:S(2)}) collective-permute-start(bf16[16,2,128,128]{3,2,1,0:T(8,128)(2,1)} %get-tuple-element.58), channel_id=1, source_target_pairs={{0,48},{16,0},{32,16},{48,32},{1,49},{17,1},{33,17},{49,33},{2,50}... | collective-permute-start | bytes 3145736 | tf_op jit(solution)/shard_map/ppermute | solution.py:292
  198.4 26.1 %collective-permute-start.17 = (bf16[16,2,128,128]{3,2,1,0:T(8,128)(2,1)}, bf16[16,2,128,128]{3,2,1,0:T(8,128)(2,1)}, u32[]{:S(2)}, u32[]{:S(2)}) collective-permute-start(bf16[16,2,128,128]{3,2,1,0:T(8,128)(2,1)} %get-tuple-element.59), channel_id=1, source_target_pairs={{0,16},{16,32},{32,48},{48,0},{1,17},{17,33},{33,49},{49,1},{2,18}... | collective-permute-start | bytes 3145736 | tf_op jit(solution)/shard_map/ppermute | solution.py:292
  200.5 29.0 %copy-start.2 = (bf16[8,3,128,128]{3,2,1,0:T(8,128)(2,1)}, bf16[8,3,128,128]{3,2,1,0:T(8,128)(2,1)S(1)}, u32[]{:S(2)}) copy-start(bf16[8,3,128,128]{3,2,1,0:T(8,128)(2,1)S(1)} %all-to-all-done.4.b_ref) | copy-start | bytes 2359300
  200.5 23.9 %copy-start.4 = (bf16[16,2,128,128]{3,2,1,0:T(8,128)(2,1)}, bf16[16,2,128,128]{3,2,1,0:T(8,128)(2,1)S(1)}, u32[]{:S(2)}) copy-start(bf16[16,2,128,128]{3,2,1,0:T(8,128)(2,1)S(1)} %collective-permute-done.14.right0) | copy-start | bytes 3145732
  200.5 1.0 copy-start.5
  201.5 27.9 %all-to-all-start.5 = ((bf16[32,128,128]{2,1,0:T(8,128)(2,1)}), bf16[32,128,128]{2,1,0:T(8,128)(2,1)S(1)}, u32[]{:S(2)}, u32[]{:S(2)}) async-start(bf16[32,128,128]{2,1,0:T(8,128)(2,1)} %pad_maximum_fusion), calls=%async_computation.5 | async-start | bytes 2097152 | tf_op jit(solution)/shard_map/all_to_all | solution.py:300
  229.5 38.2 %copy-start.1 = (bf16[32,128,128]{2,1,0:T(8,128)(2,1)}, bf16[32,128,128]{2,1,0:T(8,128)(2,1)S(1)}, u32[]{:S(2)}) copy-start(bf16[32,128,128]{2,1,0:T(8,128)(2,1)S(1)} %all-to-all-done.5) | copy-start | bytes 3145732

commit v9 on v8

--- a/solution.py
+++ b/solution.py
@@ -14,7 +14,9 @@
 BPD = 8
 MAXK = 12
 HPG = 5
-GROUP = 4
+WAYS = 2
+BUCKETS = (4, 6, 8, 10, 12)
+STEP = 2
 ATTENTION_COST = 10
 VMEM_LIMIT = 56 * 2**20
 NEG = -1e30
@@ -35,39 +37,51 @@
     return x.reshape(-1, 8, HD)
 
 
-def query_block(n_keys, b, ids_ref, count, qd, keys, values, acc, dq, kcat, s_scr, dp_scr, ds_scr):
-    q = qd[b, 0]
-    do = qd[b, 1]
-    base = b * MAXK
-    m8 = jnp.full((8, HD), NEG, F32)
-    index = [ids_ref[base + s] for s in range(n_keys)]
-    for s in range(n_keys):
-        k = keys[index[s]]
-        kcat[pl.ds(s * BLK, BLK), :] = k
-        st = dot(k, q, NT)
-        if s > n_keys - GROUP:
-            st = jnp.where(s < count, st, NEG)
-        s_scr[s] = st
-        m8 = jnp.maximum(m8, jnp.max(fold(st), axis=0))
-        dp_scr[s] = dot(values[index[s]], do, NT)
-    m = jnp.max(m8, axis=0, keepdims=True) * (SCALE * LOG2E)
-    l8 = jnp.zeros((8, HD), F32)
-    r8 = jnp.zeros((8, HD), F32)
-    for s in range(n_keys):
-        p = jnp.exp2(s_scr[s] * (SCALE * LOG2E) - m)
-        s_scr[s] = p
-        l8 += jnp.sum(fold(p), axis=0)
-        r8 += jnp.sum(fold(p * dp_scr[s]), axis=0)
-    inv = 1.0 / jnp.sum(l8, axis=0, keepdims=True)
-    rd = jnp.sum(r8, axis=0, keepdims=True) * inv
-    for s in range(n_keys):
-        p = s_scr[s] * inv
-        ds = (p * (dp_scr[s] - rd)).astype(BF16)
-        ds_scr[pl.ds(s * BLK, BLK), :] = ds
-        acc[index[s], 0] += dot(ds, q, NN)
-        acc[index[s], 1] += dot(p.astype(BF16), do, NN)
-    rows = pl.ds(0, n_keys * BLK)
-    dq[...] = (dot(ds_scr[rows, :], kcat[rows, :], TN) * SCALE).astype(BF16)
+def query_blocks(n_keys, blocks, ids_ref, counts, qd, kv, acc, dq, kv_cat, sd_scr, x_cat):
+    ways = range(len(blocks))
+    index = [[ids_ref[b * MAXK + s] for s in range(n_keys)] for b in blocks]
+    rows = [pl.ds(s * BLK, BLK) for s in range(n_keys)]
+    for i in ways:
+        for s in range(n_keys):
+            kv_cat[i, rows[s], :] = kv[index[i][s]]
+    w_t = [qd[b] for b in blocks]
+    for s in range(0, n_keys, STEP):
+        part = pl.ds(s * BLK, min(STEP, n_keys - s) * BLK)
+        for i in ways:
+            sd_scr[i, part, :] = dot(kv_cat[i, part, :], w_t[i], NT)
+    top = []
+    for i in ways:
+        m8 = jnp.full((8, HD), NEG, F32)
+        for s in range(n_keys):
+            st = sd_scr[i, rows[s], :HD]
+            if s > 0:
+                st = jnp.where(s < counts[i], st, NEG)
+                sd_scr[i, rows[s], :HD] = st
+            m8 = jnp.maximum(m8, jnp.max(fold(st), axis=0))
+        top.append(jnp.max(m8, axis=0, keepdims=True) * (SCALE * LOG2E))
+    inv, rd = [], []
+    for i in ways:
+        l8 = jnp.zeros((8, HD), F32)
+        r8 = jnp.zeros((8, HD), F32)
+        for s in range(n_keys):
+            p = jnp.exp2(sd_scr[i, rows[s], :HD] * (SCALE * LOG2E) - top[i])
+            sd_scr[i, rows[s], :HD] = p
+            l8 += jnp.sum(fold(p), axis=0)
+            r8 += jnp.sum(fold(p * sd_scr[i, rows[s], HD:]), axis=0)
+        inv.append(1.0 / jnp.sum(l8, axis=0, keepdims=True))
+        rd.append(jnp.sum(r8, axis=0, keepdims=True) * inv[i])
+    for i in ways:
+        for s in range(n_keys):
+            p = sd_scr[i, rows[s], :HD] * inv[i]
+            x_cat[i, rows[s], :HD] = (p * (sd_scr[i, rows[s], HD:] - rd[i])).astype(BF16)
+            x_cat[i, rows[s], HD:] = p.astype(BF16)
+        for s in range(0, n_keys, STEP):
+            n = min(STEP, n_keys - s)
+            terms = dot(x_cat[i, pl.ds(s * BLK, n * BLK), :], qd[blocks[i]], NN)
+            for j in range(n):
+                acc[index[i][s + j]] += terms[j * BLK : (j + 1) * BLK]
+        every = pl.ds(0, n_keys * BLK)
+        dq[blocks[i]] = (dot(x_cat[i, every, :HD], kv_cat[i, every, :HD], TN) * SCALE).astype(BF16)
 
 
 def attention_kernel(size, n_query, fetches, ids_ref, cnt_ref, place_ref, *refs):
@@ -76,40 +90,57 @@
     qd_in, dq_out, targets = refs[0], refs[1], refs[2:5]
     if shared:
         give_out, refs = refs[5], refs[1:]
-    keys, values, qd, acc, stage, dq, kcat, s_scr, dp_scr, ds_scr, in_sem, out_sem = refs[5:]
+    kv, qd, acc, stage, dq, kv_cat, sd_scr, x_cat, order, in_sem, out_sem = refs[5:]
     copies = []
     for source, fetch in zip(sources, fetches):
         for src, t, row in fetch(source, place_ref):
-            dst = (keys, values)[t].at[pl.ds(row, src.shape[0])]
+            dst = kv.at[pl.ds(row, src.shape[0]), :, pl.ds(t * HD, HD)]
             copies.append(pltpu.make_async_copy(src, dst, in_sem.at[len(copies)]))
-    q_rows = qd_in.at[pl.ds(pl.multiple_of(place_ref[0], 8), n_query), pl.ds(qd_in.shape[1] - 2, 2)]
-    copies.append(pltpu.make_async_copy(q_rows, qd, in_sem.at[len(copies)]))
+    q_rows = pl.ds(pl.multiple_of(place_ref[0], 8), n_query)
+    for t in range(2):
+        src = qd_in.at[q_rows, qd_in.shape[1] - 2 + t]
+        dst = qd.at[:, pl.ds(t * HD, HD), pl.ds(t * HD, HD)]
+        copies.append(pltpu.make_async_copy(src, dst, in_sem.at[len(copies)]))
     for copy in copies:
         copy.start()
     acc[...] = jnp.zeros_like(acc)
+    for t in range(2):
+        qd[:, t * HD : (t + 1) * HD, (1 - t) * HD : (2 - t) * HD] = jnp.zeros((n_query, HD, HD), BF16)
+    def rank(k, at):
+        def place(b, at):
+            hit = cnt_ref[b] == MAXK - k
+
+            @pl.when(hit)
+            def _():
+                order[at] = b
+
+            return at + hit.astype(jnp.int32)
+
+        return lax.fori_loop(0, n_query, place, at)
+
+    lax.fori_loop(0, MAXK, rank, 0)
     for copy in copies:
         copy.wait()
 
-    def one(b, carry):
-        count = cnt_ref[b]
-        for upto in range(GROUP, MAXK + 1, GROUP):
-
-            @pl.when((count > upto - GROUP) & (count <= upto))
+    def some(k, carry):
+        blocks = [order[k * WAYS + i] for i in range(WAYS)]
+        counts = [cnt_ref[b] for b in blocks]
+        for least, upto in zip((0, *BUCKETS), BUCKETS):
+
+            @pl.when((counts[0] > least) & (counts[0] <= upto))
             def _():
-                query_block(
-                    upto, b, ids_ref, count, qd, keys, values, acc, dq.at[b], kcat, s_scr, dp_scr, ds_scr
-                )
+                query_blocks(upto, blocks, ids_ref, counts, qd, kv, acc, dq, kv_cat, sd_scr, x_cat)
 
         return carry
 
-    lax.fori_loop(0, n_query, one, 0)
+    lax.fori_loop(0, n_query // WAYS, some, 0)
     puts = [pltpu.make_async_copy(dq, dq_out, out_sem.at[3])]
     puts[0].start()
     for i, target in enumerate(targets):
 
         def convert(j, carry):
-            stage[j, 0] = (acc[j, 0] * SCALE).astype(BF16)
-            stage[j, 1] = acc[j, 1].astype(BF16)
+            stage[j, 0] = (acc[j, :, :HD] * SCALE).astype(BF16)
+            stage[j, 1] = acc[j, :, HD:].astype(BF16)
             return carry
 
         lax.fori_loop(i * size, (i + 1) * size, convert, 0)
@@ -142,17 +173,16 @@
         in_specs=[smem] * 3 + [hbm] * (len(sources) + 1),
         out_specs=[hbm] * (4 + len(given)),
         scratch_shapes=[
-            pltpu.VMEM((window, BLK, HD), BF16),
-            pltpu.VMEM((window, BLK, HD), BF16),
-            pltpu.VMEM((n_query, 2, BLK, HD), BF16),
-            pltpu.VMEM((window, 2, BLK, HD), F32),
+            pltpu.VMEM((window, BLK, 2 * HD), BF16),
+            pltpu.VMEM((n_query, 2 * HD, 2 * HD), BF16),
+            pltpu.VMEM((window, BLK, 2 * HD), F32),
             pltpu.VMEM((window, 2, BLK, HD), BF16),
             pltpu.VMEM((n_query, BLK, HD), BF16),
-            pltpu.VMEM((MAXK * BLK, HD), BF16),
-            pltpu.VMEM((MAXK, BLK, HD), F32),
-            pltpu.VMEM((MAXK, BLK, HD), F32),
-            pltpu.VMEM((MAXK * BLK, HD), BF16),
-            pltpu.SemaphoreType.DMA((13,)),
+            pltpu.VMEM((WAYS, MAXK * BLK, 2 * HD), BF16),
+            pltpu.VMEM((WAYS, MAXK * BLK, 2 * HD), F32),
+            pltpu.VMEM((WAYS, MAXK * BLK, 2 * HD), BF16),
+            pltpu.SMEM((n_query,), jnp.int32),
+            pltpu.SemaphoreType.DMA((14,)),
             pltpu.SemaphoreType.DMA((7,)),
         ],
         compiler_params=pltpu.CompilerParams(vmem_limit_bytes=VMEM_LIMIT),

time: 274 us -> 261 us (0.953)
  Pallas kernels: 78.6 us -> 66.4 us
  waiting for transfers between devices: 56.5 us -> 61.9 us
  starting transfers between devices: 53.4 us -> 50 us
    pallas_call x3, Pallas kernels: 60.9 us -> 48.7 us  [attention(): pl.pallas_call(functools.partial(attention_kernel, size, n_query, fetches...]
    ppermute x12, waiting for transfers between devices: 40.3 us -> 45.7 us  [shift(): lax.ppermute(value, axes, [(s, (s + steps) % count) for s in range(count)])]
  transfers between devices with their start and end apart: 23 -> 23, of which waited for: 11 -> 11; matrix products, arithmetic and copies ran while one was open for 4% -> 4% of each run, Pallas kernels for 25% -> 22%
where the time goes in v9:
time: 261 us; the launch traced here: 260 us
  blocking collectives  66.6 us (26%)
  Pallas kernels  66.4 us (25%)
  waiting for transfers between devices  61.9 us (24%)
  starting transfers between devices  50 us (19%)
  local copies, waits for them, and re-layouts  9.01 us (3%)
  other arithmetic  5.77 us (2%)
    all_to_all x2, blocking collectives, exchange(): return lax.all_to_all(x, axes, 0, 0, tiled=True)  61.3 us
    pallas_call x3, Pallas kernels, attention(): pl.pallas_call(functools.partial(attention_kernel, size, n_query, fetches...  48.7 us
    ppermute x12, waiting for transfers between devices, shift(): lax.ppermute(value, axes, [(s, (s + steps) % count) for s in range(count)])  45.7 us
    all_to_all x5, starting transfers between devices, exchange(): return lax.all_to_all(x, axes, 0, 0, tiled=True)  31.7 us
    ppermute x12, starting transfers between devices, shift(): lax.ppermute(value, axes, [(s, (s + steps) % count) for s in range(count)])  17.5 us
    all_to_all x5, waiting for transfers between devices, exchange(): return lax.all_to_all(x, axes, 0, 0, tiled=True)  16 us
    pallas_call x1, Pallas kernels, split_heads(): pl.pallas_call(split_kernel, grid=(groups // step,), out_shape=tuple((jax...  5.47 us
    all_gather x1, blocking collectives, shards(): gathered = lax.all_gather(packed, ('half', 'core'))  5.28 us
  transfers between devices with their start and end apart: 23, of which 11 were waited for; matrix products, arithmetic and copies ran while one was open for 4% of the time, Pallas kernels for 22%

profile of v9, /device:TPU:8, one launch (start us, length us, event | category | flops | bytes accessed | tf_op | source)
XLA Modules:
  0.0 260.4 jit_solution(10320794932667153004)
XLA Ops:
  0.6 0.8 copy.15
  1.4 0.8 pad_add_fusion
  2.2 5.3 %all-gather = s32[20,8,13]{2,1,0:T(8,128)S(1)} all-gather(s32[5,8,13]{2,1,0:T(8,128)S(1)} %pad_add_fusion), channel_id=2, replica_groups=mesh['half'=2,'x'=4,'core'=2,'group'=8] {'half','core'}, dimensions={0}, use_global_device_ids=true | all-gather | bytes 10400 | tf_op jit(solution)/shard_map/all_gather | solution.py:345
  7.5 5.5 %split_heads.1 = (bf16[4,8,128,128]{3,2,1,0:T(8,128)(2,1)}, bf16[4,8,128,128]{3,2,1,0:T(8,128)(2,1)}, bf16[4,8,2,128,128]{4,3,2,1,0:T(8,128)(2,1)}, bf16[8,4,128,128]{3,2,1,0:T(8,128)(2,1)}) custom-call(bf16[128,5120]{1,0:T(8,128)(2,1)} %k_ref.1, bf16[128,5120]{1,0:T(8,128)(2,1)} %v_ref.1, bf16[128,5120]{1,0:T(8,128)(2,1)} %q_ref.1, bf16[128,5120]{1,0:T(8,128)(2,1)} %g_ref.1), custom_call_target="tpu_custom_call" | custom-call | bytes 10485760 | tf_op jit(solution)/shard_map/split_heads/pallas_call | solution.py:220
  13.0 24.8 %all_to_all.35.refs_6_ = bf16[8,4,128,128]{3,2,1,0:T(8,128)(2,1)S(1)} all-to-all(bf16[8,4,128,128]{3,2,1,0:T(8,128)(2,1)} %get-tuple-element.34), channel_id=1, replica_groups=mesh['half'=2,'x'=4,'core'=2,'group'=8] {'group'}, dimensions={0} | all-to-all | bytes 2097152 | tf_op jit(solution)/shard_map/all_to_all | solution.py:330
  37.7 4.8 %all-to-all-start.1 = ((bf16[32,128,128]{2,1,0:T(8,128)(2,1)}), bf16[32,128,128]{2,1,0:T(8,128)(2,1)S(1)}, u32[]{:S(2)}, u32[]{:S(2)}) async-start(bf16[32,128,128]{2,1,0:T(8,128)(2,1)} %bitcast.32), calls=%async_computation.1 | async-start | bytes 2097152 | tf_op jit(solution)/shard_map/all_to_all | solution.py:330
  42.6 3.8 %collective-permute-start.3 = (bf16[8,2,128,128]{3,2,1,0:T(8,128)(2,1)S(1)}, bf16[8,2,128,128]{3,2,1,0:T(8,128)(2,1)S(1)}, u32[]{:S(2)}, u32[]{:S(2)}) collective-permute-start(bf16[8,2,128,128]{3,2,1,0:T(8,128)(2,1)S(1)} %slice.52.refs_1_), channel_id=1, source_target_pairs={{0,112},{16,0},{32,16},{48,32},{64,48},{80,64},{96,80},{112,96},{1... | collective-permute-start | bytes 1572872 | tf_op jit(solution)/shard_map/ppermute | solution.py:322
  46.4 0.0 collective-permute-start.2
  46.4 18.0 %collective-permute-done.3.refs_2_ = bf16[8,2,128,128]{3,2,1,0:T(8,128)(2,1)S(1)} collective-permute-done((bf16[8,2,128,128]{3,2,1,0:T(8,128)(2,1)S(1)}, bf16[8,2,128,128]{3,2,1,0:T(8,128)(2,1)S(1)}, u32[]{:S(2)}, u32[]{:S(2)}) %collective-permute-start.3) | collective-permute-done | bytes 524320 | tf_op jit(solution)/shard_map/ppermute | solution.py:322
  64.4 2.4 collective-permute-done.2.refs_0_
  66.8 1.7 all-to-all-done.1.refs_1_
  68.5 7.0 %all-to-all-start.2 = ((bf16[32,128,128]{2,1,0:T(8,128)(2,1)}), bf16[32,128,128]{2,1,0:T(8,128)(2,1)S(1)}, u32[]{:S(2)}, u32[]{:S(2)}) async-start(bf16[32,128,128]{2,1,0:T(8,128)(2,1)} %bitcast.31), calls=%async_computation.2 | async-start | bytes 2097152 | tf_op jit(solution)/shard_map/all_to_all | solution.py:330
  75.5 2.4 collective-permute-start.1
  77.9 14.3 %all-to-all-done.2.refs_4_ = bf16[32,128,128]{2,1,0:T(8,128)(2,1)S(1)} async-done(((bf16[32,128,128]{2,1,0:T(8,128)(2,1)}), bf16[32,128,128]{2,1,0:T(8,128)(2,1)S(1)}, u32[]{:S(2)}, u32[]{:S(2)}) %all-to-all-start.2) | async-done | bytes 1048608 | tf_op jit(solution)/shard_map/all_to_all | solution.py:330
  92.2 2.4 collective-permute-start.5
  94.6 5.6 %all-to-all-start.3 = ((bf16[32,2,128,128]{3,2,1,0:T(8,128)(2,1)}), bf16[32,2,128,128]{3,2,1,0:T(8,128)(2,1)}, u32[]{:S(2)}, u32[]{:S(2)}) async-start(bf16[32,2,128,128]{3,2,1,0:T(8,128)(2,1)} %bitcast.8), calls=%async_computation.3 | async-start | bytes 4194304 | tf_op jit(solution)/shard_map/all_to_all | solution.py:330
  100.3 0.2 collective-permute-start.7
  100.5 1.2 collective-permute-done.1.refs_2_
  101.7 3.6 %collective-permute-done.refs_0_ = bf16[32,128,128]{2,1,0:T(8,128)(2,1)} collective-permute-done((bf16[32,128,128]{2,1,0:T(8,128)(2,1)S(1)}, bf16[32,128,128]{2,1,0:T(8,128)(2,1)}, u32[]{:S(2)}, u32[]{:S(2)}) %collective-permute-start) | collective-permute-done | bytes 1048608 | tf_op jit(solution)/shard_map/ppermute | solution.py:322
  105.3 0.0 collective-permute-start.6
  105.3 0.6 reshape.50.ids_ref
  105.9 0.7 pad_add_fusion.3.place_ref
  106.6 0.7 slice_reduce_fusion.cnt_ref
  107.2 0.0 collective-permute-done.7.refs_4_
  107.3 0.0 collective-permute-done.8.refs_5_
  107.3 0.2 collective-permute-done.6.refs_3_
  107.4 0.8 copy-done.12
  108.2 10.2 %attention.4 = (bf16[8,128,128]{2,1,0:T(8,128)(2,1)}, bf16[8,2,128,128]{3,2,1,0:T(8,128)(2,1)}, bf16[8,2,128,128]{3,2,1,0:T(8,128)(2,1)}, bf16[8,2,128,128]{3,2,1,0:T(8,128)(2,1)}, bf16[3,8,2,128,128]{4,3,2,1,0:T(8,128)(2,1)}) custom-call(s32[96]{0:T(128)} %reshape.50.ids_ref, s32[8]{0:T(128)} %slice_reduce_fusion.cnt_ref, s32[2]{0:T(128)} %pad_add_fusion.3.place_ref, ...), custom_call_target="tpu_custom_call" | custom-call | tf_op jit(solution)/shard_map/attention/pallas_call | solution.py:170
  118.4 5.0 %collective-permute-done.5.refs_5_ = bf16[32,128,128]{2,1,0:T(8,128)(2,1)} collective-permute-done((bf16[32,128,128]{2,1,0:T(8,128)(2,1)S(1)}, bf16[32,128,128]{2,1,0:T(8,128)(2,1)}, u32[]{:S(2)}, u32[]{:S(2)}) %collective-permute-start.5) | collective-permute-done | bytes 1048608 | tf_op jit(solution)/shard_map/ppermute | solution.py:322
  123.4 3.3 %collective-permute-done.4.refs_3_ = bf16[32,128,128]{2,1,0:T(8,128)(2,1)} collective-permute-done((bf16[32,128,128]{2,1,0:T(8,128)(2,1)S(1)}, bf16[32,128,128]{2,1,0:T(8,128)(2,1)}, u32[]{:S(2)}, u32[]{:S(2)}) %collective-permute-start.4) | collective-permute-done | bytes 1048608 | tf_op jit(solution)/shard_map/ppermute | solution.py:322
  126.7 2.3 slice_bitcast_fusion
  129.0 0.0 collective-permute-start.11
  129.0 0.5 collective-permute-start.10
  129.5 0.7 pad_add_fusion.1.place_ref
  130.2 0.1 slice.51
  130.2 0.7 copy.18
  130.9 0.6 reshape.44.ids_ref
  131.5 0.1 collective-permute-start.9
  131.6 0.1 add_convert_fusion
  131.8 0.0 collective-permute-done.10
  131.8 0.1 add_convert_fusion.1
  131.9 1.3 collective-permute-start.12
  133.2 0.8 collective-permute-start.13
  134.0 19.2 %attention.3 = (bf16[16,128,128]{2,1,0:T(8,128)(2,1)}, bf16[16,2,128,128]{3,2,1,0:T(8,128)(2,1)}, bf16[16,2,128,128]{3,2,1,0:T(8,128)(2,1)}, bf16[16,2,128,128]{3,2,1,0:T(8,128)(2,1)}) custom-call(s32[192]{0:T(256)} %reshape.44.ids_ref, s32[16]{0:T(128)} %bitcast.36, s32[4]{0:T(128)} %pad_add_fusion.1.place_ref, ...), custom_call_target="tpu_custom_call" | custom-call | flops 2684354560 | bytes 7340032 | tf_op jit(solution)/shard_map/attention/pallas_call | solution.py:170
  153.2 2.5 collective-permute-start.14
  155.7 0.0 collective-permute-start.15
  155.7 2.5 total_grads.1
  158.3 8.6 %all-to-all-start.4 = ((bf16[8,3,128,128]{3,2,1,0:T(8,128)(2,1)}), bf16[8,3,128,128]{3,2,1,0:T(8,128)(2,1)S(1)}, u32[]{:S(2)}, u32[]{:S(2)}) async-start(bf16[8,3,128,128]{3,2,1,0:T(8,128)(2,1)} %total_grads.1), calls=%async_computation.4 | async-start | bytes 1572864 | tf_op jit(solution)/shard_map/all_to_all | solution.py:330
  166.8 0.1 slice.54
  166.9 0.6 copy.19
  167.5 0.6 reshape.49.ids_ref
  168.1 0.6 pad_add_fusion.2.place_ref
  168.7 19.3 %attention.5 = (bf16[16,128,128]{2,1,0:T(8,128)(2,1)}, bf16[16,2,128,128]{3,2,1,0:T(8,128)(2,1)}, bf16[16,2,128,128]{3,2,1,0:T(8,128)(2,1)}, bf16[16,2,128,128]{3,2,1,0:T(8,128)(2,1)}) custom-call(s32[192]{0:T(256)} %reshape.49.ids_ref, s32[16]{0:T(128)} %bitcast.37, s32[4]{0:T(128)} %pad_add_fusion.2.place_ref, ...), custom_call_target="tpu_custom_call" | custom-call | flops 2684354560 | bytes 7340032 | tf_op jit(solution)/shard_map/attention/pallas_call | solution.py:170
  188.0 4.3 %collective-permute-start.16 = (bf16[16,2,128,128]{3,2,1,0:T(8,128)(2,1)}, bf16[16,2,128,128]{3,2,1,0:T(8,128)(2,1)}, u32[]{:S(2)}, u32[]{:S(2)}) collective-permute-start(bf16[16,2,128,128]{3,2,1,0:T(8,128)(2,1)} %get-tuple-element.58), channel_id=1, source_target_pairs={{0,48},{16,0},{32,16},{48,32},{1,49},{17,1},{33,17},{49,33},{2,50}... | collective-permute-start | bytes 3145736 | tf_op jit(solution)/shard_map/ppermute | solution.py:322
  192.3 2.1 pad_maximum_fusion
  194.4 0.0 copy-start.4
  194.5 1.0 copy-done.5
  195.5 5.8 %all-to-all-start.5 = ((bf16[32,128,128]{2,1,0:T(8,128)(2,1)}), bf16[32,128,128]{2,1,0:T(8,128)(2,1)S(1)}, u32[]{:S(2)}, u32[]{:S(2)}) async-start(bf16[32,128,128]{2,1,0:T(8,128)(2,1)} %pad_maximum_fusion), calls=%async_computation.5 | async-start | bytes 2097152 | tf_op jit(solution)/shard_map/all_to_all | solution.py:330
  201.3 0.7 pad_add_fusion.4.x_ref
  201.9 8.8 %collective-permute-done.16.right1 = bf16[16,2,128,128]{3,2,1,0:T(8,128)(2,1)} collective-permute-done((bf16[16,2,128,128]{3,2,1,0:T(8,128)(2,1)}, bf16[16,2,128,128]{3,2,1,0:T(8,128)(2,1)}, u32[]{:S(2)}, u32[]{:S(2)}) %collective-permute-start.16) | collective-permute-done | bytes 1048608 | tf_op jit(solution)/shard_map/ppermute | solution.py:322
  210.8 3.4 %collective-permute-done.17.left1 = bf16[16,2,128,128]{3,2,1,0:T(8,128)(2,1)} collective-permute-done((bf16[16,2,128,128]{3,2,1,0:T(8,128)(2,1)}, bf16[16,2,128,128]{3,2,1,0:T(8,128)(2,1)}, u32[]{:S(2)}, u32[]{:S(2)}) %collective-permute-start.17) | collective-permute-done | bytes 1048608 | tf_op jit(solution)/shard_map/ppermute | solution.py:322
  214.2 5.0 %both_halves.1 = bf16[2,16,2,128,128]{4,3,2,1,0:T(8,128)(2,1)} custom-call(s32[2]{0:T(128)} %pad_add_fusion.4.x_ref, bf16[16,2,128,128]{3,2,1,0:T(8,128)(2,1)} %get-tuple-element.56.own0, bf16[16,2,128,128]{3,2,1,0:T(8,128)(2,1)} %get-tuple-element.57.own1, bf16[16,2,128,128]{3,2,1,0:T(8,128)(2,1)} %copy-done.4, ...), custom_call_target="tpu_custom_call" | custom-call | bytes 8388608 | tf_op jit(solution)/shard_map/both_halves/pallas_call | solution.py:303
  219.2 36.5 %all_to_all.36 = bf16[32,2,128,128]{3,2,1,0:T(8,128)(2,1)} all-to-all(bf16[32,2,128,128]{3,2,1,0:T(8,128)(2,1)} %bitcast.29), channel_id=1, replica_groups=mesh['half'=2,'x'=4,'core'=2,'group'=8] {'half','core','group'}, dimensions={0} | all-to-all | bytes 4194304 | tf_op jit(solution)/shard_map/all_to_all | solution.py:330
  255.7 4.7 %join_heads.1 = (bf16[128,5120]{1,0:T(8,128)(2,1)}, bf16[128,5120]{1,0:T(8,128)(2,1)}, bf16[128,5120]{1,0:T(8,128)(2,1)}) custom-call(bf16[4,8,128,128]{3,2,1,0:T(8,128)(2,1)} %bitcast.30, bf16[4,8,2,128,128]{4,3,2,1,0:T(8,128)(2,1)} %bitcast.28, bf16[8,3,128,128]{3,2,1,0:T(8,128)(2,1)} %copy-done.2), custom_call_target="tpu_custom_call" | custom-call | bytes 7864320 | tf_op jit(solution)/shard_map/join_heads/pallas_call | solution.py:248
  (43 shorter events, 0.1 us)
Async XLA Ops:
  37.7 4.8 %copy-start = (bf16[8,4,128,128]{3,2,1,0:T(8,128)(2,1)}, bf16[8,4,128,128]{3,2,1,0:T(8,128)(2,1)S(1)}, u32[]{:S(2)}) copy-start(bf16[8,4,128,128]{3,2,1,0:T(8,128)(2,1)S(1)} %all_to_all.35.refs_6_) | copy-start | bytes 3145732
  37.7 30.8 %all-to-all-start.1 = ((bf16[32,128,128]{2,1,0:T(8,128)(2,1)}), bf16[32,128,128]{2,1,0:T(8,128)(2,1)S(1)}, u32[]{:S(2)}, u32[]{:S(2)}) async-start(bf16[32,128,128]{2,1,0:T(8,128)(2,1)} %bitcast.32), calls=%async_computation.1 | async-start | bytes 2097152 | tf_op jit(solution)/shard_map/all_to_all | solution.py:330
  42.6 57.7 %copy-start.3 = (bf16[8,2,128,128]{3,2,1,0:T(8,128)(2,1)}, bf16[8,2,128,128]{3,2,1,0:T(8,128)(2,1)S(1)}, u32[]{:S(2)}) copy-start(bf16[8,2,128,128]{3,2,1,0:T(8,128)(2,1)S(1)} %slice.52.refs_1_) | copy-start | bytes 1572868
  42.6 21.8 %collective-permute-start.3 = (bf16[8,2,128,128]{3,2,1,0:T(8,128)(2,1)S(1)}, bf16[8,2,128,128]{3,2,1,0:T(8,128)(2,1)S(1)}, u32[]{:S(2)}, u32[]{:S(2)}) collective-permute-start(bf16[8,2,128,128]{3,2,1,0:T(8,128)(2,1)S(1)} %slice.52.refs_1_), channel_id=1, source_target_pairs={{0,112},{16,0},{32,16},{48,32},{64,48},{80,64},{96,80},{112,96},{1... | collective-permute-start | bytes 1572872 | tf_op jit(solution)/shard_map/ppermute | solution.py:322
  46.4 20.4 %collective-permute-start.2 = (bf16[8,2,128,128]{3,2,1,0:T(8,128)(2,1)S(1)}, bf16[8,2,128,128]{3,2,1,0:T(8,128)(2,1)S(1)}, u32[]{:S(2)}, u32[]{:S(2)}) collective-permute-start(bf16[8,2,128,128]{3,2,1,0:T(8,128)(2,1)S(1)} %slice.52.refs_1_), channel_id=1, source_target_pairs={{0,16},{16,32},{32,48},{48,64},{64,80},{80,96},{96,112},{112,0},{1... | collective-permute-start | bytes 1572872 | tf_op jit(solution)/shard_map/ppermute | solution.py:322
  64.4 37.3 %copy-start.8 = (bf16[8,2,128,128]{3,2,1,0:T(8,128)(2,1)}, bf16[8,2,128,128]{3,2,1,0:T(8,128)(2,1)S(1)}, u32[]{:S(2)}) copy-start(bf16[8,2,128,128]{3,2,1,0:T(8,128)(2,1)S(1)} %collective-permute-done.3.refs_2_) | copy-start | bytes 1572868
  66.8 1.7 copy-start.9
  68.5 26.1 %copy-start.6 = (bf16[32,128,128]{2,1,0:T(8,128)(2,1)}, bf16[32,128,128]{2,1,0:T(8,128)(2,1)S(1)}, u32[]{:S(2)}) copy-start(bf16[32,128,128]{2,1,0:T(8,128)(2,1)S(1)} %all-to-all-done.1.refs_1_) | copy-start | bytes 3145732
  68.5 23.7 %all-to-all-start.2 = ((bf16[32,128,128]{2,1,0:T(8,128)(2,1)}), bf16[32,128,128]{2,1,0:T(8,128)(2,1)S(1)}, u32[]{:S(2)}, u32[]{:S(2)}) async-start(bf16[32,128,128]{2,1,0:T(8,128)(2,1)} %bitcast.31), calls=%async_computation.2 | async-start | bytes 2097152 | tf_op jit(solution)/shard_map/all_to_all | solution.py:330
  75.5 26.2 %collective-permute-start.1 = (bf16[32,128,128]{2,1,0:T(8,128)(2,1)S(1)}, bf16[32,128,128]{2,1,0:T(8,128)(2,1)}, u32[]{:S(2)}, u32[]{:S(2)}) collective-permute-start(bf16[32,128,128]{2,1,0:T(8,128)(2,1)S(1)} %all-to-all-done.1.refs_1_), channel_id=1, source_target_pairs={{0,48},{16,0},{32,16},{48,32},{1,49},{17,1},{33,17},{49,33},{2,50}... | collective-permute-start | bytes 3145736 | tf_op jit(solution)/shard_map/ppermute | solution.py:322
  77.9 27.4 %collective-permute-start = (bf16[32,128,128]{2,1,0:T(8,128)(2,1)S(1)}, bf16[32,128,128]{2,1,0:T(8,128)(2,1)}, u32[]{:S(2)}, u32[]{:S(2)}) collective-permute-start(bf16[32,128,128]{2,1,0:T(8,128)(2,1)S(1)} %all-to-all-done.1.refs_1_), channel_id=1, source_target_pairs={{0,16},{16,32},{32,48},{48,0},{1,17},{17,33},{33,49},{49,1},{2,18}... | collective-permute-start | bytes 3145736 | tf_op jit(solution)/shard_map/ppermute | solution.py:322
  92.2 2.4 copy-start.7
  92.2 31.1 %collective-permute-start.5 = (bf16[32,128,128]{2,1,0:T(8,128)(2,1)S(1)}, bf16[32,128,128]{2,1,0:T(8,128)(2,1)}, u32[]{:S(2)}, u32[]{:S(2)}) collective-permute-start(bf16[32,128,128]{2,1,0:T(8,128)(2,1)S(1)} %all-to-all-done.2.refs_4_), channel_id=1, source_target_pairs={{0,48},{16,0},{32,16},{48,32},{1,49},{17,1},{33,17},{49,33},{2,50}... | collective-permute-start | bytes 3145736 | tf_op jit(solution)/shard_map/ppermute | solution.py:322
  94.6 32.1 %collective-permute-start.4 = (bf16[32,128,128]{2,1,0:T(8,128)(2,1)S(1)}, bf16[32,128,128]{2,1,0:T(8,128)(2,1)}, u32[]{:S(2)}, u32[]{:S(2)}) collective-permute-start(bf16[32,128,128]{2,1,0:T(8,128)(2,1)S(1)} %all-to-all-done.2.refs_4_), channel_id=1, source_target_pairs={{0,16},{16,32},{32,48},{48,0},{1,17},{17,33},{33,49},{49,1},{2,18}... | collective-permute-start | bytes 3145736 | tf_op jit(solution)/shard_map/ppermute | solution.py:322
  94.6 39.4 %all-to-all-start.3 = ((bf16[32,2,128,128]{3,2,1,0:T(8,128)(2,1)}), bf16[32,2,128,128]{3,2,1,0:T(8,128)(2,1)}, u32[]{:S(2)}, u32[]{:S(2)}) async-start(bf16[32,2,128,128]{3,2,1,0:T(8,128)(2,1)} %bitcast.8), calls=%async_computation.3 | async-start | bytes 4194304 | tf_op jit(solution)/shard_map/all_to_all | solution.py:330
  100.3 7.0 %collective-permute-start.7 = (bf16[8,2,128,128]{3,2,1,0:T(8,128)(2,1)S(1)}, bf16[8,2,128,128]{3,2,1,0:T(8,128)(2,1)}, u32[]{:S(2)}, u32[]{:S(2)}) collective-permute-start(bf16[8,2,128,128]{3,2,1,0:T(8,128)(2,1)S(1)} %slice.52.refs_1_), channel_id=1, source_target_pairs={{0,8},{8,0},{1,9},{9,1},{2,10},{10,2},{3,11},{11,3},{4,12},{12,4},... | collective-permute-start | bytes 1572872 | tf_op jit(solution)/shard_map/ppermute | solution.py:338
  101.7 5.6 %collective-permute-start.8 = (bf16[8,2,128,128]{3,2,1,0:T(8,128)(2,1)S(1)}, bf16[8,2,128,128]{3,2,1,0:T(8,128)(2,1)}, u32[]{:S(2)}, u32[]{:S(2)}) collective-permute-start(bf16[8,2,128,128]{3,2,1,0:T(8,128)(2,1)S(1)} %collective-permute-done.3.refs_2_), channel_id=1, source_target_pairs={{0,8},{8,0},{1,9},{9,1},{2,10},{10,2},{3,11},{11,3},{4,12},{12,4},... | collective-permute-start | bytes 1572872 | tf_op jit(solution)/shard_map/ppermute | solution.py:338
  105.3 2.1 collective-permute-start.6
  107.4 0.8 copy-start.12
  126.7 5.0 %copy-start.11 = (bf16[8,2,128,128]{3,2,1,0:T(8,128)(2,1)S(1)}, bf16[8,2,128,128]{3,2,1,0:T(8,128)(2,1)}, u32[]{:S(2)}) copy-start(bf16[8,2,128,128]{3,2,1,0:T(8,128)(2,1)} %get-tuple-element.48) | copy-start | bytes 1572868
  129.0 2.8 %copy-start.10 = (bf16[8,2,128,128]{3,2,1,0:T(8,128)(2,1)S(1)}, bf16[8,2,128,128]{3,2,1,0:T(8,128)(2,1)}, u32[]{:S(2)}) copy-start(bf16[8,2,128,128]{3,2,1,0:T(8,128)(2,1)} %get-tuple-element.47) | copy-start | bytes 1572868
  129.0 2.6 %collective-permute-start.11 = (bf16[8,2,128,128]{3,2,1,0:T(8,128)(2,1)S(1)}, bf16[8,2,128,128]{3,2,1,0:T(8,128)(2,1)S(1)}, u32[]{:S(2)}, u32[]{:S(2)}) collective-permute-start(bf16[8,2,128,128]{3,2,1,0:T(8,128)(2,1)S(1)} %get-tuple-element.61), channel_id=1, source_target_pairs={{0,8},{8,0},{1,9},{9,1},{2,10},{10,2},{3,11},{11,3},{4,12},{12,4},... | collective-permute-start | bytes 1572872 | tf_op jit(solution)/shard_map/ppermute | solution.py:338
  129.0 2.8 %collective-permute-start.10 = (bf16[8,2,128,128]{3,2,1,0:T(8,128)(2,1)S(1)}, bf16[8,2,128,128]{3,2,1,0:T(8,128)(2,1)S(1)}, u32[]{:S(2)}, u32[]{:S(2)}) collective-permute-start(bf16[8,2,128,128]{3,2,1,0:T(8,128)(2,1)S(1)} %get-tuple-element.62), channel_id=1, source_target_pairs={{0,8},{8,0},{1,9},{9,1},{2,10},{10,2},{3,11},{11,3},{4,12},{12,4},... | collective-permute-start | bytes 1572872 | tf_op jit(solution)/shard_map/ppermute | solution.py:338
  131.5 24.2 %collective-permute-start.9 = (bf16[8,2,128,128]{3,2,1,0:T(8,128)(2,1)}, bf16[8,2,128,128]{3,2,1,0:T(8,128)(2,1)}, u32[]{:S(2)}, u32[]{:S(2)}) collective-permute-start(bf16[8,2,128,128]{3,2,1,0:T(8,128)(2,1)} %get-tuple-element.63), channel_id=1, source_target_pairs={{0,8},{8,0},{1,9},{9,1},{2,10},{10,2},{3,11},{11,3},{4,12},{12,4},... | collective-permute-start | bytes 1572872 | tf_op jit(solution)/shard_map/ppermute | solution.py:338
  131.9 23.8 %collective-permute-start.12 = (bf16[8,2,128,128]{3,2,1,0:T(8,128)(2,1)S(1)}, bf16[8,2,128,128]{3,2,1,0:T(8,128)(2,1)}, u32[]{:S(2)}, u32[]{:S(2)}) collective-permute-start(bf16[8,2,128,128]{3,2,1,0:T(8,128)(2,1)S(1)} %add_convert_fusion.1), channel_id=1, source_target_pairs={{0,112},{16,0},{32,16},{48,32},{64,48},{80,64},{96,80},{112,96},{1... | collective-permute-start | bytes 1572872 | tf_op jit(solution)/shard_map/ppermute | solution.py:322
  133.2 22.5 %collective-permute-start.13 = (bf16[8,2,128,128]{3,2,1,0:T(8,128)(2,1)S(1)}, bf16[8,2,128,128]{3,2,1,0:T(8,128)(2,1)}, u32[]{:S(2)}, u32[]{:S(2)}) collective-permute-start(bf16[8,2,128,128]{3,2,1,0:T(8,128)(2,1)S(1)} %add_convert_fusion), channel_id=1, source_target_pairs={{0,16},{16,32},{32,48},{48,64},{64,80},{80,96},{96,112},{112,0},{1... | collective-permute-start | bytes 1572872 | tf_op jit(solution)/shard_map/ppermute | solution.py:322
  153.2 41.2 %collective-permute-start.14 = (bf16[16,2,128,128]{3,2,1,0:T(8,128)(2,1)}, bf16[16,2,128,128]{3,2,1,0:T(8,128)(2,1)S(1)}, u32[]{:S(2)}, u32[]{:S(2)}) collective-permute-start(bf16[16,2,128,128]{3,2,1,0:T(8,128)(2,1)} %get-tuple-element.53), channel_id=1, source_target_pairs={{0,48},{16,0},{32,16},{48,32},{1,49},{17,1},{33,17},{49,33},{2,50}... | collective-permute-start | bytes 3145736 | tf_op jit(solution)/shard_map/ppermute | solution.py:322
  155.7 38.7 %collective-permute-start.15 = (bf16[16,2,128,128]{3,2,1,0:T(8,128)(2,1)}, bf16[16,2,128,128]{3,2,1,0:T(8,128)(2,1)S(1)}, u32[]{:S(2)}, u32[]{:S(2)}) collective-permute-start(bf16[16,2,128,128]{3,2,1,0:T(8,128)(2,1)} %get-tuple-element.54), channel_id=1, source_target_pairs={{0,16},{16,32},{32,48},{48,0},{1,17},{17,33},{33,49},{49,1},{2,18}... | collective-permute-start | bytes 3145736 | tf_op jit(solution)/shard_map/ppermute | solution.py:322
  158.3 36.2 %all-to-all-start.4 = ((bf16[8,3,128,128]{3,2,1,0:T(8,128)(2,1)}), bf16[8,3,128,128]{3,2,1,0:T(8,128)(2,1)S(1)}, u32[]{:S(2)}, u32[]{:S(2)}) async-start(bf16[8,3,128,128]{3,2,1,0:T(8,128)(2,1)} %total_grads.1), calls=%async_computation.4 | async-start | bytes 1572864 | tf_op jit(solution)/shard_map/all_to_all | solution.py:330
  168.7 23.6 %copy-start.13 = (bf16[16,128,128]{2,1,0:T(8,128)(2,1)S(1)}, bf16[16,128,128]{2,1,0:T(8,128)(2,1)}, u32[]{:S(2)}) copy-start(bf16[16,128,128]{2,1,0:T(8,128)(2,1)} %get-tuple-element.40) | copy-start | bytes 1572868
  188.0 22.7 %collective-permute-start.16 = (bf16[16,2,128,128]{3,2,1,0:T(8,128)(2,1)}, bf16[16,2,128,128]{3,2,1,0:T(8,128)(2,1)}, u32[]{:S(2)}, u32[]{:S(2)}) collective-permute-start(bf16[16,2,128,128]{3,2,1,0:T(8,128)(2,1)} %get-tuple-element.58), channel_id=1, source_target_pairs={{0,48},{16,0},{32,16},{48,32},{1,49},{17,1},{33,17},{49,33},{2,50}... | collective-permute-start | bytes 3145736 | tf_op jit(solution)/shard_map/ppermute | solution.py:322
  192.3 21.9 %collective-permute-start.17 = (bf16[16,2,128,128]{3,2,1,0:T(8,128)(2,1)}, bf16[16,2,128,128]{3,2,1,0:T(8,128)(2,1)}, u32[]{:S(2)}, u32[]{:S(2)}) collective-permute-start(bf16[16,2,128,128]{3,2,1,0:T(8,128)(2,1)} %get-tuple-element.59), channel_id=1, source_target_pairs={{0,16},{16,32},{32,48},{48,0},{1,17},{17,33},{33,49},{49,1},{2,18}... | collective-permute-start | bytes 3145736 | tf_op jit(solution)/shard_map/ppermute | solution.py:322
  194.4 24.8 %copy-start.2 = (bf16[8,3,128,128]{3,2,1,0:T(8,128)(2,1)}, bf16[8,3,128,128]{3,2,1,0:T(8,128)(2,1)S(1)}, u32[]{:S(2)}) copy-start(bf16[8,3,128,128]{3,2,1,0:T(8,128)(2,1)S(1)} %all-to-all-done.4.b_ref) | copy-start | bytes 2359300
  194.4 19.8 %copy-start.4 = (bf16[16,2,128,128]{3,2,1,0:T(8,128)(2,1)}, bf16[16,2,128,128]{3,2,1,0:T(8,128)(2,1)S(1)}, u32[]{:S(2)}) copy-start(bf16[16,2,128,128]{3,2,1,0:T(8,128)(2,1)S(1)} %collective-permute-done.14.right0) | copy-start | bytes 3145732
  194.5 1.1 copy-start.5
  195.5 23.7 %all-to-all-start.5 = ((bf16[32,128,128]{2,1,0:T(8,128)(2,1)}), bf16[32,128,128]{2,1,0:T(8,128)(2,1)S(1)}, u32[]{:S(2)}, u32[]{:S(2)}) async-start(bf16[32,128,128]{2,1,0:T(8,128)(2,1)} %pad_maximum_fusion), calls=%async_computation.5 | async-start | bytes 2097152 | tf_op jit(solution)/shard_map/all_to_all | solution.py:330
  219.2 36.5 %copy-start.1 = (bf16[32,128,128]{2,1,0:T(8,128)(2,1)}, bf16[32,128,128]{2,1,0:T(8,128)(2,1)S(1)}, u32[]{:S(2)}) copy-start(bf16[32,128,128]{2,1,0:T(8,128)(2,1)S(1)} %all-to-all-done.5) | copy-start | bytes 3145732

commit v10 on v9

--- a/solution.py
+++ b/solution.py
@@ -89,7 +89,7 @@
     shared = n_query < size
     qd_in, dq_out, targets = refs[0], refs[1], refs[2:5]
     if shared:
-        give_out, refs = refs[5], refs[1:]
+        give_out, refs = refs[5:8], refs[3:]
     kv, qd, acc, stage, dq, kv_cat, sd_scr, x_cat, order, in_sem, out_sem = refs[5:]
     copies = []
     for source, fetch in zip(sources, fetches):
@@ -150,7 +150,7 @@
             give = pl.multiple_of(i * size + n_query - place_ref[1], 8)
             rows = pl.ds(keep, n_query)
             puts.append(
-                pltpu.make_async_copy(stage.at[pl.ds(give, n_query)], give_out.at[i], out_sem.at[4 + i])
+                pltpu.make_async_copy(stage.at[pl.ds(give, n_query)], give_out[i], out_sem.at[4 + i])
             )
             puts[-1].start()
         puts.append(pltpu.make_async_copy(stage.at[rows], target, out_sem.at[i]))
@@ -163,7 +163,7 @@
     window = 3 * size
     shared = n_query < size
     kept = jax.ShapeDtypeStruct((n_query, 2, BLK, HD), BF16)
-    given = [jax.ShapeDtypeStruct((3, n_query, 2, BLK, HD), BF16)] if shared else []
+    given = [kept] * 3 if shared else []
     smem = pl.BlockSpec(memory_space=pltpu.SMEM)
     hbm = pl.BlockSpec(memory_space=pl.ANY)
     pairs = n_query * 8
@@ -196,71 +196,99 @@
     return out[0], out[1:]
 
 
-def split_kernel(k_ref, v_ref, q_ref, g_ref, ka_ref, va_ref, qda_ref, b_ref):
+def split_kernel(k_ref, v_ref, q_ref, g_ref, ka_ref, va_ref, qda_ref):
     for j in range(ka_ref.shape[1]):
-
-        def head(ref, m):
-            return ref[:, (j * HPG + m) * HD : (j * HPG + m + 1) * HD]
-
         for m in range(4):
-            ka_ref[m, j] = head(k_ref, m)
-            va_ref[m, j] = head(v_ref, m)
-            qda_ref[m, j, 0] = head(q_ref, m)
-            qda_ref[m, j, 1] = head(g_ref, m)
-        for t, ref in enumerate((k_ref, v_ref, q_ref, g_ref)):
-            b_ref[j, t] = head(ref, 4)
+            cols = slice((j * HPG + m) * HD, (j * HPG + m + 1) * HD)
+            ka_ref[m, j] = k_ref[:, cols]
+            va_ref[m, j] = v_ref[:, cols]
+            qda_ref[m, j, 0] = q_ref[:, cols]
+            qda_ref[m, j, 1] = g_ref[:, cols]
 
 
 def split_heads(key_in, value_in, query_in, out_grad):
     groups, step = key_in.shape[1] // (HPG * HD), 2
     one = pl.BlockSpec((4, step, BLK, HD), lambda j: (0, j, 0, 0))
     two = pl.BlockSpec((4, step, 2, BLK, HD), lambda j: (0, j, 0, 0, 0))
-    four = pl.BlockSpec((step, 4, BLK, HD), lambda j: (j, 0, 0, 0))
-    shapes = ((4, groups), (4, groups), (4, groups, 2), (groups, 4))
-    ka, va, qda, b = pl.pallas_call(
+    shapes = ((4, groups), (4, groups), (4, groups, 2))
+    ka, va, qda = pl.pallas_call(
         split_kernel,
         grid=(groups // step,),
         out_shape=tuple(jax.ShapeDtypeStruct((*x, BLK, HD), BF16) for x in shapes),
         in_specs=[pl.BlockSpec((BLK, step * HPG * HD), lambda j: (0, j))] * 4,
-        out_specs=(one, one, two, four),
+        out_specs=(one, one, two),
         compiler_params=pltpu.CompilerParams(vmem_limit_bytes=VMEM_LIMIT),
         cost_estimate=pl.CostEstimate(flops=0, bytes_accessed=16 * key_in.size, transcendentals=0),
         name="split_heads",
     )(key_in, value_in, query_in, out_grad)
     flat = 4 * groups
-    return ka.reshape(flat, BLK, HD), va.reshape(flat, BLK, HD), qda.reshape(flat, 2, BLK, HD), b
-
-
-def join_kernel(dqa_ref, dkva_ref, b_ref, *outs):
+    return ka.reshape(flat, BLK, HD), va.reshape(flat, BLK, HD), qda.reshape(flat, 2, BLK, HD)
+
+
+def fifth_kernel(k_ref, v_ref, q_ref, g_ref, out_ref, held, sem_in, sem_out):
+    groups = out_ref.shape[0]
+    fetches, puts = [], []
+    for j in range(groups):
+        cols = pl.ds((j * HPG + HPG - 1) * HD, HD)
+        for t, ref in enumerate((k_ref, v_ref, q_ref, g_ref)):
+            fetches.append(pltpu.make_async_copy(ref.at[:, cols], held.at[j, t], sem_in.at[j, t]))
+            fetches[-1].start()
+    for j in range(groups):
+        for t in range(4):
+            fetches[4 * j + t].wait()
+        puts.append(pltpu.make_async_copy(held.at[j], out_ref.at[j], sem_out.at[j]))
+        puts[-1].start()
+    for put in puts:
+        put.wait()
+
+
+def fifth_heads(*arrays):
+    groups = arrays[0].shape[1] // (HPG * HD)
+    hbm = pl.BlockSpec(memory_space=pl.ANY)
+    return pl.pallas_call(
+        fifth_kernel,
+        out_shape=jax.ShapeDtypeStruct((groups, 4, BLK, HD), BF16),
+        in_specs=[hbm] * 4,
+        out_specs=hbm,
+        scratch_shapes=[
+            pltpu.VMEM((groups, 4, BLK, HD), BF16),
+            pltpu.SemaphoreType.DMA((groups, 4)),
+            pltpu.SemaphoreType.DMA((groups,)),
+        ],
+        compiler_params=pltpu.CompilerParams(vmem_limit_bytes=VMEM_LIMIT),
+        cost_estimate=pl.CostEstimate(
+            flops=0, bytes_accessed=groups * 16 * BLK * HD, transcendentals=0
+        ),
+        name="fifth_heads",
+    )(*arrays)
+
+
+def join_kernel(first, a_ref, b_ref, *outs):
     for t, ref in enumerate(outs):
         for j in range(b_ref.shape[0]):
             for m in range(HPG):
-                if m == 4:
-                    value = b_ref[j, t]
-                else:
-                    value = dqa_ref[m, j] if t == 0 else dkva_ref[m, j, t - 1]
+                value = b_ref[j, first + t] if m == 4 else a_ref[m, j, t]
                 ref[:, (j * HPG + m) * HD : (j * HPG + m + 1) * HD] = value
 
 
-def join_heads(dqa, dkva, back_b):
-    groups, step = back_b.shape[0], 2
+def join_heads(back_a, back_b, first):
+    groups, step, n = back_b.shape[0], 2, back_a.shape[1]
     out = jax.ShapeDtypeStruct((BLK, groups * HPG * HD), BF16)
     return pl.pallas_call(
-        join_kernel,
+        functools.partial(join_kernel, first),
         grid=(groups // step,),
-        out_shape=(out,) * 3,
+        out_shape=(out,) * n,
         in_specs=[
-            pl.BlockSpec((4, step, BLK, HD), lambda j: (0, j, 0, 0)),
-            pl.BlockSpec((4, step, 2, BLK, HD), lambda j: (0, j, 0, 0, 0)),
+            pl.BlockSpec((4, step, n, BLK, HD), lambda j: (0, j, 0, 0, 0)),
             pl.BlockSpec((step, 3, BLK, HD), lambda j: (j, 0, 0, 0)),
         ],
-        out_specs=(pl.BlockSpec((BLK, step * HPG * HD), lambda j: (0, j)),) * 3,
+        out_specs=(pl.BlockSpec((BLK, step * HPG * HD), lambda j: (0, j)),) * n,
         compiler_params=pltpu.CompilerParams(vmem_limit_bytes=VMEM_LIMIT),
         cost_estimate=pl.CostEstimate(
-            flops=0, bytes_accessed=groups * HPG * 3 * BLK * HD * 4, transcendentals=0
+            flops=0, bytes_accessed=groups * HPG * n * BLK * HD * 4, transcendentals=0
         ),
         name="join_heads",
-    )(dqa.reshape(4, groups, BLK, HD), dkva.reshape(4, groups, 2, BLK, HD), back_b)
+    )(back_a.reshape(4, groups, n, BLK, HD), back_b)
 
 
 def total_kernel(dq_ref, own_ref, *refs):
@@ -319,7 +347,8 @@
 
 def shift(value, axes, steps):
     count = lax.axis_size(axes)
-    return lax.ppermute(value, axes, [(s, (s + steps) % count) for s in range(count)])
+    ends = range(count) if axes == "x" else range(max(0, -steps), min(count, count - steps))
+    return lax.ppermute(value, axes, [(s, (s + steps) % count) for s in ends])
 
 
 def add(a, b):
@@ -342,22 +371,23 @@
     half, x, core = (lax.axis_index(name) for name in ("half", "x", "core"))
     last, size = lax.axis_size("x") - 1, 2 * BPD
     packed = jnp.concatenate([key_blocks, block_count[:, :, None]], axis=2)
-    gathered = lax.all_gather(packed, ("half", "core"))
+    b = fifth_heads(key_in, value_in, query_in, out_grad)
+    gathered = lax.all_gather(after(packed, b), ("half", "core"))
     list_b = gathered[2 * half + core, 4]
     lists = lax.dynamic_index_in_dim(gathered, 2 * half + core, 1, False)
-    ka, va, qda, b = split_heads(key_in, value_in, query_in, out_grad)
+    ka, va, qda = split_heads(*lax.optimization_barrier((key_in, value_in, query_in, out_grad, b))[:4])
 
     def plain(lists, chip):
         lists = lists.reshape(-1, MAXK + 1)
         first_block = (chip - 1) * 2 * BPD
         return (lists[:, :MAXK] - first_block).reshape(-1), lists[:, MAXK]
 
-    own_b = exchange(after(b, gathered), "group")
+    own_b = exchange(b, "group")
     pairs_b = own_b[:, :2]
     mine = (shift(pairs_b, CHIPS, 1), pairs_b, shift(pairs_b, CHIPS, -1))
     theirs = tuple(swap(pairs) for pairs in mine)
 
-    keys = exchange(after(ka, own_b), WIDE)
+    keys = exchange(after(ka, own_b, gathered), WIDE)
     key_near = [shift(keys, "x", 1), shift(keys, "x", -1)]
     values = exchange(after(va, keys, *mine), WIDE)
     value_near = [shift(values, "x", 1), shift(values, "x", -1)]
@@ -372,11 +402,10 @@
     ids, counts = plain(list_b, half * (last + 1) + x)
     place = jnp.stack([jnp.int32(0), core * BPD])
     fetches = [run(i, other) for other in range(2) for i in range(3)]
-    dq_b, (left_b, mine_b, right_b, give_b) = attention(
+    dq_b, (left_b, mine_b, right_b, *give_b) = attention(
         ids, counts, place, mine + theirs, fetches, after(own_b, values, *key_near), BPD, size
     )
-    give_b = after(give_b, *value_near)
-    got_b = [swap(give_b[i]) for i in range(3)]
+    got_b = [swap(after(give, *value_near)) for give in give_b]
     out_b = lax.optimization_barrier((add(left_b, got_b[0]), add(right_b, got_b[2])))
     terms_b = [got_b[1], shift(out_b[0], CHIPS, -1), shift(out_b[1], CHIPS, 1)]
 
@@ -402,7 +431,7 @@
     dqa = exchange(after(jnp.concatenate([d[0] for d in done]), *done[0][2:], back_b), WIDE)
     dkva = both_halves(x, last, [d[1][1] for d in done], [d[2] for d in done], [d[3] for d in done])
     dkva = exchange(after(dkva, dqa), WIDE)
-    return tuple(join_heads(dqa, dkva, back_b))
+    return (*join_heads(dqa[:, None], back_b, 0), *join_heads(dkva, back_b, 1))
 
 
 def solution(mesh):

time: 261 us -> 259 us (level)
  blocking collectives: 66.6 us -> 7.05 us
  starting transfers between devices: 50 us -> 83.1 us
  waiting for transfers between devices: 61.9 us -> 79.4 us
  Pallas kernels: 66.4 us -> 70.5 us
    all_to_all x2 -> x0, blocking collectives: 61.3 us -> none  [exchange(): return lax.all_to_all(x, axes, 0, 0, tiled=True)]
    all_to_all x5 -> x7, waiting for transfers between devices: 16 us -> 43.8 us  [exchange(): return lax.all_to_all(x, axes, 0, 0, tiled=True)]
    all_to_all x5 -> x7, starting transfers between devices: 31.7 us -> 58 us  [exchange(): return lax.all_to_all(x, axes, 0, 0, tiled=True)]
    ppermute x12, waiting for transfers between devices: 45.7 us -> 35.5 us  [shift(): return lax.ppermute(value, axes, [(s, (s + steps) % count) for s in ends])]
    ppermute x12, starting transfers between devices: 17.5 us -> 24.3 us  [shift(): return lax.ppermute(value, axes, [(s, (s + steps) % count) for s in ends])]
    pallas_call x1 -> x3, Pallas kernels: 4.69 us -> 9.94 us  [the longest x2 7.73 us: join_heads(): pl.pallas_call(functools.partial(join_kernel, first), grid=(groups // ste...]
    unnamed x30 -> x36, local copies, waits for them, and re-layouts: 3.14 us -> 6.28 us
  transfers between devices with their start and end apart: 23 -> 25, of which waited for: 11 -> 13; matrix products, arithmetic and copies ran while one was open for 4% -> 4% of each run, Pallas kernels for 22% -> 25%
where the time goes in v10:
time: 259 us; the launch traced here: 257 us
  starting transfers between devices  83.1 us (32%)
  waiting for transfers between devices  79.4 us (31%)
  Pallas kernels  70.5 us (27%)
  local copies, waits for them, and re-layouts  9.3 us (4%)
  blocking collectives  7.05 us (3%)
  other arithmetic  6.86 us (3%)
    all_to_all x7, starting transfers between devices, exchange(): return lax.all_to_all(x, axes, 0, 0, tiled=True)  58 us
    pallas_call x3, Pallas kernels, attention(): pl.pallas_call(functools.partial(attention_kernel, size, n_query, fetches...  48 us
    all_to_all x7, waiting for transfers between devices, exchange(): return lax.all_to_all(x, axes, 0, 0, tiled=True)  43.8 us
    ppermute x12, waiting for transfers between devices, shift(): return lax.ppermute(value, axes, [(s, (s + steps) % count) for s in ends])  35.5 us
    ppermute x12, starting transfers between devices, shift(): return lax.ppermute(value, axes, [(s, (s + steps) % count) for s in ends])  24.3 us
    pallas_call x2, Pallas kernels, join_heads(): pl.pallas_call(functools.partial(join_kernel, first), grid=(groups // ste...  7.73 us
    all_gather x1, blocking collectives, shards(): gathered = lax.all_gather(after(packed, b), ('half', 'core'))  7.05 us
    unnamed x36, local copies, waits for them, and re-layouts  6.28 us
  transfers between devices with their start and end apart: 25, of which 13 were waited for; matrix products, arithmetic and copies ran while one was open for 4% of the time, Pallas kernels for 25%

profile of v10, /device:TPU:8, one launch (start us, length us, event | category | flops | bytes accessed | tf_op | source)
XLA Modules:
  0.0 257.1 jit_solution(14298059665573551847)
XLA Ops:
  0.6 2.2 fifth_heads.1
  2.8 0.0 copy-start.16
  2.9 0.0 copy-start.15
  2.9 8.2 %all-to-all-start = ((bf16[8,4,128,128]{3,2,1,0:T(8,128)(2,1)}), bf16[8,4,128,128]{3,2,1,0:T(8,128)(2,1)S(1)}, u32[]{:S(2)}, u32[]{:S(2)}) async-start(bf16[8,4,128,128]{3,2,1,0:T(8,128)(2,1)} %fifth_heads.1), calls=%async_computation | async-start | bytes 2097152 | tf_op jit(solution)/shard_map/all_to_all | solution.py:359
  11.1 0.1 copy.15
  11.2 0.1 pad_add_fusion
  11.3 5.1 %split_heads.1 = (bf16[4,8,128,128]{3,2,1,0:T(8,128)(2,1)}, bf16[4,8,128,128]{3,2,1,0:T(8,128)(2,1)}, bf16[4,8,2,128,128]{4,3,2,1,0:T(8,128)(2,1)}) custom-call(bf16[128,5120]{1,0:T(8,128)(2,1)} %k_ref.2, bf16[128,5120]{1,0:T(8,128)(2,1)} %v_ref.2, bf16[128,5120]{1,0:T(8,128)(2,1)} %q_ref.2, bf16[128,5120]{1,0:T(8,128)(2,1)} %g_ref.2), custom_call_target="tpu_custom_call" | custom-call | bytes 10485760 | tf_op jit(solution)/shard_map/split_heads/pallas_call | solution.py:214
  16.4 7.1 %all-gather = s32[20,8,13]{2,1,0:T(8,128)S(1)} all-gather(s32[5,8,13]{2,1,0:T(8,128)S(1)} %pad_add_fusion), channel_id=2, replica_groups=mesh['half'=2,'x'=4,'core'=2,'group'=8] {'half','core'}, dimensions={0}, use_global_device_ids=true | all-gather | bytes 10400 | tf_op jit(solution)/shard_map/all_gather | solution.py:375
  23.5 3.7 %all-to-all-done.refs_6_ = bf16[8,4,128,128]{3,2,1,0:T(8,128)(2,1)S(1)} async-done(((bf16[8,4,128,128]{3,2,1,0:T(8,128)(2,1)}), bf16[8,4,128,128]{3,2,1,0:T(8,128)(2,1)S(1)}, u32[]{:S(2)}, u32[]{:S(2)}) %all-to-all-start) | async-done | bytes 1048608 | tf_op jit(solution)/shard_map/all_to_all | solution.py:359
  27.1 5.8 %all-to-all-start.1 = ((bf16[32,128,128]{2,1,0:T(8,128)(2,1)}), bf16[32,128,128]{2,1,0:T(8,128)(2,1)S(1)}, u32[]{:S(2)}, u32[]{:S(2)}) async-start(bf16[32,128,128]{2,1,0:T(8,128)(2,1)} %bitcast.26), calls=%async_computation.1 | async-start | bytes 2097152 | tf_op jit(solution)/shard_map/all_to_all | solution.py:359
  33.0 1.3 collective-permute-start.3
  34.3 4.6 %collective-permute-start.2 = (bf16[8,2,128,128]{3,2,1,0:T(8,128)(2,1)S(1)}, bf16[8,2,128,128]{3,2,1,0:T(8,128)(2,1)S(1)}, u32[]{:S(2)}, u32[]{:S(2)}) collective-permute-start(bf16[8,2,128,128]{3,2,1,0:T(8,128)(2,1)S(1)} %slice.40.refs_1_), channel_id=1, source_target_pairs={{0,16},{16,32},{32,48},{48,64},{64,80},{80,96},{96,112},{1,17},{17... | collective-permute-start | bytes 1572872 | tf_op jit(solution)/shard_map/ppermute | solution.py:351
  38.9 10.0 %collective-permute-done.3.refs_2_ = bf16[8,2,128,128]{3,2,1,0:T(8,128)(2,1)S(1)} collective-permute-done((bf16[8,2,128,128]{3,2,1,0:T(8,128)(2,1)S(1)}, bf16[8,2,128,128]{3,2,1,0:T(8,128)(2,1)S(1)}, u32[]{:S(2)}, u32[]{:S(2)}) %collective-permute-start.3) | collective-permute-done | bytes 524320 | tf_op jit(solution)/shard_map/ppermute | solution.py:351
  48.9 1.2 collective-permute-done.2.refs_0_
  50.1 0.9 all-to-all-done.1.refs_1_
  51.0 14.6 %all-to-all-start.2 = ((bf16[32,128,128]{2,1,0:T(8,128)(2,1)}), bf16[32,128,128]{2,1,0:T(8,128)(2,1)S(1)}, u32[]{:S(2)}, u32[]{:S(2)}) async-start(bf16[32,128,128]{2,1,0:T(8,128)(2,1)} %bitcast.25), calls=%async_computation.2 | async-start | bytes 2097152 | tf_op jit(solution)/shard_map/all_to_all | solution.py:359
  65.6 3.1 %collective-permute-start.1 = (bf16[32,128,128]{2,1,0:T(8,128)(2,1)S(1)}, bf16[32,128,128]{2,1,0:T(8,128)(2,1)}, u32[]{:S(2)}, u32[]{:S(2)}) collective-permute-start(bf16[32,128,128]{2,1,0:T(8,128)(2,1)S(1)} %all-to-all-done.1.refs_1_), channel_id=1, source_target_pairs={{0,48},{16,0},{32,16},{48,32},{1,49},{17,1},{33,17},{49,33},{2,50}... | collective-permute-start | bytes 3145736 | tf_op jit(solution)/shard_map/ppermute | solution.py:351
  68.6 13.7 %all-to-all-done.2.refs_4_ = bf16[32,128,128]{2,1,0:T(8,128)(2,1)S(1)} async-done(((bf16[32,128,128]{2,1,0:T(8,128)(2,1)}), bf16[32,128,128]{2,1,0:T(8,128)(2,1)S(1)}, u32[]{:S(2)}, u32[]{:S(2)}) %all-to-all-start.2) | async-done | bytes 1048608 | tf_op jit(solution)/shard_map/all_to_all | solution.py:359
  82.3 3.0 %collective-permute-start.5 = (bf16[32,128,128]{2,1,0:T(8,128)(2,1)S(1)}, bf16[32,128,128]{2,1,0:T(8,128)(2,1)}, u32[]{:S(2)}, u32[]{:S(2)}) collective-permute-start(bf16[32,128,128]{2,1,0:T(8,128)(2,1)S(1)} %all-to-all-done.2.refs_4_), channel_id=1, source_target_pairs={{0,48},{16,0},{32,16},{48,32},{1,49},{17,1},{33,17},{49,33},{2,50}... | collective-permute-start | bytes 3145736 | tf_op jit(solution)/shard_map/ppermute | solution.py:351
  85.3 5.6 %all-to-all-start.3 = ((bf16[32,2,128,128]{3,2,1,0:T(8,128)(2,1)}), bf16[32,2,128,128]{3,2,1,0:T(8,128)(2,1)}, u32[]{:S(2)}, u32[]{:S(2)}) async-start(bf16[32,2,128,128]{3,2,1,0:T(8,128)(2,1)} %bitcast.8), calls=%async_computation.3 | async-start | bytes 4194304 | tf_op jit(solution)/shard_map/all_to_all | solution.py:359
  91.0 0.2 collective-permute-start.7
  91.2 0.9 collective-permute-done.1.refs_2_
  92.2 3.8 %collective-permute-done.refs_0_ = bf16[32,128,128]{2,1,0:T(8,128)(2,1)} collective-permute-done((bf16[32,128,128]{2,1,0:T(8,128)(2,1)S(1)}, bf16[32,128,128]{2,1,0:T(8,128)(2,1)}, u32[]{:S(2)}, u32[]{:S(2)}) %collective-permute-start) | collective-permute-done | bytes 1048608 | tf_op jit(solution)/shard_map/ppermute | solution.py:351
  96.0 0.7 reshape.47.ids_ref
  96.7 0.6 pad_add_fusion.3.place_ref
  97.3 0.7 slice_reduce_fusion.cnt_ref
  98.0 0.1 collective-permute-done.6.refs_3_
  98.1 0.8 copy-done.12
  98.9 11.8 %attention.4 = (bf16[8,128,128]{2,1,0:T(8,128)(2,1)}, bf16[8,2,128,128]{3,2,1,0:T(8,128)(2,1)}, bf16[8,2,128,128]{3,2,1,0:T(8,128)(2,1)}, bf16[8,2,128,128]{3,2,...) custom-call(s32[96]{0:T(128)} %reshape.47.ids_ref, ...), custom_call_target="tpu_custom_call" | custom-call | tf_op jit(solution)/shard_map/attention/pallas_call | solution.py:170
  110.7 3.2 %collective-permute-done.5.refs_5_ = bf16[32,128,128]{2,1,0:T(8,128)(2,1)} collective-permute-done((bf16[32,128,128]{2,1,0:T(8,128)(2,1)S(1)}, bf16[32,128,128]{2,1,0:T(8,128)(2,1)}, u32[]{:S(2)}, u32[]{:S(2)}) %collective-permute-start.5) | collective-permute-done | bytes 1048608 | tf_op jit(solution)/shard_map/ppermute | solution.py:351
  113.8 3.5 %collective-permute-done.4.refs_3_ = bf16[32,128,128]{2,1,0:T(8,128)(2,1)} collective-permute-done((bf16[32,128,128]{2,1,0:T(8,128)(2,1)S(1)}, bf16[32,128,128]{2,1,0:T(8,128)(2,1)}, u32[]{:S(2)}, u32[]{:S(2)}) %collective-permute-start.4) | collective-permute-done | bytes 1048608 | tf_op jit(solution)/shard_map/ppermute | solution.py:351
  117.3 0.5 collective-permute-start.10
  117.9 0.7 pad_add_fusion.1.place_ref
  118.5 0.1 slice.39
  118.6 0.7 copy.18
  119.3 0.7 reshape.41.ids_ref
  119.9 1.2 add_convert_fusion
  121.1 0.9 add_convert_fusion.1
  122.1 1.3 collective-permute-start.12
  123.4 5.3 %collective-permute-start.13 = (bf16[8,2,128,128]{3,2,1,0:T(8,128)(2,1)S(1)}, bf16[8,2,128,128]{3,2,1,0:T(8,128)(2,1)}, u32[]{:S(2)}, u32[]{:S(2)}) collective-permute-start(bf16[8,2,128,128]{3,2,1,0:T(8,128)(2,1)S(1)} %add_convert_fusion), channel_id=1, source_target_pairs={{0,16},{16,32},{32,48},{48,64},{64,80},{80,96},{96,112},{1,17},{17... | collective-permute-start | bytes 1572872 | tf_op jit(solution)/shard_map/ppermute | solution.py:351
  128.7 18.6 %attention.3 = (bf16[16,128,128]{2,1,0:T(8,128)(2,1)}, bf16[16,2,128,128]{3,2,1,0:T(8,128)(2,1)}, bf16[16,2,128,128]{3,2,1,0:T(8,128)(2,1)}, bf16[16,2,128,128]{3,2,1,0:T(8,128)(2,1)}) custom-call(s32[192]{0:T(256)} %reshape.41.ids_ref, s32[16]{0:T(128)} %bitcast.30, s32[4]{0:T(128)} %pad_add_fusion.1.place_ref, ...), custom_call_target="tpu_custom_call" | custom-call | flops 2684354560 | bytes 7340032 | tf_op jit(solution)/shard_map/attention/pallas_call | solution.py:170
  147.3 2.6 collective-permute-start.14
  149.9 0.8 copy-done.14
  150.6 2.5 total_grads.1
  153.1 6.7 %all-to-all-start.4 = ((bf16[8,3,128,128]{3,2,1,0:T(8,128)(2,1)}), bf16[8,3,128,128]{3,2,1,0:T(8,128)(2,1)S(1)}, u32[]{:S(2)}, u32[]{:S(2)}) async-start(bf16[8,3,128,128]{3,2,1,0:T(8,128)(2,1)} %total_grads.1), calls=%async_computation.4 | async-start | bytes 1572864 | tf_op jit(solution)/shard_map/all_to_all | solution.py:359
  159.9 0.1 slice.42
  160.0 0.7 copy.19
  160.6 0.7 reshape.46.ids_ref
  161.3 0.6 pad_add_fusion.2.place_ref
  161.9 17.7 %attention.5 = (bf16[16,128,128]{2,1,0:T(8,128)(2,1)}, bf16[16,2,128,128]{3,2,1,0:T(8,128)(2,1)}, bf16[16,2,128,128]{3,2,1,0:T(8,128)(2,1)}, bf16[16,2,128,128]{3,2,1,0:T(8,128)(2,1)}) custom-call(s32[192]{0:T(256)} %reshape.46.ids_ref, s32[16]{0:T(128)} %bitcast.31, s32[4]{0:T(128)} %pad_add_fusion.2.place_ref, ...), custom_call_target="tpu_custom_call" | custom-call | flops 2684354560 | bytes 7340032 | tf_op jit(solution)/shard_map/attention/pallas_call | solution.py:170
  179.6 3.2 %collective-permute-start.16 = (bf16[16,2,128,128]{3,2,1,0:T(8,128)(2,1)}, bf16[16,2,128,128]{3,2,1,0:T(8,128)(2,1)}, u32[]{:S(2)}, u32[]{:S(2)}) collective-permute-start(bf16[16,2,128,128]{3,2,1,0:T(8,128)(2,1)} %get-tuple-element.74), channel_id=1, source_target_pairs={{0,48},{16,0},{32,16},{48,32},{1,49},{17,1},{33,17},{49,33},{2,50}... | collective-permute-start | bytes 3145736 | tf_op jit(solution)/shard_map/ppermute | solution.py:351
  182.8 2.1 pad_maximum_fusion
  184.9 1.0 copy-done.6
  186.0 7.8 %all-to-all-start.5 = ((bf16[32,128,128]{2,1,0:T(8,128)(2,1)}), bf16[32,128,128]{2,1,0:T(8,128)(2,1)S(1)}, u32[]{:S(2)}, u32[]{:S(2)}) async-start(bf16[32,128,128]{2,1,0:T(8,128)(2,1)} %pad_maximum_fusion), calls=%async_computation.5 | async-start | bytes 2097152 | tf_op jit(solution)/shard_map/all_to_all | solution.py:359
  193.8 0.7 pad_add_fusion.4.x_ref
  194.4 10.6 %collective-permute-done.16.right1 = bf16[16,2,128,128]{3,2,1,0:T(8,128)(2,1)} collective-permute-done((bf16[16,2,128,128]{3,2,1,0:T(8,128)(2,1)}, bf16[16,2,128,128]{3,2,1,0:T(8,128)(2,1)}, u32[]{:S(2)}, u32[]{:S(2)}) %collective-permute-start.16) | collective-permute-done | bytes 1048608 | tf_op jit(solution)/shard_map/ppermute | solution.py:351
  205.0 2.3 collective-permute-done.17.left1
  207.3 5.0 %both_halves.1 = bf16[2,16,2,128,128]{4,3,2,1,0:T(8,128)(2,1)} custom-call(s32[2]{0:T(128)} %pad_add_fusion.4.x_ref, bf16[16,2,128,128]{3,2,1,0:T(8,128)(2,1)} %get-tuple-element.72.own0, bf16[16,2,128,128]{3,2,1,0:T(8,128)(2,1)} %get-tuple-element.73.own1, bf16[16,2,128,128]{3,2,1,0:T(8,128)(2,1)} %copy-done.5, ...), custom_call_target="tpu_custom_call" | custom-call | bytes 8388608 | tf_op jit(solution)/shard_map/both_halves/pallas_call | solution.py:331
  212.4 1.0 copy-done.3
  213.3 9.2 %all-to-all-start.6 = ((bf16[32,2,128,128]{3,2,1,0:T(8,128)(2,1)}), bf16[32,2,128,128]{3,2,1,0:T(8,128)(2,1)S(1)}, u32[]{:S(2)}, u32[]{:S(2)}) async-start(bf16[32,2,128,128]{3,2,1,0:T(8,128)(2,1)} %bitcast.23), calls=%async_computation.6 | async-start | bytes 4194304 | tf_op jit(solution)/shard_map/all_to_all | solution.py:359
  222.5 3.6 %join_heads.2 = bf16[128,5120]{1,0:T(8,128)(2,1)} custom-call(bf16[4,8,1,128,128]{4,3,2,1,0:T(8,128)(2,1)} %bitcast.24, bf16[8,3,128,128]{3,2,1,0:T(8,128)(2,1)} %copy-done.1), custom_call_target="tpu_custom_call" | custom-call | bytes 2621440 | tf_op jit(solution)/shard_map/join_heads/pallas_call | solution.py:277
  226.2 25.5 %all-to-all-done.6 = bf16[32,2,128,128]{3,2,1,0:T(8,128)(2,1)S(1)} async-done(((bf16[32,2,128,128]{3,2,1,0:T(8,128)(2,1)}), bf16[32,2,128,128]{3,2,1,0:T(8,128)(2,1)S(1)}, u32[]{:S(2)}, u32[]{:S(2)}) %all-to-all-start.6) | async-done | bytes 2097184 | tf_op jit(solution)/shard_map/all_to_all | solution.py:359
  251.7 1.3 copy-done
  253.0 4.1 %join_heads.3 = (bf16[128,5120]{1,0:T(8,128)(2,1)}, bf16[128,5120]{1,0:T(8,128)(2,1)}) custom-call(bf16[4,8,2,128,128]{4,3,2,1,0:T(8,128)(2,1)} %bitcast.22, bf16[8,3,128,128]{3,2,1,0:T(8,128)(2,1)} %copy-done.1), custom_call_target="tpu_custom_call" | custom-call | bytes 5242880 | tf_op jit(solution)/shard_map/join_heads/pallas_call | solution.py:277
  (52 shorter events, 0.2 us)
Async XLA Ops:
  2.8 8.3 %copy-start.16 = (s32[5,8]{1,0:T(8,128)S(1)}, s32[5,8]{1,0:T(8,128)}, u32[]{:S(2)}) copy-start(s32[5,8]{1,0:T(8,128)} %param.11) | copy-start | bytes 484
  2.9 8.4 %copy-start.15 = (s32[5,8,12]{2,1,0:T(8,128)S(1)}, s32[5,8,12]{2,1,0:T(8,128)}, u32[]{:S(2)}) copy-start(s32[5,8,12]{2,1,0:T(8,128)} %param.10) | copy-start | bytes 5764
  2.9 24.3 %all-to-all-start = ((bf16[8,4,128,128]{3,2,1,0:T(8,128)(2,1)}), bf16[8,4,128,128]{3,2,1,0:T(8,128)(2,1)S(1)}, u32[]{:S(2)}, u32[]{:S(2)}) async-start(bf16[8,4,128,128]{3,2,1,0:T(8,128)(2,1)} %fifth_heads.1), calls=%async_computation | async-start | bytes 2097152 | tf_op jit(solution)/shard_map/all_to_all | solution.py:359
  27.1 5.8 %copy-start.2 = (bf16[8,4,128,128]{3,2,1,0:T(8,128)(2,1)}, bf16[8,4,128,128]{3,2,1,0:T(8,128)(2,1)S(1)}, u32[]{:S(2)}) copy-start(bf16[8,4,128,128]{3,2,1,0:T(8,128)(2,1)S(1)} %all-to-all-done.refs_6_) | copy-start | bytes 3145732
  27.1 23.8 %all-to-all-start.1 = ((bf16[32,128,128]{2,1,0:T(8,128)(2,1)}), bf16[32,128,128]{2,1,0:T(8,128)(2,1)S(1)}, u32[]{:S(2)}, u32[]{:S(2)}) async-start(bf16[32,128,128]{2,1,0:T(8,128)(2,1)} %bitcast.26), calls=%async_computation.1 | async-start | bytes 2097152 | tf_op jit(solution)/shard_map/all_to_all | solution.py:359
  33.0 58.0 %copy-start.4 = (bf16[8,2,128,128]{3,2,1,0:T(8,128)(2,1)}, bf16[8,2,128,128]{3,2,1,0:T(8,128)(2,1)S(1)}, u32[]{:S(2)}) copy-start(bf16[8,2,128,128]{3,2,1,0:T(8,128)(2,1)S(1)} %slice.40.refs_1_) | copy-start | bytes 1572868
  33.0 15.9 %collective-permute-start.3 = (bf16[8,2,128,128]{3,2,1,0:T(8,128)(2,1)S(1)}, bf16[8,2,128,128]{3,2,1,0:T(8,128)(2,1)S(1)}, u32[]{:S(2)}, u32[]{:S(2)}) collective-permute-start(bf16[8,2,128,128]{3,2,1,0:T(8,128)(2,1)S(1)} %slice.40.refs_1_), channel_id=1, source_target_pairs={{16,0},{32,16},{48,32},{64,48},{80,64},{96,80},{112,96},{17,1},{33... | collective-permute-start | bytes 1572872 | tf_op jit(solution)/shard_map/ppermute | solution.py:351
  34.3 15.8 %collective-permute-start.2 = (bf16[8,2,128,128]{3,2,1,0:T(8,128)(2,1)S(1)}, bf16[8,2,128,128]{3,2,1,0:T(8,128)(2,1)S(1)}, u32[]{:S(2)}, u32[]{:S(2)}) collective-permute-start(bf16[8,2,128,128]{3,2,1,0:T(8,128)(2,1)S(1)} %slice.40.refs_1_), channel_id=1, source_target_pairs={{0,16},{16,32},{32,48},{48,64},{64,80},{80,96},{96,112},{1,17},{17... | collective-permute-start | bytes 1572872 | tf_op jit(solution)/shard_map/ppermute | solution.py:351
  48.9 43.3 %copy-start.9 = (bf16[8,2,128,128]{3,2,1,0:T(8,128)(2,1)}, bf16[8,2,128,128]{3,2,1,0:T(8,128)(2,1)S(1)}, u32[]{:S(2)}) copy-start(bf16[8,2,128,128]{3,2,1,0:T(8,128)(2,1)S(1)} %collective-permute-done.3.refs_2_) | copy-start | bytes 1572868
  50.1 0.9 copy-start.10
  51.0 34.3 %copy-start.7 = (bf16[32,128,128]{2,1,0:T(8,128)(2,1)}, bf16[32,128,128]{2,1,0:T(8,128)(2,1)S(1)}, u32[]{:S(2)}) copy-start(bf16[32,128,128]{2,1,0:T(8,128)(2,1)S(1)} %all-to-all-done.1.refs_1_) | copy-start | bytes 3145732
  51.0 31.3 %all-to-all-start.2 = ((bf16[32,128,128]{2,1,0:T(8,128)(2,1)}), bf16[32,128,128]{2,1,0:T(8,128)(2,1)S(1)}, u32[]{:S(2)}, u32[]{:S(2)}) async-start(bf16[32,128,128]{2,1,0:T(8,128)(2,1)} %bitcast.25), calls=%async_computation.2 | async-start | bytes 2097152 | tf_op jit(solution)/shard_map/all_to_all | solution.py:359
  65.6 26.6 %collective-permute-start.1 = (bf16[32,128,128]{2,1,0:T(8,128)(2,1)S(1)}, bf16[32,128,128]{2,1,0:T(8,128)(2,1)}, u32[]{:S(2)}, u32[]{:S(2)}) collective-permute-start(bf16[32,128,128]{2,1,0:T(8,128)(2,1)S(1)} %all-to-all-done.1.refs_1_), channel_id=1, source_target_pairs={{0,48},{16,0},{32,16},{48,32},{1,49},{17,1},{33,17},{49,33},{2,50}... | collective-permute-start | bytes 3145736 | tf_op jit(solution)/shard_map/ppermute | solution.py:351
  68.6 27.4 %collective-permute-start = (bf16[32,128,128]{2,1,0:T(8,128)(2,1)S(1)}, bf16[32,128,128]{2,1,0:T(8,128)(2,1)}, u32[]{:S(2)}, u32[]{:S(2)}) collective-permute-start(bf16[32,128,128]{2,1,0:T(8,128)(2,1)S(1)} %all-to-all-done.1.refs_1_), channel_id=1, source_target_pairs={{0,16},{16,32},{32,48},{48,0},{1,17},{17,33},{33,49},{49,1},{2,18}... | collective-permute-start | bytes 3145736 | tf_op jit(solution)/shard_map/ppermute | solution.py:351
  82.3 3.0 %copy-start.8 = (bf16[32,128,128]{2,1,0:T(8,128)(2,1)}, bf16[32,128,128]{2,1,0:T(8,128)(2,1)S(1)}, u32[]{:S(2)}) copy-start(bf16[32,128,128]{2,1,0:T(8,128)(2,1)S(1)} %all-to-all-done.2.refs_4_) | copy-start | bytes 3145732
  82.3 31.5 %collective-permute-start.5 = (bf16[32,128,128]{2,1,0:T(8,128)(2,1)S(1)}, bf16[32,128,128]{2,1,0:T(8,128)(2,1)}, u32[]{:S(2)}, u32[]{:S(2)}) collective-permute-start(bf16[32,128,128]{2,1,0:T(8,128)(2,1)S(1)} %all-to-all-done.2.refs_4_), channel_id=1, source_target_pairs={{0,48},{16,0},{32,16},{48,32},{1,49},{17,1},{33,17},{49,33},{2,50}... | collective-permute-start | bytes 3145736 | tf_op jit(solution)/shard_map/ppermute | solution.py:351
  85.3 32.1 %collective-permute-start.4 = (bf16[32,128,128]{2,1,0:T(8,128)(2,1)S(1)}, bf16[32,128,128]{2,1,0:T(8,128)(2,1)}, u32[]{:S(2)}, u32[]{:S(2)}) collective-permute-start(bf16[32,128,128]{2,1,0:T(8,128)(2,1)S(1)} %all-to-all-done.2.refs_4_), channel_id=1, source_target_pairs={{0,16},{16,32},{32,48},{48,0},{1,17},{17,33},{33,49},{49,1},{2,18}... | collective-permute-start | bytes 3145736 | tf_op jit(solution)/shard_map/ppermute | solution.py:351
  85.3 43.4 %all-to-all-start.3 = ((bf16[32,2,128,128]{3,2,1,0:T(8,128)(2,1)}), bf16[32,2,128,128]{3,2,1,0:T(8,128)(2,1)}, u32[]{:S(2)}, u32[]{:S(2)}) async-start(bf16[32,2,128,128]{3,2,1,0:T(8,128)(2,1)} %bitcast.8), calls=%async_computation.3 | async-start | bytes 4194304 | tf_op jit(solution)/shard_map/all_to_all | solution.py:359
  91.0 7.0 %collective-permute-start.7 = (bf16[8,2,128,128]{3,2,1,0:T(8,128)(2,1)S(1)}, bf16[8,2,128,128]{3,2,1,0:T(8,128)(2,1)}, u32[]{:S(2)}, u32[]{:S(2)}) collective-permute-start(bf16[8,2,128,128]{3,2,1,0:T(8,128)(2,1)S(1)} %slice.40.refs_1_), channel_id=1, source_target_pairs={{0,8},{8,0},{1,9},{9,1},{2,10},{10,2},{3,11},{11,3},{4,12},{12,4},... | collective-permute-start | bytes 1572872 | tf_op jit(solution)/shard_map/ppermute | solution.py:367
  92.1 5.8 %collective-permute-start.8 = (bf16[8,2,128,128]{3,2,1,0:T(8,128)(2,1)S(1)}, bf16[8,2,128,128]{3,2,1,0:T(8,128)(2,1)}, u32[]{:S(2)}, u32[]{:S(2)}) collective-permute-start(bf16[8,2,128,128]{3,2,1,0:T(8,128)(2,1)S(1)} %collective-permute-done.3.refs_2_), channel_id=1, source_target_pairs={{0,8},{8,0},{1,9},{9,1},{2,10},{10,2},{3,11},{11,3},{4,12},{12,4},... | collective-permute-start | bytes 1572872 | tf_op jit(solution)/shard_map/ppermute | solution.py:367
  96.0 2.1 collective-permute-start.6
  98.1 0.8 copy-start.12
  110.7 10.5 %copy-start.11 = (bf16[8,2,128,128]{3,2,1,0:T(8,128)(2,1)S(1)}, bf16[8,2,128,128]{3,2,1,0:T(8,128)(2,1)}, u32[]{:S(2)}) copy-start(bf16[8,2,128,128]{3,2,1,0:T(8,128)(2,1)} %get-tuple-element.59) | copy-start | bytes 1572868
  117.3 2.6 %collective-permute-start.11 = (bf16[8,2,128,128]{3,2,1,0:T(8,128)(2,1)}, bf16[8,2,128,128]{3,2,1,0:T(8,128)(2,1)S(1)}, u32[]{:S(2)}, u32[]{:S(2)}) collective-permute-start(bf16[8,2,128,128]{3,2,1,0:T(8,128)(2,1)} %get-tuple-element.64), channel_id=1, source_target_pairs={{0,8},{8,0},{1,9},{9,1},{2,10},{10,2},{3,11},{11,3},{4,12},{12,4},... | collective-permute-start | bytes 1572872 | tf_op jit(solution)/shard_map/ppermute | solution.py:367
  117.3 3.8 %collective-permute-start.10 = (bf16[8,2,128,128]{3,2,1,0:T(8,128)(2,1)}, bf16[8,2,128,128]{3,2,1,0:T(8,128)(2,1)S(1)}, u32[]{:S(2)}, u32[]{:S(2)}) collective-permute-start(bf16[8,2,128,128]{3,2,1,0:T(8,128)(2,1)} %get-tuple-element.61), channel_id=1, source_target_pairs={{0,8},{8,0},{1,9},{9,1},{2,10},{10,2},{3,11},{11,3},{4,12},{12,4},... | collective-permute-start | bytes 1572872 | tf_op jit(solution)/shard_map/ppermute | solution.py:367
  119.9 29.9 %collective-permute-start.9 = (bf16[8,2,128,128]{3,2,1,0:T(8,128)(2,1)}, bf16[8,2,128,128]{3,2,1,0:T(8,128)(2,1)}, u32[]{:S(2)}, u32[]{:S(2)}) collective-permute-start(bf16[8,2,128,128]{3,2,1,0:T(8,128)(2,1)} %get-tuple-element.58), channel_id=1, source_target_pairs={{0,8},{8,0},{1,9},{9,1},{2,10},{10,2},{3,11},{11,3},{4,12},{12,4},... | collective-permute-start | bytes 1572872 | tf_op jit(solution)/shard_map/ppermute | solution.py:367
  122.1 27.8 %collective-permute-start.12 = (bf16[8,2,128,128]{3,2,1,0:T(8,128)(2,1)}, bf16[8,2,128,128]{3,2,1,0:T(8,128)(2,1)S(1)}, u32[]{:S(2)}, u32[]{:S(2)}) collective-permute-start(bf16[8,2,128,128]{3,2,1,0:T(8,128)(2,1)} %add_convert_fusion.1), channel_id=1, source_target_pairs={{16,0},{32,16},{48,32},{64,48},{80,64},{96,80},{112,96},{17,1},{33... | collective-permute-start | bytes 1572872 | tf_op jit(solution)/shard_map/ppermute | solution.py:351
  123.4 26.5 %collective-permute-start.13 = (bf16[8,2,128,128]{3,2,1,0:T(8,128)(2,1)S(1)}, bf16[8,2,128,128]{3,2,1,0:T(8,128)(2,1)}, u32[]{:S(2)}, u32[]{:S(2)}) collective-permute-start(bf16[8,2,128,128]{3,2,1,0:T(8,128)(2,1)S(1)} %add_convert_fusion), channel_id=1, source_target_pairs={{0,16},{16,32},{32,48},{48,64},{64,80},{80,96},{96,112},{1,17},{17... | collective-permute-start | bytes 1572872 | tf_op jit(solution)/shard_map/ppermute | solution.py:351
  147.3 37.6 %collective-permute-start.14 = (bf16[16,2,128,128]{3,2,1,0:T(8,128)(2,1)}, bf16[16,2,128,128]{3,2,1,0:T(8,128)(2,1)S(1)}, u32[]{:S(2)}, u32[]{:S(2)}) collective-permute-start(bf16[16,2,128,128]{3,2,1,0:T(8,128)(2,1)} %get-tuple-element.69), channel_id=1, source_target_pairs={{0,48},{16,0},{32,16},{48,32},{1,49},{17,1},{33,17},{49,33},{2,50}... | collective-permute-start | bytes 3145736 | tf_op jit(solution)/shard_map/ppermute | solution.py:351
  149.8 35.1 %collective-permute-start.15 = (bf16[16,2,128,128]{3,2,1,0:T(8,128)(2,1)}, bf16[16,2,128,128]{3,2,1,0:T(8,128)(2,1)S(1)}, u32[]{:S(2)}, u32[]{:S(2)}) collective-permute-start(bf16[16,2,128,128]{3,2,1,0:T(8,128)(2,1)} %get-tuple-element.70), channel_id=1, source_target_pairs={{0,16},{16,32},{32,48},{48,0},{1,17},{17,33},{33,49},{49,1},{2,18}... | collective-permute-start | bytes 3145736 | tf_op jit(solution)/shard_map/ppermute | solution.py:351
  149.8 0.8 copy-start.14
  153.1 31.8 %all-to-all-start.4 = ((bf16[8,3,128,128]{3,2,1,0:T(8,128)(2,1)}), bf16[8,3,128,128]{3,2,1,0:T(8,128)(2,1)S(1)}, u32[]{:S(2)}, u32[]{:S(2)}) async-start(bf16[8,3,128,128]{3,2,1,0:T(8,128)(2,1)} %total_grads.1), calls=%async_computation.4 | async-start | bytes 1572864 | tf_op jit(solution)/shard_map/all_to_all | solution.py:359
  161.9 20.9 %copy-start.13 = (bf16[16,128,128]{2,1,0:T(8,128)(2,1)S(1)}, bf16[16,128,128]{2,1,0:T(8,128)(2,1)}, u32[]{:S(2)}) copy-start(bf16[16,128,128]{2,1,0:T(8,128)(2,1)} %get-tuple-element.52) | copy-start | bytes 1572868
  179.6 25.5 %collective-permute-start.16 = (bf16[16,2,128,128]{3,2,1,0:T(8,128)(2,1)}, bf16[16,2,128,128]{3,2,1,0:T(8,128)(2,1)}, u32[]{:S(2)}, u32[]{:S(2)}) collective-permute-start(bf16[16,2,128,128]{3,2,1,0:T(8,128)(2,1)} %get-tuple-element.74), channel_id=1, source_target_pairs={{0,48},{16,0},{32,16},{48,32},{1,49},{17,1},{33,17},{49,33},{2,50}... | collective-permute-start | bytes 3145736 | tf_op jit(solution)/shard_map/ppermute | solution.py:351
  182.8 24.5 %collective-permute-start.17 = (bf16[16,2,128,128]{3,2,1,0:T(8,128)(2,1)}, bf16[16,2,128,128]{3,2,1,0:T(8,128)(2,1)}, u32[]{:S(2)}, u32[]{:S(2)}) collective-permute-start(bf16[16,2,128,128]{3,2,1,0:T(8,128)(2,1)} %get-tuple-element.75), channel_id=1, source_target_pairs={{0,16},{16,32},{32,48},{48,0},{1,17},{17,33},{33,49},{49,1},{2,18}... | collective-permute-start | bytes 3145736 | tf_op jit(solution)/shard_map/ppermute | solution.py:351
  184.9 27.4 %copy-start.1 = (bf16[8,3,128,128]{3,2,1,0:T(8,128)(2,1)}, bf16[8,3,128,128]{3,2,1,0:T(8,128)(2,1)S(1)}, u32[]{:S(2)}) copy-start(bf16[8,3,128,128]{3,2,1,0:T(8,128)(2,1)S(1)} %all-to-all-done.4.b_ref) | copy-start | bytes 2359300
  184.9 22.4 %copy-start.5 = (bf16[16,2,128,128]{3,2,1,0:T(8,128)(2,1)}, bf16[16,2,128,128]{3,2,1,0:T(8,128)(2,1)S(1)}, u32[]{:S(2)}) copy-start(bf16[16,2,128,128]{3,2,1,0:T(8,128)(2,1)S(1)} %collective-permute-done.14.right0) | copy-start | bytes 3145732
  184.9 1.1 copy-start.6
  186.0 26.4 %all-to-all-start.5 = ((bf16[32,128,128]{2,1,0:T(8,128)(2,1)}), bf16[32,128,128]{2,1,0:T(8,128)(2,1)S(1)}, u32[]{:S(2)}, u32[]{:S(2)}) async-start(bf16[32,128,128]{2,1,0:T(8,128)(2,1)} %pad_maximum_fusion), calls=%async_computation.5 | async-start | bytes 2097152 | tf_op jit(solution)/shard_map/all_to_all | solution.py:359
  212.3 1.0 copy-start.3
  213.3 38.4 %all-to-all-start.6 = ((bf16[32,2,128,128]{3,2,1,0:T(8,128)(2,1)}), bf16[32,2,128,128]{3,2,1,0:T(8,128)(2,1)S(1)}, u32[]{:S(2)}, u32[]{:S(2)}) async-start(bf16[32,2,128,128]{3,2,1,0:T(8,128)(2,1)} %bitcast.23), calls=%async_computation.6 | async-start | bytes 4194304 | tf_op jit(solution)/shard_map/all_to_all | solution.py:359
  251.7 1.3 copy-start

commit v11 on v10

--- a/solution.py
+++ b/solution.py
@@ -347,8 +347,7 @@
 
 def shift(value, axes, steps):
     count = lax.axis_size(axes)
-    ends = range(count) if axes == "x" else range(max(0, -steps), min(count, count - steps))
-    return lax.ppermute(value, axes, [(s, (s + steps) % count) for s in ends])
+    return lax.ppermute(value, axes, [(s, (s + steps) % count) for s in range(count)])
 
 
 def add(a, b):
@@ -385,12 +384,13 @@
     own_b = exchange(b, "group")
     pairs_b = own_b[:, :2]
     mine = (shift(pairs_b, CHIPS, 1), pairs_b, shift(pairs_b, CHIPS, -1))
-    theirs = tuple(swap(pairs) for pairs in mine)
 
     keys = exchange(after(ka, own_b, gathered), WIDE)
     key_near = [shift(keys, "x", 1), shift(keys, "x", -1)]
-    values = exchange(after(va, keys, *mine), WIDE)
+    values = first_values = exchange(after(va, keys, *mine), WIDE)
+    values = after(values, *key_near)
     value_near = [shift(values, "x", 1), shift(values, "x", -1)]
+    theirs = tuple(swap(after(pairs, values, *key_near)) for pairs in mine)
 
     def run(i, other):
         def fetch(ref, place):
@@ -406,27 +406,27 @@
         ids, counts, place, mine + theirs, fetches, after(own_b, values, *key_near), BPD, size
     )
     got_b = [swap(after(give, *value_near)) for give in give_b]
-    out_b = lax.optimization_barrier((add(left_b, got_b[0]), add(right_b, got_b[2])))
-    terms_b = [got_b[1], shift(out_b[0], CHIPS, -1), shift(out_b[1], CHIPS, 1)]
-
-    queries = exchange(after(qda, values), WIDE)
+
+    queries = exchange(after(qda, first_values), WIDE)
 
     def third(t, i):
         return lambda ref, place: [(ref.at[pl.ds(pl.multiple_of(place[1 + i], 8), size)], t, i * size)]
 
     fetches = [third(t, i) for t in range(2) for i in range(3)]
     sources = (key_near[0], keys, key_near[1], value_near[0], values, value_near[1])
-    done, back_b = [], ()
+    done = []
     for s in range(2):
         ids, counts = plain(lists[2 * s : 2 * s + 2], s * (last + 1) + x)
         left = jnp.where(x == 0, 1 - s, s) * size
         right = jnp.where(x == last, 1 - s, s) * size
-        place = after(jnp.stack([jnp.int32(s * size), left, jnp.int32(s * size), right]), *back_b)
+        place = jnp.stack([jnp.int32(s * size), left, jnp.int32(s * size), right])
+        place = after(place, *[d[0] for d in done])
         dq, grads = attention(ids, counts, place, sources, fetches, queries, size, size)
         done.append((dq, grads, shift(grads[0], "x", -1), shift(grads[2], "x", 1)))
         if s == 0:
-            total_b = total_grads(after(dq_b, dq), mine_b, terms_b)
-            back_b = (total_b,)
+            left_b, right_b = add(after(left_b, dq), got_b[0]), add(after(right_b, dq), got_b[2])
+            terms_b = [got_b[1], shift(left_b, CHIPS, -1), shift(right_b, CHIPS, 1)]
+    total_b = total_grads(after(dq_b, done[1][0]), mine_b, terms_b)
     back_b = exchange(total_b, "group")
     dqa = exchange(after(jnp.concatenate([d[0] for d in done]), *done[0][2:], back_b), WIDE)
     dkva = both_halves(x, last, [d[1][1] for d in done], [d[2] for d in done], [d[3] for d in done])

time: 259 us -> 256 us (0.988)
  waiting for transfers between devices: 79.4 us -> 99.8 us
  starting transfers between devices: 83.1 us -> 63.2 us
    all_to_all x7, starting transfers between devices: 58 us -> 43.5 us  [exchange(): return lax.all_to_all(x, axes, 0, 0, tiled=True)]
    all_to_all x7, waiting for transfers between devices: 43.8 us -> 55.7 us  [exchange(): return lax.all_to_all(x, axes, 0, 0, tiled=True)]
    ppermute x12, waiting for transfers between devices: 35.5 us -> 43.2 us  [shift(): lax.ppermute(value, axes, [(s, (s + steps) % count) for s in range(count)])]
    ppermute x12, starting transfers between devices: 24.3 us -> 18.4 us  [shift(): lax.ppermute(value, axes, [(s, (s + steps) % count) for s in range(count)])]
    unnamed x36 -> x38, local copies, waits for them, and re-layouts: 6.28 us -> 4.25 us
  transfers between devices with their start and end apart: 25 -> 25, of which waited for: 13 -> 16; matrix products, arithmetic and copies ran while one was open for 4% -> 4% of each run, Pallas kernels for 25% -> 25%
where the time goes in v11:
time: 256 us; the launch traced here: 254 us
  waiting for transfers between devices  99.8 us (39%)
  Pallas kernels  70.9 us (28%)
  starting transfers between devices  63.2 us (25%)
  local copies, waits for them, and re-layouts  7.1 us (3%)
  blocking collectives  7.05 us (3%)
  other arithmetic  4.88 us (2%)
    all_to_all x7, waiting for transfers between devices, exchange(): return lax.all_to_all(x, axes, 0, 0, tiled=True)  55.7 us
    pallas_call x3, Pallas kernels, attention(): pl.pallas_call(functools.partial(attention_kernel, size, n_query, fetches...  48.4 us
    all_to_all x7, starting transfers between devices, exchange(): return lax.all_to_all(x, axes, 0, 0, tiled=True)  43.5 us
    ppermute x12, waiting for transfers between devices, shift(): lax.ppermute(value, axes, [(s, (s + steps) % count) for s in range(count)])  43.2 us
    ppermute x12, starting transfers between devices, shift(): lax.ppermute(value, axes, [(s, (s + steps) % count) for s in range(count)])  18.4 us
    pallas_call x2, Pallas kernels, join_heads(): pl.pallas_call(functools.partial(join_kernel, first), grid=(groups // ste...  7.73 us
    all_gather x1, blocking collectives, shards(): gathered = lax.all_gather(after(packed, b), ('half', 'core'))  7.05 us
  transfers between devices with their start and end apart: 25, of which 16 were waited for; matrix products, arithmetic and copies ran while one was open for 4% of the time, Pallas kernels for 25%

profile of v11, /device:TPU:8, one launch (start us, length us, event | category | flops | bytes accessed | tf_op | source)
XLA Modules:
  0.0 253.8 jit_solution(1092586881115019048)
XLA Ops:
  0.6 2.2 fifth_heads.1
  2.9 8.2 %all-to-all-start = ((bf16[8,4,128,128]{3,2,1,0:T(8,128)(2,1)}), bf16[8,4,128,128]{3,2,1,0:T(8,128)(2,1)S(1)}, u32[]{:S(2)}, u32[]{:S(2)}) async-start(bf16[8,4,128,128]{3,2,1,0:T(8,128)(2,1)} %fifth_heads.1), calls=%async_computation | async-start | bytes 2097152 | tf_op jit(solution)/shard_map/all_to_all | solution.py:358
  11.1 0.1 copy.15
  11.2 0.1 pad_add_fusion
  11.3 5.1 %split_heads.1 = (bf16[4,8,128,128]{3,2,1,0:T(8,128)(2,1)}, bf16[4,8,128,128]{3,2,1,0:T(8,128)(2,1)}, bf16[4,8,2,128,128]{4,3,2,1,0:T(8,128)(2,1)}) custom-call(bf16[128,5120]{1,0:T(8,128)(2,1)} %k_ref.2, bf16[128,5120]{1,0:T(8,128)(2,1)} %v_ref.2, bf16[128,5120]{1,0:T(8,128)(2,1)} %q_ref.2, bf16[128,5120]{1,0:T(8,128)(2,1)} %g_ref.2), custom_call_target="tpu_custom_call" | custom-call | bytes 10485760 | tf_op jit(solution)/shard_map/split_heads/pallas_call | solution.py:214
  16.4 7.0 %all-gather = s32[20,8,13]{2,1,0:T(8,128)S(1)} all-gather(s32[5,8,13]{2,1,0:T(8,128)S(1)} %pad_add_fusion), channel_id=2, replica_groups=mesh['half'=2,'x'=4,'core'=2,'group'=8] {'half','core'}, dimensions={0}, use_global_device_ids=true | all-gather | bytes 10400 | tf_op jit(solution)/shard_map/all_gather | solution.py:374
  23.5 3.7 %all-to-all-done.refs_6_ = bf16[8,4,128,128]{3,2,1,0:T(8,128)(2,1)S(1)} async-done(((bf16[8,4,128,128]{3,2,1,0:T(8,128)(2,1)}), bf16[8,4,128,128]{3,2,1,0:T(8,128)(2,1)S(1)}, u32[]{:S(2)}, u32[]{:S(2)}) %all-to-all-start) | async-done | bytes 1048608 | tf_op jit(solution)/shard_map/all_to_all | solution.py:358
  27.1 5.8 %all-to-all-start.1 = ((bf16[32,128,128]{2,1,0:T(8,128)(2,1)}), bf16[32,128,128]{2,1,0:T(8,128)(2,1)S(1)}, u32[]{:S(2)}, u32[]{:S(2)}) async-start(bf16[32,128,128]{2,1,0:T(8,128)(2,1)} %bitcast.26), calls=%async_computation.1 | async-start | bytes 2097152 | tf_op jit(solution)/shard_map/all_to_all | solution.py:358
  33.0 3.7 %collective-permute-start.3 = (bf16[8,2,128,128]{3,2,1,0:T(8,128)(2,1)S(1)}, bf16[8,2,128,128]{3,2,1,0:T(8,128)(2,1)S(1)}, u32[]{:S(2)}, u32[]{:S(2)}) collective-permute-start(bf16[8,2,128,128]{3,2,1,0:T(8,128)(2,1)S(1)} %slice.40.refs_1_), channel_id=1, source_target_pairs={{0,112},{16,0},{32,16},{48,32},{64,48},{80,64},{96,80},{112,96},{1... | collective-permute-start | bytes 1572872 | tf_op jit(solution)/shard_map/ppermute | solution.py:350
  36.8 18.0 %collective-permute-done.3.refs_2_ = bf16[8,2,128,128]{3,2,1,0:T(8,128)(2,1)S(1)} collective-permute-done((bf16[8,2,128,128]{3,2,1,0:T(8,128)(2,1)S(1)}, bf16[8,2,128,128]{3,2,1,0:T(8,128)(2,1)S(1)}, u32[]{:S(2)}, u32[]{:S(2)}) %collective-permute-start.3) | collective-permute-done | bytes 524320 | tf_op jit(solution)/shard_map/ppermute | solution.py:350
  54.8 2.4 collective-permute-done.2.refs_0_
  57.1 1.8 all-to-all-done.1.refs_1_
  59.0 6.9 %all-to-all-start.2 = ((bf16[32,128,128]{2,1,0:T(8,128)(2,1)}), bf16[32,128,128]{2,1,0:T(8,128)(2,1)S(1)}, u32[]{:S(2)}, u32[]{:S(2)}) async-start(bf16[32,128,128]{2,1,0:T(8,128)(2,1)} %bitcast.25), calls=%async_computation.2 | async-start | bytes 2097152 | tf_op jit(solution)/shard_map/all_to_all | solution.py:358
  65.9 2.4 collective-permute-start.1
  68.3 14.3 %all-to-all-done.2.refs_4_ = bf16[32,128,128]{2,1,0:T(8,128)(2,1)S(1)} async-done(((bf16[32,128,128]{2,1,0:T(8,128)(2,1)}), bf16[32,128,128]{2,1,0:T(8,128)(2,1)S(1)}, u32[]{:S(2)}, u32[]{:S(2)}) %all-to-all-start.2) | async-done | bytes 1048608 | tf_op jit(solution)/shard_map/all_to_all | solution.py:358
  82.6 5.6 %all-to-all-start.3 = ((bf16[32,2,128,128]{3,2,1,0:T(8,128)(2,1)}), bf16[32,2,128,128]{3,2,1,0:T(8,128)(2,1)}, u32[]{:S(2)}, u32[]{:S(2)}) async-start(bf16[32,2,128,128]{3,2,1,0:T(8,128)(2,1)} %bitcast.8), calls=%async_computation.3 | async-start | bytes 4194304 | tf_op jit(solution)/shard_map/all_to_all | solution.py:358
  88.3 3.0 %collective-permute-done.1.refs_2_ = bf16[32,128,128]{2,1,0:T(8,128)(2,1)} collective-permute-done((bf16[32,128,128]{2,1,0:T(8,128)(2,1)S(1)}, bf16[32,128,128]{2,1,0:T(8,128)(2,1)}, u32[]{:S(2)}, u32[]{:S(2)}) %collective-permute-start.1) | collective-permute-done | bytes 1048608 | tf_op jit(solution)/shard_map/ppermute | solution.py:350
  91.3 3.2 %collective-permute-done.refs_0_ = bf16[32,128,128]{2,1,0:T(8,128)(2,1)} collective-permute-done((bf16[32,128,128]{2,1,0:T(8,128)(2,1)S(1)}, bf16[32,128,128]{2,1,0:T(8,128)(2,1)}, u32[]{:S(2)}, u32[]{:S(2)}) %collective-permute-start) | collective-permute-done | bytes 1048608 | tf_op jit(solution)/shard_map/ppermute | solution.py:350
  94.5 0.3 collective-permute-start.5
  94.8 1.7 collective-permute-start.4
  96.6 0.5 collective-permute-start.9
  97.1 0.3 collective-permute-start.10
  97.4 0.6 reshape.47.ids_ref
  98.0 0.6 pad_add_fusion.3.place_ref
  98.6 0.7 slice_reduce_fusion.cnt_ref
  99.3 0.7 collective-permute-done.9.refs_4_
  100.0 0.1 collective-permute-done.10.refs_5_
  100.1 0.7 copy-done.14
  100.8 11.8 %attention.5 = (bf16[8,128,128]{2,1,0:T(8,128)(2,1)}, bf16[8,2,128,128]{3,2,1,0:T(8,128)(2,1)}, bf16[8,2,128,128]{3,2,1,0:T(8,128)(2,1)}, bf16[8,2,128,128]{3,2,...) custom-call(s32[96]{0:T(128)} %reshape.47.ids_ref, ...), custom_call_target="tpu_custom_call" | custom-call | tf_op jit(solution)/shard_map/attention/pallas_call | solution.py:170
  112.6 6.2 %collective-permute-done.5.refs_5_ = bf16[32,128,128]{2,1,0:T(8,128)(2,1)} collective-permute-done((bf16[32,128,128]{2,1,0:T(8,128)(2,1)S(1)}, bf16[32,128,128]{2,1,0:T(8,128)(2,1)}, u32[]{:S(2)}, u32[]{:S(2)}) %collective-permute-start.5) | collective-permute-done | bytes 1048608 | tf_op jit(solution)/shard_map/ppermute | solution.py:350
  118.7 1.5 collective-permute-done.4.refs_3_
  120.3 0.5 collective-permute-start.14
  120.8 0.6 pad_add_fusion.1.place_ref
  121.4 0.1 slice.39
  121.4 0.6 copy.18
  122.0 0.7 reshape.41.ids_ref
  122.7 18.4 %attention.3 = (bf16[16,128,128]{2,1,0:T(8,128)(2,1)}, bf16[16,2,128,128]{3,2,1,0:T(8,128)(2,1)}, bf16[16,2,128,128]{3,2,1,0:T(8,128)(2,1)}, bf16[16,2,128,128]{3,2,1,0:T(8,128)(2,1)}) custom-call(s32[192]{0:T(256)} %reshape.41.ids_ref, s32[16]{0:T(128)} %bitcast.31, s32[4]{0:T(128)} %pad_add_fusion.1.place_ref, ...), custom_call_target="tpu_custom_call" | custom-call | flops 2684354560 | bytes 7340032 | tf_op jit(solution)/shard_map/attention/pallas_call | solution.py:170
  141.1 0.1 add_convert_fusion.1
  141.3 1.7 collective-permute-start.13
  143.0 0.1 add_convert_fusion
  143.1 0.5 collective-permute-start.15
  143.6 0.1 slice.42
  143.6 0.6 copy.19
  144.3 0.6 reshape.46.ids_ref
  144.9 4.3 %collective-permute-start.6 = (bf16[16,2,128,128]{3,2,1,0:T(8,128)(2,1)}, bf16[16,2,128,128]{3,2,1,0:T(8,128)(2,1)S(1)}, u32[]{:S(2)}, u32[]{:S(2)}) collective-permute-start(bf16[16,2,128,128]{3,2,1,0:T(8,128)(2,1)} %get-tuple-element.60), channel_id=1, source_target_pairs={{0,48},{16,0},{32,16},{48,32},{1,49},{17,1},{33,17},{49,33},{2,50}... | collective-permute-start | bytes 3145736 | tf_op jit(solution)/shard_map/ppermute | solution.py:350
  149.2 0.6 pad_add_fusion.2.place_ref
  149.7 18.2 %attention.4 = (bf16[16,128,128]{2,1,0:T(8,128)(2,1)}, bf16[16,2,128,128]{3,2,1,0:T(8,128)(2,1)}, bf16[16,2,128,128]{3,2,1,0:T(8,128)(2,1)}, bf16[16,2,128,128]{3,2,1,0:T(8,128)(2,1)}) custom-call(s32[192]{0:T(256)} %reshape.46.ids_ref, s32[16]{0:T(128)} %bitcast.30, s32[4]{0:T(128)} %pad_add_fusion.2.place_ref, ...), custom_call_target="tpu_custom_call" | custom-call | flops 2684354560 | bytes 7340032 | tf_op jit(solution)/shard_map/attention/pallas_call | solution.py:170
  168.0 2.5 total_grads.1
  170.5 7.1 %all-to-all-start.4 = ((bf16[8,3,128,128]{3,2,1,0:T(8,128)(2,1)}), bf16[8,3,128,128]{3,2,1,0:T(8,128)(2,1)S(1)}, u32[]{:S(2)}, u32[]{:S(2)}) async-start(bf16[8,3,128,128]{3,2,1,0:T(8,128)(2,1)} %total_grads.1), calls=%async_computation.4 | async-start | bytes 1572864 | tf_op jit(solution)/shard_map/all_to_all | solution.py:358
  177.6 3.8 %collective-permute-start.16 = (bf16[16,2,128,128]{3,2,1,0:T(8,128)(2,1)}, bf16[16,2,128,128]{3,2,1,0:T(8,128)(2,1)}, u32[]{:S(2)}, u32[]{:S(2)}) collective-permute-start(bf16[16,2,128,128]{3,2,1,0:T(8,128)(2,1)} %get-tuple-element.82), channel_id=1, source_target_pairs={{0,48},{16,0},{32,16},{48,32},{1,49},{17,1},{33,17},{49,33},{2,50}... | collective-permute-start | bytes 3145736 | tf_op jit(solution)/shard_map/ppermute | solution.py:350
  181.4 2.1 pad_maximum_fusion
  183.5 8.1 %all-to-all-done.4.b_ref = bf16[8,3,128,128]{3,2,1,0:T(8,128)(2,1)S(1)} async-done(((bf16[8,3,128,128]{3,2,1,0:T(8,128)(2,1)}), bf16[8,3,128,128]{3,2,1,0:T(8,128)(2,1)S(1)}, u32[]{:S(2)}, u32[]{:S(2)}) %all-to-all-start.4) | async-done | bytes 786464 | tf_op jit(solution)/shard_map/all_to_all | solution.py:358
  191.6 4.8 %all-to-all-start.5 = ((bf16[32,128,128]{2,1,0:T(8,128)(2,1)}), bf16[32,128,128]{2,1,0:T(8,128)(2,1)S(1)}, u32[]{:S(2)}, u32[]{:S(2)}) async-start(bf16[32,128,128]{2,1,0:T(8,128)(2,1)} %pad_maximum_fusion), calls=%async_computation.5 | async-start | bytes 2097152 | tf_op jit(solution)/shard_map/all_to_all | solution.py:358
  196.3 0.6 pad_add_fusion.4.x_ref
  197.0 6.0 %collective-permute-done.16.right1 = bf16[16,2,128,128]{3,2,1,0:T(8,128)(2,1)} collective-permute-done((bf16[16,2,128,128]{3,2,1,0:T(8,128)(2,1)}, bf16[16,2,128,128]{3,2,1,0:T(8,128)(2,1)}, u32[]{:S(2)}, u32[]{:S(2)}) %collective-permute-start.16) | collective-permute-done | bytes 1048608 | tf_op jit(solution)/shard_map/ppermute | solution.py:350
  203.0 2.8 %collective-permute-done.17.left1 = bf16[16,2,128,128]{3,2,1,0:T(8,128)(2,1)} collective-permute-done((bf16[16,2,128,128]{3,2,1,0:T(8,128)(2,1)}, bf16[16,2,128,128]{3,2,1,0:T(8,128)(2,1)}, u32[]{:S(2)}, u32[]{:S(2)}) %collective-permute-start.17) | collective-permute-done | bytes 1048608 | tf_op jit(solution)/shard_map/ppermute | solution.py:350
  205.8 5.0 %both_halves.1 = bf16[2,16,2,128,128]{4,3,2,1,0:T(8,128)(2,1)} custom-call(s32[2]{0:T(128)} %pad_add_fusion.4.x_ref, bf16[16,2,128,128]{3,2,1,0:T(8,128)(2,1)} %get-tuple-element.80.own0, bf16[16,2,128,128]{3,2,1,0:T(8,128)(2,1)} %get-tuple-element.81.own1, bf16[16,2,128,128]{3,2,1,0:T(8,128)(2,1)} %copy-done.5, ...), custom_call_target="tpu_custom_call" | custom-call | bytes 8388608 | tf_op jit(solution)/shard_map/both_halves/pallas_call | solution.py:331
  210.9 2.3 all-to-all-done.5
  213.1 1.0 copy-done.3
  214.1 5.1 %all-to-all-start.6 = ((bf16[32,2,128,128]{3,2,1,0:T(8,128)(2,1)}), bf16[32,2,128,128]{3,2,1,0:T(8,128)(2,1)S(1)}, u32[]{:S(2)}, u32[]{:S(2)}) async-start(bf16[32,2,128,128]{3,2,1,0:T(8,128)(2,1)} %bitcast.23), calls=%async_computation.6 | async-start | bytes 4194304 | tf_op jit(solution)/shard_map/all_to_all | solution.py:358
  219.2 3.6 %join_heads.2 = bf16[128,5120]{1,0:T(8,128)(2,1)} custom-call(bf16[4,8,1,128,128]{4,3,2,1,0:T(8,128)(2,1)} %bitcast.24, bf16[8,3,128,128]{3,2,1,0:T(8,128)(2,1)} %copy-done.1), custom_call_target="tpu_custom_call" | custom-call | bytes 2621440 | tf_op jit(solution)/shard_map/join_heads/pallas_call | solution.py:277
  222.8 25.5 %all-to-all-done.6 = bf16[32,2,128,128]{3,2,1,0:T(8,128)(2,1)S(1)} async-done(((bf16[32,2,128,128]{3,2,1,0:T(8,128)(2,1)}), bf16[32,2,128,128]{3,2,1,0:T(8,128)(2,1)S(1)}, u32[]{:S(2)}, u32[]{:S(2)}) %all-to-all-start.6) | async-done | bytes 2097184 | tf_op jit(solution)/shard_map/all_to_all | solution.py:358
  248.3 1.3 copy-done
  249.7 4.1 %join_heads.3 = (bf16[128,5120]{1,0:T(8,128)(2,1)}, bf16[128,5120]{1,0:T(8,128)(2,1)}) custom-call(bf16[4,8,2,128,128]{4,3,2,1,0:T(8,128)(2,1)} %bitcast.22, bf16[8,3,128,128]{3,2,1,0:T(8,128)(2,1)} %copy-done.1), custom_call_target="tpu_custom_call" | custom-call | bytes 5242880 | tf_op jit(solution)/shard_map/join_heads/pallas_call | solution.py:277
  (54 shorter events, 0.2 us)
Async XLA Ops:
  2.8 8.3 %copy-start.17 = (s32[5,8]{1,0:T(8,128)S(1)}, s32[5,8]{1,0:T(8,128)}, u32[]{:S(2)}) copy-start(s32[5,8]{1,0:T(8,128)} %param.11) | copy-start | bytes 484
  2.9 8.4 %copy-start.16 = (s32[5,8,12]{2,1,0:T(8,128)S(1)}, s32[5,8,12]{2,1,0:T(8,128)}, u32[]{:S(2)}) copy-start(s32[5,8,12]{2,1,0:T(8,128)} %param.10) | copy-start | bytes 5764
  2.9 24.3 %all-to-all-start = ((bf16[8,4,128,128]{3,2,1,0:T(8,128)(2,1)}), bf16[8,4,128,128]{3,2,1,0:T(8,128)(2,1)S(1)}, u32[]{:S(2)}, u32[]{:S(2)}) async-start(bf16[8,4,128,128]{3,2,1,0:T(8,128)(2,1)} %fifth_heads.1), calls=%async_computation | async-start | bytes 2097152 | tf_op jit(solution)/shard_map/all_to_all | solution.py:358
  27.1 5.8 %copy-start.2 = (bf16[8,4,128,128]{3,2,1,0:T(8,128)(2,1)}, bf16[8,4,128,128]{3,2,1,0:T(8,128)(2,1)S(1)}, u32[]{:S(2)}) copy-start(bf16[8,4,128,128]{3,2,1,0:T(8,128)(2,1)S(1)} %all-to-all-done.refs_6_) | copy-start | bytes 3145732
  27.1 31.8 %all-to-all-start.1 = ((bf16[32,128,128]{2,1,0:T(8,128)(2,1)}), bf16[32,128,128]{2,1,0:T(8,128)(2,1)S(1)}, u32[]{:S(2)}, u32[]{:S(2)}) async-start(bf16[32,128,128]{2,1,0:T(8,128)(2,1)} %bitcast.26), calls=%async_computation.1 | async-start | bytes 2097152 | tf_op jit(solution)/shard_map/all_to_all | solution.py:358
  33.0 63.6 %copy-start.4 = (bf16[8,2,128,128]{3,2,1,0:T(8,128)(2,1)}, bf16[8,2,128,128]{3,2,1,0:T(8,128)(2,1)S(1)}, u32[]{:S(2)}) copy-start(bf16[8,2,128,128]{3,2,1,0:T(8,128)(2,1)S(1)} %slice.40.refs_1_) | copy-start | bytes 1572868
  33.0 21.7 %collective-permute-start.3 = (bf16[8,2,128,128]{3,2,1,0:T(8,128)(2,1)S(1)}, bf16[8,2,128,128]{3,2,1,0:T(8,128)(2,1)S(1)}, u32[]{:S(2)}, u32[]{:S(2)}) collective-permute-start(bf16[8,2,128,128]{3,2,1,0:T(8,128)(2,1)S(1)} %slice.40.refs_1_), channel_id=1, source_target_pairs={{0,112},{16,0},{32,16},{48,32},{64,48},{80,64},{96,80},{112,96},{1... | collective-permute-start | bytes 1572872 | tf_op jit(solution)/shard_map/ppermute | solution.py:350
  36.7 20.4 %collective-permute-start.2 = (bf16[8,2,128,128]{3,2,1,0:T(8,128)(2,1)S(1)}, bf16[8,2,128,128]{3,2,1,0:T(8,128)(2,1)S(1)}, u32[]{:S(2)}, u32[]{:S(2)}) collective-permute-start(bf16[8,2,128,128]{3,2,1,0:T(8,128)(2,1)S(1)} %slice.40.refs_1_), channel_id=1, source_target_pairs={{0,16},{16,32},{32,48},{48,64},{64,80},{80,96},{96,112},{112,0},{1... | collective-permute-start | bytes 1572872 | tf_op jit(solution)/shard_map/ppermute | solution.py:350
  54.8 42.3 %copy-start.9 = (bf16[8,2,128,128]{3,2,1,0:T(8,128)(2,1)}, bf16[8,2,128,128]{3,2,1,0:T(8,128)(2,1)S(1)}, u32[]{:S(2)}) copy-start(bf16[8,2,128,128]{3,2,1,0:T(8,128)(2,1)S(1)} %collective-permute-done.3.refs_2_) | copy-start | bytes 1572868
  57.1 1.8 copy-start.10
  59.0 23.7 %copy-start.7 = (bf16[32,128,128]{2,1,0:T(8,128)(2,1)}, bf16[32,128,128]{2,1,0:T(8,128)(2,1)S(1)}, u32[]{:S(2)}) copy-start(bf16[32,128,128]{2,1,0:T(8,128)(2,1)S(1)} %all-to-all-done.1.refs_1_) | copy-start | bytes 3145732
  59.0 23.7 %all-to-all-start.2 = ((bf16[32,128,128]{2,1,0:T(8,128)(2,1)}), bf16[32,128,128]{2,1,0:T(8,128)(2,1)S(1)}, u32[]{:S(2)}, u32[]{:S(2)}) async-start(bf16[32,128,128]{2,1,0:T(8,128)(2,1)} %bitcast.25), calls=%async_computation.2 | async-start | bytes 2097152 | tf_op jit(solution)/shard_map/all_to_all | solution.py:358
  65.9 25.4 %collective-permute-start.1 = (bf16[32,128,128]{2,1,0:T(8,128)(2,1)S(1)}, bf16[32,128,128]{2,1,0:T(8,128)(2,1)}, u32[]{:S(2)}, u32[]{:S(2)}) collective-permute-start(bf16[32,128,128]{2,1,0:T(8,128)(2,1)S(1)} %all-to-all-done.1.refs_1_), channel_id=1, source_target_pairs={{0,48},{16,0},{32,16},{48,32},{1,49},{17,1},{33,17},{49,33},{2,50}... | collective-permute-start | bytes 3145736 | tf_op jit(solution)/shard_map/ppermute | solution.py:350
  68.3 26.2 %collective-permute-start = (bf16[32,128,128]{2,1,0:T(8,128)(2,1)S(1)}, bf16[32,128,128]{2,1,0:T(8,128)(2,1)}, u32[]{:S(2)}, u32[]{:S(2)}) collective-permute-start(bf16[32,128,128]{2,1,0:T(8,128)(2,1)S(1)} %all-to-all-done.1.refs_1_), channel_id=1, source_target_pairs={{0,16},{16,32},{32,48},{48,0},{1,17},{17,33},{33,49},{49,1},{2,18}... | collective-permute-start | bytes 3145736 | tf_op jit(solution)/shard_map/ppermute | solution.py:350
  82.6 12.2 %copy-start.8 = (bf16[32,128,128]{2,1,0:T(8,128)(2,1)}, bf16[32,128,128]{2,1,0:T(8,128)(2,1)S(1)}, u32[]{:S(2)}) copy-start(bf16[32,128,128]{2,1,0:T(8,128)(2,1)S(1)} %all-to-all-done.2.refs_4_) | copy-start | bytes 3145732
  82.6 40.0 %all-to-all-start.3 = ((bf16[32,2,128,128]{3,2,1,0:T(8,128)(2,1)}), bf16[32,2,128,128]{3,2,1,0:T(8,128)(2,1)}, u32[]{:S(2)}, u32[]{:S(2)}) async-start(bf16[32,2,128,128]{3,2,1,0:T(8,128)(2,1)} %bitcast.8), calls=%async_computation.3 | async-start | bytes 4194304 | tf_op jit(solution)/shard_map/all_to_all | solution.py:358
  94.5 24.2 %collective-permute-start.5 = (bf16[32,128,128]{2,1,0:T(8,128)(2,1)S(1)}, bf16[32,128,128]{2,1,0:T(8,128)(2,1)}, u32[]{:S(2)}, u32[]{:S(2)}) collective-permute-start(bf16[32,128,128]{2,1,0:T(8,128)(2,1)S(1)} %all-to-all-done.2.refs_4_), channel_id=1, source_target_pairs={{0,48},{16,0},{32,16},{48,32},{1,49},{17,1},{33,17},{49,33},{2,50}... | collective-permute-start | bytes 3145736 | tf_op jit(solution)/shard_map/ppermute | solution.py:350
  94.8 25.4 %collective-permute-start.4 = (bf16[32,128,128]{2,1,0:T(8,128)(2,1)S(1)}, bf16[32,128,128]{2,1,0:T(8,128)(2,1)}, u32[]{:S(2)}, u32[]{:S(2)}) collective-permute-start(bf16[32,128,128]{2,1,0:T(8,128)(2,1)S(1)} %all-to-all-done.2.refs_4_), channel_id=1, source_target_pairs={{0,16},{16,32},{32,48},{48,0},{1,17},{17,33},{33,49},{49,1},{2,18}... | collective-permute-start | bytes 3145736 | tf_op jit(solution)/shard_map/ppermute | solution.py:350
  96.6 2.7 %collective-permute-start.8 = (bf16[8,2,128,128]{3,2,1,0:T(8,128)(2,1)}, bf16[8,2,128,128]{3,2,1,0:T(8,128)(2,1)S(1)}, u32[]{:S(2)}, u32[]{:S(2)}) collective-permute-start(bf16[8,2,128,128]{3,2,1,0:T(8,128)(2,1)} %copy-done.10), channel_id=1, source_target_pairs={{0,8},{8,0},{1,9},{9,1},{2,10},{10,2},{3,11},{11,3},{4,12},{12,4},... | collective-permute-start | bytes 1572872 | tf_op jit(solution)/shard_map/ppermute | solution.py:366
  96.6 3.4 %collective-permute-start.9 = (bf16[8,2,128,128]{3,2,1,0:T(8,128)(2,1)S(1)}, bf16[8,2,128,128]{3,2,1,0:T(8,128)(2,1)S(1)}, u32[]{:S(2)}, u32[]{:S(2)}) collective-permute-start(bf16[8,2,128,128]{3,2,1,0:T(8,128)(2,1)S(1)} %slice.40.refs_1_), channel_id=1, source_target_pairs={{0,8},{8,0},{1,9},{9,1},{2,10},{10,2},{3,11},{11,3},{4,12},{12,4},... | collective-permute-start | bytes 1572872 | tf_op jit(solution)/shard_map/ppermute | solution.py:366
  97.1 3.0 %collective-permute-start.10 = (bf16[8,2,128,128]{3,2,1,0:T(8,128)(2,1)S(1)}, bf16[8,2,128,128]{3,2,1,0:T(8,128)(2,1)}, u32[]{:S(2)}, u32[]{:S(2)}) collective-permute-start(bf16[8,2,128,128]{3,2,1,0:T(8,128)(2,1)S(1)} %collective-permute-done.3.refs_2_), channel_id=1, source_target_pairs={{0,8},{8,0},{1,9},{9,1},{2,10},{10,2},{3,11},{11,3},{4,12},{12,4},... | collective-permute-start | bytes 1572872 | tf_op jit(solution)/shard_map/ppermute | solution.py:366
  99.3 0.9 copy-start.13
  100.0 0.8 copy-start.14
  120.3 20.8 %collective-permute-start.12 = (bf16[8,2,128,128]{3,2,1,0:T(8,128)(2,1)}, bf16[8,2,128,128]{3,2,1,0:T(8,128)(2,1)S(1)}, u32[]{:S(2)}, u32[]{:S(2)}) collective-permute-start(bf16[8,2,128,128]{3,2,1,0:T(8,128)(2,1)} %get-tuple-element.74), channel_id=1, source_target_pairs={{0,8},{8,0},{1,9},{9,1},{2,10},{10,2},{3,11},{11,3},{4,12},{12,4},... | collective-permute-start | bytes 1572872 | tf_op jit(solution)/shard_map/ppermute | solution.py:366
  120.3 22.7 %collective-permute-start.14 = (bf16[8,2,128,128]{3,2,1,0:T(8,128)(2,1)}, bf16[8,2,128,128]{3,2,1,0:T(8,128)(2,1)S(1)}, u32[]{:S(2)}, u32[]{:S(2)}) collective-permute-start(bf16[8,2,128,128]{3,2,1,0:T(8,128)(2,1)} %get-tuple-element.78), channel_id=1, source_target_pairs={{0,8},{8,0},{1,9},{9,1},{2,10},{10,2},{3,11},{11,3},{4,12},{12,4},... | collective-permute-start | bytes 1572872 | tf_op jit(solution)/shard_map/ppermute | solution.py:366
  122.7 45.3 %collective-permute-start.11 = (bf16[8,2,128,128]{3,2,1,0:T(8,128)(2,1)}, bf16[8,2,128,128]{3,2,1,0:T(8,128)(2,1)}, u32[]{:S(2)}, u32[]{:S(2)}) collective-permute-start(bf16[8,2,128,128]{3,2,1,0:T(8,128)(2,1)} %get-tuple-element.70), channel_id=1, source_target_pairs={{0,8},{8,0},{1,9},{9,1},{2,10},{10,2},{3,11},{11,3},{4,12},{12,4},... | collective-permute-start | bytes 1572872 | tf_op jit(solution)/shard_map/ppermute | solution.py:366
  122.7 18.4 %copy-start.12 = (bf16[8,2,128,128]{3,2,1,0:T(8,128)(2,1)S(1)}, bf16[8,2,128,128]{3,2,1,0:T(8,128)(2,1)}, u32[]{:S(2)}) copy-start(bf16[8,2,128,128]{3,2,1,0:T(8,128)(2,1)} %get-tuple-element.72) | copy-start | bytes 1572868
  141.1 1.9 copy-start.11
  141.3 26.7 %collective-permute-start.13 = (bf16[8,2,128,128]{3,2,1,0:T(8,128)(2,1)S(1)}, bf16[8,2,128,128]{3,2,1,0:T(8,128)(2,1)}, u32[]{:S(2)}, u32[]{:S(2)}) collective-permute-start(bf16[8,2,128,128]{3,2,1,0:T(8,128)(2,1)S(1)} %add_convert_fusion.1), channel_id=1, source_target_pairs={{0,112},{16,0},{32,16},{48,32},{64,48},{80,64},{96,80},{112,96},{1... | collective-permute-start | bytes 1572872 | tf_op jit(solution)/shard_map/ppermute | solution.py:350
  143.1 24.9 %collective-permute-start.15 = (bf16[8,2,128,128]{3,2,1,0:T(8,128)(2,1)S(1)}, bf16[8,2,128,128]{3,2,1,0:T(8,128)(2,1)}, u32[]{:S(2)}, u32[]{:S(2)}) collective-permute-start(bf16[8,2,128,128]{3,2,1,0:T(8,128)(2,1)S(1)} %add_convert_fusion), channel_id=1, source_target_pairs={{0,16},{16,32},{32,48},{48,64},{64,80},{80,96},{96,112},{112,0},{1... | collective-permute-start | bytes 1572872 | tf_op jit(solution)/shard_map/ppermute | solution.py:350
  144.9 38.6 %collective-permute-start.6 = (bf16[16,2,128,128]{3,2,1,0:T(8,128)(2,1)}, bf16[16,2,128,128]{3,2,1,0:T(8,128)(2,1)S(1)}, u32[]{:S(2)}, u32[]{:S(2)}) collective-permute-start(bf16[16,2,128,128]{3,2,1,0:T(8,128)(2,1)} %get-tuple-element.60), channel_id=1, source_target_pairs={{0,48},{16,0},{32,16},{48,32},{1,49},{17,1},{33,17},{49,33},{2,50}... | collective-permute-start | bytes 3145736 | tf_op jit(solution)/shard_map/ppermute | solution.py:350
  149.2 34.4 %collective-permute-start.7 = (bf16[16,2,128,128]{3,2,1,0:T(8,128)(2,1)}, bf16[16,2,128,128]{3,2,1,0:T(8,128)(2,1)S(1)}, u32[]{:S(2)}, u32[]{:S(2)}) collective-permute-start(bf16[16,2,128,128]{3,2,1,0:T(8,128)(2,1)} %get-tuple-element.61), channel_id=1, source_target_pairs={{0,16},{16,32},{32,48},{48,0},{1,17},{17,33},{33,49},{49,1},{2,18}... | collective-permute-start | bytes 3145736 | tf_op jit(solution)/shard_map/ppermute | solution.py:350
  170.5 10.9 %copy-start.15 = (bf16[16,128,128]{2,1,0:T(8,128)(2,1)S(1)}, bf16[16,128,128]{2,1,0:T(8,128)(2,1)}, u32[]{:S(2)}) copy-start(bf16[16,128,128]{2,1,0:T(8,128)(2,1)} %get-tuple-element.57) | copy-start | bytes 1572868
  170.5 21.1 %all-to-all-start.4 = ((bf16[8,3,128,128]{3,2,1,0:T(8,128)(2,1)}), bf16[8,3,128,128]{3,2,1,0:T(8,128)(2,1)S(1)}, u32[]{:S(2)}, u32[]{:S(2)}) async-start(bf16[8,3,128,128]{3,2,1,0:T(8,128)(2,1)} %total_grads.1), calls=%async_computation.4 | async-start | bytes 1572864 | tf_op jit(solution)/shard_map/all_to_all | solution.py:358
  177.6 25.4 %collective-permute-start.16 = (bf16[16,2,128,128]{3,2,1,0:T(8,128)(2,1)}, bf16[16,2,128,128]{3,2,1,0:T(8,128)(2,1)}, u32[]{:S(2)}, u32[]{:S(2)}) collective-permute-start(bf16[16,2,128,128]{3,2,1,0:T(8,128)(2,1)} %get-tuple-element.82), channel_id=1, source_target_pairs={{0,48},{16,0},{32,16},{48,32},{1,49},{17,1},{33,17},{49,33},{2,50}... | collective-permute-start | bytes 3145736 | tf_op jit(solution)/shard_map/ppermute | solution.py:350
  181.4 24.4 %collective-permute-start.17 = (bf16[16,2,128,128]{3,2,1,0:T(8,128)(2,1)}, bf16[16,2,128,128]{3,2,1,0:T(8,128)(2,1)}, u32[]{:S(2)}, u32[]{:S(2)}) collective-permute-start(bf16[16,2,128,128]{3,2,1,0:T(8,128)(2,1)} %get-tuple-element.83), channel_id=1, source_target_pairs={{0,16},{16,32},{32,48},{48,0},{1,17},{17,33},{33,49},{49,1},{2,18}... | collective-permute-start | bytes 3145736 | tf_op jit(solution)/shard_map/ppermute | solution.py:350
  183.5 22.3 %copy-start.5 = (bf16[16,2,128,128]{3,2,1,0:T(8,128)(2,1)}, bf16[16,2,128,128]{3,2,1,0:T(8,128)(2,1)S(1)}, u32[]{:S(2)}) copy-start(bf16[16,2,128,128]{3,2,1,0:T(8,128)(2,1)S(1)} %collective-permute-done.6.right0) | copy-start | bytes 3145732
  183.5 8.1 %copy-start.6 = (bf16[16,2,128,128]{3,2,1,0:T(8,128)(2,1)}, bf16[16,2,128,128]{3,2,1,0:T(8,128)(2,1)S(1)}, u32[]{:S(2)}) copy-start(bf16[16,2,128,128]{3,2,1,0:T(8,128)(2,1)S(1)} %collective-permute-done.7.left0) | copy-start | bytes 3145732
  191.6 19.3 %copy-start.1 = (bf16[8,3,128,128]{3,2,1,0:T(8,128)(2,1)}, bf16[8,3,128,128]{3,2,1,0:T(8,128)(2,1)S(1)}, u32[]{:S(2)}) copy-start(bf16[8,3,128,128]{3,2,1,0:T(8,128)(2,1)S(1)} %all-to-all-done.4.b_ref) | copy-start | bytes 2359300
  191.6 21.6 %all-to-all-start.5 = ((bf16[32,128,128]{2,1,0:T(8,128)(2,1)}), bf16[32,128,128]{2,1,0:T(8,128)(2,1)S(1)}, u32[]{:S(2)}, u32[]{:S(2)}) async-start(bf16[32,128,128]{2,1,0:T(8,128)(2,1)} %pad_maximum_fusion), calls=%async_computation.5 | async-start | bytes 2097152 | tf_op jit(solution)/shard_map/all_to_all | solution.py:358
  213.1 1.0 copy-start.3
  214.1 34.2 %all-to-all-start.6 = ((bf16[32,2,128,128]{3,2,1,0:T(8,128)(2,1)}), bf16[32,2,128,128]{3,2,1,0:T(8,128)(2,1)S(1)}, u32[]{:S(2)}, u32[]{:S(2)}) async-start(bf16[32,2,128,128]{3,2,1,0:T(8,128)(2,1)} %bitcast.23), calls=%async_computation.6 | async-start | bytes 4194304 | tf_op jit(solution)/shard_map/all_to_all | solution.py:358
  248.3 1.3 copy-start

commit v12 on v11

--- a/solution.py
+++ b/solution.py
@@ -15,6 +15,7 @@
 MAXK = 12
 HPG = 5
 WAYS = 2
+PLACES = 7
 BUCKETS = (4, 6, 8, 10, 12)
 STEP = 2
 ATTENTION_COST = 10
@@ -37,9 +38,9 @@
     return x.reshape(-1, 8, HD)
 
 
-def query_blocks(n_keys, blocks, ids_ref, counts, qd, kv, acc, dq, kv_cat, sd_scr, x_cat):
+def query_blocks(n_keys, blocks, ids, counts, qd, kv, acc, dq, kv_cat, sd_scr, x_cat):
     ways = range(len(blocks))
-    index = [[ids_ref[b * MAXK + s] for s in range(n_keys)] for b in blocks]
+    index = [[ids(b, s) for s in range(n_keys)] for b in blocks]
     rows = [pl.ds(s * BLK, BLK) for s in range(n_keys)]
     for i in ways:
         for s in range(n_keys):
@@ -49,22 +50,19 @@
         part = pl.ds(s * BLK, min(STEP, n_keys - s) * BLK)
         for i in ways:
             sd_scr[i, part, :] = dot(kv_cat[i, part, :], w_t[i], NT)
+    hidden = [[jnp.where(s < counts[i], 0.0, NEG) for s in range(n_keys)] for i in ways]
     top = []
     for i in ways:
         m8 = jnp.full((8, HD), NEG, F32)
         for s in range(n_keys):
-            st = sd_scr[i, rows[s], :HD]
-            if s > 0:
-                st = jnp.where(s < counts[i], st, NEG)
-                sd_scr[i, rows[s], :HD] = st
-            m8 = jnp.maximum(m8, jnp.max(fold(st), axis=0))
+            m8 = jnp.maximum(m8, jnp.max(fold(sd_scr[i, rows[s], :HD]), axis=0) + hidden[i][s])
         top.append(jnp.max(m8, axis=0, keepdims=True) * (SCALE * LOG2E))
     inv, rd = [], []
     for i in ways:
         l8 = jnp.zeros((8, HD), F32)
         r8 = jnp.zeros((8, HD), F32)
         for s in range(n_keys):
-            p = jnp.exp2(sd_scr[i, rows[s], :HD] * (SCALE * LOG2E) - top[i])
+            p = jnp.exp2(sd_scr[i, rows[s], :HD] * (SCALE * LOG2E) - (top[i] - hidden[i][s]))
             sd_scr[i, rows[s], :HD] = p
             l8 += jnp.sum(fold(p), axis=0)
             r8 += jnp.sum(fold(p * sd_scr[i, rows[s], HD:]), axis=0)
@@ -84,19 +82,20 @@
         dq[blocks[i]] = (dot(x_cat[i, every, :HD], kv_cat[i, every, :HD], TN) * SCALE).astype(BF16)
 
 
-def attention_kernel(size, n_query, fetches, ids_ref, cnt_ref, place_ref, *refs):
+def attention_kernel(part, size, n_query, fetches, lists_ref, places_ref, *refs):
+    place = [places_ref[part * PLACES + i] for i in range(PLACES)]
     sources, refs = refs[: len(fetches)], refs[len(fetches) :]
     shared = n_query < size
     qd_in, dq_out, targets = refs[0], refs[1], refs[2:5]
     if shared:
         give_out, refs = refs[5:8], refs[3:]
-    kv, qd, acc, stage, dq, kv_cat, sd_scr, x_cat, order, in_sem, out_sem = refs[5:]
+    kv, qd, acc, stage, dq, kv_cat, sd_scr, x_cat, order, counted, in_sem, out_sem = refs[5:]
     copies = []
     for source, fetch in zip(sources, fetches):
-        for src, t, row in fetch(source, place_ref):
+        for src, t, row in fetch(source, place):
             dst = kv.at[pl.ds(row, src.shape[0]), :, pl.ds(t * HD, HD)]
             copies.append(pltpu.make_async_copy(src, dst, in_sem.at[len(copies)]))
-    q_rows = pl.ds(pl.multiple_of(place_ref[0], 8), n_query)
+    q_rows = pl.ds(pl.multiple_of(place[0], 8), n_query)
     for t in range(2):
         src = qd_in.at[q_rows, qd_in.shape[1] - 2 + t]
         dst = qd.at[:, pl.ds(t * HD, HD), pl.ds(t * HD, HD)]
@@ -106,9 +105,22 @@
     acc[...] = jnp.zeros_like(acc)
     for t in range(2):
         qd[:, t * HD : (t + 1) * HD, (1 - t) * HD : (2 - t) * HD] = jnp.zeros((n_query, HD, HD), BF16)
+    def entry(b, s):
+        run = lax.shift_right_logical(b, 3)
+        return lists_ref[place[4] + run * place[6] + (b - run * BPD) * (MAXK + 1) + s]
+
+    def ids(b, s):
+        return entry(b, s) - place[5]
+
+    def note(b, carry):
+        counted[b] = entry(b, MAXK)
+        return carry
+
+    lax.fori_loop(0, n_query, note, 0)
+
     def rank(k, at):
-        def place(b, at):
-            hit = cnt_ref[b] == MAXK - k
+        def put(b, at):
+            hit = counted[b] == MAXK - k
 
             @pl.when(hit)
             def _():
@@ -116,7 +128,7 @@
 
             return at + hit.astype(jnp.int32)
 
-        return lax.fori_loop(0, n_query, place, at)
+        return lax.fori_loop(0, n_query, put, at)
 
     lax.fori_loop(0, MAXK, rank, 0)
     for copy in copies:
@@ -124,12 +136,12 @@
 
     def some(k, carry):
         blocks = [order[k * WAYS + i] for i in range(WAYS)]
-        counts = [cnt_ref[b] for b in blocks]
+        counts = [counted[b] for b in blocks]
         for least, upto in zip((0, *BUCKETS), BUCKETS):
 
             @pl.when((counts[0] > least) & (counts[0] <= upto))
             def _():
-                query_blocks(upto, blocks, ids_ref, counts, qd, kv, acc, dq, kv_cat, sd_scr, x_cat)
+                query_blocks(upto, blocks, ids, counts, qd, kv, acc, dq, kv_cat, sd_scr, x_cat)
 
         return carry
 
@@ -146,8 +158,8 @@
         lax.fori_loop(i * size, (i + 1) * size, convert, 0)
         rows = pl.ds(i * size, size)
         if shared:
-            keep = pl.multiple_of(i * size + place_ref[1], 8)
-            give = pl.multiple_of(i * size + n_query - place_ref[1], 8)
+            keep = pl.multiple_of(i * size + place[1], 8)
+            give = pl.multiple_of(i * size + n_query - place[1], 8)
             rows = pl.ds(keep, n_query)
             puts.append(
                 pltpu.make_async_copy(stage.at[pl.ds(give, n_query)], give_out[i], out_sem.at[4 + i])
@@ -159,7 +171,7 @@
         copy.wait()
 
 
-def attention(ids, counts, place, sources, fetches, qd, n_query, size):
+def attention(part, lists, places, sources, fetches, qd, n_query, size):
     window = 3 * size
     shared = n_query < size
     kept = jax.ShapeDtypeStruct((n_query, 2, BLK, HD), BF16)
@@ -168,9 +180,9 @@
     hbm = pl.BlockSpec(memory_space=pl.ANY)
     pairs = n_query * 8
     out = pl.pallas_call(
-        functools.partial(attention_kernel, size, n_query, fetches),
+        functools.partial(attention_kernel, part, size, n_query, fetches),
         out_shape=[jax.ShapeDtypeStruct((n_query, BLK, HD), BF16)] + [kept] * 3 + given,
-        in_specs=[smem] * 3 + [hbm] * (len(sources) + 1),
+        in_specs=[smem] * 2 + [hbm] * (len(sources) + 1),
         out_specs=[hbm] * (4 + len(given)),
         scratch_shapes=[
             pltpu.VMEM((window, BLK, 2 * HD), BF16),
@@ -182,6 +194,7 @@
             pltpu.VMEM((WAYS, MAXK * BLK, 2 * HD), F32),
             pltpu.VMEM((WAYS, MAXK * BLK, 2 * HD), BF16),
             pltpu.SMEM((n_query,), jnp.int32),
+            pltpu.SMEM((n_query,), jnp.int32),
             pltpu.SemaphoreType.DMA((14,)),
             pltpu.SemaphoreType.DMA((7,)),
         ],
@@ -192,7 +205,7 @@
             transcendentals=0 if shared else pairs * BLK * BLK,
         ),
         name="attention",
-    )(ids, counts, place, *sources, qd)
+    )(lists, places, *sources, qd)
     return out[0], out[1:]
 
 
@@ -372,20 +385,23 @@
     packed = jnp.concatenate([key_blocks, block_count[:, :, None]], axis=2)
     b = fifth_heads(key_in, value_in, query_in, out_grad)
     gathered = lax.all_gather(after(packed, b), ("half", "core"))
-    list_b = gathered[2 * half + core, 4]
-    lists = lax.dynamic_index_in_dim(gathered, 2 * half + core, 1, False)
+    runs_first = [(h * (last + 1) + x - 1) * size for h in (0, 1, half)]
+    heads = BPD * (MAXK + 1)
+    places = []
+    for s in range(2):
+        left, right = jnp.where(x == 0, 1 - s, s) * size, jnp.where(x == last, 1 - s, s) * size
+        begin = (2 * s * HPG + 2 * half + core) * heads
+        places += [s * size, left, s * size, right, begin, runs_first[s], HPG * heads]
+    places += [0, core * BPD, 0, 0, ((2 * half + core) * HPG + HPG - 1) * heads, runs_first[2], 0]
+    places = jnp.stack([jnp.asarray(p, jnp.int32) for p in places])
+    lists, places = lax.optimization_barrier((gathered.reshape(-1), places))
     ka, va, qda = split_heads(*lax.optimization_barrier((key_in, value_in, query_in, out_grad, b))[:4])
-
-    def plain(lists, chip):
-        lists = lists.reshape(-1, MAXK + 1)
-        first_block = (chip - 1) * 2 * BPD
-        return (lists[:, :MAXK] - first_block).reshape(-1), lists[:, MAXK]
 
     own_b = exchange(b, "group")
     pairs_b = own_b[:, :2]
     mine = (shift(pairs_b, CHIPS, 1), pairs_b, shift(pairs_b, CHIPS, -1))
 
-    keys = exchange(after(ka, own_b, gathered), WIDE)
+    keys = exchange(after(ka, own_b, lists, places), WIDE)
     key_near = [shift(keys, "x", 1), shift(keys, "x", -1)]
     values = first_values = exchange(after(va, keys, *mine), WIDE)
     values = after(values, *key_near)
@@ -399,11 +415,9 @@
 
         return fetch
 
-    ids, counts = plain(list_b, half * (last + 1) + x)
-    place = jnp.stack([jnp.int32(0), core * BPD])
     fetches = [run(i, other) for other in range(2) for i in range(3)]
     dq_b, (left_b, mine_b, right_b, *give_b) = attention(
-        ids, counts, place, mine + theirs, fetches, after(own_b, values, *key_near), BPD, size
+        2, lists, places, mine + theirs, fetches, after(own_b, values, *key_near), BPD, size
     )
     got_b = [swap(after(give, *value_near)) for give in give_b]
 
@@ -416,12 +430,8 @@
     sources = (key_near[0], keys, key_near[1], value_near[0], values, value_near[1])
     done = []
     for s in range(2):
-        ids, counts = plain(lists[2 * s : 2 * s + 2], s * (last + 1) + x)
-        left = jnp.where(x == 0, 1 - s, s) * size
-        right = jnp.where(x == last, 1 - s, s) * size
-        place = jnp.stack([jnp.int32(s * size), left, jnp.int32(s * size), right])
-        place = after(place, *[d[0] for d in done])
-        dq, grads = attention(ids, counts, place, sources, fetches, queries, size, size)
+        part_places = after(places, *[d[0] for d in done])
+        dq, grads = attention(s, lists, part_places, sources, fetches, queries, size, size)
         done.append((dq, grads, shift(grads[0], "x", -1), shift(grads[2], "x", 1)))
         if s == 0:
             left_b, right_b = add(after(left_b, dq), got_b[0]), add(after(right_b, dq), got_b[2])

time: 256 us -> 261 us (1.020)
  starting transfers between devices: 63.2 us -> 69.5 us
    all_to_all x7, starting transfers between devices: 43.5 us -> 53 us  [exchange(): return lax.all_to_all(x, axes, 0, 0, tiled=True)]
    ppermute x12, starting transfers between devices: 18.4 us -> 15.1 us  [shift(): lax.ppermute(value, axes, [(s, (s + steps) % count) for s in range(count)])]
    unnamed x38 -> x46, local copies, waits for them, and re-layouts: 4.25 us -> 5.57 us
  transfers between devices with their start and end apart: 25 -> 25, of which waited for: 16 -> 16; matrix products, arithmetic and copies ran while one was open for 4% -> 2% of each run, Pallas kernels for 25% -> 25%
where the time goes in v12:
time: 261 us; the launch traced here: 259 us
  waiting for transfers between devices  101 us (39%)
  Pallas kernels  70.5 us (27%)
  starting transfers between devices  69.5 us (27%)
  local copies, waits for them, and re-layouts  7.19 us (3%)
  blocking collectives  6.44 us (2%)
  other arithmetic  3.11 us (1%)
    all_to_all x7, waiting for transfers between devices, exchange(): return lax.all_to_all(x, axes, 0, 0, tiled=True)  55.1 us
    all_to_all x7, starting transfers between devices, exchange(): return lax.all_to_all(x, axes, 0, 0, tiled=True)  53 us
    pallas_call x3, Pallas kernels, attention(): pl.pallas_call(functools.partial(attention_kernel, part, size, n_query, f...  48 us
    ppermute x12, waiting for transfers between devices, shift(): lax.ppermute(value, axes, [(s, (s + steps) % count) for s in range(count)])  43.4 us
    ppermute x12, starting transfers between devices, shift(): lax.ppermute(value, axes, [(s, (s + steps) % count) for s in range(count)])  15.1 us
    pallas_call x2, Pallas kernels, join_heads(): pl.pallas_call(functools.partial(join_kernel, first), grid=(groups // ste...  7.73 us
    all_gather x1, blocking collectives, shards(): gathered = lax.all_gather(after(packed, b), ('half', 'core'))  6.44 us
    unnamed x46, local copies, waits for them, and re-layouts  5.57 us
  transfers between devices with their start and end apart: 25, of which 16 were waited for; matrix products, arithmetic and copies ran while one was open for 2% of the time, Pallas kernels for 25%

profile of v12, /device:TPU:8, one launch (start us, length us, event | category | flops | bytes accessed | tf_op | source)
XLA Modules:
  0.0 258.8 jit_solution(12754689524295471564)
XLA Ops:
  0.6 2.2 fifth_heads.1
  2.8 0.0 copy-start.20
  2.9 0.0 copy-start.19
  2.9 8.2 %all-to-all-start = ((bf16[8,4,128,128]{3,2,1,0:T(8,128)(2,1)}), bf16[8,4,128,128]{3,2,1,0:T(8,128)(2,1)S(1)}, u32[]{:S(2)}, u32[]{:S(2)}) async-start(bf16[8,4,128,128]{3,2,1,0:T(8,128)(2,1)} %fifth_heads.1), calls=%async_computation | async-start | bytes 2097152 | tf_op jit(solution)/shard_map/all_to_all | solution.py:371
  11.1 0.1 copy.11
  11.2 0.1 pad_add_fusion
  11.3 6.4 %all-gather = s32[20,8,13]{2,1,0:T(8,128)S(1)} all-gather(s32[5,8,13]{2,1,0:T(8,128)S(1)} %pad_add_fusion), channel_id=2, replica_groups=mesh['half'=2,'x'=4,'core'=2,'group'=8] {'half','core'}, dimensions={0}, use_global_device_ids=true | all-gather | bytes 10400 | tf_op jit(solution)/shard_map/all_gather | solution.py:387
  17.7 0.8 reshape.24.lists_ref
  18.5 0.7 stack.53.places_ref
  19.2 5.1 %split_heads.1 = (bf16[4,8,128,128]{3,2,1,0:T(8,128)(2,1)}, bf16[4,8,128,128]{3,2,1,0:T(8,128)(2,1)}, bf16[4,8,2,128,128]{4,3,2,1,0:T(8,128)(2,1)}) custom-call(bf16[128,5120]{1,0:T(8,128)(2,1)} %k_ref.2, bf16[128,5120]{1,0:T(8,128)(2,1)} %v_ref.2, bf16[128,5120]{1,0:T(8,128)(2,1)} %q_ref.2, bf16[128,5120]{1,0:T(8,128)(2,1)} %g_ref.2), custom_call_target="tpu_custom_call" | custom-call | bytes 10485760 | tf_op jit(solution)/shard_map/split_heads/pallas_call | solution.py:227
  24.3 2.8 %all-to-all-done.refs_6_ = bf16[8,4,128,128]{3,2,1,0:T(8,128)(2,1)S(1)} async-done(((bf16[8,4,128,128]{3,2,1,0:T(8,128)(2,1)}), bf16[8,4,128,128]{3,2,1,0:T(8,128)(2,1)S(1)}, u32[]{:S(2)}, u32[]{:S(2)}) %all-to-all-start) | async-done | bytes 1048608 | tf_op jit(solution)/shard_map/all_to_all | solution.py:371
  27.1 12.4 %all-to-all-start.1 = ((bf16[32,128,128]{2,1,0:T(8,128)(2,1)}), bf16[32,128,128]{2,1,0:T(8,128)(2,1)S(1)}, u32[]{:S(2)}, u32[]{:S(2)}) async-start(bf16[32,128,128]{2,1,0:T(8,128)(2,1)} %bitcast.24), calls=%async_computation.1 | async-start | bytes 2097152 | tf_op jit(solution)/shard_map/all_to_all | solution.py:371
  39.6 3.7 %collective-permute-start.3 = (bf16[8,2,128,128]{3,2,1,0:T(8,128)(2,1)S(1)}, bf16[8,2,128,128]{3,2,1,0:T(8,128)(2,1)S(1)}, u32[]{:S(2)}, u32[]{:S(2)}) collective-permute-start(bf16[8,2,128,128]{3,2,1,0:T(8,128)(2,1)S(1)} %slice.4.refs_1_), channel_id=1, source_target_pairs={{0,112},{16,0},{32,16},{48,32},{64,48},{80,64},{96,80},{112,96},{1... | collective-permute-start | bytes 1572872 | tf_op jit(solution)/shard_map/ppermute | solution.py:363
  43.3 18.0 %collective-permute-done.3.refs_2_ = bf16[8,2,128,128]{3,2,1,0:T(8,128)(2,1)S(1)} collective-permute-done((bf16[8,2,128,128]{3,2,1,0:T(8,128)(2,1)S(1)}, bf16[8,2,128,128]{3,2,1,0:T(8,128)(2,1)S(1)}, u32[]{:S(2)}, u32[]{:S(2)}) %collective-permute-start.3) | collective-permute-done | bytes 524320 | tf_op jit(solution)/shard_map/ppermute | solution.py:363
  61.3 2.5 collective-permute-done.2.refs_0_
  63.8 1.7 all-to-all-done.1.refs_1_
  65.6 6.9 %all-to-all-start.2 = ((bf16[32,128,128]{2,1,0:T(8,128)(2,1)}), bf16[32,128,128]{2,1,0:T(8,128)(2,1)S(1)}, u32[]{:S(2)}, u32[]{:S(2)}) async-start(bf16[32,128,128]{2,1,0:T(8,128)(2,1)} %bitcast.23), calls=%async_computation.2 | async-start | bytes 2097152 | tf_op jit(solution)/shard_map/all_to_all | solution.py:371
  72.5 2.4 collective-permute-start.1
  74.9 14.3 %all-to-all-done.2.refs_4_ = bf16[32,128,128]{2,1,0:T(8,128)(2,1)S(1)} async-done(((bf16[32,128,128]{2,1,0:T(8,128)(2,1)}), bf16[32,128,128]{2,1,0:T(8,128)(2,1)S(1)}, u32[]{:S(2)}, u32[]{:S(2)}) %all-to-all-start.2) | async-done | bytes 1048608 | tf_op jit(solution)/shard_map/all_to_all | solution.py:371
  89.2 5.6 %all-to-all-start.3 = ((bf16[32,2,128,128]{3,2,1,0:T(8,128)(2,1)}), bf16[32,2,128,128]{3,2,1,0:T(8,128)(2,1)}, u32[]{:S(2)}, u32[]{:S(2)}) async-start(bf16[32,2,128,128]{3,2,1,0:T(8,128)(2,1)} %bitcast.22), calls=%async_computation.3 | async-start | bytes 4194304 | tf_op jit(solution)/shard_map/all_to_all | solution.py:371
  94.9 3.0 %collective-permute-done.1.refs_2_ = bf16[32,128,128]{2,1,0:T(8,128)(2,1)} collective-permute-done((bf16[32,128,128]{2,1,0:T(8,128)(2,1)S(1)}, bf16[32,128,128]{2,1,0:T(8,128)(2,1)}, u32[]{:S(2)}, u32[]{:S(2)}) %collective-permute-start.1) | collective-permute-done | bytes 1048608 | tf_op jit(solution)/shard_map/ppermute | solution.py:363
  97.9 3.2 %collective-permute-done.refs_0_ = bf16[32,128,128]{2,1,0:T(8,128)(2,1)} collective-permute-done((bf16[32,128,128]{2,1,0:T(8,128)(2,1)S(1)}, bf16[32,128,128]{2,1,0:T(8,128)(2,1)}, u32[]{:S(2)}, u32[]{:S(2)}) %collective-permute-start) | collective-permute-done | bytes 1048608 | tf_op jit(solution)/shard_map/ppermute | solution.py:363
  101.1 0.3 collective-permute-start.5
  101.4 1.7 collective-permute-start.4
  103.2 0.5 collective-permute-start.9
  103.7 0.3 collective-permute-start.10
  103.9 2.0 collective-permute-done.8.refs_3_
  106.0 0.6 collective-permute-done.10.refs_5_
  106.6 0.2 copy-done.12
  106.8 0.2 copy-done.13
  106.9 0.8 copy-done.14
  107.7 11.2 %attention.5 = (bf16[8,128,128]{2,1,0:T(8,128)(2,1)}, bf16[8,2,128,128]{3,2,1,0:T(8,128)(2,1)}, bf16[8,2,128,128]{3,2,1,0:T(8,128)(2,1)}, bf16[8,2,128,128]{3,2,...) custom-call(s32[2080]{0:T(1024)} %reshape.24.lists_ref, ...), custom_call_target="tpu_custom_call" | custom-call | tf_op jit(solution)/shard_map/attention/pallas_call | solution.py:182
  119.0 6.2 %collective-permute-done.5.refs_5_ = bf16[32,128,128]{2,1,0:T(8,128)(2,1)S(1)} collective-permute-done((bf16[32,128,128]{2,1,0:T(8,128)(2,1)S(1)}, bf16[32,128,128]{2,1,0:T(8,128)(2,1)S(1)}, u32[]{:S(2)}, u32[]{:S(2)}) %collective-permute-start.5) | collective-permute-done | bytes 1048608 | tf_op jit(solution)/shard_map/ppermute | solution.py:363
  125.2 1.5 collective-permute-done.4.refs_3_
  126.7 0.5 collective-permute-start.14
  127.3 0.5 copy-done.22
  127.7 19.1 %attention.3 = (bf16[16,128,128]{2,1,0:T(8,128)(2,1)}, bf16[16,2,128,128]{3,2,1,0:T(8,128)(2,1)}, bf16[16,2,128,128]{3,2,1,0:T(8,128)(2,1)}, bf16[16,2,128,128]{3,2,1,0:T(8,128)(2,1)}) custom-call(s32[2080]{0:T(1024)} %reshape.24.lists_ref, s32[21]{0:T(128)} %stack.53.places_ref, bf16[32,128,128]{2,1,0:T(8,128)(2,1)} %collective-permute-done.refs_0_, ...), custom_call_target="tpu_custom_call" | custom-call | flops 2684354560 | bytes 7340032 | tf_op jit(solution)/shard_map/attention/pallas_call | solution.py:182
  146.8 0.1 add_convert_fusion.1
  147.0 0.4 collective-permute-start.13
  147.4 0.5 copy-done.10
  147.9 0.1 add_convert_fusion
  148.0 1.3 collective-permute-start.15
  149.3 2.1 collective-permute-start.6
  151.4 17.7 %attention.4 = (bf16[16,128,128]{2,1,0:T(8,128)(2,1)}, bf16[16,2,128,128]{3,2,1,0:T(8,128)(2,1)}, bf16[16,2,128,128]{3,2,1,0:T(8,128)(2,1)}, bf16[16,2,128,128]{3,2,1,0:T(8,128)(2,1)}) custom-call(s32[2080]{0:T(1024)} %reshape.24.lists_ref, s32[21]{0:T(128)} %stack.53.places_ref, bf16[32,128,128]{2,1,0:T(8,128)(2,1)} %collective-permute-done.refs_0_, ...), custom_call_target="tpu_custom_call" | custom-call | flops 2684354560 | bytes 7340032 | tf_op jit(solution)/shard_map/attention/pallas_call | solution.py:182
  169.1 0.8 copy-done.18
  170.0 0.1 copy-done.16
  170.1 0.2 copy-done.17
  170.2 2.5 total_grads.1
  172.7 9.7 %all-to-all-start.4 = ((bf16[8,3,128,128]{3,2,1,0:T(8,128)(2,1)}), bf16[8,3,128,128]{3,2,1,0:T(8,128)(2,1)S(1)}, u32[]{:S(2)}, u32[]{:S(2)}) async-start(bf16[8,3,128,128]{3,2,1,0:T(8,128)(2,1)} %total_grads.1), calls=%async_computation.4 | async-start | bytes 1572864 | tf_op jit(solution)/shard_map/all_to_all | solution.py:371
  182.4 3.2 %collective-permute-start.16 = (bf16[16,2,128,128]{3,2,1,0:T(8,128)(2,1)}, bf16[16,2,128,128]{3,2,1,0:T(8,128)(2,1)}, u32[]{:S(2)}, u32[]{:S(2)}) collective-permute-start(bf16[16,2,128,128]{3,2,1,0:T(8,128)(2,1)} %get-tuple-element.86), channel_id=1, source_target_pairs={{0,48},{16,0},{32,16},{48,32},{1,49},{17,1},{33,17},{49,33},{2,50}... | collective-permute-start | bytes 3145736 | tf_op jit(solution)/shard_map/ppermute | solution.py:363
  185.6 2.1 pad_maximum_fusion
  187.7 8.5 %all-to-all-done.4.b_ref = bf16[8,3,128,128]{3,2,1,0:T(8,128)(2,1)S(1)} async-done(((bf16[8,3,128,128]{3,2,1,0:T(8,128)(2,1)}), bf16[8,3,128,128]{3,2,1,0:T(8,128)(2,1)S(1)}, u32[]{:S(2)}, u32[]{:S(2)}) %all-to-all-start.4) | async-done | bytes 786464 | tf_op jit(solution)/shard_map/all_to_all | solution.py:371
  196.2 4.8 %all-to-all-start.5 = ((bf16[32,128,128]{2,1,0:T(8,128)(2,1)}), bf16[32,128,128]{2,1,0:T(8,128)(2,1)S(1)}, u32[]{:S(2)}, u32[]{:S(2)}) async-start(bf16[32,128,128]{2,1,0:T(8,128)(2,1)} %pad_maximum_fusion), calls=%async_computation.5 | async-start | bytes 2097152 | tf_op jit(solution)/shard_map/all_to_all | solution.py:371
  201.0 0.6 pad_add_fusion.1.x_ref
  201.6 6.0 %collective-permute-done.16.right1 = bf16[16,2,128,128]{3,2,1,0:T(8,128)(2,1)} collective-permute-done((bf16[16,2,128,128]{3,2,1,0:T(8,128)(2,1)}, bf16[16,2,128,128]{3,2,1,0:T(8,128)(2,1)}, u32[]{:S(2)}, u32[]{:S(2)}) %collective-permute-start.16) | collective-permute-done | bytes 1048608 | tf_op jit(solution)/shard_map/ppermute | solution.py:363
  207.6 2.9 %collective-permute-done.17.left1 = bf16[16,2,128,128]{3,2,1,0:T(8,128)(2,1)} collective-permute-done((bf16[16,2,128,128]{3,2,1,0:T(8,128)(2,1)}, bf16[16,2,128,128]{3,2,1,0:T(8,128)(2,1)}, u32[]{:S(2)}, u32[]{:S(2)}) %collective-permute-start.17) | collective-permute-done | bytes 1048608 | tf_op jit(solution)/shard_map/ppermute | solution.py:363
  210.6 5.0 %both_halves.1 = bf16[2,16,2,128,128]{4,3,2,1,0:T(8,128)(2,1)} custom-call(s32[2]{0:T(128)} %pad_add_fusion.1.x_ref, bf16[16,2,128,128]{3,2,1,0:T(8,128)(2,1)} %get-tuple-element.84.own0, bf16[16,2,128,128]{3,2,1,0:T(8,128)(2,1)} %get-tuple-element.85.own1, bf16[16,2,128,128]{3,2,1,0:T(8,128)(2,1)} %copy-done.5, ...), custom_call_target="tpu_custom_call" | custom-call | bytes 8388608 | tf_op jit(solution)/shard_map/both_halves/pallas_call | solution.py:344
  215.6 2.2 all-to-all-done.5
  217.8 1.0 copy-done.3
  218.8 5.4 %all-to-all-start.6 = ((bf16[32,2,128,128]{3,2,1,0:T(8,128)(2,1)}), bf16[32,2,128,128]{3,2,1,0:T(8,128)(2,1)S(1)}, u32[]{:S(2)}, u32[]{:S(2)}) async-start(bf16[32,2,128,128]{3,2,1,0:T(8,128)(2,1)} %bitcast.20), calls=%async_computation.6 | async-start | bytes 4194304 | tf_op jit(solution)/shard_map/all_to_all | solution.py:371
  224.2 3.6 %join_heads.2 = bf16[128,5120]{1,0:T(8,128)(2,1)} custom-call(bf16[4,8,1,128,128]{4,3,2,1,0:T(8,128)(2,1)} %bitcast.21, bf16[8,3,128,128]{3,2,1,0:T(8,128)(2,1)} %copy-done.1), custom_call_target="tpu_custom_call" | custom-call | bytes 2621440 | tf_op jit(solution)/shard_map/join_heads/pallas_call | solution.py:290
  227.8 25.5 %all-to-all-done.6 = bf16[32,2,128,128]{3,2,1,0:T(8,128)(2,1)S(1)} async-done(((bf16[32,2,128,128]{3,2,1,0:T(8,128)(2,1)}), bf16[32,2,128,128]{3,2,1,0:T(8,128)(2,1)S(1)}, u32[]{:S(2)}, u32[]{:S(2)}) %all-to-all-start.6) | async-done | bytes 2097184 | tf_op jit(solution)/shard_map/all_to_all | solution.py:371
  253.3 1.4 copy-done
  254.7 4.1 %join_heads.3 = (bf16[128,5120]{1,0:T(8,128)(2,1)}, bf16[128,5120]{1,0:T(8,128)(2,1)}) custom-call(bf16[4,8,2,128,128]{4,3,2,1,0:T(8,128)(2,1)} %bitcast.19, bf16[8,3,128,128]{3,2,1,0:T(8,128)(2,1)} %copy-done.1), custom_call_target="tpu_custom_call" | custom-call | bytes 5242880 | tf_op jit(solution)/shard_map/join_heads/pallas_call | solution.py:290
  (52 shorter events, 0.2 us)
Async XLA Ops:
  2.8 8.3 %copy-start.20 = (s32[5,8]{1,0:T(8,128)S(1)}, s32[5,8]{1,0:T(8,128)}, u32[]{:S(2)}) copy-start(s32[5,8]{1,0:T(8,128)} %param.11) | copy-start | bytes 484
  2.9 8.4 %copy-start.19 = (s32[5,8,12]{2,1,0:T(8,128)S(1)}, s32[5,8,12]{2,1,0:T(8,128)}, u32[]{:S(2)}) copy-start(s32[5,8,12]{2,1,0:T(8,128)} %param.10) | copy-start | bytes 5764
  2.9 24.3 %all-to-all-start = ((bf16[8,4,128,128]{3,2,1,0:T(8,128)(2,1)}), bf16[8,4,128,128]{3,2,1,0:T(8,128)(2,1)S(1)}, u32[]{:S(2)}, u32[]{:S(2)}) async-start(bf16[8,4,128,128]{3,2,1,0:T(8,128)(2,1)} %fifth_heads.1), calls=%async_computation | async-start | bytes 2097152 | tf_op jit(solution)/shard_map/all_to_all | solution.py:371
  27.1 12.4 %copy-start.2 = (bf16[8,4,128,128]{3,2,1,0:T(8,128)(2,1)}, bf16[8,4,128,128]{3,2,1,0:T(8,128)(2,1)S(1)}, u32[]{:S(2)}) copy-start(bf16[8,4,128,128]{3,2,1,0:T(8,128)(2,1)S(1)} %all-to-all-done.refs_6_) | copy-start | bytes 3145732
  27.1 38.4 %all-to-all-start.1 = ((bf16[32,128,128]{2,1,0:T(8,128)(2,1)}), bf16[32,128,128]{2,1,0:T(8,128)(2,1)S(1)}, u32[]{:S(2)}, u32[]{:S(2)}) async-start(bf16[32,128,128]{2,1,0:T(8,128)(2,1)} %bitcast.24), calls=%async_computation.1 | async-start | bytes 2097152 | tf_op jit(solution)/shard_map/all_to_all | solution.py:371
  39.6 63.6 %copy-start.4 = (bf16[8,2,128,128]{3,2,1,0:T(8,128)(2,1)}, bf16[8,2,128,128]{3,2,1,0:T(8,128)(2,1)S(1)}, u32[]{:S(2)}) copy-start(bf16[8,2,128,128]{3,2,1,0:T(8,128)(2,1)S(1)} %slice.4.refs_1_) | copy-start | bytes 1572868
  39.6 21.7 %collective-permute-start.3 = (bf16[8,2,128,128]{3,2,1,0:T(8,128)(2,1)S(1)}, bf16[8,2,128,128]{3,2,1,0:T(8,128)(2,1)S(1)}, u32[]{:S(2)}, u32[]{:S(2)}) collective-permute-start(bf16[8,2,128,128]{3,2,1,0:T(8,128)(2,1)S(1)} %slice.4.refs_1_), channel_id=1, source_target_pairs={{0,112},{16,0},{32,16},{48,32},{64,48},{80,64},{96,80},{112,96},{1... | collective-permute-start | bytes 1572872 | tf_op jit(solution)/shard_map/ppermute | solution.py:363
  43.3 20.5 %collective-permute-start.2 = (bf16[8,2,128,128]{3,2,1,0:T(8,128)(2,1)S(1)}, bf16[8,2,128,128]{3,2,1,0:T(8,128)(2,1)}, u32[]{:S(2)}, u32[]{:S(2)}) collective-permute-start(bf16[8,2,128,128]{3,2,1,0:T(8,128)(2,1)S(1)} %slice.4.refs_1_), channel_id=1, source_target_pairs={{0,16},{16,32},{32,48},{48,64},{64,80},{80,96},{96,112},{112,0},{1... | collective-permute-start | bytes 1572872 | tf_op jit(solution)/shard_map/ppermute | solution.py:363
  61.3 42.3 %copy-start.9 = (bf16[8,2,128,128]{3,2,1,0:T(8,128)(2,1)}, bf16[8,2,128,128]{3,2,1,0:T(8,128)(2,1)S(1)}, u32[]{:S(2)}) copy-start(bf16[8,2,128,128]{3,2,1,0:T(8,128)(2,1)S(1)} %collective-permute-done.3.refs_2_) | copy-start | bytes 1572868
  65.5 23.7 %copy-start.7 = (bf16[32,128,128]{2,1,0:T(8,128)(2,1)}, bf16[32,128,128]{2,1,0:T(8,128)(2,1)S(1)}, u32[]{:S(2)}) copy-start(bf16[32,128,128]{2,1,0:T(8,128)(2,1)S(1)} %all-to-all-done.1.refs_1_) | copy-start | bytes 3145732
  65.6 23.7 %all-to-all-start.2 = ((bf16[32,128,128]{2,1,0:T(8,128)(2,1)}), bf16[32,128,128]{2,1,0:T(8,128)(2,1)S(1)}, u32[]{:S(2)}, u32[]{:S(2)}) async-start(bf16[32,128,128]{2,1,0:T(8,128)(2,1)} %bitcast.23), calls=%async_computation.2 | async-start | bytes 2097152 | tf_op jit(solution)/shard_map/all_to_all | solution.py:371
  72.5 25.4 %collective-permute-start.1 = (bf16[32,128,128]{2,1,0:T(8,128)(2,1)S(1)}, bf16[32,128,128]{2,1,0:T(8,128)(2,1)}, u32[]{:S(2)}, u32[]{:S(2)}) collective-permute-start(bf16[32,128,128]{2,1,0:T(8,128)(2,1)S(1)} %all-to-all-done.1.refs_1_), channel_id=1, source_target_pairs={{0,48},{16,0},{32,16},{48,32},{1,49},{17,1},{33,17},{49,33},{2,50}... | collective-permute-start | bytes 3145736 | tf_op jit(solution)/shard_map/ppermute | solution.py:363
  74.9 26.2 %collective-permute-start = (bf16[32,128,128]{2,1,0:T(8,128)(2,1)S(1)}, bf16[32,128,128]{2,1,0:T(8,128)(2,1)}, u32[]{:S(2)}, u32[]{:S(2)}) collective-permute-start(bf16[32,128,128]{2,1,0:T(8,128)(2,1)S(1)} %all-to-all-done.1.refs_1_), channel_id=1, source_target_pairs={{0,16},{16,32},{32,48},{48,0},{1,17},{17,33},{33,49},{49,1},{2,18}... | collective-permute-start | bytes 3145736 | tf_op jit(solution)/shard_map/ppermute | solution.py:363
  89.2 12.2 %copy-start.8 = (bf16[32,128,128]{2,1,0:T(8,128)(2,1)}, bf16[32,128,128]{2,1,0:T(8,128)(2,1)S(1)}, u32[]{:S(2)}) copy-start(bf16[32,128,128]{2,1,0:T(8,128)(2,1)S(1)} %all-to-all-done.2.refs_4_) | copy-start | bytes 3145732
  89.2 38.5 %all-to-all-start.3 = ((bf16[32,2,128,128]{3,2,1,0:T(8,128)(2,1)}), bf16[32,2,128,128]{3,2,1,0:T(8,128)(2,1)}, u32[]{:S(2)}, u32[]{:S(2)}) async-start(bf16[32,2,128,128]{3,2,1,0:T(8,128)(2,1)} %bitcast.22), calls=%async_computation.3 | async-start | bytes 4194304 | tf_op jit(solution)/shard_map/all_to_all | solution.py:371
  101.1 24.1 %collective-permute-start.5 = (bf16[32,128,128]{2,1,0:T(8,128)(2,1)S(1)}, bf16[32,128,128]{2,1,0:T(8,128)(2,1)S(1)}, u32[]{:S(2)}, u32[]{:S(2)}) collective-permute-start(bf16[32,128,128]{2,1,0:T(8,128)(2,1)S(1)} %all-to-all-done.2.refs_4_), channel_id=1, source_target_pairs={{0,48},{16,0},{32,16},{48,32},{1,49},{17,1},{33,17},{49,33},{2,50}... | collective-permute-start | bytes 3145736 | tf_op jit(solution)/shard_map/ppermute | solution.py:363
  101.4 25.3 %collective-permute-start.4 = (bf16[32,128,128]{2,1,0:T(8,128)(2,1)S(1)}, bf16[32,128,128]{2,1,0:T(8,128)(2,1)S(1)}, u32[]{:S(2)}, u32[]{:S(2)}) collective-permute-start(bf16[32,128,128]{2,1,0:T(8,128)(2,1)S(1)} %all-to-all-done.2.refs_4_), channel_id=1, source_target_pairs={{0,16},{16,32},{32,48},{48,0},{1,17},{17,33},{33,49},{49,1},{2,18}... | collective-permute-start | bytes 3145736 | tf_op jit(solution)/shard_map/ppermute | solution.py:363
  103.2 2.8 %collective-permute-start.8 = (bf16[8,2,128,128]{3,2,1,0:T(8,128)(2,1)}, bf16[8,2,128,128]{3,2,1,0:T(8,128)(2,1)S(1)}, u32[]{:S(2)}, u32[]{:S(2)}) collective-permute-start(bf16[8,2,128,128]{3,2,1,0:T(8,128)(2,1)} %collective-permute-done.2.refs_0_), channel_id=1, source_target_pairs={{0,8},{8,0},{1,9},{9,1},{2,10},{10,2},{3,11},{11,3},{4,12},{12,4},... | collective-permute-start | bytes 1572872 | tf_op jit(solution)/shard_map/ppermute | solution.py:379
  103.2 2.8 %collective-permute-start.9 = (bf16[8,2,128,128]{3,2,1,0:T(8,128)(2,1)S(1)}, bf16[8,2,128,128]{3,2,1,0:T(8,128)(2,1)S(1)}, u32[]{:S(2)}, u32[]{:S(2)}) collective-permute-start(bf16[8,2,128,128]{3,2,1,0:T(8,128)(2,1)S(1)} %slice.4.refs_1_), channel_id=1, source_target_pairs={{0,8},{8,0},{1,9},{9,1},{2,10},{10,2},{3,11},{11,3},{4,12},{12,4},... | collective-permute-start | bytes 1572872 | tf_op jit(solution)/shard_map/ppermute | solution.py:379
  103.7 2.9 %collective-permute-start.10 = (bf16[8,2,128,128]{3,2,1,0:T(8,128)(2,1)S(1)}, bf16[8,2,128,128]{3,2,1,0:T(8,128)(2,1)S(1)}, u32[]{:S(2)}, u32[]{:S(2)}) collective-permute-start(bf16[8,2,128,128]{3,2,1,0:T(8,128)(2,1)S(1)} %collective-permute-done.3.refs_2_), channel_id=1, source_target_pairs={{0,8},{8,0},{1,9},{9,1},{2,10},{10,2},{3,11},{11,3},{4,12},{12,4},... | collective-permute-start | bytes 1572872 | tf_op jit(solution)/shard_map/ppermute | solution.py:379
  106.0 0.8 copy-start.12
  106.0 1.0 copy-start.13
  106.9 0.8 copy-start.14
  125.2 2.1 copy-start.21
  126.7 1.0 copy-start.22
  126.7 20.1 %collective-permute-start.12 = (bf16[8,2,128,128]{3,2,1,0:T(8,128)(2,1)}, bf16[8,2,128,128]{3,2,1,0:T(8,128)(2,1)S(1)}, u32[]{:S(2)}, u32[]{:S(2)}) collective-permute-start(bf16[8,2,128,128]{3,2,1,0:T(8,128)(2,1)} %get-tuple-element.78), channel_id=1, source_target_pairs={{0,8},{8,0},{1,9},{9,1},{2,10},{10,2},{3,11},{11,3},{4,12},{12,4},... | collective-permute-start | bytes 1572872 | tf_op jit(solution)/shard_map/ppermute | solution.py:379
  126.7 20.6 %collective-permute-start.14 = (bf16[8,2,128,128]{3,2,1,0:T(8,128)(2,1)}, bf16[8,2,128,128]{3,2,1,0:T(8,128)(2,1)S(1)}, u32[]{:S(2)}, u32[]{:S(2)}) collective-permute-start(bf16[8,2,128,128]{3,2,1,0:T(8,128)(2,1)} %get-tuple-element.82), channel_id=1, source_target_pairs={{0,8},{8,0},{1,9},{9,1},{2,10},{10,2},{3,11},{11,3},{4,12},{12,4},... | collective-permute-start | bytes 1572872 | tf_op jit(solution)/shard_map/ppermute | solution.py:379
  127.7 19.1 %copy-start.11 = (bf16[8,2,128,128]{3,2,1,0:T(8,128)(2,1)S(1)}, bf16[8,2,128,128]{3,2,1,0:T(8,128)(2,1)}, u32[]{:S(2)}) copy-start(bf16[8,2,128,128]{3,2,1,0:T(8,128)(2,1)} %get-tuple-element.76) | copy-start | bytes 1572868
  127.7 41.4 %collective-permute-start.11 = (bf16[8,2,128,128]{3,2,1,0:T(8,128)(2,1)}, bf16[8,2,128,128]{3,2,1,0:T(8,128)(2,1)S(1)}, u32[]{:S(2)}, u32[]{:S(2)}) collective-permute-start(bf16[8,2,128,128]{3,2,1,0:T(8,128)(2,1)} %get-tuple-element.74), channel_id=1, source_target_pairs={{0,8},{8,0},{1,9},{9,1},{2,10},{10,2},{3,11},{11,3},{4,12},{12,4},... | collective-permute-start | bytes 1572872 | tf_op jit(solution)/shard_map/ppermute | solution.py:379
  146.8 1.0 copy-start.10
  147.0 22.1 %collective-permute-start.13 = (bf16[8,2,128,128]{3,2,1,0:T(8,128)(2,1)S(1)}, bf16[8,2,128,128]{3,2,1,0:T(8,128)(2,1)S(1)}, u32[]{:S(2)}, u32[]{:S(2)}) collective-permute-start(bf16[8,2,128,128]{3,2,1,0:T(8,128)(2,1)S(1)} %add_convert_fusion.1), channel_id=1, source_target_pairs={{0,112},{16,0},{32,16},{48,32},{64,48},{80,64},{96,80},{112,96},{1... | collective-permute-start | bytes 1572872 | tf_op jit(solution)/shard_map/ppermute | solution.py:363
  148.0 21.1 %collective-permute-start.15 = (bf16[8,2,128,128]{3,2,1,0:T(8,128)(2,1)S(1)}, bf16[8,2,128,128]{3,2,1,0:T(8,128)(2,1)S(1)}, u32[]{:S(2)}, u32[]{:S(2)}) collective-permute-start(bf16[8,2,128,128]{3,2,1,0:T(8,128)(2,1)S(1)} %add_convert_fusion), channel_id=1, source_target_pairs={{0,16},{16,32},{32,48},{48,64},{64,80},{80,96},{96,112},{112,0},{1... | collective-permute-start | bytes 1572872 | tf_op jit(solution)/shard_map/ppermute | solution.py:363
  149.3 38.4 %collective-permute-start.6 = (bf16[16,2,128,128]{3,2,1,0:T(8,128)(2,1)}, bf16[16,2,128,128]{3,2,1,0:T(8,128)(2,1)S(1)}, u32[]{:S(2)}, u32[]{:S(2)}) collective-permute-start(bf16[16,2,128,128]{3,2,1,0:T(8,128)(2,1)} %get-tuple-element.64), channel_id=1, source_target_pairs={{0,48},{16,0},{32,16},{48,32},{1,49},{17,1},{33,17},{49,33},{2,50}... | collective-permute-start | bytes 3145736 | tf_op jit(solution)/shard_map/ppermute | solution.py:363
  151.4 36.3 %collective-permute-start.7 = (bf16[16,2,128,128]{3,2,1,0:T(8,128)(2,1)}, bf16[16,2,128,128]{3,2,1,0:T(8,128)(2,1)S(1)}, u32[]{:S(2)}, u32[]{:S(2)}) collective-permute-start(bf16[16,2,128,128]{3,2,1,0:T(8,128)(2,1)} %get-tuple-element.65), channel_id=1, source_target_pairs={{0,16},{16,32},{32,48},{48,0},{1,17},{17,33},{33,49},{49,1},{2,18}... | collective-permute-start | bytes 3145736 | tf_op jit(solution)/shard_map/ppermute | solution.py:363
  169.1 1.0 copy-start.16
  169.1 1.1 copy-start.17
  169.1 0.8 copy-start.18
  172.7 12.9 %copy-start.15 = (bf16[16,128,128]{2,1,0:T(8,128)(2,1)S(1)}, bf16[16,128,128]{2,1,0:T(8,128)(2,1)}, u32[]{:S(2)}) copy-start(bf16[16,128,128]{2,1,0:T(8,128)(2,1)} %get-tuple-element.61) | copy-start | bytes 1572868
  172.7 23.5 %all-to-all-start.4 = ((bf16[8,3,128,128]{3,2,1,0:T(8,128)(2,1)}), bf16[8,3,128,128]{3,2,1,0:T(8,128)(2,1)S(1)}, u32[]{:S(2)}, u32[]{:S(2)}) async-start(bf16[8,3,128,128]{3,2,1,0:T(8,128)(2,1)} %total_grads.1), calls=%async_computation.4 | async-start | bytes 1572864 | tf_op jit(solution)/shard_map/all_to_all | solution.py:371
  182.4 25.2 %collective-permute-start.16 = (bf16[16,2,128,128]{3,2,1,0:T(8,128)(2,1)}, bf16[16,2,128,128]{3,2,1,0:T(8,128)(2,1)}, u32[]{:S(2)}, u32[]{:S(2)}) collective-permute-start(bf16[16,2,128,128]{3,2,1,0:T(8,128)(2,1)} %get-tuple-element.86), channel_id=1, source_target_pairs={{0,48},{16,0},{32,16},{48,32},{1,49},{17,1},{33,17},{49,33},{2,50}... | collective-permute-start | bytes 3145736 | tf_op jit(solution)/shard_map/ppermute | solution.py:363
  185.6 25.0 %collective-permute-start.17 = (bf16[16,2,128,128]{3,2,1,0:T(8,128)(2,1)}, bf16[16,2,128,128]{3,2,1,0:T(8,128)(2,1)}, u32[]{:S(2)}, u32[]{:S(2)}) collective-permute-start(bf16[16,2,128,128]{3,2,1,0:T(8,128)(2,1)} %get-tuple-element.87), channel_id=1, source_target_pairs={{0,16},{16,32},{32,48},{48,0},{1,17},{17,33},{33,49},{49,1},{2,18}... | collective-permute-start | bytes 3145736 | tf_op jit(solution)/shard_map/ppermute | solution.py:363
  187.7 22.9 %copy-start.5 = (bf16[16,2,128,128]{3,2,1,0:T(8,128)(2,1)}, bf16[16,2,128,128]{3,2,1,0:T(8,128)(2,1)S(1)}, u32[]{:S(2)}) copy-start(bf16[16,2,128,128]{3,2,1,0:T(8,128)(2,1)S(1)} %collective-permute-done.6.right0) | copy-start | bytes 3145732
  187.7 8.5 %copy-start.6 = (bf16[16,2,128,128]{3,2,1,0:T(8,128)(2,1)}, bf16[16,2,128,128]{3,2,1,0:T(8,128)(2,1)S(1)}, u32[]{:S(2)}) copy-start(bf16[16,2,128,128]{3,2,1,0:T(8,128)(2,1)S(1)} %collective-permute-done.7.left0) | copy-start | bytes 3145732
  196.2 19.4 %copy-start.1 = (bf16[8,3,128,128]{3,2,1,0:T(8,128)(2,1)}, bf16[8,3,128,128]{3,2,1,0:T(8,128)(2,1)S(1)}, u32[]{:S(2)}) copy-start(bf16[8,3,128,128]{3,2,1,0:T(8,128)(2,1)S(1)} %all-to-all-done.4.b_ref) | copy-start | bytes 2359300
  196.2 21.6 %all-to-all-start.5 = ((bf16[32,128,128]{2,1,0:T(8,128)(2,1)}), bf16[32,128,128]{2,1,0:T(8,128)(2,1)S(1)}, u32[]{:S(2)}, u32[]{:S(2)}) async-start(bf16[32,128,128]{2,1,0:T(8,128)(2,1)} %pad_maximum_fusion), calls=%async_computation.5 | async-start | bytes 2097152 | tf_op jit(solution)/shard_map/all_to_all | solution.py:371
  217.8 1.0 copy-start.3
  218.8 34.6 %all-to-all-start.6 = ((bf16[32,2,128,128]{3,2,1,0:T(8,128)(2,1)}), bf16[32,2,128,128]{3,2,1,0:T(8,128)(2,1)S(1)}, u32[]{:S(2)}, u32[]{:S(2)}) async-start(bf16[32,2,128,128]{3,2,1,0:T(8,128)(2,1)} %bitcast.20), calls=%async_computation.6 | async-start | bytes 4194304 | tf_op jit(solution)/shard_map/all_to_all | solution.py:371
  253.3 1.4 copy-start

commit v13 on v12

--- a/solution.py
+++ b/solution.py
@@ -384,7 +384,8 @@
     last, size = lax.axis_size("x") - 1, 2 * BPD
     packed = jnp.concatenate([key_blocks, block_count[:, :, None]], axis=2)
     b = fifth_heads(key_in, value_in, query_in, out_grad)
-    gathered = lax.all_gather(after(packed, b), ("half", "core"))
+    ka, va, qda = split_heads(*lax.optimization_barrier((key_in, value_in, query_in, out_grad, b))[:4])
+    gathered = lax.all_gather(after(packed, ka), ("half", "core"))
     runs_first = [(h * (last + 1) + x - 1) * size for h in (0, 1, half)]
     heads = BPD * (MAXK + 1)
     places = []
@@ -395,7 +396,6 @@
     places += [0, core * BPD, 0, 0, ((2 * half + core) * HPG + HPG - 1) * heads, runs_first[2], 0]
     places = jnp.stack([jnp.asarray(p, jnp.int32) for p in places])
     lists, places = lax.optimization_barrier((gathered.reshape(-1), places))
-    ka, va, qda = split_heads(*lax.optimization_barrier((key_in, value_in, query_in, out_grad, b))[:4])
 
     own_b = exchange(b, "group")
     pairs_b = own_b[:, :2]

time: 261 us -> 256 us (0.981)
  starting transfers between devices: 69.5 us -> 64.5 us
    all_to_all x7, starting transfers between devices: 53 us -> 49.1 us  [exchange(): return lax.all_to_all(x, axes, 0, 0, tiled=True)]
  transfers between devices with their start and end apart: 25 -> 25, of which waited for: 16 -> 16; matrix products, arithmetic and copies ran while one was open for 2% -> 2% of each run, Pallas kernels for 25% -> 26%
where the time goes in v13:
time: 256 us; the launch traced here: 255 us
  waiting for transfers between devices  99.3 us (39%)
  Pallas kernels  72.3 us (28%)
  starting transfers between devices  64.5 us (25%)
  local copies, waits for them, and re-layouts  7.49 us (3%)
  blocking collectives  7.04 us (3%)
  other arithmetic  3.13 us (1%)
    all_to_all x7, waiting for transfers between devices, exchange(): return lax.all_to_all(x, axes, 0, 0, tiled=True)  53.6 us
    pallas_call x3, Pallas kernels, attention(): pl.pallas_call(functools.partial(attention_kernel, part, size, n_query, f...  49.8 us
    all_to_all x7, starting transfers between devices, exchange(): return lax.all_to_all(x, axes, 0, 0, tiled=True)  49.1 us
    ppermute x12, waiting for transfers between devices, shift(): lax.ppermute(value, axes, [(s, (s + steps) % count) for s in range(count)])  43.1 us
    ppermute x12, starting transfers between devices, shift(): lax.ppermute(value, axes, [(s, (s + steps) % count) for s in range(count)])  14.1 us
    pallas_call x2, Pallas kernels, join_heads(): pl.pallas_call(functools.partial(join_kernel, first), grid=(groups // ste...  7.73 us
    all_gather x1, blocking collectives, shards(): gathered = lax.all_gather(after(packed, ka), ('half', 'core'))  7.04 us
    unnamed x46, local copies, waits for them, and re-layouts  5.86 us
  transfers between devices with their start and end apart: 25, of which 16 were waited for; matrix products, arithmetic and copies ran while one was open for 2% of the time, Pallas kernels for 26%

profile of v13, /device:TPU:8, one launch (start us, length us, event | category | flops | bytes accessed | tf_op | source)
XLA Modules:
  0.0 254.7 jit_solution(10755022709559586656)
XLA Ops:
  0.6 2.2 fifth_heads.1
  2.9 8.2 %all-to-all-start = ((bf16[8,4,128,128]{3,2,1,0:T(8,128)(2,1)}), bf16[8,4,128,128]{3,2,1,0:T(8,128)(2,1)S(1)}, u32[]{:S(2)}, u32[]{:S(2)}) async-start(bf16[8,4,128,128]{3,2,1,0:T(8,128)(2,1)} %fifth_heads.1), calls=%async_computation | async-start | bytes 2097152 | tf_op jit(solution)/shard_map/all_to_all | solution.py:371
  11.1 0.1 copy.11
  11.2 5.1 %split_heads.1 = (bf16[4,8,128,128]{3,2,1,0:T(8,128)(2,1)}, bf16[4,8,128,128]{3,2,1,0:T(8,128)(2,1)}, bf16[4,8,2,128,128]{4,3,2,1,0:T(8,128)(2,1)}) custom-call(bf16[128,5120]{1,0:T(8,128)(2,1)} %k_ref.2, bf16[128,5120]{1,0:T(8,128)(2,1)} %v_ref.2, bf16[128,5120]{1,0:T(8,128)(2,1)} %q_ref.2, bf16[128,5120]{1,0:T(8,128)(2,1)} %g_ref.2), custom_call_target="tpu_custom_call" | custom-call | bytes 10485760 | tf_op jit(solution)/shard_map/split_heads/pallas_call | solution.py:227
  16.3 0.1 pad_add_fusion
  16.4 7.0 %all-gather = s32[20,8,13]{2,1,0:T(8,128)S(1)} all-gather(s32[5,8,13]{2,1,0:T(8,128)S(1)} %pad_add_fusion), channel_id=2, replica_groups=mesh['half'=2,'x'=4,'core'=2,'group'=8] {'half','core'}, dimensions={0}, use_global_device_ids=true | all-gather | bytes 10400 | tf_op jit(solution)/shard_map/all_gather | solution.py:388
  23.4 0.8 reshape.25.lists_ref
  24.2 0.7 stack.53.places_ref
  24.9 2.2 all-to-all-done.refs_6_
  27.1 7.3 %all-to-all-start.1 = ((bf16[32,128,128]{2,1,0:T(8,128)(2,1)}), bf16[32,128,128]{2,1,0:T(8,128)(2,1)S(1)}, u32[]{:S(2)}, u32[]{:S(2)}) async-start(bf16[32,128,128]{2,1,0:T(8,128)(2,1)} %bitcast.24), calls=%async_computation.1 | async-start | bytes 2097152 | tf_op jit(solution)/shard_map/all_to_all | solution.py:371
  34.5 3.7 %collective-permute-start.3 = (bf16[8,2,128,128]{3,2,1,0:T(8,128)(2,1)S(1)}, bf16[8,2,128,128]{3,2,1,0:T(8,128)(2,1)S(1)}, u32[]{:S(2)}, u32[]{:S(2)}) collective-permute-start(bf16[8,2,128,128]{3,2,1,0:T(8,128)(2,1)S(1)} %slice.4.refs_1_), channel_id=1, source_target_pairs={{0,112},{16,0},{32,16},{48,32},{64,48},{80,64},{96,80},{112,96},{1... | collective-permute-start | bytes 1572872 | tf_op jit(solution)/shard_map/ppermute | solution.py:363
  38.2 18.0 %collective-permute-done.3.refs_2_ = bf16[8,2,128,128]{3,2,1,0:T(8,128)(2,1)S(1)} collective-permute-done((bf16[8,2,128,128]{3,2,1,0:T(8,128)(2,1)S(1)}, bf16[8,2,128,128]{3,2,1,0:T(8,128)(2,1)S(1)}, u32[]{:S(2)}, u32[]{:S(2)}) %collective-permute-start.3) | collective-permute-done | bytes 524320 | tf_op jit(solution)/shard_map/ppermute | solution.py:363
  56.2 2.5 collective-permute-done.2.refs_0_
  58.7 1.7 all-to-all-done.1.refs_1_
  60.4 6.9 %all-to-all-start.2 = ((bf16[32,128,128]{2,1,0:T(8,128)(2,1)}), bf16[32,128,128]{2,1,0:T(8,128)(2,1)S(1)}, u32[]{:S(2)}, u32[]{:S(2)}) async-start(bf16[32,128,128]{2,1,0:T(8,128)(2,1)} %bitcast.23), calls=%async_computation.2 | async-start | bytes 2097152 | tf_op jit(solution)/shard_map/all_to_all | solution.py:371
  67.4 2.4 collective-permute-start.1
  69.8 14.3 %all-to-all-done.2.refs_4_ = bf16[32,128,128]{2,1,0:T(8,128)(2,1)S(1)} async-done(((bf16[32,128,128]{2,1,0:T(8,128)(2,1)}), bf16[32,128,128]{2,1,0:T(8,128)(2,1)S(1)}, u32[]{:S(2)}, u32[]{:S(2)}) %all-to-all-start.2) | async-done | bytes 1048608 | tf_op jit(solution)/shard_map/all_to_all | solution.py:371
  84.1 5.6 %all-to-all-start.3 = ((bf16[32,2,128,128]{3,2,1,0:T(8,128)(2,1)}), bf16[32,2,128,128]{3,2,1,0:T(8,128)(2,1)}, u32[]{:S(2)}, u32[]{:S(2)}) async-start(bf16[32,2,128,128]{3,2,1,0:T(8,128)(2,1)} %bitcast.22), calls=%async_computation.3 | async-start | bytes 4194304 | tf_op jit(solution)/shard_map/all_to_all | solution.py:371
  89.7 3.0 %collective-permute-done.1.refs_2_ = bf16[32,128,128]{2,1,0:T(8,128)(2,1)} collective-permute-done((bf16[32,128,128]{2,1,0:T(8,128)(2,1)S(1)}, bf16[32,128,128]{2,1,0:T(8,128)(2,1)}, u32[]{:S(2)}, u32[]{:S(2)}) %collective-permute-start.1) | collective-permute-done | bytes 1048608 | tf_op jit(solution)/shard_map/ppermute | solution.py:363
  92.8 3.2 %collective-permute-done.refs_0_ = bf16[32,128,128]{2,1,0:T(8,128)(2,1)} collective-permute-done((bf16[32,128,128]{2,1,0:T(8,128)(2,1)S(1)}, bf16[32,128,128]{2,1,0:T(8,128)(2,1)}, u32[]{:S(2)}, u32[]{:S(2)}) %collective-permute-start) | collective-permute-done | bytes 1048608 | tf_op jit(solution)/shard_map/ppermute | solution.py:363
  96.0 0.3 collective-permute-start.5
  96.3 1.7 collective-permute-start.4
  98.0 0.5 collective-permute-start.9
  98.6 0.3 collective-permute-start.10
  98.8 2.0 collective-permute-done.8.refs_3_
  100.9 0.6 collective-permute-done.10.refs_5_
  101.5 0.2 copy-done.12
  101.6 0.2 copy-done.13
  101.8 0.8 copy-done.14
  102.6 12.5 %attention.5 = (bf16[8,128,128]{2,1,0:T(8,128)(2,1)}, bf16[8,2,128,128]{3,2,1,0:T(8,128)(2,1)}, bf16[8,2,128,128]{3,2,1,0:T(8,128)(2,1)}, bf16[8,2,128,128]{3,2,...) custom-call(s32[2080]{0:T(1024)} %reshape.25.lists_ref, ...), custom_call_target="tpu_custom_call" | custom-call | tf_op jit(solution)/shard_map/attention/pallas_call | solution.py:182
  115.1 5.0 %collective-permute-done.5.refs_5_ = bf16[32,128,128]{2,1,0:T(8,128)(2,1)S(1)} collective-permute-done((bf16[32,128,128]{2,1,0:T(8,128)(2,1)S(1)}, bf16[32,128,128]{2,1,0:T(8,128)(2,1)S(1)}, u32[]{:S(2)}, u32[]{:S(2)}) %collective-permute-start.5) | collective-permute-done | bytes 1048608 | tf_op jit(solution)/shard_map/ppermute | solution.py:363
  120.1 1.5 collective-permute-done.4.refs_3_
  121.6 0.5 collective-permute-start.14
  122.1 0.5 copy-done.22
  122.6 19.3 %attention.3 = (bf16[16,128,128]{2,1,0:T(8,128)(2,1)}, bf16[16,2,128,128]{3,2,1,0:T(8,128)(2,1)}, bf16[16,2,128,128]{3,2,1,0:T(8,128)(2,1)}, bf16[16,2,128,128]{3,2,1,0:T(8,128)(2,1)}) custom-call(s32[2080]{0:T(1024)} %reshape.25.lists_ref, s32[21]{0:T(128)} %stack.53.places_ref, bf16[32,128,128]{2,1,0:T(8,128)(2,1)} %collective-permute-done.refs_0_, ...), custom_call_target="tpu_custom_call" | custom-call | flops 2684354560 | bytes 7340032 | tf_op jit(solution)/shard_map/attention/pallas_call | solution.py:182
  142.0 0.1 add_convert_fusion.1
  142.1 0.1 collective-permute-start.13
  142.2 0.8 copy-done.10
  143.0 0.1 add_convert_fusion
  143.1 1.3 collective-permute-start.15
  144.4 1.6 collective-permute-start.6
  146.0 0.4 collective-permute-start.7
  146.5 18.0 %attention.4 = (bf16[16,128,128]{2,1,0:T(8,128)(2,1)}, bf16[16,2,128,128]{3,2,1,0:T(8,128)(2,1)}, bf16[16,2,128,128]{3,2,1,0:T(8,128)(2,1)}, bf16[16,2,128,128]{3,2,1,0:T(8,128)(2,1)}) custom-call(s32[2080]{0:T(1024)} %reshape.25.lists_ref, s32[21]{0:T(128)} %stack.53.places_ref, bf16[32,128,128]{2,1,0:T(8,128)(2,1)} %collective-permute-done.refs_0_, ...), custom_call_target="tpu_custom_call" | custom-call | flops 2684354560 | bytes 7340032 | tf_op jit(solution)/shard_map/attention/pallas_call | solution.py:182
  164.5 0.0 copy-start.16
  164.5 0.8 copy-done.18
  165.4 0.1 copy-done.16
  165.4 0.2 copy-done.17
  165.6 2.5 total_grads.1
  168.1 9.6 %all-to-all-start.4 = ((bf16[8,3,128,128]{3,2,1,0:T(8,128)(2,1)}), bf16[8,3,128,128]{3,2,1,0:T(8,128)(2,1)S(1)}, u32[]{:S(2)}, u32[]{:S(2)}) async-start(bf16[8,3,128,128]{3,2,1,0:T(8,128)(2,1)} %total_grads.1), calls=%async_computation.4 | async-start | bytes 1572864 | tf_op jit(solution)/shard_map/all_to_all | solution.py:371
  177.7 2.5 collective-permute-start.16
  180.2 2.1 pad_maximum_fusion
  182.3 8.5 %all-to-all-done.4.b_ref = bf16[8,3,128,128]{3,2,1,0:T(8,128)(2,1)S(1)} async-done(((bf16[8,3,128,128]{3,2,1,0:T(8,128)(2,1)}), bf16[8,3,128,128]{3,2,1,0:T(8,128)(2,1)S(1)}, u32[]{:S(2)}, u32[]{:S(2)}) %all-to-all-start.4) | async-done | bytes 786464 | tf_op jit(solution)/shard_map/all_to_all | solution.py:371
  190.8 4.8 %all-to-all-start.5 = ((bf16[32,128,128]{2,1,0:T(8,128)(2,1)}), bf16[32,128,128]{2,1,0:T(8,128)(2,1)S(1)}, u32[]{:S(2)}, u32[]{:S(2)}) async-start(bf16[32,128,128]{2,1,0:T(8,128)(2,1)} %pad_maximum_fusion), calls=%async_computation.5 | async-start | bytes 2097152 | tf_op jit(solution)/shard_map/all_to_all | solution.py:371
  195.6 0.7 pad_add_fusion.1.x_ref
  196.2 6.4 %collective-permute-done.16.right1 = bf16[16,2,128,128]{3,2,1,0:T(8,128)(2,1)} collective-permute-done((bf16[16,2,128,128]{3,2,1,0:T(8,128)(2,1)}, bf16[16,2,128,128]{3,2,1,0:T(8,128)(2,1)}, u32[]{:S(2)}, u32[]{:S(2)}) %collective-permute-start.16) | collective-permute-done | bytes 1048608 | tf_op jit(solution)/shard_map/ppermute | solution.py:363
  202.7 3.4 %collective-permute-done.17.left1 = bf16[16,2,128,128]{3,2,1,0:T(8,128)(2,1)} collective-permute-done((bf16[16,2,128,128]{3,2,1,0:T(8,128)(2,1)}, bf16[16,2,128,128]{3,2,1,0:T(8,128)(2,1)}, u32[]{:S(2)}, u32[]{:S(2)}) %collective-permute-start.17) | collective-permute-done | bytes 1048608 | tf_op jit(solution)/shard_map/ppermute | solution.py:363
  206.1 5.0 %both_halves.1 = bf16[2,16,2,128,128]{4,3,2,1,0:T(8,128)(2,1)} custom-call(s32[2]{0:T(128)} %pad_add_fusion.1.x_ref, bf16[16,2,128,128]{3,2,1,0:T(8,128)(2,1)} %get-tuple-element.84.own0, bf16[16,2,128,128]{3,2,1,0:T(8,128)(2,1)} %get-tuple-element.85.own1, bf16[16,2,128,128]{3,2,1,0:T(8,128)(2,1)} %copy-done.5, ...), custom_call_target="tpu_custom_call" | custom-call | bytes 8388608 | tf_op jit(solution)/shard_map/both_halves/pallas_call | solution.py:344
  211.1 1.3 all-to-all-done.5
  212.4 1.0 copy-done.3
  213.3 6.7 %all-to-all-start.6 = ((bf16[32,2,128,128]{3,2,1,0:T(8,128)(2,1)}), bf16[32,2,128,128]{3,2,1,0:T(8,128)(2,1)S(1)}, u32[]{:S(2)}, u32[]{:S(2)}) async-start(bf16[32,2,128,128]{3,2,1,0:T(8,128)(2,1)} %bitcast.20), calls=%async_computation.6 | async-start | bytes 4194304 | tf_op jit(solution)/shard_map/all_to_all | solution.py:371
  220.1 3.6 %join_heads.2 = bf16[128,5120]{1,0:T(8,128)(2,1)} custom-call(bf16[4,8,1,128,128]{4,3,2,1,0:T(8,128)(2,1)} %bitcast.21, bf16[8,3,128,128]{3,2,1,0:T(8,128)(2,1)} %copy-done.1), custom_call_target="tpu_custom_call" | custom-call | bytes 2621440 | tf_op jit(solution)/shard_map/join_heads/pallas_call | solution.py:290
  223.7 25.5 %all-to-all-done.6 = bf16[32,2,128,128]{3,2,1,0:T(8,128)(2,1)S(1)} async-done(((bf16[32,2,128,128]{3,2,1,0:T(8,128)(2,1)}), bf16[32,2,128,128]{3,2,1,0:T(8,128)(2,1)S(1)}, u32[]{:S(2)}, u32[]{:S(2)}) %all-to-all-start.6) | async-done | bytes 2097184 | tf_op jit(solution)/shard_map/all_to_all | solution.py:371
  249.2 1.4 copy-done
  250.6 4.1 %join_heads.3 = (bf16[128,5120]{1,0:T(8,128)(2,1)}, bf16[128,5120]{1,0:T(8,128)(2,1)}) custom-call(bf16[4,8,2,128,128]{4,3,2,1,0:T(8,128)(2,1)} %bitcast.19, bf16[8,3,128,128]{3,2,1,0:T(8,128)(2,1)} %copy-done.1), custom_call_target="tpu_custom_call" | custom-call | bytes 5242880 | tf_op jit(solution)/shard_map/join_heads/pallas_call | solution.py:290
  (52 shorter events, 0.2 us)
Async XLA Ops:
  2.8 8.3 %copy-start.20 = (s32[5,8]{1,0:T(8,128)S(1)}, s32[5,8]{1,0:T(8,128)}, u32[]{:S(2)}) copy-start(s32[5,8]{1,0:T(8,128)} %param.11) | copy-start | bytes 484
  2.9 24.3 %all-to-all-start = ((bf16[8,4,128,128]{3,2,1,0:T(8,128)(2,1)}), bf16[8,4,128,128]{3,2,1,0:T(8,128)(2,1)S(1)}, u32[]{:S(2)}, u32[]{:S(2)}) async-start(bf16[8,4,128,128]{3,2,1,0:T(8,128)(2,1)} %fifth_heads.1), calls=%async_computation | async-start | bytes 2097152 | tf_op jit(solution)/shard_map/all_to_all | solution.py:371
  11.2 5.1 %copy-start.19 = (s32[5,8,12]{2,1,0:T(8,128)S(1)}, s32[5,8,12]{2,1,0:T(8,128)}, u32[]{:S(2)}) copy-start(s32[5,8,12]{2,1,0:T(8,128)} %param.10) | copy-start | bytes 5764
  27.1 7.3 %copy-start.2 = (bf16[8,4,128,128]{3,2,1,0:T(8,128)(2,1)}, bf16[8,4,128,128]{3,2,1,0:T(8,128)(2,1)S(1)}, u32[]{:S(2)}) copy-start(bf16[8,4,128,128]{3,2,1,0:T(8,128)(2,1)S(1)} %all-to-all-done.refs_6_) | copy-start | bytes 3145732
  27.1 33.3 %all-to-all-start.1 = ((bf16[32,128,128]{2,1,0:T(8,128)(2,1)}), bf16[32,128,128]{2,1,0:T(8,128)(2,1)S(1)}, u32[]{:S(2)}, u32[]{:S(2)}) async-start(bf16[32,128,128]{2,1,0:T(8,128)(2,1)} %bitcast.24), calls=%async_computation.1 | async-start | bytes 2097152 | tf_op jit(solution)/shard_map/all_to_all | solution.py:371
  34.5 63.6 %copy-start.4 = (bf16[8,2,128,128]{3,2,1,0:T(8,128)(2,1)}, bf16[8,2,128,128]{3,2,1,0:T(8,128)(2,1)S(1)}, u32[]{:S(2)}) copy-start(bf16[8,2,128,128]{3,2,1,0:T(8,128)(2,1)S(1)} %slice.4.refs_1_) | copy-start | bytes 1572868
  34.5 21.7 %collective-permute-start.3 = (bf16[8,2,128,128]{3,2,1,0:T(8,128)(2,1)S(1)}, bf16[8,2,128,128]{3,2,1,0:T(8,128)(2,1)S(1)}, u32[]{:S(2)}, u32[]{:S(2)}) collective-permute-start(bf16[8,2,128,128]{3,2,1,0:T(8,128)(2,1)S(1)} %slice.4.refs_1_), channel_id=1, source_target_pairs={{0,112},{16,0},{32,16},{48,32},{64,48},{80,64},{96,80},{112,96},{1... | collective-permute-start | bytes 1572872 | tf_op jit(solution)/shard_map/ppermute | solution.py:363
  38.2 20.5 %collective-permute-start.2 = (bf16[8,2,128,128]{3,2,1,0:T(8,128)(2,1)S(1)}, bf16[8,2,128,128]{3,2,1,0:T(8,128)(2,1)}, u32[]{:S(2)}, u32[]{:S(2)}) collective-permute-start(bf16[8,2,128,128]{3,2,1,0:T(8,128)(2,1)S(1)} %slice.4.refs_1_), channel_id=1, source_target_pairs={{0,16},{16,32},{32,48},{48,64},{64,80},{80,96},{96,112},{112,0},{1... | collective-permute-start | bytes 1572872 | tf_op jit(solution)/shard_map/ppermute | solution.py:363
  56.2 42.3 %copy-start.9 = (bf16[8,2,128,128]{3,2,1,0:T(8,128)(2,1)}, bf16[8,2,128,128]{3,2,1,0:T(8,128)(2,1)S(1)}, u32[]{:S(2)}) copy-start(bf16[8,2,128,128]{3,2,1,0:T(8,128)(2,1)S(1)} %collective-permute-done.3.refs_2_) | copy-start | bytes 1572868
  60.4 23.7 %copy-start.7 = (bf16[32,128,128]{2,1,0:T(8,128)(2,1)}, bf16[32,128,128]{2,1,0:T(8,128)(2,1)S(1)}, u32[]{:S(2)}) copy-start(bf16[32,128,128]{2,1,0:T(8,128)(2,1)S(1)} %all-to-all-done.1.refs_1_) | copy-start | bytes 3145732
  60.4 23.7 %all-to-all-start.2 = ((bf16[32,128,128]{2,1,0:T(8,128)(2,1)}), bf16[32,128,128]{2,1,0:T(8,128)(2,1)S(1)}, u32[]{:S(2)}, u32[]{:S(2)}) async-start(bf16[32,128,128]{2,1,0:T(8,128)(2,1)} %bitcast.23), calls=%async_computation.2 | async-start | bytes 2097152 | tf_op jit(solution)/shard_map/all_to_all | solution.py:371
  67.4 25.4 %collective-permute-start.1 = (bf16[32,128,128]{2,1,0:T(8,128)(2,1)S(1)}, bf16[32,128,128]{2,1,0:T(8,128)(2,1)}, u32[]{:S(2)}, u32[]{:S(2)}) collective-permute-start(bf16[32,128,128]{2,1,0:T(8,128)(2,1)S(1)} %all-to-all-done.1.refs_1_), channel_id=1, source_target_pairs={{0,48},{16,0},{32,16},{48,32},{1,49},{17,1},{33,17},{49,33},{2,50}... | collective-permute-start | bytes 3145736 | tf_op jit(solution)/shard_map/ppermute | solution.py:363
  69.8 26.2 %collective-permute-start = (bf16[32,128,128]{2,1,0:T(8,128)(2,1)S(1)}, bf16[32,128,128]{2,1,0:T(8,128)(2,1)}, u32[]{:S(2)}, u32[]{:S(2)}) collective-permute-start(bf16[32,128,128]{2,1,0:T(8,128)(2,1)S(1)} %all-to-all-done.1.refs_1_), channel_id=1, source_target_pairs={{0,16},{16,32},{32,48},{48,0},{1,17},{17,33},{33,49},{49,1},{2,18}... | collective-permute-start | bytes 3145736 | tf_op jit(solution)/shard_map/ppermute | solution.py:363
  84.1 12.2 %copy-start.8 = (bf16[32,128,128]{2,1,0:T(8,128)(2,1)}, bf16[32,128,128]{2,1,0:T(8,128)(2,1)S(1)}, u32[]{:S(2)}) copy-start(bf16[32,128,128]{2,1,0:T(8,128)(2,1)S(1)} %all-to-all-done.2.refs_4_) | copy-start | bytes 3145732
  84.1 38.5 %all-to-all-start.3 = ((bf16[32,2,128,128]{3,2,1,0:T(8,128)(2,1)}), bf16[32,2,128,128]{3,2,1,0:T(8,128)(2,1)}, u32[]{:S(2)}, u32[]{:S(2)}) async-start(bf16[32,2,128,128]{3,2,1,0:T(8,128)(2,1)} %bitcast.22), calls=%async_computation.3 | async-start | bytes 4194304 | tf_op jit(solution)/shard_map/all_to_all | solution.py:371
  96.0 24.1 %collective-permute-start.5 = (bf16[32,128,128]{2,1,0:T(8,128)(2,1)S(1)}, bf16[32,128,128]{2,1,0:T(8,128)(2,1)S(1)}, u32[]{:S(2)}, u32[]{:S(2)}) collective-permute-start(bf16[32,128,128]{2,1,0:T(8,128)(2,1)S(1)} %all-to-all-done.2.refs_4_), channel_id=1, source_target_pairs={{0,48},{16,0},{32,16},{48,32},{1,49},{17,1},{33,17},{49,33},{2,50}... | collective-permute-start | bytes 3145736 | tf_op jit(solution)/shard_map/ppermute | solution.py:363
  96.3 25.3 %collective-permute-start.4 = (bf16[32,128,128]{2,1,0:T(8,128)(2,1)S(1)}, bf16[32,128,128]{2,1,0:T(8,128)(2,1)S(1)}, u32[]{:S(2)}, u32[]{:S(2)}) collective-permute-start(bf16[32,128,128]{2,1,0:T(8,128)(2,1)S(1)} %all-to-all-done.2.refs_4_), channel_id=1, source_target_pairs={{0,16},{16,32},{32,48},{48,0},{1,17},{17,33},{33,49},{49,1},{2,18}... | collective-permute-start | bytes 3145736 | tf_op jit(solution)/shard_map/ppermute | solution.py:363
  98.0 2.8 %collective-permute-start.8 = (bf16[8,2,128,128]{3,2,1,0:T(8,128)(2,1)}, bf16[8,2,128,128]{3,2,1,0:T(8,128)(2,1)S(1)}, u32[]{:S(2)}, u32[]{:S(2)}) collective-permute-start(bf16[8,2,128,128]{3,2,1,0:T(8,128)(2,1)} %collective-permute-done.2.refs_0_), channel_id=1, source_target_pairs={{0,8},{8,0},{1,9},{9,1},{2,10},{10,2},{3,11},{11,3},{4,12},{12,4},... | collective-permute-start | bytes 1572872 | tf_op jit(solution)/shard_map/ppermute | solution.py:379
  98.0 2.8 %collective-permute-start.9 = (bf16[8,2,128,128]{3,2,1,0:T(8,128)(2,1)S(1)}, bf16[8,2,128,128]{3,2,1,0:T(8,128)(2,1)S(1)}, u32[]{:S(2)}, u32[]{:S(2)}) collective-permute-start(bf16[8,2,128,128]{3,2,1,0:T(8,128)(2,1)S(1)} %slice.4.refs_1_), channel_id=1, source_target_pairs={{0,8},{8,0},{1,9},{9,1},{2,10},{10,2},{3,11},{11,3},{4,12},{12,4},... | collective-permute-start | bytes 1572872 | tf_op jit(solution)/shard_map/ppermute | solution.py:379
  98.6 2.9 %collective-permute-start.10 = (bf16[8,2,128,128]{3,2,1,0:T(8,128)(2,1)S(1)}, bf16[8,2,128,128]{3,2,1,0:T(8,128)(2,1)S(1)}, u32[]{:S(2)}, u32[]{:S(2)}) collective-permute-start(bf16[8,2,128,128]{3,2,1,0:T(8,128)(2,1)S(1)} %collective-permute-done.3.refs_2_), channel_id=1, source_target_pairs={{0,8},{8,0},{1,9},{9,1},{2,10},{10,2},{3,11},{11,3},{4,12},{12,4},... | collective-permute-start | bytes 1572872 | tf_op jit(solution)/shard_map/ppermute | solution.py:379
  100.9 0.8 copy-start.12
  100.9 1.0 copy-start.13
  101.8 0.8 copy-start.14
  120.1 2.1 copy-start.21
  121.6 1.0 copy-start.22
  121.6 20.3 %collective-permute-start.12 = (bf16[8,2,128,128]{3,2,1,0:T(8,128)(2,1)}, bf16[8,2,128,128]{3,2,1,0:T(8,128)(2,1)S(1)}, u32[]{:S(2)}, u32[]{:S(2)}) collective-permute-start(bf16[8,2,128,128]{3,2,1,0:T(8,128)(2,1)} %get-tuple-element.78), channel_id=1, source_target_pairs={{0,8},{8,0},{1,9},{9,1},{2,10},{10,2},{3,11},{11,3},{4,12},{12,4},... | collective-permute-start | bytes 1572872 | tf_op jit(solution)/shard_map/ppermute | solution.py:379
  121.6 20.6 %collective-permute-start.14 = (bf16[8,2,128,128]{3,2,1,0:T(8,128)(2,1)}, bf16[8,2,128,128]{3,2,1,0:T(8,128)(2,1)S(1)}, u32[]{:S(2)}, u32[]{:S(2)}) collective-permute-start(bf16[8,2,128,128]{3,2,1,0:T(8,128)(2,1)} %get-tuple-element.82), channel_id=1, source_target_pairs={{0,8},{8,0},{1,9},{9,1},{2,10},{10,2},{3,11},{11,3},{4,12},{12,4},... | collective-permute-start | bytes 1572872 | tf_op jit(solution)/shard_map/ppermute | solution.py:379
  122.6 19.4 %copy-start.11 = (bf16[8,2,128,128]{3,2,1,0:T(8,128)(2,1)S(1)}, bf16[8,2,128,128]{3,2,1,0:T(8,128)(2,1)}, u32[]{:S(2)}) copy-start(bf16[8,2,128,128]{3,2,1,0:T(8,128)(2,1)} %get-tuple-element.76) | copy-start | bytes 1572868
  122.6 41.9 %collective-permute-start.11 = (bf16[8,2,128,128]{3,2,1,0:T(8,128)(2,1)}, bf16[8,2,128,128]{3,2,1,0:T(8,128)(2,1)S(1)}, u32[]{:S(2)}, u32[]{:S(2)}) collective-permute-start(bf16[8,2,128,128]{3,2,1,0:T(8,128)(2,1)} %get-tuple-element.74), channel_id=1, source_target_pairs={{0,8},{8,0},{1,9},{9,1},{2,10},{10,2},{3,11},{11,3},{4,12},{12,4},... | collective-permute-start | bytes 1572872 | tf_op jit(solution)/shard_map/ppermute | solution.py:379
  141.9 1.0 copy-start.10
  142.1 22.4 %collective-permute-start.13 = (bf16[8,2,128,128]{3,2,1,0:T(8,128)(2,1)S(1)}, bf16[8,2,128,128]{3,2,1,0:T(8,128)(2,1)S(1)}, u32[]{:S(2)}, u32[]{:S(2)}) collective-permute-start(bf16[8,2,128,128]{3,2,1,0:T(8,128)(2,1)S(1)} %add_convert_fusion.1), channel_id=1, source_target_pairs={{0,112},{16,0},{32,16},{48,32},{64,48},{80,64},{96,80},{112,96},{1... | collective-permute-start | bytes 1572872 | tf_op jit(solution)/shard_map/ppermute | solution.py:363
  143.1 21.4 %collective-permute-start.15 = (bf16[8,2,128,128]{3,2,1,0:T(8,128)(2,1)S(1)}, bf16[8,2,128,128]{3,2,1,0:T(8,128)(2,1)S(1)}, u32[]{:S(2)}, u32[]{:S(2)}) collective-permute-start(bf16[8,2,128,128]{3,2,1,0:T(8,128)(2,1)S(1)} %add_convert_fusion), channel_id=1, source_target_pairs={{0,16},{16,32},{32,48},{48,64},{64,80},{80,96},{96,112},{112,0},{1... | collective-permute-start | bytes 1572872 | tf_op jit(solution)/shard_map/ppermute | solution.py:363
  144.4 37.9 %collective-permute-start.6 = (bf16[16,2,128,128]{3,2,1,0:T(8,128)(2,1)}, bf16[16,2,128,128]{3,2,1,0:T(8,128)(2,1)S(1)}, u32[]{:S(2)}, u32[]{:S(2)}) collective-permute-start(bf16[16,2,128,128]{3,2,1,0:T(8,128)(2,1)} %get-tuple-element.64), channel_id=1, source_target_pairs={{0,48},{16,0},{32,16},{48,32},{1,49},{17,1},{33,17},{49,33},{2,50}... | collective-permute-start | bytes 3145736 | tf_op jit(solution)/shard_map/ppermute | solution.py:363
  146.0 36.3 %collective-permute-start.7 = (bf16[16,2,128,128]{3,2,1,0:T(8,128)(2,1)}, bf16[16,2,128,128]{3,2,1,0:T(8,128)(2,1)S(1)}, u32[]{:S(2)}, u32[]{:S(2)}) collective-permute-start(bf16[16,2,128,128]{3,2,1,0:T(8,128)(2,1)} %get-tuple-element.65), channel_id=1, source_target_pairs={{0,16},{16,32},{32,48},{48,0},{1,17},{17,33},{33,49},{49,1},{2,18}... | collective-permute-start | bytes 3145736 | tf_op jit(solution)/shard_map/ppermute | solution.py:363
  164.5 1.0 copy-start.16
  164.5 1.1 copy-start.17
  164.5 0.8 copy-start.18
  168.1 12.1 %copy-start.15 = (bf16[16,128,128]{2,1,0:T(8,128)(2,1)S(1)}, bf16[16,128,128]{2,1,0:T(8,128)(2,1)}, u32[]{:S(2)}) copy-start(bf16[16,128,128]{2,1,0:T(8,128)(2,1)} %get-tuple-element.61) | copy-start | bytes 1572868
  168.1 22.7 %all-to-all-start.4 = ((bf16[8,3,128,128]{3,2,1,0:T(8,128)(2,1)}), bf16[8,3,128,128]{3,2,1,0:T(8,128)(2,1)S(1)}, u32[]{:S(2)}, u32[]{:S(2)}) async-start(bf16[8,3,128,128]{3,2,1,0:T(8,128)(2,1)} %total_grads.1), calls=%async_computation.4 | async-start | bytes 1572864 | tf_op jit(solution)/shard_map/all_to_all | solution.py:371
  177.7 25.0 %collective-permute-start.16 = (bf16[16,2,128,128]{3,2,1,0:T(8,128)(2,1)}, bf16[16,2,128,128]{3,2,1,0:T(8,128)(2,1)}, u32[]{:S(2)}, u32[]{:S(2)}) collective-permute-start(bf16[16,2,128,128]{3,2,1,0:T(8,128)(2,1)} %get-tuple-element.86), channel_id=1, source_target_pairs={{0,48},{16,0},{32,16},{48,32},{1,49},{17,1},{33,17},{49,33},{2,50}... | collective-permute-start | bytes 3145736 | tf_op jit(solution)/shard_map/ppermute | solution.py:363
  180.2 25.9 %collective-permute-start.17 = (bf16[16,2,128,128]{3,2,1,0:T(8,128)(2,1)}, bf16[16,2,128,128]{3,2,1,0:T(8,128)(2,1)}, u32[]{:S(2)}, u32[]{:S(2)}) collective-permute-start(bf16[16,2,128,128]{3,2,1,0:T(8,128)(2,1)} %get-tuple-element.87), channel_id=1, source_target_pairs={{0,16},{16,32},{32,48},{48,0},{1,17},{17,33},{33,49},{49,1},{2,18}... | collective-permute-start | bytes 3145736 | tf_op jit(solution)/shard_map/ppermute | solution.py:363
  182.3 23.8 %copy-start.5 = (bf16[16,2,128,128]{3,2,1,0:T(8,128)(2,1)}, bf16[16,2,128,128]{3,2,1,0:T(8,128)(2,1)S(1)}, u32[]{:S(2)}) copy-start(bf16[16,2,128,128]{3,2,1,0:T(8,128)(2,1)S(1)} %collective-permute-done.6.right0) | copy-start | bytes 3145732
  182.3 8.5 %copy-start.6 = (bf16[16,2,128,128]{3,2,1,0:T(8,128)(2,1)}, bf16[16,2,128,128]{3,2,1,0:T(8,128)(2,1)S(1)}, u32[]{:S(2)}) copy-start(bf16[16,2,128,128]{3,2,1,0:T(8,128)(2,1)S(1)} %collective-permute-done.7.left0) | copy-start | bytes 3145732
  190.8 20.3 %copy-start.1 = (bf16[8,3,128,128]{3,2,1,0:T(8,128)(2,1)}, bf16[8,3,128,128]{3,2,1,0:T(8,128)(2,1)S(1)}, u32[]{:S(2)}) copy-start(bf16[8,3,128,128]{3,2,1,0:T(8,128)(2,1)S(1)} %all-to-all-done.4.b_ref) | copy-start | bytes 2359300
  190.8 21.6 %all-to-all-start.5 = ((bf16[32,128,128]{2,1,0:T(8,128)(2,1)}), bf16[32,128,128]{2,1,0:T(8,128)(2,1)S(1)}, u32[]{:S(2)}, u32[]{:S(2)}) async-start(bf16[32,128,128]{2,1,0:T(8,128)(2,1)} %pad_maximum_fusion), calls=%async_computation.5 | async-start | bytes 2097152 | tf_op jit(solution)/shard_map/all_to_all | solution.py:371
  212.4 1.0 copy-start.3
  213.3 35.9 %all-to-all-start.6 = ((bf16[32,2,128,128]{3,2,1,0:T(8,128)(2,1)}), bf16[32,2,128,128]{3,2,1,0:T(8,128)(2,1)S(1)}, u32[]{:S(2)}, u32[]{:S(2)}) async-start(bf16[32,2,128,128]{3,2,1,0:T(8,128)(2,1)} %bitcast.20), calls=%async_computation.6 | async-start | bytes 4194304 | tf_op jit(solution)/shard_map/all_to_all | solution.py:371
  249.2 1.4 copy-start
